TPU v7x, 128 devices: a whole 4x4x4 slice. The times are simulated.
128 devices in a mesh: lat: 8 (over x_lo, y), lon: 16 (over x_hi, z, core).
Axes of the slice: x: 4 (x_hi: 2, x_lo: 2; x = x_hi * 2 + x_lo), y: 4, z: 4, core: 2. Of those that a mesh axis runs over, the one named last changes fastest.
Arguments:
- field_in: bfloat16 [256, 1024, 256], P('lat', 'lon'), may hold values from -6 to 6
- cotangent: bfloat16 [256, 1024, 256], P('lat', 'lon'), may hold values from -6 to 6
- expand_weight: bfloat16 [256, 1024], replicated, may hold values from -0.375 to 0.375
- depth_kernel: float32 [3, 3, 1024], replicated, may hold values from -2 to 2
- project_weight: bfloat16 [1024, 256], replicated, may hold values from -0.1875 to 0.1875
- qkv_weight: bfloat16 [256, 768], replicated, may hold values from -0.375 to 0.375
- out_weight: bfloat16 [256, 256], replicated, may hold values from -0.375 to 0.375
- rel_bias: float32 [4, 15, 15], replicated, may hold values from -2 to 250
Outputs:
- grad_in: bfloat16 [256, 1024, 256], P('lat', 'lon')
- expand_grad: float32 [256, 1024], replicated
- depth_grad: float32 [3, 3, 1024], replicated
- project_grad: float32 [1024, 256], replicated
- qkv_grad: float32 [256, 768], replicated
- out_grad: float32 [256, 256], replicated
- bias_grad: float32 [4, 15, 15], replicated
All inputs are finite; a program needn't handle non-finite values.
Results may differ from a plain program's by a relative error of at most 0.013.
Values may be sent and summed in bfloat16 or wider, within the bound.
No kernel may reach another device: no remote copies, remote signals or barrier semaphores. Data moves between devices by JAX's collectives and lax.ppermute only.
A program may use at most 192 MiB of HBM per device.

v0:
```python
import math

import jax
import jax.numpy as jnp
from jax import lax
from jax.sharding import PartitionSpec as P

EPSILON = 1e-05
GELU_C = math.sqrt(2.0 / math.pi)


def extended(cells, sides, width, closed):
    for axis, dim in sides:
        count = lax.axis_size(axis)
        ends = count if closed else count - 1
        head = lax.slice_in_dim(cells, 0, width, axis=dim)
        tail = lax.slice_in_dim(cells, cells.shape[dim] - width, cells.shape[dim], axis=dim)
        cells = jnp.concatenate(
            [
                lax.ppermute(tail, axis, [(i, (i + 1) % count) for i in range(ends)]),
                cells,
                lax.ppermute(head, axis, [((i + 1) % count, i) for i in range(ends)]),
            ],
            axis=dim,
        )
    return cells


def layer_norm(values):
    average = jnp.mean(values, axis=-1, keepdims=True)
    centred = values - average
    variance = jnp.mean(centred * centred, axis=-1, keepdims=True)
    inv_std = lax.rsqrt(variance + EPSILON)
    return (centred * inv_std, inv_std)


def layer_norm_back(normed, inv_std, grads):
    mean_grad = jnp.mean(grads, axis=-1, keepdims=True)
    mean_cross = jnp.mean(grads * normed, axis=-1, keepdims=True)
    return (grads - mean_grad - normed * mean_cross) * inv_std


def gelu_slope(values):
    inner_arg = GELU_C * (values + 0.044715 * values * values * values)
    tanh_val = jnp.tanh(inner_arg)
    result = 0.5 * values * (1.0 + tanh_val)
    slopes = 0.5 * (1.0 + tanh_val) + 0.5 * values * (1.0 - tanh_val * tanh_val) * GELU_C * (
        1.0 + 3.0 * 0.044715 * values * values
    )
    return (result, slopes)


def extend(field):
    with_rows = extended(field, (("lat", 0),), 1, False)
    return extended(with_rows, (("lon", 1),), 1, True)


def depthwise(padded, kernel):
    n_rows = padded.shape[0] - 2
    n_cols = padded.shape[1] - 2
    summed = jnp.zeros((n_rows, n_cols, padded.shape[2]), jnp.float32)
    for row_off in range(3):
        for col_off in range(3):
            summed = (
                summed
                + padded[row_off : row_off + n_rows, col_off : col_off + n_cols].astype(jnp.float32)
                * kernel[row_off, col_off]
            )
    return summed


def depthwise_back(padded_grad, kernel):
    n_rows = padded_grad.shape[0] - 2
    n_cols = padded_grad.shape[1] - 2
    summed = jnp.zeros((n_rows, n_cols, padded_grad.shape[2]), jnp.float32)
    for row_off in range(3):
        for col_off in range(3):
            summed = (
                summed
                + padded_grad[
                    2 - row_off : 2 - row_off + n_rows, 2 - col_off : 2 - col_off + n_cols
                ].astype(jnp.float32)
                * kernel[row_off, col_off]
            )
    return summed


def kernel_grad(padded, grads):
    n_rows, n_cols = (grads.shape[0], grads.shape[1])
    grads32 = grads.astype(jnp.float32)
    outer_list = []
    for row_off in range(3):
        inner_list = []
        for col_off in range(3):
            window = padded[row_off : row_off + n_rows, col_off : col_off + n_cols].astype(
                jnp.float32
            )
            inner_list.append(jnp.sum(window * grads32, axis=(0, 1)))
        outer_list.append(jnp.stack(inner_list))
    return jnp.stack(outer_list)


def product(form, left, right):
    return jnp.einsum(form, left, right, preferred_element_type=jnp.float32)


def contract_rows(left, right):
    return lax.dot_general(
        left, right, (((0,), (0,)), ((), ())), preferred_element_type=jnp.float32
    )


def rel_table():
    position = jnp.arange(64)
    pos_row = position // 8
    pos_col = position % 8
    rel_index = (pos_row[:, None] - pos_row[None, :] + 7) * 15 + (
        pos_col[:, None] - pos_col[None, :] + 7
    )
    return (rel_index[:, :, None] == jnp.arange(225)[None, None, :]).astype(jnp.float32)


def grid_attention_back(tokens, grads, qkv_weight, out_weight, rel_bias):
    n_groups = tokens.shape[0]
    n_chan = tokens.shape[2]
    n_heads = rel_bias.shape[0]
    head_dim = n_chan // n_heads
    head_scale = head_dim ** (-0.5)
    onehot = rel_table()
    bias_full = jnp.einsum(
        "ijr,hr->hij", onehot, rel_bias.reshape(n_heads, 225), precision=lax.Precision.HIGHEST
    )
    normed, inv_std = layer_norm(tokens.astype(jnp.float32))
    normed_b = normed.astype(jnp.bfloat16)
    projected = product("gtc,cf->gtf", normed_b, qkv_weight).astype(jnp.bfloat16)
    queries = projected[..., :n_chan].reshape(n_groups, 64, n_heads, head_dim)
    keys_h = projected[..., n_chan : 2 * n_chan].reshape(n_groups, 64, n_heads, head_dim)
    values = projected[..., 2 * n_chan :].reshape(n_groups, 64, n_heads, head_dim)
    scores = product("gthd,gshd->ghts", queries, keys_h) * head_scale + bias_full[None]
    attn_w = jax.nn.softmax(scores, axis=-1)
    attn_b = attn_w.astype(jnp.bfloat16)
    attended = (
        product("ghts,gshd->gthd", attn_b, values)
        .astype(jnp.bfloat16)
        .reshape(n_groups, 64, n_chan)
    )
    out_sum = product("gtc,gtf->cf", attended, grads)
    d_att = (
        product("gtf,cf->gtc", grads, out_weight)
        .astype(jnp.bfloat16)
        .reshape(n_groups, 64, n_heads, head_dim)
    )
    d_probs = product("gthd,gshd->ghts", d_att, values)
    d_value = product("ghts,gthd->gshd", attn_b, d_att).astype(jnp.bfloat16)
    d_scores = attn_w * (d_probs - jnp.sum(attn_w * d_probs, axis=-1, keepdims=True))
    bias_sum = jnp.einsum(
        "ghts,tsr->hr", d_scores, onehot, precision=lax.Precision.HIGHEST
    ).reshape(n_heads, 15, 15)
    d_scores_b = d_scores.astype(jnp.bfloat16)
    d_query = (product("ghts,gshd->gthd", d_scores_b, keys_h) * head_scale).astype(jnp.bfloat16)
    d_key = (product("ghts,gthd->gshd", d_scores_b, queries) * head_scale).astype(jnp.bfloat16)
    d_proj = jnp.concatenate(
        [
            d_query.reshape(n_groups, 64, n_chan),
            d_key.reshape(n_groups, 64, n_chan),
            d_value.reshape(n_groups, 64, n_chan),
        ],
        axis=-1,
    )
    qkv_sum = product("gtc,gtf->cf", normed_b, d_proj)
    d_normed = product("gtf,cf->gtc", d_proj, qkv_weight)
    d_tokens = layer_norm_back(normed, inv_std, d_normed).astype(jnp.bfloat16)
    return (d_tokens, qkv_sum, out_sum, bias_sum)


def layout(n_rows, n_cols):
    n_lat = lax.axis_size("lat")
    n_lon = lax.axis_size("lon")
    rep_r = max(1, 8 // n_lat)
    rep_c = max(1, 8 // n_lon)
    return (n_lat, n_lon, rep_r, n_rows // (rep_r * n_lat), rep_c, n_cols // (rep_c * n_lon))


def to_groups(fields):
    n_rows, n_cols, n_chan = fields[0].shape
    n_lat, n_lon, rep_r, blk_r, rep_c, blk_c = layout(n_rows, n_cols)
    shaped = tuple(
        (piece.reshape(rep_r, n_lat, blk_r, rep_c, n_lon, blk_c, n_chan) for piece in fields)
    )
    moved_parts = (
        lax.all_to_all(
            lax.all_to_all(shaped[0], "lat", split_axis=1, concat_axis=0, tiled=True),
            "lon",
            split_axis=4,
            concat_axis=3,
            tiled=True,
        ),
        lax.all_to_all(
            lax.all_to_all(shaped[1], "lat", split_axis=1, concat_axis=0, tiled=True),
            "lon",
            split_axis=4,
            concat_axis=3,
            tiled=True,
        ),
    )
    return tuple(
        (
            piece.reshape(8, n_rows // 8, 8, n_cols // 8, n_chan)
            .transpose(1, 3, 0, 2, 4)
            .reshape(-1, 64, n_chan)
            for piece in moved_parts
        )
    )


def from_groups(field, n_rows, n_cols):
    n_chan = field.shape[-1]
    n_lat, n_lon, rep_r, blk_r, rep_c, blk_c = layout(n_rows, n_cols)
    grid_view = field.reshape(n_rows // 8, n_cols // 8, 8, 8, n_chan).transpose(2, 0, 3, 1, 4)
    restored = lax.all_to_all(
        lax.all_to_all(
            grid_view.reshape(rep_r * n_lat, 1, blk_r, rep_c * n_lon, 1, blk_c, n_chan),
            "lat",
            split_axis=0,
            concat_axis=1,
            tiled=True,
        ),
        "lon",
        split_axis=3,
        concat_axis=4,
        tiled=True,
    )
    return restored.reshape(n_rows, n_cols, n_chan)


def on_device(
    field_in,
    cotangent,
    expand_weight,
    depth_kernel,
    project_weight,
    qkv_weight,
    out_weight,
    rel_bias,
):
    n_rows, n_cols, n_chan = field_in.shape
    n_flat = n_rows * n_cols
    n_exp = expand_weight.shape[1]
    normed, inv_std = layer_norm(field_in.astype(jnp.float32))
    normed_b = normed.astype(jnp.bfloat16)
    pre_act = jnp.dot(
        normed_b.reshape(n_flat, n_chan), expand_weight, preferred_element_type=jnp.float32
    )
    act_val, act_slope = gelu_slope(pre_act)
    hidden = act_val.astype(jnp.bfloat16).reshape(n_rows, n_cols, n_exp)
    padded_hidden = extend(hidden)
    mixed_pre = depthwise(padded_hidden, depth_kernel)
    mixed_val, mixed_slope = gelu_slope(mixed_pre)
    mixed_b = mixed_val.astype(jnp.bfloat16).reshape(n_flat, n_exp)
    branch = jnp.dot(mixed_b, project_weight, preferred_element_type=jnp.float32)
    section = (field_in.astype(jnp.float32) + branch.reshape(n_rows, n_cols, n_chan)).astype(
        jnp.bfloat16
    )
    grouped, grouped_grad = to_groups((section, cotangent))
    d_groups, qkv_sum, out_sum, bias_sum = grid_attention_back(
        grouped, grouped_grad, qkv_weight, out_weight, rel_bias
    )
    d_branch = from_groups(d_groups, n_rows, n_cols)
    d_section = cotangent.astype(jnp.float32) + d_branch.astype(jnp.float32)
    d_section_b = d_section.astype(jnp.bfloat16).reshape(n_flat, n_chan)
    project_sum = contract_rows(mixed_b, d_section_b)
    d_mixed_val = jnp.dot(d_section_b, project_weight.T, preferred_element_type=jnp.float32)
    d_mixed = (
        (d_mixed_val * mixed_slope.reshape(n_flat, n_exp))
        .astype(jnp.bfloat16)
        .reshape(n_rows, n_cols, n_exp)
    )
    depth_sum = kernel_grad(padded_hidden, d_mixed)
    d_hidden = depthwise_back(extend(d_mixed), depth_kernel).reshape(n_flat, n_exp)
    d_pre = (d_hidden * act_slope).astype(jnp.bfloat16)
    expand_sum = contract_rows(normed_b.reshape(n_flat, n_chan), d_pre)
    d_normed = jnp.dot(d_pre, expand_weight.T, preferred_element_type=jnp.float32)
    d_input = layer_norm_back(normed, inv_std, d_normed.reshape(n_rows, n_cols, n_chan))
    grad_in = (d_section + d_input).astype(jnp.bfloat16)
    summed_grads = lax.psum(
        (expand_sum, depth_sum, project_sum, qkv_sum, out_sum, bias_sum), ("lat", "lon")
    )
    factor = float(n_flat * lax.axis_size("lat") * lax.axis_size("lon")) ** (-0.5)
    return (
        grad_in,
        summed_grads[0] * factor,
        summed_grads[1] * factor,
        summed_grads[2] * factor,
        summed_grads[3] * factor,
        summed_grads[4] * factor,
        summed_grads[5] * factor,
    )


def solution(mesh):
    placed = (P("lat", "lon", None), P("lat", "lon", None), P(), P(), P(), P(), P(), P())
    return jax.shard_map(
        on_device,
        mesh=mesh,
        in_specs=placed,
        out_specs=(P("lat", "lon", None), P(), P(), P(), P(), P(), P()),
        check_vma=False,
    )
```

profile of v0, /device:TPU:1, one launch (start us, length us, event | category | flops | bytes accessed | tf_op | source)
XLA Modules:
  0.0 566.0 jit_solution(5382805444539265636)
XLA Ops:
  12.5 4.9 multiply_convert_fusion.1
  19.6 4.0 collective-permute-start
  26.2 5.9 %all-to-all-start.2 = ((bf16[1,8,4,1,16,4,256]{6,5,4,2,3,0,1:T(4,128)(2,1)}), bf16[1,8,4,1,16,4,256]{6,5,4,2,3,0,1:T(4,128)(2,1)S(1)}, u32[]{:S(2)}, u32[]{:S(2)}) async-start(bf16[1,8,4,1,16,4,256]{6,5,4,2,3,0,1:T(4,128)(2,1)} %bitcast.171), calls=%async_computation.2 | async-start | bytes 2097152 | tf_op jit(solution)/shard_map/all_to_all | solution.py:199
  33.7 3.1 collective-permute-start.2
  38.8 2.8 collective-permute-done.3
  41.6 3.3 maximum_maximum_fusion
  44.9 16.0 %fusion.15 = (f32[32,64,1024]{2,1,0:T(8,128)}, f32[32,64,1024]{2,1,0:T(8,128)S(1)}) fusion(f32[1024]{0:T(1024)S(1)} %bitcast.198, bf16[34,65,1024]{2,1,0:T(8,128)(2,1)S(1)} %get-tuple-element.37, f32[1024]{0:T(1024)S(1)} %bitcast.200, bf16[1,64,1024]{2,1,0:T(8,128)(2,1)S(1)} %collective-permute-done.1, bf16[32,64,1024]{2,1,0:T(8,128)(2,1)S(1)} %bitcast.152, ...), kind=kLoop, calls=%fused_computation.36 | loop fusion | flops 94371840 | bytes 46436352 | tf_op jit(solution)/shard_map/add | solution.py:47
  60.9 2.7 multiply_convert_fusion
  69.9 5.4 all-to-all-start
  76.8 8.1 %all-to-all-done = bf16[1,8,4,1,16,4,256]{6,5,4,2,3,0,1:T(4,128)(2,1)} async-done(((bf16[1,8,4,1,16,4,256]{6,5,4,2,3,0,1:T(4,128)(2,1)}), bf16[1,8,4,1,16,4,256]{6,5,4,2,3,0,1:T(4,128)(2,1)}, u32[]{:S(2)}, u32[]{:S(2)}) %all-to-all-start) | async-done | bytes 1048608 | tf_op jit(solution)/shard_map/all_to_all | solution.py:192
  84.9 14.5 %all-to-all-start.3 = ((bf16[8,1,4,1,16,4,256]{6,5,2,0,3,1,4:T(4,128)(2,1)}), bf16[8,1,4,1,16,4,256]{6,5,2,0,3,1,4:T(4,128)(2,1)S(1)}, u32[]{:S(2)}, u32[]{:S(2)}) async-start(bf16[8,1,4,1,16,4,256]{6,5,2,0,3,1,4:T(4,128)(2,1)} %copy.190), calls=%async_computation.3 | async-start | bytes 2097152 | tf_op jit(solution)/shard_map/all_to_all | solution.py:198
  99.4 2.7 copy.180
  102.1 14.6 %all-to-all-done.3 = bf16[8,1,4,1,16,4,256]{6,5,2,0,3,1,4:T(4,128)(2,1)S(1)} async-done(((bf16[8,1,4,1,16,4,256]{6,5,2,0,3,1,4:T(4,128)(2,1)}), bf16[8,1,4,1,16,4,256]{6,5,2,0,3,1,4:T(4,128)(2,1)S(1)}, u32[]{:S(2)}, u32[]{:S(2)}) %all-to-all-start.3) | async-done | bytes 1048608 | tf_op jit(solution)/shard_map/all_to_all | solution.py:198
  116.7 5.6 all-to-all-start.1
  123.1 2.8 fusion.63
  130.6 8.9 %all-to-all-done.1 = bf16[8,1,4,1,16,4,256]{6,5,2,0,3,1,4:T(4,128)(2,1)} async-done(((bf16[8,1,4,1,16,4,256]{6,5,2,0,3,1,4:T(4,128)(2,1)}), bf16[8,1,4,1,16,4,256]{6,5,2,0,3,1,4:T(4,128)(2,1)}, u32[]{:S(2)}, u32[]{:S(2)}) %all-to-all-start.1) | async-done | bytes 1048608 | tf_op jit(solution)/shard_map/all_to_all | solution.py:191
  144.3 2.8 copy.182
  150.4 2.7 copy.225
  153.2 2.7 copy.223
  157.9 6.0 %fusion.87 = (f32[32,4,64]{2,1,0:T(4,128)S(1)}, f32[32,4,64,64]{2,3,1,0:T(8,128)}) fusion(f32[4,64,64]{1,2,0:T(8,128)S(1)} %copy.188, bf16[32,64,4,64]{1,3,2,0:T(8,128)(2,1)} %bitcast.163, bf16[32,64,4,64]{1,3,2,0:T(8,128)(2,1)} %bitcast.165), kind=kOutput, calls=%fused_computation.176 | convolution fusion | flops 69206080 | bytes 4292608 | tf_op jit(solution)/shard_map/sub | solution.py:140
  163.9 5.5 convolution_convert_fusion.2
  172.4 2.5 fusion.57
  174.9 2.6 fusion.56
  179.4 5.3 copy.198
  184.7 4.5 reshape.305
  189.2 5.0 copy.202
  194.2 4.3 reshape.306
  198.5 3.4 fusion.83
  205.2 3.6 all-to-all-start.4
  208.8 4.8 convolution_convert_fusion.1
  213.7 9.7 %all-to-all-done.4 = bf16[8,1,4,16,1,4,256]{6,5,3,2,4,1,0:T(4,128)(2,1)S(1)} async-done(((bf16[8,1,4,16,1,4,256]{6,5,3,2,4,1,0:T(4,128)(2,1)}), bf16[8,1,4,16,1,4,256]{6,5,3,2,4,1,0:T(4,128)(2,1)S(1)}, u32[]{:S(2)}, u32[]{:S(2)}) %all-to-all-start.4) | async-done | bytes 1048608 | tf_op jit(solution)/shard_map/all_to_all | solution.py:221
  224.9 4.9 all-to-all-start.5
  230.2 13.2 %fusion.64 = f32[4,15,15]{2,0,1:T(4,128)S(1)} fusion(s32[15,15]{1,0:T(8,128)S(1)} %multiply_add_fusion.6, s32[64,64]{1,0:T(8,128)S(1)} %copy-done.37, f32[4,64,64]{1,2,0:T(8,128)S(1)} %get-tuple-element.30), kind=kOutput, calls=%fused_computation.122 | convolution fusion | flops 45158400 | bytes 86420 | tf_op jit(solution)/shard_map/ghts,tsr->hr/dot_general | solution.py:156
  243.5 3.1 convolution_bitcast_fusion.2
  246.6 2.5 convolution_bitcast_fusion.1
  250.3 3.1 copy.209
  253.4 3.1 reshape.317
  261.6 20.8 %fusion.26 = (f32[1024]{0:T(1024)S(1)}, f32[1024]{0:T(1024)S(1)}, f32[1024]{0:T(1024)S(1)}, f32[1024]{0:T(1024)S(1)}, f32[1024]{0:T(1024)S(1)}, /*index=5*/f32[1...) fusion(bf16[34,65,1024]{2,1,0:T(8,128)(2,1)} %copy-done.4, ...), kind=kOutput, calls=%fused_computation.47 | convolution fusion | flops 1134551040 | bytes 43810816 | tf_op jit(solution)/shard_map/dot_general | solution.py:272
  282.3 5.1 multiply_reduce_fusion
  288.4 2.5 collective-permute-start.4
  292.3 70.1 %all-reduce = (f32[3,3,1024]{2,1,0:T(4,128)S(1)}, f32[4,15,15]{2,0,1:T(4,128)S(1)}) all-reduce(f32[3,3,1024]{2,1,0:T(4,128)S(1)} %pad_maximum_fusion.15, f32[4,15,15]{2,0,1:T(4,128)S(1)} %fusion.64), channel_id=1, replica_groups=mesh['lat'=8,'lon'=16] {'lat','lon'}, use_global_device_ids=true, to_apply=%region_21.22 | all-reduce | flops 10116 | bytes 80928 | tf_op jit(solution)/shard_map/psum | solution.py:285
  368.6 3.4 pad_maximum_fusion.1
  372.0 12.1 %fusion.25 = f32[32,64,1024]{2,1,0:T(8,128)S(1)} fusion(bf16[32,64,1024]{2,1,0:T(8,128)(2,1)S(1)} %bitcast.155, bf16[34,65,1024]{2,1,0:T(8,128)(2,1)S(1)} %get-tuple-element.33, bf16[1,64,1024]{2,1,0:T(8,128)(2,1)S(1)} %collective-permute-done.4, bf16[34,65,1024]{2,1,0:T(8,128)(2,1)S(1)} %get-tuple-element.32, ...), kind=kLoop, calls=%fused_computation.46 | loop fusion | flops 58720256 | bytes 38047744 | tf_op jit(solution)/shard_map/add | solution.py:79
  384.1 7.3 %fusion.20 = bf16[2048,1024]{1,0:T(8,128)(2,1)S(1)} fusion(f32[2048,1024]{1,0:T(8,128)} %get-tuple-element.59, f32[32,64,1024]{2,1,0:T(8,128)S(1)} %fusion.25), kind=kLoop, calls=%fused_computation.41 | loop fusion | flops 39845888 | bytes 20971520 | tf_op jit(solution)/shard_map/convert_element_type | solution.py:280
  396.2 4.9 fusion.88
  401.2 2.4 fusion.46
  403.6 4.0 fusion.50
  407.7 144.1 %all-reduce.4.cloned.1.call-done = (f32[256,1024]{1,0:T(8,128)}, f32[1024,256]{1,0:T(8,128)}, f32[256,768]{1,0:T(8,128)}, f32[256,256]{1,0:T(8,128)}) async-done(((f32[256,1024]{1,0:T(8,128)}, f32[1024,256]{1,0:T(8,128)}, f32[256,768]{1,0:T(8,128)}, f32[256,256]{1,0:T(8,128)}), (f32[256,1024]{1,0:T(8,128)}, f32[1024,256]{1,0:T(8,128)}, f32[256,768]{1,0:T(8,128)}, ...) | async-done | bytes 3145744 | tf_op jit(solution)/shard_map/psum | solution.py:285
  (161 shorter events, 73.6 us)
Async XLA Ops:
  7.2 5.4 copy-start
  8.8 3.7 copy-start.30
  12.5 5.0 copy-start.26
  12.5 12.5 %copy-start.11 = (bf16[32,64,256]{2,1,0:T(8,128)(2,1)S(1)}, bf16[32,64,256]{2,1,0:T(8,128)(2,1)}, u32[]{:S(2)}) copy-start(bf16[32,64,256]{2,1,0:T(8,128)(2,1)} %param.9) | copy-start | bytes 3145732
  19.6 12.5 %collective-permute-start = (bf16[1,64,1024]{2,1,0:T(8,128)(2,1)S(1)}, bf16[1,64,1024]{2,1,0:T(8,128)(2,1)S(1)}, u32[]{:S(2)}, u32[]{:S(2)}) collective-permute-start(bf16[1,64,1024]{2,1,0:T(8,128)(2,1)S(1)} %get-tuple-element.42), channel_id=1, source_target_pairs={{0,16},{16,32},{32,48},{48,64},{64,80},{80,96},{96,112},{1,17},{17... | collective-permute-start | bytes 393224 | tf_op jit(solution)/shard_map/ppermute | solution.py:20
  23.6 13.2 %copy-start.39 = (f32[3,3,1024]{2,1,0:T(4,128)S(1)}, f32[3,3,1024]{2,1,0:T(4,128)}, u32[]{:S(2)}) copy-start(f32[3,3,1024]{2,1,0:T(4,128)} %param.11) | copy-start | bytes 110596
  23.6 8.5 %collective-permute-start.1 = (bf16[1,64,1024]{2,1,0:T(8,128)(2,1)S(1)}, bf16[1,64,1024]{2,1,0:T(8,128)(2,1)S(1)}, u32[]{:S(2)}, u32[]{:S(2)}) collective-permute-start(bf16[1,64,1024]{2,1,0:T(8,128)(2,1)S(1)} %get-tuple-element.43), channel_id=1, source_target_pairs={{16,0},{32,16},{48,32},{64,48},{80,64},{96,80},{112,96},{17,1},{33... | collective-permute-start | bytes 393224 | tf_op jit(solution)/shard_map/ppermute | solution.py:22
  26.2 43.7 %all-to-all-start.2 = ((bf16[1,8,4,1,16,4,256]{6,5,4,2,3,0,1:T(4,128)(2,1)}), bf16[1,8,4,1,16,4,256]{6,5,4,2,3,0,1:T(4,128)(2,1)S(1)}, u32[]{:S(2)}, u32[]{:S(2)}) async-start(bf16[1,8,4,1,16,4,256]{6,5,4,2,3,0,1:T(4,128)(2,1)} %bitcast.171), calls=%async_computation.2 | async-start | bytes 2097152 | tf_op jit(solution)/shard_map/all_to_all | solution.py:199
  32.1 9.5 %copy-start.2 = (bf16[2048,1024]{1,0:T(8,128)(2,1)S(1)}, bf16[2048,1024]{1,0:T(8,128)(2,1)}, u32[]{:S(2)}) copy-start(bf16[2048,1024]{1,0:T(8,128)(2,1)} %copy-done.1) | copy-start | bytes 12582916
  33.7 5.1 collective-permute-start.2
  36.8 4.8 collective-permute-start.3
  44.9 16.0 %copy-start.4 = (bf16[34,65,1024]{2,1,0:T(8,128)(2,1)}, bf16[34,65,1024]{2,1,0:T(8,128)(2,1)S(1)}, u32[]{:S(2)}) copy-start(bf16[34,65,1024]{2,1,0:T(8,128)(2,1)S(1)} %get-tuple-element.36) | copy-start | bytes 13578244
  44.9 16.0 %copy-start.5 = (bf16[34,65,1024]{2,1,0:T(8,128)(2,1)}, bf16[34,65,1024]{2,1,0:T(8,128)(2,1)S(1)}, u32[]{:S(2)}) copy-start(bf16[34,65,1024]{2,1,0:T(8,128)(2,1)S(1)} %get-tuple-element.37) | copy-start | bytes 13578244
  60.9 4.6 copy-start.6
  60.9 4.6 copy-start.40
  69.9 15.0 %all-to-all-start = ((bf16[1,8,4,1,16,4,256]{6,5,4,2,3,0,1:T(4,128)(2,1)}), bf16[1,8,4,1,16,4,256]{6,5,4,2,3,0,1:T(4,128)(2,1)}, u32[]{:S(2)}, u32[]{:S(2)}) async-start(bf16[1,8,4,1,16,4,256]{6,5,4,2,3,0,1:T(4,128)(2,1)} %bitcast.173), calls=%async_computation | async-start | bytes 2097152 | tf_op jit(solution)/shard_map/all_to_all | solution.py:192
  75.3 47.0 %copy-start.38 = (f32[4,15,15]{2,0,1:T(4,128)S(1)}, f32[4,15,15]{2,0,1:T(4,128)}, u32[]{:S(2)}) copy-start(f32[4,15,15]{2,0,1:T(4,128)} %param.15) | copy-start | bytes 10804
  84.9 31.8 %all-to-all-start.3 = ((bf16[8,1,4,1,16,4,256]{6,5,2,0,3,1,4:T(4,128)(2,1)}), bf16[8,1,4,1,16,4,256]{6,5,2,0,3,1,4:T(4,128)(2,1)S(1)}, u32[]{:S(2)}, u32[]{:S(2)}) async-start(bf16[8,1,4,1,16,4,256]{6,5,2,0,3,1,4:T(4,128)(2,1)} %copy.190), calls=%async_computation.3 | async-start | bytes 2097152 | tf_op jit(solution)/shard_map/all_to_all | solution.py:198
  102.1 26.3 %copy-start.36 = (bf16[256,256]{1,0:T(8,128)(2,1)S(1)}, bf16[256,256]{1,0:T(8,128)(2,1)}, u32[]{:S(2)}) copy-start(bf16[256,256]{1,0:T(8,128)(2,1)} %param.14) | copy-start | bytes 393220
  116.7 22.8 %all-to-all-start.1 = ((bf16[8,1,4,1,16,4,256]{6,5,2,0,3,1,4:T(4,128)(2,1)}), bf16[8,1,4,1,16,4,256]{6,5,2,0,3,1,4:T(4,128)(2,1)}, u32[]{:S(2)}, u32[]{:S(2)}) async-start(bf16[8,1,4,1,16,4,256]{6,5,2,0,3,1,4:T(4,128)(2,1)} %copy.180), calls=%async_computation.1 | async-start | bytes 2097152 | tf_op jit(solution)/shard_map/all_to_all | solution.py:191
  144.0 3.2 copy-start.32
  147.1 3.3 copy-start.8
  163.9 5.6 copy-start.19
  163.9 5.5 copy-start.20
  163.9 5.5 copy-start.21
  172.3 2.6 copy-start.14
  179.4 19.1 %copy-start.22 = (bf16[32,64,256]{2,1,0:T(8,128)(2,1)}, bf16[32,64,256]{2,1,0:T(8,128)(2,1)S(1)}, u32[]{:S(2)}) copy-start(bf16[32,64,256]{2,1,0:T(8,128)(2,1)S(1)} %copy.205) | copy-start | bytes 3145732
  189.2 9.3 %copy-start.33 = (bf16[256,768]{1,0:T(8,128)(2,1)S(1)}, bf16[256,768]{1,0:T(8,128)(2,1)}, u32[]{:S(2)}) copy-start(bf16[256,768]{1,0:T(8,128)(2,1)} %param.13) | copy-start | bytes 1179652
  198.5 3.4 copy-start.9
  205.2 18.1 %all-to-all-start.4 = ((bf16[8,1,4,16,1,4,256]{6,5,3,2,4,1,0:T(4,128)(2,1)}), bf16[8,1,4,16,1,4,256]{6,5,3,2,4,1,0:T(4,128)(2,1)S(1)}, u32[]{:S(2)}, u32[]{:S(2)}) async-start(bf16[8,1,4,16,1,4,256]{6,5,3,2,4,1,0:T(4,128)(2,1)} %reshape.309), calls=%async_computation.4 | async-start | bytes 2097152 | tf_op jit(solution)/shard_map/all_to_all | solution.py:221
  213.7 16.6 %copy-start.37 = (s32[64,64]{1,0:T(8,128)S(1)}, s32[64,64]{1,0:T(8,128)}, u32[]{:S(2)}) copy-start(s32[64,64]{1,0:T(8,128)} %get-tuple-element.56) | copy-start | bytes 49156
  224.9 24.2 %all-to-all-start.5 = ((bf16[1,8,4,16,1,4,256]{6,5,2,1,4,0,3:T(4,128)(2,1)}), bf16[1,8,4,16,1,4,256]{6,5,2,1,4,0,3:T(4,128)(2,1)S(1)}, u32[]{:S(2)}, u32[]{:S(2)}) async-start(bf16[1,8,4,16,1,4,256]{6,5,2,1,4,0,3:T(4,128)(2,1)} %copy.207), calls=%async_computation.5 | async-start | bytes 2097152 | tf_op jit(solution)/shard_map/all_to_all | solution.py:220
  229.7 322.0 %all-reduce.4.cloned.1.call-start = ((), (), s32[]{:S(2)}) async-start(), calls=%async_computation.6 | async-start | bytes 6291456 | tf_op jit(solution)/shard_map/psum | solution.py:285
  230.2 16.4 %copy-start.10 = (f32[4,8,8,8,256]{4,3,2,1,0:T(8,128)S(1)}, f32[4,8,8,8,256]{4,3,2,1,0:T(8,128)}, u32[]{:S(2)}) copy-start(f32[4,8,8,8,256]{4,3,2,1,0:T(8,128)} %copy-done.8) | copy-start | bytes 6291460
  230.2 16.4 %copy-start.23 = (bf16[32,64,256]{2,1,0:T(8,128)(2,1)S(1)}, bf16[32,64,256]{2,1,0:T(8,128)(2,1)}, u32[]{:S(2)}) copy-start(bf16[32,64,256]{2,1,0:T(8,128)(2,1)} %copy-done.22) | copy-start | bytes 3145732
  230.2 16.4 %copy-start.24 = (bf16[32,64,256]{2,1,0:T(8,128)(2,1)S(1)}, bf16[32,64,256]{2,1,0:T(8,128)(2,1)}, u32[]{:S(2)}) copy-start(bf16[32,64,256]{2,1,0:T(8,128)(2,1)} %reshape.305) | copy-start | bytes 3145732
  230.2 16.4 %copy-start.25 = (bf16[32,64,256]{2,1,0:T(8,128)(2,1)S(1)}, bf16[32,64,256]{2,1,0:T(8,128)(2,1)}, u32[]{:S(2)}) copy-start(bf16[32,64,256]{2,1,0:T(8,128)(2,1)} %reshape.306) | copy-start | bytes 3145732
  250.3 6.2 %copy-start.12 = (bf16[32,64,256]{2,1,0:T(8,128)(2,1)S(1)}, bf16[32,64,256]{2,1,0:T(8,128)(2,1)}, u32[]{:S(2)}) copy-start(bf16[32,64,256]{2,1,0:T(8,128)(2,1)} %param.9) | copy-start | bytes 3145732
  256.5 2.8 copy-start.16
  288.4 74.1 %collective-permute-start.4 = (bf16[1,64,1024]{2,1,0:T(8,128)(2,1)S(1)}, bf16[1,64,1024]{2,1,0:T(8,128)(2,1)S(1)}, u32[]{:S(2)}, u32[]{:S(2)}) collective-permute-start(bf16[1,64,1024]{2,1,0:T(8,128)(2,1)S(1)} %get-tuple-element.40), channel_id=1, source_target_pairs={{0,16},{16,32},{32,48},{48,64},{64,80},{80,96},{96,112},{1,17},{17... | collective-permute-start | bytes 393224 | tf_op jit(solution)/shard_map/ppermute | solution.py:20
  290.9 71.6 %collective-permute-start.5 = (bf16[1,64,1024]{2,1,0:T(8,128)(2,1)S(1)}, bf16[1,64,1024]{2,1,0:T(8,128)(2,1)S(1)}, u32[]{:S(2)}, u32[]{:S(2)}) collective-permute-start(bf16[1,64,1024]{2,1,0:T(8,128)(2,1)S(1)} %get-tuple-element.41), channel_id=1, source_target_pairs={{16,0},{32,16},{48,32},{64,48},{80,64},{96,80},{112,96},{17,1},{33... | collective-permute-start | bytes 393224 | tf_op jit(solution)/shard_map/ppermute | solution.py:22
  362.4 6.2 %copy-start.3 = (bf16[2048,1024]{1,0:T(8,128)(2,1)S(1)}, bf16[2048,1024]{1,0:T(8,128)(2,1)}, u32[]{:S(2)}) copy-start(bf16[2048,1024]{1,0:T(8,128)(2,1)} %get-tuple-element.67) | copy-start | bytes 12582916
  364.0 4.5 collective-permute-start.6
  364.9 3.7 collective-permute-start.7
  384.1 9.3 %copy-start.27 = (bf16[32,64,256]{2,1,0:T(8,128)(2,1)S(1)}, bf16[32,64,256]{2,1,0:T(8,128)(2,1)}, u32[]{:S(2)}) copy-start(bf16[32,64,256]{2,1,0:T(8,128)(2,1)} %copy-done.26) | copy-start | bytes 3145732
  396.2 4.9 copy-start.31
  396.2 4.9 copy-start.35
  551.8 6.1 %copy-start.28 = (f32[1024,256]{1,0:T(8,128)S(1)}, f32[1024,256]{1,0:T(8,128)}, u32[]{:S(2)}) copy-start(f32[1024,256]{1,0:T(8,128)} %get-tuple-element.25) | copy-start | bytes 3145732
  (8 other events, 15.1 us)
Sparse Core Ops, SparseCore 0:
  395.7 155.9 all-reduce.3
where the time goes:
time: 575 us; the launch traced here: 566 us
  waiting for transfers between devices  192 us (33%)
  matrix products  87.1 us (15%)
  other arithmetic  82.6 us (14%)
  blocking collectives  70.1 us (12%)
  local copies, waits for them, and re-layouts  64.4 us (11%)
  starting transfers between devices  54.5 us (9%)
  between operations  15 us (3%)
    psum x1, waiting for transfers between devices, on_device(): lax.psum((expand_sum, depth_sum, project_sum, qkv_sum, out_sum, bias_sum)...  144 us
    psum x1, blocking collectives, on_device(): lax.psum((expand_sum, depth_sum, project_sum, qkv_sum, out_sum, bias_sum)...  70.1 us
    dot_general x10, matrix products, product(): return jnp.einsum(form, left, right, preferred_element_type=jnp.float32)  27.8 us
    dot_general x1, matrix products, on_device(): jnp.dot(d_section_b, project_weight.T, preferred_element_type=jnp.float32)  20.8 us
    add x1, other arithmetic, gelu_slope(): 0.5 * (1.0 + tanh_val)  16 us
    all_to_all x1, waiting for transfers between devices, to_groups(): lax.all_to_all(lax.all_to_all(shaped[1], 'lat', split_axis=1, concat_axis...  14.6 us
    all_to_all x1, starting transfers between devices, to_groups(): lax.all_to_all(lax.all_to_all(shaped[1], 'lat', split_axis=1, concat_axis...  14.5 us
    dot_general x1, matrix products, grid_attention_back(): jnp.einsum('ghts,tsr->hr', d_scores, onehot, precision=lax.Precision.HIGH...  13.2 us
  transfers between devices with their start and end apart: 15, of which 8 were waited for; matrix products, arithmetic and copies ran while one was open for 14% of the time, Pallas kernels for 0%

commit v1 on v0

v1 whole, which is shorter than its diff:
```python
import math

import jax
import jax.numpy as jnp
import numpy as np
from jax import lax
from jax.experimental import pallas as pl
from jax.experimental.pallas import tpu as pltpu
from jax.sharding import PartitionSpec as P

EPSILON = 1e-05
GELU_C = math.sqrt(2.0 / math.pi)
F32 = jnp.float32
BF16 = jnp.bfloat16
MIB = 1 << 20

ROWS, COLS, CHAN, EXP = 32, 64, 256, 1024
BLK = 4
STEPS = ROWS // BLK
TOK = BLK * COLS
LANES = 128
EDGE = 40
HALO = 2 * COLS + 2 * EDGE


def layer_norm(values):
    average = jnp.mean(values, axis=-1, keepdims=True)
    centred = values - average
    variance = jnp.mean(centred * centred, axis=-1, keepdims=True)
    inv_std = lax.rsqrt(variance + EPSILON)
    return (centred * inv_std, inv_std)


def layer_norm_back(normed, inv_std, grads):
    mean_grad = jnp.mean(grads, axis=-1, keepdims=True)
    mean_cross = jnp.mean(grads * normed, axis=-1, keepdims=True)
    return (grads - mean_grad - normed * mean_cross) * inv_std


def gelu_slope(values):
    squared = values * values
    tanh_val = jnp.tanh(values * (GELU_C + (GELU_C * 0.044715) * squared))
    gate = 0.5 + 0.5 * tanh_val
    result = values * gate
    slopes = gate + result * (1.0 - gate) * (2.0 * GELU_C + (6.0 * GELU_C * 0.044715) * squared)
    return (result, slopes)


def dot(left, right):
    return lax.dot_general(left, right, (((1,), (0,)), ((), ())), preferred_element_type=F32)


def dot_nt(left, right):
    return lax.dot_general(left, right, (((1,), (1,)), ((), ())), preferred_element_type=F32)


def dot_tn(left, right):
    return lax.dot_general(left, right, (((0,), (0,)), ((), ())), preferred_element_type=F32)


def params(mib):
    return pltpu.CompilerParams(vmem_limit_bytes=mib * MIB)


def whole(shape):
    return pl.BlockSpec(shape, lambda i: (0,) * len(shape))


def band(shape):
    return pl.BlockSpec(shape, lambda i: (i,) + (0,) * (len(shape) - 1))


ROW_BEFORE = pl.BlockSpec((1, COLS, EXP), lambda i: (jnp.maximum(BLK * i - 1, 0), 0, 0))
ROW_AFTER = pl.BlockSpec((1, COLS, EXP), lambda i: (jnp.minimum(BLK * i + BLK, ROWS - 1), 0, 0))


def expand_body(x_ref, we_ref, hid_ref, slope_ref):
    normed, _ = layer_norm(x_ref[...].reshape(TOK, CHAN).astype(F32))
    normed_b = normed.astype(BF16)
    for at in range(0, EXP, 256):
        val, slope = gelu_slope(dot(normed_b, we_ref[:, at : at + 256]))
        hid_ref[:, :, at : at + 256] = val.astype(BF16).reshape(BLK, COLS, 256)
        slope_ref[:, :, at : at + 256] = slope.astype(BF16).reshape(BLK, COLS, 256)


def expand(x, we):
    wide = jax.ShapeDtypeStruct((ROWS, COLS, EXP), BF16)
    return pl.pallas_call(
        expand_body,
        grid=(STEPS,),
        in_specs=[band((BLK, COLS, CHAN)), whole((CHAN, EXP))],
        out_specs=[band((BLK, COLS, EXP))] * 2,
        out_shape=[wide, wide],
        compiler_params=params(32),
        cost_estimate=pl.CostEstimate(
            flops=2 * ROWS * COLS * CHAN * EXP, bytes_accessed=10 * MIB, transcendentals=ROWS * COLS * EXP
        ),
        name="expand",
    )(x, we)


def mix_body(
    cur_ref, before_ref, after_ref, halo_ref, we_ref, dk_ref, wp_ref, x_ref,
    section_ref, mixed_ref, slope_ref, top_ref, bottom_ref, left_ref, right_ref,
):
    step = pl.program_id(0)

    @pl.when(step == 0)
    def _():
        normed, _ = layer_norm(halo_ref[...].astype(F32))
        normed_b = normed.astype(BF16)
        for at in range(0, EXP, 256):
            span = slice(at, at + 256)
            val, _ = gelu_slope(dot(normed_b, we_ref[:, span]))
            val = val.astype(BF16).astype(F32)
            top_ref[:, span] = val[:COLS]
            bottom_ref[:, span] = val[COLS : 2 * COLS]
            for ref, base, col in ((left_ref, 2 * COLS, 0), (right_ref, 2 * COLS + EDGE, 2)):
                total = 0.0
                for a in range(3):
                    total = total + dk_ref[3 * a + col, span][None] * val[base + a : base + a + ROWS]
                for s in range(STEPS):
                    ref[s, :BLK, span] = total[BLK * s : BLK * s + BLK]

    first, last = step == 0, step == STEPS - 1
    for at in range(0, EXP, LANES):
        span = slice(at, at + LANES)
        rows = [jnp.where(first, top_ref[:, span], before_ref[0, :, span].astype(F32))]
        rows += [cur_ref[r, :, span].astype(F32) for r in range(BLK)]
        rows += [jnp.where(last, bottom_ref[:, span], after_ref[0, :, span].astype(F32))]
        kern = [dk_ref[n, span][None] for n in range(9)]
        for r in range(BLK):
            parts = [
                kern[b] * rows[r] + kern[3 + b] * rows[r + 1] + kern[6 + b] * rows[r + 2]
                for b in range(3)
            ]
            left = left_ref[step, r : r + 1, span]
            right = right_ref[step, r : r + 1, span]
            pre = (
                parts[1]
                + jnp.concatenate([left, parts[0][:-1]], axis=0)
                + jnp.concatenate([parts[2][1:], right], axis=0)
            )
            val, slope = gelu_slope(pre)
            mixed_ref[r, :, span] = val.astype(BF16)
            slope_ref[r, :, span] = slope.astype(BF16)
    branch = dot(mixed_ref[...].reshape(TOK, EXP), wp_ref[...])
    section = (x_ref[...].reshape(TOK, CHAN).astype(F32) + branch).astype(BF16)
    section = section.reshape(2, 2, 4, 16, CHAN)
    for pair in range(2):
        for quad in range(4):
            section_ref[4 * pair + quad] = section[pair, :, quad].reshape(32, CHAN)


def mix(hidden, halo, we, dk, wp, x):
    wide = jax.ShapeDtypeStruct((ROWS, COLS, EXP), BF16)
    return pl.pallas_call(
        mix_body,
        grid=(STEPS,),
        in_specs=[
            band((BLK, COLS, EXP)), ROW_BEFORE, ROW_AFTER, whole((HALO, CHAN)), whole((CHAN, EXP)),
            whole((9, EXP)), whole((EXP, CHAN)), band((BLK, COLS, CHAN)),
        ],
        out_specs=[band((8, 32, CHAN)), band((BLK, COLS, EXP)), band((BLK, COLS, EXP))],
        out_shape=[jax.ShapeDtypeStruct((64, 32, CHAN), BF16), wide, wide],
        scratch_shapes=[pltpu.VMEM((COLS, EXP), F32)] * 2 + [pltpu.VMEM((STEPS, 8, EXP), F32)] * 2,
        compiler_params=params(48),
        cost_estimate=pl.CostEstimate(
            flops=2 * ROWS * COLS * CHAN * EXP, bytes_accessed=16 * MIB, transcendentals=ROWS * COLS * EXP
        ),
        name="mix",
    )(hidden, hidden, hidden, halo, we, dk, wp, x)


SWAP = np.zeros((256, 256), np.float32)
for _s in range(16):
    for _g in range(16):
        SWAP[_g * 16 + _s, _s * 16 + _g] = 1.0


def diagonal(full, low):
    halves = []
    for half in range(2):
        lanes = slice(half * 128, half * 128 + 128)
        at = half * 128
        halves.append(jnp.where(low, full[at : at + 64, lanes], full[at + 64 : at + 128, lanes]))
    return jnp.concatenate(halves, axis=1)


def attention_body(
    x_ref, cot_ref, wqkv_ref, wout_ref, bias_ref, swap_ref,
    out_ref, qkv_sum_ref, out_sum_ref, bias_sum_ref, xs_ref, cs_ref, ds_ref,
):
    step = pl.program_id(0)
    n_groups = x_ref.shape[1]

    @pl.when(step == 0)
    def _():
        qkv_sum_ref[...] = jnp.zeros_like(qkv_sum_ref)
        out_sum_ref[...] = jnp.zeros_like(out_sum_ref)
        bias_sum_ref[...] = jnp.zeros_like(bias_sum_ref)
        for src, dst in ((x_ref, xs_ref), (cot_ref, cs_ref)):
            for s in range(0, 64, 16):
                for g in range(0, n_groups, 16):
                    tile = src[s : s + 16, g : g + 16].reshape(256, CHAN)
                    moved = dot(swap_ref[...], tile).astype(BF16)
                    dst[g : g + 16, s : s + 16] = moved.reshape(16, 16, CHAN)

    groups = pl.ds(step * 4, 4)
    tokens = xs_ref[groups].reshape(256, CHAN)
    grads = cs_ref[groups].reshape(256, CHAN)
    normed, inv_std = layer_norm(tokens.astype(F32))
    normed_b = normed.astype(BF16)
    projected = dot(normed_b, wqkv_ref[...]).astype(BF16)
    d_att = dot_nt(grads, wout_ref[...]).astype(BF16)
    low = lax.broadcasted_iota(jnp.int32, (64, 128), 1) < 64
    head_of = lax.broadcasted_iota(jnp.int32, (64, CHAN), 1) // 64
    masks = [(head_of == h).astype(F32).astype(BF16) for h in range(4)]
    attended, d_proj = [], []
    for g in range(4):
        part = slice(g * 64, g * 64 + 64)
        query = projected[part, :CHAN] * 0.125
        key = projected[part, CHAN : 2 * CHAN]
        value = projected[part, 2 * CHAN :]
        da = d_att[part]
        query_h = jnp.concatenate([query * m for m in masks], axis=0)
        da_h = jnp.concatenate([da * m for m in masks], axis=0)
        scores = dot_nt(key, query_h) + bias_ref[...]
        scores = jnp.exp(scores - jnp.max(scores, axis=0, keepdims=True))
        probs = scores * (1.0 / jnp.sum(scores, axis=0, keepdims=True))
        probs_b = probs.astype(BF16)
        d_probs = dot_nt(value, da_h)
        d_scores = probs * (d_probs - jnp.sum(probs * d_probs, axis=0, keepdims=True))
        bias_sum_ref[...] += d_scores
        d_scores_b = d_scores.astype(BF16)
        attended.append(diagonal(dot_tn(probs_b, value), low).astype(BF16))
        d_query = (diagonal(dot_tn(d_scores_b, key), low) * 0.125).astype(BF16)
        d_key = dot(d_scores_b, query_h).astype(BF16)
        d_value = dot(probs_b, da_h).astype(BF16)
        d_proj.append(jnp.concatenate([d_query, d_key, d_value], axis=1))
    attended = jnp.concatenate(attended, axis=0)
    d_proj = jnp.concatenate(d_proj, axis=0)
    out_sum_ref[...] += dot_tn(attended, grads)
    qkv_sum_ref[...] += dot_tn(normed_b, d_proj)
    d_normed = dot_nt(d_proj, wqkv_ref[...])
    d_tokens = layer_norm_back(normed, inv_std, d_normed).astype(BF16)
    ds_ref[groups] = d_tokens.reshape(4, 64, CHAN)

    @pl.when(step == n_groups // 4 - 1)
    def _():
        for s in range(0, 64, 16):
            for g in range(0, n_groups, 16):
                tile = ds_ref[g : g + 16, s : s + 16].reshape(256, CHAN)
                moved = dot(swap_ref[...], tile).astype(BF16)
                out_ref[s : s + 16, g : g + 16] = moved.reshape(16, 16, CHAN)


def attention(tokens, cot, wqkv, wout, bias):
    n_groups = tokens.shape[1]
    shape = (64, n_groups, CHAN)
    return pl.pallas_call(
        attention_body,
        grid=(n_groups // 4,),
        in_specs=[
            whole(shape), whole(shape), whole((CHAN, 3 * CHAN)), whole((CHAN, CHAN)),
            whole((64, CHAN)), whole((256, 256)),
        ],
        out_specs=[whole(shape), whole((CHAN, 3 * CHAN)), whole((CHAN, CHAN)), whole((64, CHAN))],
        out_shape=[
            jax.ShapeDtypeStruct(shape, BF16),
            jax.ShapeDtypeStruct((CHAN, 3 * CHAN), F32),
            jax.ShapeDtypeStruct((CHAN, CHAN), F32),
            jax.ShapeDtypeStruct((64, CHAN), F32),
        ],
        scratch_shapes=[pltpu.VMEM((n_groups, 64, CHAN), BF16)] * 3,
        compiler_params=params(48),
        cost_estimate=pl.CostEstimate(
            flops=n_groups * 64 * 4 * CHAN * CHAN * 5, bytes_accessed=6 * MIB, transcendentals=n_groups * 64 * 256
        ),
        name="attention",
    )(tokens, cot, wqkv, wout, bias, jnp.asarray(SWAP, BF16))


def project_body(cot_ref, db_ref, mixed_ref, slope_ref, wp_ref, ds_ref, dm_ref, sum_ref):
    @pl.when(pl.program_id(0) == 0)
    def _():
        sum_ref[...] = jnp.zeros_like(sum_ref)

    pieces = db_ref[...].reshape(2, 4, 2, 16, CHAN)
    branch = jnp.concatenate(
        [pieces[pair, quad, r] for pair in range(2) for r in range(2) for quad in range(4)], axis=0
    )
    d_section = cot_ref[...].reshape(TOK, CHAN).astype(F32) + branch.astype(F32)
    ds_ref[...] = d_section.reshape(BLK, COLS, CHAN)
    d_section_b = d_section.astype(BF16)
    sum_ref[...] += dot_tn(d_section_b, mixed_ref[...].reshape(TOK, EXP))
    for at in range(0, EXP, 256):
        grads = dot_nt(d_section_b, wp_ref[at : at + 256, :])
        slope = slope_ref[:, :, at : at + 256].reshape(TOK, 256).astype(F32)
        dm_ref[:, :, at : at + 256] = (grads * slope).astype(BF16).reshape(BLK, COLS, 256)


def project_back(cot, db, mixed, slope, wp):
    return pl.pallas_call(
        project_body,
        grid=(STEPS,),
        in_specs=[
            band((BLK, COLS, CHAN)), band((8, 32, CHAN)), band((BLK, COLS, EXP)),
            band((BLK, COLS, EXP)), whole((EXP, CHAN)),
        ],
        out_specs=[band((BLK, COLS, CHAN)), band((BLK, COLS, EXP)), whole((CHAN, EXP))],
        out_shape=[
            jax.ShapeDtypeStruct((ROWS, COLS, CHAN), F32),
            jax.ShapeDtypeStruct((ROWS, COLS, EXP), BF16),
            jax.ShapeDtypeStruct((CHAN, EXP), F32),
        ],
        compiler_params=params(48),
        cost_estimate=pl.CostEstimate(
            flops=4 * ROWS * COLS * CHAN * EXP, bytes_accessed=16 * MIB, transcendentals=0
        ),
        name="project_back",
    )(cot, db, mixed, slope, wp)


def expand_back_body(
    cur_ref, before_ref, after_ref, halo_ref, halo_slope_ref, wp_ref, hid_ref, slope_ref, x_ref,
    ds_ref, dk_ref, we_ref,
    grad_ref, sum_ref, depth_ref, top_ref, bottom_ref, left_ref, right_ref, acc_ref, dpre_ref,
):
    step = pl.program_id(0)

    @pl.when(step == 0)
    def _():
        sum_ref[...] = jnp.zeros_like(sum_ref)
        acc_ref[...] = jnp.zeros_like(acc_ref)
        for at in range(0, EXP, 256):
            span = slice(at, at + 256)
            grads = dot_nt(halo_ref[...], wp_ref[at : at + 256, :])
            grads = (grads * halo_slope_ref[:, span].astype(F32)).astype(BF16).astype(F32)
            top_ref[:, span] = grads[:COLS]
            bottom_ref[:, span] = grads[COLS : 2 * COLS]
            for ref, base in ((left_ref, 2 * COLS), (right_ref, 2 * COLS + EDGE)):
                for s in range(STEPS):
                    ref[s, : BLK + 2, span] = grads[base + BLK * s : base + BLK * s + BLK + 2]

    first, last = step == 0, step == STEPS - 1
    for at in range(0, EXP, LANES):
        span = slice(at, at + LANES)
        rows = [jnp.where(first, top_ref[:, span], before_ref[0, :, span].astype(F32))]
        rows += [cur_ref[r, :, span].astype(F32) for r in range(BLK)]
        rows += [jnp.where(last, bottom_ref[:, span], after_ref[0, :, span].astype(F32))]
        shifted = []
        for r in range(BLK + 2):
            left = left_ref[step, r : r + 1, span]
            right = right_ref[step, r : r + 1, span]
            shifted.append(
                (
                    jnp.concatenate([rows[r][1:], right], axis=0),
                    rows[r],
                    jnp.concatenate([left, rows[r][:-1]], axis=0),
                )
            )
        sums = [acc_ref[n, :, span] for n in range(9)]
        for r in range(BLK):
            hid = hid_ref[r, :, span].astype(F32)
            total = 0.0
            for a in range(3):
                for b in range(3):
                    piece = shifted[r + 2 - a][b]
                    n = 3 * a + b
                    total = total + dk_ref[n, span][None] * piece
                    sums[n] = sums[n] + jnp.sum((hid * piece).reshape(8, 8, LANES), axis=0)
            d_pre = total * slope_ref[r, :, span].astype(F32)
            dpre_ref[r * COLS : (r + 1) * COLS, span] = d_pre.astype(BF16)
        for n in range(9):
            acc_ref[n, :, span] = sums[n]

    normed, inv_std = layer_norm(x_ref[...].reshape(TOK, CHAN).astype(F32))
    sum_ref[...] += dot_tn(normed.astype(BF16), dpre_ref[...])
    d_normed = dot_nt(dpre_ref[...], we_ref[...])
    d_input = layer_norm_back(normed, inv_std, d_normed)
    grad_ref[...] = (ds_ref[...].reshape(TOK, CHAN) + d_input).astype(BF16).reshape(BLK, COLS, CHAN)

    @pl.when(last)
    def _():
        depth_ref[...] = jnp.sum(acc_ref[...], axis=1)


def expand_back(d_mixed, halo, halo_slope, wp, hidden, slope, x, ds, dk, we):
    return pl.pallas_call(
        expand_back_body,
        grid=(STEPS,),
        in_specs=[
            band((BLK, COLS, EXP)), ROW_BEFORE, ROW_AFTER, whole((HALO, CHAN)), whole((HALO, EXP)),
            whole((EXP, CHAN)), band((BLK, COLS, EXP)), band((BLK, COLS, EXP)),
            band((BLK, COLS, CHAN)), band((BLK, COLS, CHAN)), whole((9, EXP)), whole((CHAN, EXP)),
        ],
        out_specs=[band((BLK, COLS, CHAN)), whole((CHAN, EXP)), whole((9, EXP))],
        out_shape=[
            jax.ShapeDtypeStruct((ROWS, COLS, CHAN), BF16),
            jax.ShapeDtypeStruct((CHAN, EXP), F32),
            jax.ShapeDtypeStruct((9, EXP), F32),
        ],
        scratch_shapes=[pltpu.VMEM((COLS, EXP), F32)] * 2
        + [pltpu.VMEM((STEPS, 8, EXP), F32)] * 2
        + [pltpu.VMEM((9, 8, EXP), F32), pltpu.VMEM((TOK, EXP), BF16)],
        compiler_params=params(56),
        cost_estimate=pl.CostEstimate(
            flops=4 * ROWS * COLS * CHAN * EXP, bytes_accessed=20 * MIB, transcendentals=0
        ),
        name="expand_back",
    )(d_mixed, d_mixed, d_mixed, halo, halo_slope, wp, hidden, slope, x, ds, dk, we)


def halo_of(top, bottom, left, right):
    n_lat, n_lon = lax.axis_size("lat"), lax.axis_size("lon")
    south = [(i, i + 1) for i in range(n_lat - 1)]
    north = [(i + 1, i) for i in range(n_lat - 1)]
    east = [(i, (i + 1) % n_lon) for i in range(n_lon)]
    west = [((i + 1) % n_lon, i) for i in range(n_lon)]
    above = lax.ppermute(bottom, "lat", south)
    below = lax.ppermute(top, "lat", north)
    pad = jnp.zeros((EDGE - ROWS - 2, top.shape[1]), top.dtype)
    from_west = lax.ppermute(
        jnp.concatenate([above[-1:], right, below[-1:], pad], axis=0), "lon", east
    )
    from_east = lax.ppermute(
        jnp.concatenate([above[:1], left, below[:1], pad], axis=0), "lon", west
    )
    return jnp.concatenate([above, below, from_west, from_east], axis=0)


def halo_of_field(field):
    return halo_of(field[0], field[-1], field[:, 0], field[:, -1])


def exchange(pieces):
    n_lat, n_lon = lax.axis_size("lat"), lax.axis_size("lon")
    order = np.arange(n_lat * n_lon).reshape(n_lat, n_lon // 2, 2)
    members = order.transpose(2, 0, 1).reshape(2, -1).tolist()
    return lax.all_to_all(
        pieces, ("lat", "lon"), split_axis=0, concat_axis=0, axis_index_groups=members, tiled=True
    )


def to_pieces(field):
    shaped = field.reshape(16, 2, 4, 16, CHAN).transpose(0, 2, 1, 3, 4)
    return shaped.reshape(64, 32, CHAN)


def edge_cells(pieces):
    shaped = pieces.reshape(16, 4, 2, 16, CHAN)
    top = shaped[0, :, 0].reshape(COLS, CHAN)
    bottom = shaped[-1, :, -1].reshape(COLS, CHAN)
    left = shaped[:, 0, :, 0].reshape(ROWS, CHAN)
    right = shaped[:, -1, :, -1].reshape(ROWS, CHAN)
    return (top, bottom, left, right)


def rel_table():
    position = np.arange(64)
    pos_row, pos_col = position // 8, position % 8
    rel_index = (pos_row[:, None] - pos_row[None, :] + 7) * 15 + (
        pos_col[:, None] - pos_col[None, :] + 7
    )
    return jnp.asarray(rel_index)[:, :, None] == jnp.arange(225)[None, None, :]


def on_device(
    field_in, cotangent, expand_weight, depth_kernel, project_weight, qkv_weight, out_weight, rel_bias
):
    onehot = rel_table().astype(F32)
    bias = jnp.einsum(
        "tsr,hr->sht", onehot, rel_bias.reshape(4, 225), precision=lax.Precision.HIGHEST
    ).reshape(64, 256)
    dk = depth_kernel.reshape(9, EXP)

    field_halo = halo_of_field(field_in)
    cot_groups = exchange(to_pieces(cotangent))
    hidden, act_slope = expand(field_in, expand_weight)
    section, mixed, mixed_slope = mix(
        hidden, field_halo, expand_weight, dk, project_weight, field_in
    )
    slope_halo = halo_of_field(mixed_slope)
    groups = exchange(section)
    d_groups, qkv_sum, out_sum, bias_acc = attention(groups, cot_groups, qkv_weight, out_weight, bias)
    bias_sum = jnp.einsum(
        "sht,tsr->hr", bias_acc.reshape(64, 4, 64), onehot, precision=lax.Precision.HIGHEST
    )
    d_branch = exchange(d_groups)
    cot_edges = (cotangent[0], cotangent[-1], cotangent[:, 0], cotangent[:, -1])
    d_edges = [
        (c.astype(F32) + d.astype(F32)).astype(BF16)
        for c, d in zip(cot_edges, edge_cells(d_branch))
    ]
    d_halo = halo_of(*d_edges)
    d_section, d_mixed, project_sum = project_back(
        cotangent, d_branch, mixed, mixed_slope, project_weight
    )
    grad_in, expand_sum, depth_sum = expand_back(
        d_mixed, d_halo, slope_halo, project_weight, hidden, act_slope, field_in, d_section, dk,
        expand_weight,
    )
    sums = lax.psum((expand_sum, depth_sum, project_sum, qkv_sum, out_sum, bias_sum), ("lat", "lon"))
    factor = float(ROWS * COLS * lax.axis_size("lat") * lax.axis_size("lon")) ** (-0.5)
    return (
        grad_in,
        sums[0] * factor,
        sums[1].reshape(3, 3, EXP) * factor,
        sums[2].T * factor,
        sums[3] * factor,
        sums[4] * factor,
        sums[5].reshape(4, 15, 15) * factor,
    )


def solution(mesh):
    placed = (P("lat", "lon", None), P("lat", "lon", None), P(), P(), P(), P(), P(), P())
    return jax.shard_map(
        on_device,
        mesh=mesh,
        in_specs=placed,
        out_specs=(P("lat", "lon", None), P(), P(), P(), P(), P(), P()),
        check_vma=False,
    )
```

time: 575 us -> 362 us (0.63); the launches traced: 566 us -> 361 us
  waiting for transfers between devices: 192 us -> 100 us
  matrix products: 87.1 us -> 4.24 us
  Pallas kernels: 0 us -> 78 us
  other arithmetic: 82.6 us -> 7.14 us
  local copies, waits for them, and re-layouts: 64.4 us -> 23.1 us
  starting transfers between devices: 54.5 us -> 61.2 us
    pallas_call x0 -> x5, Pallas kernels: none -> 78 us  [the longest x1 23.2 us: attention(): pl.pallas_call(attention_body, grid=(n_groups // 4,), in_specs=[whole(sha...]
    dot_general x18 -> x2, matrix products: 81.1 us -> 4.24 us  [the longest x1 2.82 us: on_device(): jnp.einsum('tsr,hr->sht', onehot, rel_bias.reshape(4, 225), precision=lax...]
    psum x1, waiting for transfers between devices: 144 us -> 83.2 us  [on_device(): lax.psum((expand_sum, depth_sum, project_sum, qkv_sum, out_sum, bias_sum)...]
    all_to_all x6 -> x3, waiting for transfers between devices: 41.3 us -> 3.05 us  [exchange(): lax.all_to_all(pieces, ('lat', 'lon'), split_axis=0, concat_axis=0, axis_...]
    add x3 -> x0, other arithmetic: 28.8 us -> none  [the longest x1 16 us: gelu_slope(): 0.5 * (1.0 + tanh_val)]
    convert_element_type x8 -> x5, other arithmetic: 21.9 us -> 0.08 us  [the longest x3 0.04 us: on_device(): (c.astype(F32) + d.astype(F32)).astype(BF16)]
    reshape x11 -> x5, local copies, waits for them, and re-layouts: 24.4 us -> 2.75 us  [the longest x1 2.39 us: to_pieces(): shaped = field.reshape(16, 2, 4, 16, CHAN).transpose(0, 2, 1, 3, 4)]
    convert_element_type x5 -> x2, local copies, waits for them, and re-layouts: 19.2 us -> 0.05 us  [on_device(): d.astype(F32)]
  transfers between devices with their start and end apart: 15 -> 16, of which waited for: 8 -> 6; matrix products, arithmetic and copies ran while one was open for 14% -> 5% of each run, Pallas kernels for 0% -> 15%
where the time goes in v1:
time: 362 us; the launch traced here: 361 us
  waiting for transfers between devices  100 us (28%)
  Pallas kernels  78 us (22%)
  blocking collectives  72.2 us (20%)
  starting transfers between devices  61.2 us (17%)
  local copies, waits for them, and re-layouts  23.1 us (6%)
  between operations  14.5 us (4%)
  other arithmetic  7.14 us (2%)
  matrix products  4.24 us (1%)
    psum x1, waiting for transfers between devices, on_device(): lax.psum((expand_sum, depth_sum, project_sum, qkv_sum, out_sum, bias_sum)...  83.2 us
    psum x1, blocking collectives, on_device(): lax.psum((expand_sum, depth_sum, project_sum, qkv_sum, out_sum, bias_sum)...  72.2 us
    all_to_all x3, starting transfers between devices, exchange(): lax.all_to_all(pieces, ('lat', 'lon'), split_axis=0, concat_axis=0, axis_...  32.9 us
    pallas_call x1, Pallas kernels, attention(): pl.pallas_call(attention_body, grid=(n_groups // 4,), in_specs=[whole(sha...  23.2 us
    pallas_call x1, Pallas kernels, expand_back(): pl.pallas_call(expand_back_body, grid=(STEPS,), in_specs=[band((BLK, COLS...  23 us
    pallas_call x1, Pallas kernels, mix(): pl.pallas_call(mix_body, grid=(STEPS,), in_specs=[band((BLK, COLS, EXP)),...  15.9 us
    ppermute x3, starting transfers between devices, halo_of(): above = lax.ppermute(bottom, 'lat', south)  11.9 us
    ppermute x3, waiting for transfers between devices, halo_of(): above = lax.ppermute(bottom, 'lat', south)  10 us
  transfers between devices with their start and end apart: 16, of which 6 were waited for; matrix products, arithmetic and copies ran while one was open for 5% of the time, Pallas kernels for 15%

profile of v1, /device:TPU:1, one launch (start us, length us, event | category | flops | bytes accessed | tf_op | source)
XLA Modules:
  0.0 361.0 jit_solution(4004141766229924290)
XLA Ops:
  7.2 0.9 slice_bitcast_fusion.5
  8.1 1.3 collective-permute-start.1
  9.4 4.7 %collective-permute-start = (bf16[64,256]{1,0:T(8,128)(2,1)S(1)}, bf16[64,256]{1,0:T(8,128)(2,1)S(1)}, u32[]{:S(2)}, u32[]{:S(2)}) collective-permute-start(bf16[64,256]{1,0:T(8,128)(2,1)S(1)} %get-tuple-element.71), channel_id=1, source_target_pairs={{0,16},{16,32},{32,48},{48,64},{64,80},{80,96},{96,112},{1,17},{17... | collective-permute-start | bytes 98312 | tf_op jit(solution)/shard_map/ppermute | solution.py:421
  14.1 2.4 copy.34
  16.5 13.2 %all-to-all-start.1 = ((bf16[64,32,256]{2,1,0:T(8,128)(2,1)}), bf16[64,32,256]{2,1,0:T(8,128)(2,1)S(1)}, u32[]{:S(2)}, u32[]{:S(2)}) async-start(bf16[64,32,256]{2,1,0:T(8,128)(2,1)} %bitcast.63), calls=%async_computation.1 | async-start | bytes 2097152 | tf_op jit(solution)/shard_map/all_to_all | solution.py:441
  30.0 1.5 collective-permute-start.3
  31.5 1.3 collective-permute-start.2
  32.8 6.6 %expand.1 = (bf16[32,64,1024]{2,1,0:T(8,128)(2,1)S(1)}, bf16[32,64,1024]{2,1,0:T(8,128)(2,1)S(1)}) custom-call(bf16[32,64,256]{2,1,0:T(8,128)(2,1)S(1)} %copy-done.1, bf16[256,1024]{1,0:T(8,128)(2,1)S(1)} %copy-done.6), custom_call_target="tpu_custom_call" | custom-call | flops 1073741824 | bytes 10485760 | tf_op jit(solution)/shard_map/expand/pallas_call | solution.py:88
  39.4 2.0 copy-done
  41.4 2.0 copy-done.4
  43.5 15.9 %mix.1 = (bf16[64,32,256]{2,1,0:T(8,128)(2,1)S(1)}, bf16[32,64,1024]{2,1,0:T(8,128)(2,1)}, bf16[32,64,1024]{2,1,0:T(8,128)(2,1)}) custom-call(bf16[32,64,1024]{2,1,0:T(8,128)(2,1)} %copy-done, bf16[32,64,1024]{2,1,0:T(8,128)(2,1)} %copy-done, bf16[32,64,1024]{2,1,0:T(8,128)(2,1)} %copy-done, bf16[208,256]{1,0:T(8,128)(2,1)S(1)} %pad_maximum_fusion.1.halo_ref, ...), custom_call_target="tpu_custom_call" | custom-call | flops 1073741824 | bytes 16777216 | tf_op jit(solution)/shard_map/mix/pallas_call | solution.py:157
  59.4 1.0 copy-done.8
  60.4 12.3 %all-to-all-start = ((bf16[64,32,256]{2,1,0:T(8,128)(2,1)}), bf16[64,32,256]{2,1,0:T(8,128)(2,1)}, u32[]{:S(2)}, u32[]{:S(2)}) async-start(bf16[64,32,256]{2,1,0:T(8,128)(2,1)} %copy-done.8), calls=%async_computation | async-start | bytes 2097152 | tf_op jit(solution)/shard_map/all_to_all | solution.py:441
  72.8 2.8 fusion.4
  75.6 0.1 reshape.62.bias_ref
  75.8 6.6 %copy.44 = bf16[32,64,1024]{2,0,1:T(8,128)(2,1)} copy(bf16[32,64,1024]{2,1,0:T(8,128)(2,1)} %get-tuple-element.26.slope_ref) | data formatting | bytes 8388608 | tf_op jit(solution)/shard_map/mix/pallas_call | solution.py:157
  82.4 1.7 slice_bitcast_fusion.1
  84.1 1.6 collective-permute-start.9
  85.7 3.0 all-to-all-done.x_ref
  88.8 23.2 %attention.1 = (bf16[64,32,256]{2,1,0:T(8,128)(2,1)S(1)}, f32[256,768]{1,0:T(8,128)}, f32[256,256]{1,0:T(8,128)}, f32[64,256]{1,0:T(8,128)S(1)}) custom-call(bf16[64,32,256]{2,1,0:T(8,128)(2,1)} %all-to-all-done.x_ref, bf16[64,32,256]{2,1,0:T(8,128)(2,1)S(1)} %all-to-all-done.1.cot_ref, bf16[256,768]{1,0:T(8,128)(2,1)S(1)} %copy-done.10, ...), custom_call_target="tpu_custom_call" | custom-call | flops 2684354560 | bytes 6291456 | tf_op jit(solution)/shard_map/attention/pallas_call | solution.py:261
  112.0 1.0 copy-done.7
  113.0 7.5 %all-to-all-start.2 = ((bf16[64,32,256]{2,1,0:T(8,128)(2,1)}), bf16[64,32,256]{2,1,0:T(8,128)(2,1)S(1)}, u32[]{:S(2)}, u32[]{:S(2)}) async-start(bf16[64,32,256]{2,1,0:T(8,128)(2,1)} %copy-done.7), calls=%async_computation.2 | async-start | bytes 2097152 | tf_op jit(solution)/shard_map/all_to_all | solution.py:441
  120.5 0.9 slice_bitcast_fusion.3
  121.4 2.9 collective-permute-start.8
  124.3 9.1 %collective-permute-done.8 = bf16[64,1024]{1,0:T(8,128)(2,1)S(1)} collective-permute-done((bf16[64,1024]{1,0:T(8,128)(2,1)}, bf16[64,1024]{1,0:T(8,128)(2,1)S(1)}, u32[]{:S(2)}, u32[]{:S(2)}) %collective-permute-start.8) | collective-permute-done | bytes 131104 | tf_op jit(solution)/shard_map/ppermute | solution.py:421
  133.6 0.2 collective-permute-start.11
  133.8 1.6 collective-permute-start.10
  135.5 2.1 collective-permute-done.11
  137.5 2.1 collective-permute-done.10
  139.7 0.8 pad_maximum_fusion.halo_slope_ref
  140.6 1.3 collective-permute-start.5
  141.9 4.3 %collective-permute-start.4 = (bf16[64,256]{1,0:T(8,128)(2,1)S(1)}, bf16[64,256]{1,0:T(8,128)(2,1)S(1)}, u32[]{:S(2)}, u32[]{:S(2)}) collective-permute-start(bf16[64,256]{1,0:T(8,128)(2,1)S(1)} %get-tuple-element.65), channel_id=1, source_target_pairs={{0,16},{16,32},{32,48},{48,64},{64,80},{80,96},{96,112},{1,17},{17... | collective-permute-start | bytes 98312 | tf_op jit(solution)/shard_map/ppermute | solution.py:421
  146.4 0.9 collective-permute-done.4
  147.3 7.6 %collective-permute-start.7 = (bf16[40,256]{1,0:T(8,128)(2,1)S(1)}, bf16[40,256]{1,0:T(8,128)(2,1)S(1)}, u32[]{:S(2)}, u32[]{:S(2)}) collective-permute-start(bf16[40,256]{1,0:T(8,128)(2,1)S(1)} %get-tuple-element.88), channel_id=1, source_target_pairs={{1,0},{2,1},{3,2},{4,3},{5,4},{6,5},{7,6},{8,7},{9,8},{10,9},{11,1... | collective-permute-start | bytes 61448 | tf_op jit(solution)/shard_map/ppermute | solution.py:427
  154.9 9.2 %project_back.1 = (f32[32,64,256]{2,1,0:T(8,128)S(1)}, bf16[32,64,1024]{2,1,0:T(8,128)(2,1)}, f32[256,1024]{1,0:T(8,128)}) custom-call(bf16[32,64,256]{2,1,0:T(8,128)(2,1)S(1)} %copy-done.2, bf16[64,32,256]{2,1,0:T(8,128)(2,1)S(1)} %all-to-all-done.2.db_ref, bf16[32,64,1024]{2,1,0:T(8,128)(2,1)} %get-tuple-element.25.mixed_ref, ...), custom_call_target="tpu_custom_call" | custom-call | flops 2147483648 | bytes 16777216 | tf_op jit(solution)/shard_map/project_back/pallas_call | solution.py:304
  164.1 1.3 copy-done.5
  165.4 0.7 pad_maximum_fusion.2.halo_ref
  166.1 23.0 %expand_back.1 = (bf16[32,64,256]{2,1,0:T(8,128)(2,1)}, f32[256,1024]{1,0:T(8,128)}, f32[9,1024]{1,0:T(8,128)}) custom-call(bf16[32,64,1024]{2,1,0:T(8,128)(2,1)} %get-tuple-element.27.cur_ref.before_ref.after_ref, bf16[32,64,1024]{2,1,0:T(8,128)(2,1)} %get-tuple-element.27.cur_ref.before_ref.after_ref, ...), custom_call_target="tpu_custom_call" | custom-call | flops 2147483648 | bytes 20971520 | tf_op jit(solution)/shard_map/expand_back/pallas_call | solution.py:390
  189.3 1.4 fusion.5
  190.7 72.2 %all-reduce = (f32[9,1024]{1,0:T(8,128)S(1)}, f32[4,225]{1,0:T(4,128)S(1)}) all-reduce(f32[9,1024]{1,0:T(8,128)S(1)} %copy-done.15, f32[4,225]{1,0:T(4,128)S(1)} %fusion.5), channel_id=1, replica_groups=mesh['lat'=8,'lon'=16] {'lat','lon'}, use_global_device_ids=true, to_apply=%region_1.0 | all-reduce | flops 10116 | bytes 80928 | tf_op jit(solution)/shard_map/psum | solution.py:504
  262.9 0.6 mul.47
  263.6 0.6 copy.47
  264.3 83.2 %all-reduce.4.cloned.1.call-done = (f32[256,1024]{1,0:T(8,128)}, f32[256,1024]{1,0:T(8,128)}, f32[256,768]{1,0:T(8,128)}, f32[256,256]{1,0:T(8,128)}) async-done(((f32[256,1024]{1,0:T(8,128)}, f32[256,1024]{1,0:T(8,128)}, f32[256,768]{1,0:T(8,128)}, f32[256,256]{1,0:T(8,128)}), (f32[256,1024]{1,0:T(8,128)}, f32[256,1024]{1,0:T(8,128)}, f32[256,768]{1,0:T(8,128)}, ...) | async-done | bytes 3145744 | tf_op jit(solution)/shard_map/psum | solution.py:504
  347.4 2.4 broadcast_multiply_fusion
  349.8 1.3 multiply_bitcast_fusion
  351.2 1.3 copy.46
  352.5 0.9 broadcast_multiply_fusion.1
  353.4 0.7 broadcast_multiply_fusion.2
  (79 shorter events, 1.2 us)
Async XLA Ops:
  7.2 22.5 %copy-start.1 = (bf16[32,64,256]{2,1,0:T(8,128)(2,1)S(1)}, bf16[32,64,256]{2,1,0:T(8,128)(2,1)}, u32[]{:S(2)}) copy-start(bf16[32,64,256]{2,1,0:T(8,128)(2,1)} %x_ref.5) | copy-start | bytes 3145732
  7.2 25.6 %copy-start.6 = (bf16[256,1024]{1,0:T(8,128)(2,1)S(1)}, bf16[256,1024]{1,0:T(8,128)(2,1)}, u32[]{:S(2)}) copy-start(bf16[256,1024]{1,0:T(8,128)(2,1)} %we_ref.5) | copy-start | bytes 1572868
  8.1 21.8 %collective-permute-start.1 = (bf16[64,256]{1,0:T(8,128)(2,1)S(1)}, bf16[64,256]{1,0:T(8,128)(2,1)S(1)}, u32[]{:S(2)}, u32[]{:S(2)}) collective-permute-start(bf16[64,256]{1,0:T(8,128)(2,1)S(1)} %get-tuple-element.72), channel_id=1, source_target_pairs={{16,0},{32,16},{48,32},{64,48},{80,64},{96,80},{112,96},{17,1},{33... | collective-permute-start | bytes 98312 | tf_op jit(solution)/shard_map/ppermute | solution.py:422
  9.4 20.5 %collective-permute-start = (bf16[64,256]{1,0:T(8,128)(2,1)S(1)}, bf16[64,256]{1,0:T(8,128)(2,1)S(1)}, u32[]{:S(2)}, u32[]{:S(2)}) collective-permute-start(bf16[64,256]{1,0:T(8,128)(2,1)S(1)} %get-tuple-element.71), channel_id=1, source_target_pairs={{0,16},{16,32},{32,48},{48,64},{64,80},{80,96},{96,112},{1,17},{17... | collective-permute-start | bytes 98312 | tf_op jit(solution)/shard_map/ppermute | solution.py:421
  14.0 29.4 %copy-start.16 = (f32[3,3,1024]{2,1,0:T(4,128)S(1)}, f32[3,3,1024]{2,1,0:T(4,128)}, u32[]{:S(2)}) copy-start(f32[3,3,1024]{2,1,0:T(4,128)} %param.13) | copy-start | bytes 110596
  14.1 29.4 %copy-start.3 = (bf16[1024,256]{1,0:T(8,128)(2,1)S(1)}, bf16[1024,256]{1,0:T(8,128)(2,1)}, u32[]{:S(2)}) copy-start(bf16[1024,256]{1,0:T(8,128)(2,1)} %wp_ref.5) | copy-start | bytes 1572868
  16.5 44.0 %all-to-all-start.1 = ((bf16[64,32,256]{2,1,0:T(8,128)(2,1)}), bf16[64,32,256]{2,1,0:T(8,128)(2,1)S(1)}, u32[]{:S(2)}, u32[]{:S(2)}) async-start(bf16[64,32,256]{2,1,0:T(8,128)(2,1)} %bitcast.63), calls=%async_computation.1 | async-start | bytes 2097152 | tf_op jit(solution)/shard_map/all_to_all | solution.py:441
  30.0 13.5 %collective-permute-start.3 = (bf16[40,256]{1,0:T(8,128)(2,1)S(1)}, bf16[40,256]{1,0:T(8,128)(2,1)S(1)}, u32[]{:S(2)}, u32[]{:S(2)}) collective-permute-start(bf16[40,256]{1,0:T(8,128)(2,1)S(1)} %get-tuple-element.90), channel_id=1, source_target_pairs={{1,0},{2,1},{3,2},{4,3},{5,4},{6,5},{7,6},{8,7},{9,8},{10,9},{11,1... | collective-permute-start | bytes 61448 | tf_op jit(solution)/shard_map/ppermute | solution.py:427
  31.5 11.9 %collective-permute-start.2 = (bf16[40,256]{1,0:T(8,128)(2,1)S(1)}, bf16[40,256]{1,0:T(8,128)(2,1)S(1)}, u32[]{:S(2)}, u32[]{:S(2)}) collective-permute-start(bf16[40,256]{1,0:T(8,128)(2,1)S(1)} %get-tuple-element.89), channel_id=1, source_target_pairs={{0,1},{1,2},{2,3},{3,4},{4,5},{5,6},{6,7},{7,8},{8,9},{9,10},{10,1... | collective-permute-start | bytes 61448 | tf_op jit(solution)/shard_map/ppermute | solution.py:424
  39.4 2.0 copy-start
  41.4 2.0 copy-start.4
  43.4 16.0 %copy-start.9 = (f32[9,1024]{1,0:T(8,128)}, f32[9,1024]{1,0:T(8,128)S(1)}, u32[]{:S(2)}) copy-start(f32[9,1024]{1,0:T(8,128)S(1)} %reshape.58.dk_ref) | copy-start | bytes 110596
  43.5 29.2 %copy-start.17 = (f32[4,15,15]{2,0,1:T(4,128)S(1)}, f32[4,15,15]{2,0,1:T(4,128)}, u32[]{:S(2)}) copy-start(f32[4,15,15]{2,0,1:T(4,128)} %param.17) | copy-start | bytes 10804
  43.5 29.3 %copy-start.18 = (s32[64,64]{0,1:T(8,128)S(1)}, s32[64,64]{0,1:T(8,128)}, u32[]{:S(2)}) copy-start(s32[64,64]{0,1:T(8,128)} %constant.6.clone) | copy-start | bytes 49156
  59.4 1.0 copy-start.8
  60.4 28.3 %all-to-all-start = ((bf16[64,32,256]{2,1,0:T(8,128)(2,1)}), bf16[64,32,256]{2,1,0:T(8,128)(2,1)}, u32[]{:S(2)}, u32[]{:S(2)}) async-start(bf16[64,32,256]{2,1,0:T(8,128)(2,1)} %copy-done.8), calls=%async_computation | async-start | bytes 2097152 | tf_op jit(solution)/shard_map/all_to_all | solution.py:441
  75.8 13.0 %copy-start.10 = (bf16[256,768]{1,0:T(8,128)(2,1)S(1)}, bf16[256,768]{1,0:T(8,128)(2,1)}, u32[]{:S(2)}) copy-start(bf16[256,768]{1,0:T(8,128)(2,1)} %wqkv_ref.1) | copy-start | bytes 1179652
  75.8 13.0 %copy-start.11 = (bf16[256,256]{1,0:T(8,128)(2,1)S(1)}, bf16[256,256]{1,0:T(8,128)(2,1)}, u32[]{:S(2)}) copy-start(bf16[256,256]{1,0:T(8,128)(2,1)} %wout_ref.1) | copy-start | bytes 393220
  75.8 13.0 %copy-start.12 = (bf16[256,256]{1,0:T(8,128)(2,1)S(1)}, bf16[256,256]{1,0:T(8,128)(2,1)}, u32[]{:S(2)}) copy-start(bf16[256,256]{1,0:T(8,128)(2,1)} %constant.7.clone.swap_ref) | copy-start | bytes 393220
  84.1 51.3 %copy-start.2 = (bf16[32,64,256]{2,1,0:T(8,128)(2,1)S(1)}, bf16[32,64,256]{2,1,0:T(8,128)(2,1)}, u32[]{:S(2)}) copy-start(bf16[32,64,256]{2,1,0:T(8,128)(2,1)} %cot_ref.1) | copy-start | bytes 3145732
  84.1 40.2 %collective-permute-start.9 = (bf16[64,1024]{1,0:T(8,128)(2,1)}, bf16[64,1024]{1,0:T(8,128)(2,1)S(1)}, u32[]{:S(2)}, u32[]{:S(2)}) collective-permute-start(bf16[64,1024]{1,0:T(8,128)(2,1)} %get-tuple-element.60), channel_id=1, source_target_pairs={{16,0},{32,16},{48,32},{64,48},{80,64},{96,80},{112,96},{17,1},{33... | collective-permute-start | bytes 393224 | tf_op jit(solution)/shard_map/ppermute | solution.py:422
  112.0 1.0 copy-start.7
  113.0 27.5 %all-to-all-start.2 = ((bf16[64,32,256]{2,1,0:T(8,128)(2,1)}), bf16[64,32,256]{2,1,0:T(8,128)(2,1)S(1)}, u32[]{:S(2)}, u32[]{:S(2)}) async-start(bf16[64,32,256]{2,1,0:T(8,128)(2,1)} %copy-done.7), calls=%async_computation.2 | async-start | bytes 2097152 | tf_op jit(solution)/shard_map/all_to_all | solution.py:441
  120.4 227.0 %all-reduce.4.cloned.1.call-start = ((), (), s32[]{:S(2)}) async-start(), calls=%async_computation.3 | async-start | bytes 6291456 | tf_op jit(solution)/shard_map/psum | solution.py:504
  121.4 12.1 %collective-permute-start.8 = (bf16[64,1024]{1,0:T(8,128)(2,1)}, bf16[64,1024]{1,0:T(8,128)(2,1)S(1)}, u32[]{:S(2)}, u32[]{:S(2)}) collective-permute-start(bf16[64,1024]{1,0:T(8,128)(2,1)} %get-tuple-element.59), channel_id=1, source_target_pairs={{0,16},{16,32},{32,48},{48,64},{64,80},{80,96},{96,112},{1,17},{17... | collective-permute-start | bytes 393224 | tf_op jit(solution)/shard_map/ppermute | solution.py:421
  133.6 3.9 %collective-permute-start.11 = (bf16[40,1024]{1,0:T(8,128)(2,1)S(1)}, bf16[40,1024]{1,0:T(8,128)(2,1)S(1)}, u32[]{:S(2)}, u32[]{:S(2)}) collective-permute-start(bf16[40,1024]{1,0:T(8,128)(2,1)S(1)} %get-tuple-element.86), channel_id=1, source_target_pairs={{1,0},{2,1},{3,2},{4,3},{5,4},{6,5},{7,6},{8,7},{9,8},{10,9},{11,1... | collective-permute-start | bytes 245768 | tf_op jit(solution)/shard_map/ppermute | solution.py:427
  133.8 5.9 %collective-permute-start.10 = (bf16[40,1024]{1,0:T(8,128)(2,1)S(1)}, bf16[40,1024]{1,0:T(8,128)(2,1)S(1)}, u32[]{:S(2)}, u32[]{:S(2)}) collective-permute-start(bf16[40,1024]{1,0:T(8,128)(2,1)S(1)} %get-tuple-element.85), channel_id=1, source_target_pairs={{0,1},{1,2},{2,3},{3,4},{4,5},{5,6},{6,7},{7,8},{8,9},{9,10},{10,1... | collective-permute-start | bytes 245768 | tf_op jit(solution)/shard_map/ppermute | solution.py:424
  140.6 5.8 %collective-permute-start.5 = (bf16[64,256]{1,0:T(8,128)(2,1)S(1)}, bf16[64,256]{1,0:T(8,128)(2,1)S(1)}, u32[]{:S(2)}, u32[]{:S(2)}) collective-permute-start(bf16[64,256]{1,0:T(8,128)(2,1)S(1)} %get-tuple-element.66), channel_id=1, source_target_pairs={{16,0},{32,16},{48,32},{64,48},{80,64},{96,80},{112,96},{17,1},{33... | collective-permute-start | bytes 98312 | tf_op jit(solution)/shard_map/ppermute | solution.py:422
  141.9 5.3 %collective-permute-start.4 = (bf16[64,256]{1,0:T(8,128)(2,1)S(1)}, bf16[64,256]{1,0:T(8,128)(2,1)S(1)}, u32[]{:S(2)}, u32[]{:S(2)}) collective-permute-start(bf16[64,256]{1,0:T(8,128)(2,1)S(1)} %get-tuple-element.65), channel_id=1, source_target_pairs={{0,16},{16,32},{32,48},{48,64},{64,80},{80,96},{96,112},{1,17},{17... | collective-permute-start | bytes 98312 | tf_op jit(solution)/shard_map/ppermute | solution.py:421
  147.3 18.1 %collective-permute-start.7 = (bf16[40,256]{1,0:T(8,128)(2,1)S(1)}, bf16[40,256]{1,0:T(8,128)(2,1)S(1)}, u32[]{:S(2)}, u32[]{:S(2)}) collective-permute-start(bf16[40,256]{1,0:T(8,128)(2,1)S(1)} %get-tuple-element.88), channel_id=1, source_target_pairs={{1,0},{2,1},{3,2},{4,3},{5,4},{6,5},{7,6},{8,7},{9,8},{10,9},{11,1... | collective-permute-start | bytes 61448 | tf_op jit(solution)/shard_map/ppermute | solution.py:427
  154.9 10.5 %collective-permute-start.6 = (bf16[40,256]{1,0:T(8,128)(2,1)S(1)}, bf16[40,256]{1,0:T(8,128)(2,1)S(1)}, u32[]{:S(2)}, u32[]{:S(2)}) collective-permute-start(bf16[40,256]{1,0:T(8,128)(2,1)S(1)} %get-tuple-element.87), channel_id=1, source_target_pairs={{0,1},{1,2},{2,3},{3,4},{4,5},{5,6},{6,7},{7,8},{8,9},{9,10},{10,1... | collective-permute-start | bytes 61448 | tf_op jit(solution)/shard_map/ppermute | solution.py:424
  164.1 1.3 copy-start.5
  166.1 23.2 %copy-start.19 = (s32[64,64]{0,1:T(8,128)S(1)}, s32[64,64]{0,1:T(8,128)}, u32[]{:S(2)}) copy-start(s32[64,64]{0,1:T(8,128)} %constant.6.clone) | copy-start | bytes 49156
  189.1 1.6 copy-start.15
  347.4 5.0 %copy-start.13 = (f32[256,768]{1,0:T(8,128)S(1)}, f32[256,768]{1,0:T(8,128)}, u32[]{:S(2)}) copy-start(f32[256,768]{1,0:T(8,128)} %get-tuple-element.55) | copy-start | bytes 2359300
  347.4 6.0 %copy-start.14 = (f32[256,256]{1,0:T(8,128)S(1)}, f32[256,256]{1,0:T(8,128)}, u32[]{:S(2)}) copy-start(f32[256,256]{1,0:T(8,128)} %get-tuple-element.56) | copy-start | bytes 786436
Sparse Core Ops, SparseCore 0:
  189.3 158.1 all-reduce.3

commit v2 on v1

v2 whole, which is shorter than its diff:
```python
import math

import jax
import jax.numpy as jnp
import numpy as np
from jax import lax
from jax.experimental import pallas as pl
from jax.experimental.pallas import tpu as pltpu
from jax.sharding import PartitionSpec as P

EPSILON = 1e-05
GELU_C = math.sqrt(2.0 / math.pi)
F32 = jnp.float32
BF16 = jnp.bfloat16
MIB = 1 << 20

ROWS, COLS, CHAN, EXP = 32, 64, 256, 1024
BLK = 4
STEPS = ROWS // BLK
TOK = BLK * COLS
LANES = 128
EDGE = 40
HALO = 2 * COLS + 2 * EDGE
LONG = 72


def layer_norm(values):
    average = jnp.mean(values, axis=-1, keepdims=True)
    centred = values - average
    variance = jnp.mean(centred * centred, axis=-1, keepdims=True)
    inv_std = lax.rsqrt(variance + EPSILON)
    return (centred * inv_std, inv_std)


def layer_norm_back(normed, inv_std, grads):
    mean_grad = jnp.mean(grads, axis=-1, keepdims=True)
    mean_cross = jnp.mean(grads * normed, axis=-1, keepdims=True)
    return (grads - mean_grad - normed * mean_cross) * inv_std


def gelu_slope(values):
    squared = values * values
    tanh_val = jnp.tanh(values * (GELU_C + (GELU_C * 0.044715) * squared))
    gate = 0.5 + 0.5 * tanh_val
    result = values * gate
    slopes = gate + result * (1.0 - gate) * (2.0 * GELU_C + (6.0 * GELU_C * 0.044715) * squared)
    return (result, slopes)


def dot(left, right):
    return lax.dot_general(left, right, (((1,), (0,)), ((), ())), preferred_element_type=F32)


def dot_nt(left, right):
    return lax.dot_general(left, right, (((1,), (1,)), ((), ())), preferred_element_type=F32)


def dot_tn(left, right):
    return lax.dot_general(left, right, (((0,), (0,)), ((), ())), preferred_element_type=F32)


def params(mib):
    return pltpu.CompilerParams(vmem_limit_bytes=mib * MIB)


def whole(shape):
    return pl.BlockSpec(shape, lambda i: (0,) * len(shape))


def band(shape):
    return pl.BlockSpec(shape, lambda i: (i,) + (0,) * (len(shape) - 1))


ROW_BEFORE = pl.BlockSpec((1, COLS, EXP), lambda i: (jnp.maximum(BLK * i - 1, 0), 0, 0))
ROW_AFTER = pl.BlockSpec((1, COLS, EXP), lambda i: (jnp.minimum(BLK * i + BLK, ROWS - 1), 0, 0))


TILED = (128, 16, 128)


def to_tiles(ref, out_ref, at):
    wide = ref.shape[1] // 128
    for r in range(ref.shape[0] // 16):
        for c in range(wide):
            tile = ref[16 * r : 16 * r + 16, 128 * c : 128 * c + 128]
            out_ref[at + wide * r + c, :16] = tile.astype(BF16)


def from_tiles(tiles, wide):
    shaped = tiles.reshape(-1, wide, 16, 128).transpose(0, 2, 1, 3)
    return shaped.reshape(-1, wide * 128).astype(F32)


def expand_body(x_ref, we_ref, hid_ref, slope_ref):
    normed, _ = layer_norm(x_ref[...].reshape(TOK, CHAN).astype(F32))
    normed_b = normed.astype(BF16)
    for at in range(0, EXP, 256):
        val, slope = gelu_slope(dot(normed_b, we_ref[:, at : at + 256]))
        hid_ref[:, :, at : at + 256] = val.astype(BF16).reshape(BLK, COLS, 256)
        slope_ref[:, :, at : at + 256] = slope.astype(BF16).reshape(BLK, COLS, 256)


def expand(x, we):
    wide = jax.ShapeDtypeStruct((ROWS, COLS, EXP), BF16)
    return pl.pallas_call(
        expand_body,
        grid=(STEPS,),
        in_specs=[band((BLK, COLS, CHAN)), whole((CHAN, EXP))],
        out_specs=[band((BLK, COLS, EXP))] * 2,
        out_shape=[wide, wide],
        compiler_params=params(58),
        cost_estimate=pl.CostEstimate(
            flops=2 * ROWS * COLS * CHAN * EXP, bytes_accessed=10 * MIB, transcendentals=ROWS * COLS * EXP
        ),
        name="expand",
    )(x, we)


def mix_body(
    cur_ref, before_ref, after_ref, top_ref, bottom_ref, left_ref, right_ref, dk_ref, wp_ref, x_ref,
    section_ref, mixed_ref, slope_ref,
):
    step = pl.program_id(0)
    first, last = step == 0, step == STEPS - 1
    for at in range(0, EXP, LANES):
        span = slice(at, at + LANES)
        rows = [jnp.where(first, top_ref[:, span], before_ref[0, :, span]).astype(F32)]
        rows += [cur_ref[r, :, span].astype(F32) for r in range(BLK)]
        rows += [jnp.where(last, bottom_ref[:, span], after_ref[0, :, span]).astype(F32)]
        kern = [dk_ref[n, span][None] for n in range(9)]
        for r in range(BLK):
            parts = [
                kern[b] * rows[r] + kern[3 + b] * rows[r + 1] + kern[6 + b] * rows[r + 2]
                for b in range(3)
            ]
            left = left_ref[step, r : r + 1, span]
            right = right_ref[step, r : r + 1, span]
            pre = (
                parts[1]
                + jnp.concatenate([left, parts[0][:-1]], axis=0)
                + jnp.concatenate([parts[2][1:], right], axis=0)
            )
            val, slope = gelu_slope(pre)
            mixed_ref[r, :, span] = val.astype(BF16)
            slope_ref[r, :, span] = slope.astype(BF16)
    branch = dot(mixed_ref[...].reshape(TOK, EXP), wp_ref[...])
    section = (x_ref[...].reshape(TOK, CHAN).astype(F32) + branch).astype(BF16)
    section = section.reshape(2, 2, 4, 16, CHAN)
    for pair in range(2):
        for quad in range(4):
            section_ref[4 * pair + quad] = section[pair, :, quad].reshape(32, CHAN)


def mix(hidden, ring_out, dk, wp, x):
    wide = jax.ShapeDtypeStruct((ROWS, COLS, EXP), BF16)
    return pl.pallas_call(
        mix_body,
        grid=(STEPS,),
        in_specs=[
            band((BLK, COLS, EXP)), ROW_BEFORE, ROW_AFTER, whole((COLS, EXP)), whole((COLS, EXP)),
            whole((STEPS, 8, EXP)), whole((STEPS, 8, EXP)),
            whole((9, EXP)), whole((EXP, CHAN)), band((BLK, COLS, CHAN)),
        ],
        out_specs=[band((8, 32, CHAN)), band((BLK, COLS, EXP)), band((BLK, COLS, EXP))],
        out_shape=[jax.ShapeDtypeStruct((64, 32, CHAN), BF16), wide, wide],
        compiler_params=params(58),
        cost_estimate=pl.CostEstimate(
            flops=2 * ROWS * COLS * CHAN * EXP, bytes_accessed=16 * MIB, transcendentals=ROWS * COLS * EXP
        ),
        name="mix",
    )(hidden, hidden, hidden, *ring_out, dk, wp, x)


def ring_body(
    above_ref, below_ref, first_ref, last_ref, west_ref, east_ref, own_west_ref, own_east_ref,
    we_ref, dk_ref,
    top_ref, bottom_ref, left_ref, right_ref, slope_ref,
):
    west, east = west_ref[...].astype(F32), east_ref[...].astype(F32)
    pad = jnp.zeros((LONG - COLS - 4, CHAN), F32)

    def along(row, at):
        return [
            west[0, at : at + 1], west[1, at : at + 1], row.astype(F32),
            east[0, at : at + 1], east[1, at : at + 1], pad,
        ]

    strips = along(above_ref[0], 0) + along(above_ref[1], 1) + along(first_ref[0], 2)
    strips += along(last_ref[0], 33) + along(below_ref[0], 34) + along(below_ref[1], 35)
    strips += [west[0], west[1], own_west_ref[0].astype(F32)]
    strips += [own_east_ref[1].astype(F32), east[0], east[1]]
    normed, _ = layer_norm(jnp.concatenate(strips, axis=0))
    normed_b = normed.astype(BF16)
    south, lefts, rights = 3 * LONG, 6 * LONG, 6 * LONG + 3 * EDGE
    for at in range(0, EXP, 256):
        span = slice(at, at + 256)
        val, _ = gelu_slope(dot(normed_b, we_ref[:, span]))
        val = val.astype(BF16).astype(F32)
        kern = [dk_ref[n, span][None] for n in range(9)]
        top_ref[:, span] = val[LONG + 2 : LONG + 2 + COLS].astype(BF16)
        bottom_ref[:, span] = val[south + LONG + 2 : south + LONG + 2 + COLS].astype(BF16)
        for ref, base, col in ((left_ref, lefts, 0), (right_ref, rights, 2)):
            total = 0.0
            for a in range(3):
                start = base + EDGE + a + 1
                total = total + kern[3 * a + col] * val[start : start + ROWS]
            for s in range(STEPS):
                ref[s, :BLK, span] = total[BLK * s : BLK * s + BLK]
        for base, out in ((0, 0), (south, COLS)):
            total = 0.0
            for a in range(3):
                for b in range(3):
                    start = base + LONG * a + b + 1
                    total = total + kern[3 * a + b] * val[start : start + COLS]
            slope_ref[out : out + COLS, span] = gelu_slope(total)[1]
        for base, out in ((lefts, 2 * COLS), (rights, 2 * COLS + EDGE)):
            total = 0.0
            for a in range(3):
                for b in range(3):
                    start = base + EDGE * b + a
                    total = total + kern[3 * a + b] * val[start : start + ROWS + 2]
            slope_ref[out : out + ROWS + 2, span] = gelu_slope(total)[1]
            slope_ref[out + ROWS + 2 : out + EDGE, span] = jnp.zeros((EDGE - ROWS - 2, 256), F32)


def ring(halo, field, we, dk):
    above, below, west, east, own_west, own_east = halo
    return pl.pallas_call(
        ring_body,
        grid=(1,),
        in_specs=[
            whole((2, COLS, CHAN)), whole((2, COLS, CHAN)),
            pl.BlockSpec((1, COLS, CHAN), lambda i: (0, 0, 0)),
            pl.BlockSpec((1, COLS, CHAN), lambda i: (ROWS - 1, 0, 0)),
            whole((2, EDGE, CHAN)), whole((2, EDGE, CHAN)), whole((2, EDGE, CHAN)), whole((2, EDGE, CHAN)),
            whole((CHAN, EXP)), whole((9, EXP)),
        ],
        out_specs=[
            whole((COLS, EXP)), whole((COLS, EXP)), whole((STEPS, 8, EXP)), whole((STEPS, 8, EXP)),
            whole((HALO, EXP)),
        ],
        out_shape=[
            jax.ShapeDtypeStruct((COLS, EXP), BF16),
            jax.ShapeDtypeStruct((COLS, EXP), BF16),
            jax.ShapeDtypeStruct((STEPS, 8, EXP), F32),
            jax.ShapeDtypeStruct((STEPS, 8, EXP), F32),
            jax.ShapeDtypeStruct((HALO, EXP), F32),
        ],
        compiler_params=params(58),
        cost_estimate=pl.CostEstimate(
            flops=2 * 672 * CHAN * EXP, bytes_accessed=3 * MIB, transcendentals=900 * EXP
        ),
        name="ring",
    )(above, below, field, field, west, east, own_west, own_east, we, dk)


SWAP = np.zeros((256, 256), np.float32)
for _s in range(16):
    for _g in range(16):
        SWAP[_g * 16 + _s, _s * 16 + _g] = 1.0


def diagonal(full, low):
    halves = []
    for half in range(2):
        lanes = slice(half * 128, half * 128 + 128)
        at = half * 128
        halves.append(jnp.where(low, full[at : at + 64, lanes], full[at + 64 : at + 128, lanes]))
    return jnp.concatenate(halves, axis=1)


def swap(src, dst, swap_ref, n_groups):
    for s in range(0, 64, 16):
        for g in range(0, n_groups, 16):
            moved = dot(swap_ref[...], src[s : s + 16, g : g + 16].reshape(256, CHAN)).astype(BF16)
            dst[g : g + 16, s : s + 16] = moved.reshape(16, 16, CHAN)


def prepare_body(cot_ref, wout_ref, swap_ref, cs_ref, da_ref):
    n_groups = cot_ref.shape[1]
    swap(cot_ref, cs_ref, swap_ref, n_groups)
    for g in range(0, n_groups, 4):
        grads = dot_nt(cs_ref[g : g + 4].reshape(256, CHAN), wout_ref[...])
        da_ref[g : g + 4] = grads.astype(BF16).reshape(4, 64, CHAN)


def prepare(cot, wout, n_groups):
    shape = (64, n_groups, CHAN)
    grouped = (n_groups, 64, CHAN)
    return pl.pallas_call(
        prepare_body,
        grid=(1,),
        in_specs=[whole(shape), whole((CHAN, CHAN)), whole((256, 256))],
        out_specs=[whole(grouped), whole(grouped)],
        out_shape=[jax.ShapeDtypeStruct(grouped, BF16)] * 2,
        compiler_params=params(58),
        cost_estimate=pl.CostEstimate(
            flops=n_groups * 64 * 4 * CHAN * CHAN, bytes_accessed=3 * MIB, transcendentals=0
        ),
        name="prepare",
    )(cot, wout, jnp.asarray(SWAP, BF16))


def attention_body(
    x_ref, da_ref, wqkv_ref, bias_ref, swap_ref,
    out_ref, att_ref, norm_ref, proj_ref, bias_sum_ref, xs_ref, ds_ref,
):
    step = pl.program_id(0)
    n_groups = x_ref.shape[1]

    @pl.when(step == 0)
    def _():
        bias_sum_ref[...] = jnp.zeros_like(bias_sum_ref)
        swap(x_ref, xs_ref, swap_ref, n_groups)

    groups = pl.ds(step * 4, 4)
    tokens = xs_ref[groups].reshape(256, CHAN)
    normed, inv_std = layer_norm(tokens.astype(F32))
    normed_b = normed.astype(BF16)
    norm_ref[...] = normed_b
    projected = dot(normed_b, wqkv_ref[...]).astype(BF16)
    low = lax.broadcasted_iota(jnp.int32, (64, 128), 1) < 64
    head_of = lax.broadcasted_iota(jnp.int32, (64, CHAN), 1) // 64
    masks = [(head_of == h).astype(F32).astype(BF16) for h in range(4)]
    for g in range(4):
        part = slice(g * 64, g * 64 + 64)
        query = projected[part, :CHAN] * 0.125
        key = projected[part, CHAN : 2 * CHAN]
        value = projected[part, 2 * CHAN :]
        da = da_ref[g]
        query_h = jnp.concatenate([query * m for m in masks], axis=0)
        da_h = jnp.concatenate([da * m for m in masks], axis=0)
        scores = dot_nt(key, query_h) + bias_ref[...]
        scores = jnp.exp(scores - jnp.max(scores, axis=0, keepdims=True))
        probs = scores * (1.0 / jnp.sum(scores, axis=0, keepdims=True))
        probs_b = probs.astype(BF16)
        d_probs = dot_nt(value, da_h)
        d_scores = probs * (d_probs - jnp.sum(probs * d_probs, axis=0, keepdims=True))
        bias_sum_ref[...] += d_scores
        d_scores_b = d_scores.astype(BF16)
        att_ref[part] = diagonal(dot_tn(probs_b, value), low).astype(BF16)
        proj_ref[part, :CHAN] = (diagonal(dot_tn(d_scores_b, key), low) * 0.125).astype(BF16)
        proj_ref[part, CHAN : 2 * CHAN] = dot(d_scores_b, query_h).astype(BF16)
        proj_ref[part, 2 * CHAN :] = dot(probs_b, da_h).astype(BF16)
    d_normed = dot_nt(proj_ref[...], wqkv_ref[...])
    d_tokens = layer_norm_back(normed, inv_std, d_normed).astype(BF16)
    ds_ref[groups] = d_tokens.reshape(4, 64, CHAN)

    @pl.when(step == n_groups // 4 - 1)
    def _():
        for s in range(0, 64, 16):
            for g in range(0, n_groups, 16):
                tile = ds_ref[g : g + 16, s : s + 16].reshape(256, CHAN)
                moved = dot(swap_ref[...], tile).astype(BF16)
                out_ref[s : s + 16, g : g + 16] = moved.reshape(16, 16, CHAN)


def attention(tokens, d_att, wqkv, bias):
    n_groups = tokens.shape[1]
    shape = (64, n_groups, CHAN)
    flat = n_groups * 64
    return pl.pallas_call(
        attention_body,
        grid=(n_groups // 4,),
        in_specs=[
            whole(shape), band((4, 64, CHAN)), whole((CHAN, 3 * CHAN)), whole((64, CHAN)),
            whole((256, 256)),
        ],
        out_specs=[
            whole(shape), band((256, CHAN)), band((256, CHAN)), band((256, 3 * CHAN)), whole((64, CHAN)),
        ],
        out_shape=[
            jax.ShapeDtypeStruct(shape, BF16),
            jax.ShapeDtypeStruct((flat, CHAN), BF16),
            jax.ShapeDtypeStruct((flat, CHAN), BF16),
            jax.ShapeDtypeStruct((flat, 3 * CHAN), BF16),
            jax.ShapeDtypeStruct((64, CHAN), F32),
        ],
        scratch_shapes=[pltpu.VMEM((n_groups, 64, CHAN), BF16)] * 2,
        compiler_params=params(58),
        cost_estimate=pl.CostEstimate(
            flops=flat * 4 * CHAN * CHAN * 5, bytes_accessed=8 * MIB, transcendentals=flat * 256
        ),
        name="attention",
    )(tokens, d_att, wqkv, bias, jnp.asarray(SWAP, BF16))


def attention_sums_body(att_ref, cot_ref, norm_ref, proj_ref, out_ref, qkv_acc, out_acc):
    step = pl.program_id(0)

    @pl.when(step == 0)
    def _():
        qkv_acc[...] = jnp.zeros_like(qkv_acc)
        out_acc[...] = jnp.zeros_like(out_acc)

    out_acc[...] += dot_tn(att_ref[...], cot_ref[...])
    qkv_acc[...] += dot_tn(norm_ref[...], proj_ref[...])

    @pl.when(step == pl.num_programs(0) - 1)
    def _():
        to_tiles(qkv_acc, out_ref, 0)
        to_tiles(out_acc, out_ref, 96)


def attention_sums(att, cot, normed, proj):
    flat = att.shape[0]
    return pl.pallas_call(
        attention_sums_body,
        grid=(flat // 512,),
        in_specs=[band((512, CHAN)), band((512, CHAN)), band((512, CHAN)), band((512, 3 * CHAN))],
        out_specs=whole(TILED),
        out_shape=jax.ShapeDtypeStruct(TILED, BF16),
        scratch_shapes=[pltpu.VMEM((CHAN, 3 * CHAN), F32), pltpu.VMEM((CHAN, CHAN), F32)],
        compiler_params=params(58),
        cost_estimate=pl.CostEstimate(
            flops=flat * 8 * CHAN * CHAN, bytes_accessed=6 * MIB, transcendentals=0
        ),
        name="attention_sums",
    )(att, cot, normed, proj)


def project_body(
    cot_ref, db_ref, mixed_ref, slope_ref, wp_ref, ds_ref, dm_ref, tiles_ref, sum_ref, turned_ref
):
    @pl.when(pl.program_id(0) == 0)
    def _():
        sum_ref[...] = jnp.zeros_like(sum_ref)

    pieces = db_ref[...].reshape(2, 4, 2, 16, CHAN)
    branch = jnp.concatenate(
        [pieces[pair, quad, r] for pair in range(2) for r in range(2) for quad in range(4)], axis=0
    )
    d_section = cot_ref[...].reshape(TOK, CHAN).astype(F32) + branch.astype(F32)
    ds_ref[...] = d_section.reshape(BLK, COLS, CHAN)
    d_section_b = d_section.astype(BF16)
    sum_ref[...] += dot_tn(d_section_b, mixed_ref[...].reshape(TOK, EXP))
    for at in range(0, EXP, 256):
        grads = dot_nt(d_section_b, wp_ref[at : at + 256, :])
        slope = slope_ref[:, :, at : at + 256].reshape(TOK, 256).astype(F32)
        dm_ref[:, :, at : at + 256] = (grads * slope).astype(BF16).reshape(BLK, COLS, 256)

    @pl.when(pl.program_id(0) == STEPS - 1)
    def _():
        turned_ref[...] = sum_ref[...].T
        to_tiles(turned_ref, tiles_ref, 0)


def project_back(cot, db, mixed, slope, wp):
    return pl.pallas_call(
        project_body,
        grid=(STEPS,),
        in_specs=[
            band((BLK, COLS, CHAN)), band((8, 32, CHAN)), band((BLK, COLS, EXP)),
            band((BLK, COLS, EXP)), whole((EXP, CHAN)),
        ],
        out_specs=[band((BLK, COLS, CHAN)), band((BLK, COLS, EXP)), whole(TILED)],
        out_shape=[
            jax.ShapeDtypeStruct((ROWS, COLS, CHAN), F32),
            jax.ShapeDtypeStruct((ROWS, COLS, EXP), BF16),
            jax.ShapeDtypeStruct(TILED, BF16),
        ],
        scratch_shapes=[pltpu.VMEM((CHAN, EXP), F32), pltpu.VMEM((EXP, CHAN), F32)],
        compiler_params=params(58),
        cost_estimate=pl.CostEstimate(
            flops=4 * ROWS * COLS * CHAN * EXP, bytes_accessed=16 * MIB, transcendentals=0
        ),
        name="project_back",
    )(cot, db, mixed, slope, wp)


def expand_back_body(
    cur_ref, before_ref, after_ref, halo_ref, halo_slope_ref, wp_ref, hid_ref, slope_ref, x_ref, dk_ref,
    dpre_ref, tiles_ref, depth_ref, top_ref, bottom_ref, left_ref, right_ref, acc_ref, sum_ref,
):
    step = pl.program_id(0)

    @pl.when(step == 0)
    def _():
        sum_ref[...] = jnp.zeros_like(sum_ref)
        acc_ref[...] = jnp.zeros_like(acc_ref)
        for at in range(0, EXP, 256):
            span = slice(at, at + 256)
            grads = dot_nt(halo_ref[...], wp_ref[at : at + 256, :])
            grads = (grads * halo_slope_ref[:, span]).astype(BF16).astype(F32)
            top_ref[:, span] = grads[:COLS]
            bottom_ref[:, span] = grads[COLS : 2 * COLS]
            for ref, base in ((left_ref, 2 * COLS), (right_ref, 2 * COLS + EDGE)):
                for s in range(STEPS):
                    ref[s, : BLK + 2, span] = grads[base + BLK * s : base + BLK * s + BLK + 2]

    first, last = step == 0, step == STEPS - 1
    for at in range(0, EXP, LANES):
        span = slice(at, at + LANES)
        rows = [jnp.where(first, top_ref[:, span], before_ref[0, :, span].astype(F32))]
        rows += [cur_ref[r, :, span].astype(F32) for r in range(BLK)]
        rows += [jnp.where(last, bottom_ref[:, span], after_ref[0, :, span].astype(F32))]
        shifted = []
        for r in range(BLK + 2):
            left = left_ref[step, r : r + 1, span]
            right = right_ref[step, r : r + 1, span]
            shifted.append(
                (
                    jnp.concatenate([rows[r][1:], right], axis=0),
                    rows[r],
                    jnp.concatenate([left, rows[r][:-1]], axis=0),
                )
            )
        sums = [acc_ref[n, :, span] for n in range(9)]
        for r in range(BLK):
            hid = hid_ref[r, :, span].astype(F32)
            total = 0.0
            for a in range(3):
                for b in range(3):
                    piece = shifted[r + 2 - a][b]
                    n = 3 * a + b
                    total = total + dk_ref[n, span][None] * piece
                    sums[n] = sums[n] + jnp.sum((hid * piece).reshape(8, 8, LANES), axis=0)
            d_pre = total * slope_ref[r, :, span].astype(F32)
            dpre_ref[r * COLS : (r + 1) * COLS, span] = d_pre.astype(BF16)
        for n in range(9):
            acc_ref[n, :, span] = sums[n]

    normed, _ = layer_norm(x_ref[...].reshape(TOK, CHAN).astype(F32))
    sum_ref[...] += dot_tn(normed.astype(BF16), dpre_ref[...])

    @pl.when(last)
    def _():
        depth_ref[...] = jnp.sum(acc_ref[...], axis=1)
        to_tiles(sum_ref, tiles_ref, 0)


def expand_back(d_mixed, halo, halo_slope, wp, hidden, slope, x, dk):
    return pl.pallas_call(
        expand_back_body,
        grid=(STEPS,),
        in_specs=[
            band((BLK, COLS, EXP)), ROW_BEFORE, ROW_AFTER, whole((HALO, CHAN)), whole((HALO, EXP)),
            whole((EXP, CHAN)), band((BLK, COLS, EXP)), band((BLK, COLS, EXP)),
            band((BLK, COLS, CHAN)), whole((9, EXP)),
        ],
        out_specs=[band((TOK, EXP)), whole(TILED), whole((9, EXP))],
        out_shape=[
            jax.ShapeDtypeStruct((ROWS * COLS, EXP), BF16),
            jax.ShapeDtypeStruct(TILED, BF16),
            jax.ShapeDtypeStruct((9, EXP), F32),
        ],
        scratch_shapes=[pltpu.VMEM((COLS, EXP), F32)] * 2
        + [pltpu.VMEM((STEPS, 8, EXP), F32)] * 2
        + [pltpu.VMEM((9, 8, EXP), F32), pltpu.VMEM((CHAN, EXP), F32)],
        compiler_params=params(58),
        cost_estimate=pl.CostEstimate(
            flops=2 * ROWS * COLS * CHAN * EXP, bytes_accessed=20 * MIB, transcendentals=0
        ),
        name="expand_back",
    )(d_mixed, d_mixed, d_mixed, halo, halo_slope, wp, hidden, slope, x, dk)


def finish_body(dpre_ref, x_ref, ds_ref, we_ref, grad_ref):
    normed, inv_std = layer_norm(x_ref[...].reshape(TOK, CHAN).astype(F32))
    d_normed = dot_nt(dpre_ref[...], we_ref[...])
    d_input = layer_norm_back(normed, inv_std, d_normed)
    grad_ref[...] = (ds_ref[...].reshape(TOK, CHAN) + d_input).astype(BF16).reshape(BLK, COLS, CHAN)


def finish(d_pre, x, d_section, we):
    return pl.pallas_call(
        finish_body,
        grid=(STEPS,),
        in_specs=[
            band((TOK, EXP)), band((BLK, COLS, CHAN)), band((BLK, COLS, CHAN)), whole((CHAN, EXP)),
        ],
        out_specs=band((BLK, COLS, CHAN)),
        out_shape=jax.ShapeDtypeStruct((ROWS, COLS, CHAN), BF16),
        compiler_params=params(58),
        cost_estimate=pl.CostEstimate(
            flops=2 * ROWS * COLS * CHAN * EXP, bytes_accessed=9 * MIB, transcendentals=0
        ),
        name="finish",
    )(d_pre, x, d_section, we)


FIRST_CELL = np.zeros((32, 512), np.float32)
LAST_CELL = np.zeros((32, 512), np.float32)
for _row in range(32):
    FIRST_CELL[_row, _row * 16] = 1.0
    LAST_CELL[_row, _row * 16 + 15] = 1.0


def edges_body(
    dt_ref, ct_ref, db_ref, cb_ref, dl_ref, cl_ref, dr_ref, cr_ref, first_ref, last_ref,
    top_ref, bottom_ref, left_ref, right_ref,
):
    def total(d_ref, c_ref):
        return (d_ref[...].astype(F32) + c_ref[...].astype(F32)).astype(BF16)

    top = total(dt_ref, ct_ref)
    bottom = total(db_ref, cb_ref)
    for quad in range(4):
        top_ref[16 * quad : 16 * quad + 16] = top[0, quad, :16]
        bottom_ref[16 * quad : 16 * quad + 16] = bottom[0, quad, 16:]
    left_ref[...] = dot(first_ref[...], total(dl_ref, cl_ref).reshape(512, CHAN)).astype(BF16)
    right_ref[...] = dot(last_ref[...], total(dr_ref, cr_ref).reshape(512, CHAN)).astype(BF16)


def edges(d_branch, cot):
    d_branch, cot = d_branch.reshape(16, 4, 32, CHAN), cot.reshape(16, 4, 32, CHAN)
    specs = []
    for row in (0, 15):
        specs += [pl.BlockSpec((1, 4, 32, CHAN), lambda i, row=row: (row, 0, 0, 0))] * 2
    for col in (0, 3):
        specs += [pl.BlockSpec((16, 1, 32, CHAN), lambda i, col=col: (0, col, 0, 0))] * 2
    return pl.pallas_call(
        edges_body,
        grid=(1,),
        in_specs=specs + [whole((32, 512))] * 2,
        out_specs=[whole((COLS, CHAN))] * 2 + [whole((ROWS, CHAN))] * 2,
        out_shape=[jax.ShapeDtypeStruct((COLS, CHAN), BF16)] * 2
        + [jax.ShapeDtypeStruct((ROWS, CHAN), BF16)] * 2,
        compiler_params=params(58),
        cost_estimate=pl.CostEstimate(flops=MIB, bytes_accessed=2 * MIB, transcendentals=0),
        name="edges",
    )(*([d_branch, cot] * 4), jnp.asarray(FIRST_CELL, BF16), jnp.asarray(LAST_CELL, BF16))


def shifts():
    n_lat, n_lon = lax.axis_size("lat"), lax.axis_size("lon")
    south = [(i, i + 1) for i in range(n_lat - 1)]
    north = [(i + 1, i) for i in range(n_lat - 1)]
    east = [(i, (i + 1) % n_lon) for i in range(n_lon)]
    west = [((i + 1) % n_lon, i) for i in range(n_lon)]
    return (south, north, east, west)


def halo_of(top, bottom, left, right):
    south, north, east, west = shifts()
    above = lax.ppermute(bottom, "lat", south)
    below = lax.ppermute(top, "lat", north)
    pad = jnp.zeros((EDGE - ROWS - 2, top.shape[1]), top.dtype)
    from_west = lax.ppermute(
        jnp.concatenate([above[-1:], right, below[-1:], pad], axis=0), "lon", east
    )
    from_east = lax.ppermute(
        jnp.concatenate([above[:1], left, below[:1], pad], axis=0), "lon", west
    )
    return jnp.concatenate([above, below, from_west, from_east], axis=0)


def wide_halo(field):
    south, north, east, west = shifts()
    above = lax.ppermute(field[-2:], "lat", south)
    below = lax.ppermute(field[:2], "lat", north)
    pad = jnp.zeros((2, EDGE - ROWS - 4, field.shape[2]), field.dtype)

    def columns(at):
        parts = [part[:, at : at + 2].transpose(1, 0, 2) for part in (above, field, below)]
        return jnp.concatenate(parts + [pad], axis=1)

    own_west, own_east = columns(0), columns(COLS - 2)
    from_west = lax.ppermute(own_east, "lon", east)
    from_east = lax.ppermute(own_west, "lon", west)
    return (above, below, from_west, from_east, own_west, own_east)


def exchange(pieces):
    n_lat, n_lon = lax.axis_size("lat"), lax.axis_size("lon")
    order = np.arange(n_lat * n_lon).reshape(n_lat, n_lon // 2, 2)
    members = order.transpose(2, 0, 1).reshape(2, -1).tolist()
    return lax.all_to_all(
        pieces, ("lat", "lon"), split_axis=0, concat_axis=0, axis_index_groups=members, tiled=True
    )


def to_pieces(field):
    shaped = field.reshape(16, 2, 4, 16, CHAN).transpose(0, 2, 1, 3, 4)
    return shaped.reshape(64, 32, CHAN)


def scatter_sum(tiles):
    terms = lax.all_to_all(tiles, ("lat", "lon"), split_axis=0, concat_axis=0, tiled=True)
    factor = float(ROWS * COLS * lax.axis_size("lat") * lax.axis_size("lon")) ** (-0.5)
    return (jnp.sum(terms.astype(F32), axis=0) * factor).astype(BF16)


def spread(tile):
    copies = jnp.broadcast_to(tile[None], (128,) + tile.shape)
    return lax.all_to_all(copies, ("lat", "lon"), split_axis=0, concat_axis=0, tiled=True)


def rel_table():
    position = np.arange(64)
    pos_row, pos_col = position // 8, position % 8
    rel_index = (pos_row[:, None] - pos_row[None, :] + 7) * 15 + (
        pos_col[:, None] - pos_col[None, :] + 7
    )
    return jnp.asarray(rel_index)[:, :, None] == jnp.arange(225)[None, None, :]


def on_device(
    field_in, cotangent, expand_weight, depth_kernel, project_weight, qkv_weight, out_weight, rel_bias
):
    onehot = rel_table().astype(F32)
    bias = jnp.einsum(
        "tsr,hr->sht", onehot, rel_bias.reshape(4, 225), precision=lax.Precision.HIGHEST
    ).reshape(64, 256)
    dk = depth_kernel.reshape(9, EXP)

    field_halo = wide_halo(field_in)
    cot_pieces = to_pieces(cotangent)
    cot_groups = exchange(cot_pieces)
    hidden, act_slope = expand(field_in, expand_weight)
    ring_out = ring(field_halo, field_in, expand_weight, dk)
    section, mixed, mixed_slope = mix(hidden, ring_out[:4], dk, project_weight, field_in)
    groups = exchange(section)
    cot_swapped, d_att = prepare(cot_groups, out_weight, 32)
    d_groups, attended, normed2, d_proj, bias_acc = attention(groups, d_att, qkv_weight, bias)
    d_branch = exchange(d_groups)
    attention_tiles = attention_sums(
        attended, cot_swapped.reshape(-1, CHAN), normed2, d_proj
    )
    bias_sum = jnp.einsum(
        "sht,tsr->hr", bias_acc.reshape(64, 4, 64), onehot, precision=lax.Precision.HIGHEST
    )
    d_halo = halo_of(*edges(d_branch, cot_pieces))
    d_section, d_mixed, project_tiles = project_back(
        cotangent, d_branch, mixed, mixed_slope, project_weight
    )
    early = scatter_sum(jnp.concatenate([attention_tiles, project_tiles], axis=1))
    d_pre, expand_tiles, depth_sum = expand_back(
        d_mixed, d_halo, ring_out[4], project_weight, hidden, act_slope, field_in, dk
    )
    small = jnp.concatenate(
        [depth_sum.reshape(-1), bias_sum.reshape(-1), jnp.zeros((128 * 128 - 9 * EXP - 900,), F32)]
    )
    small = jnp.pad(small.reshape(128, 1, 128), ((0, 0), (0, 7), (0, 0))).astype(BF16)
    late = scatter_sum(jnp.concatenate([expand_tiles, small], axis=1))
    grad_in = finish(d_pre, field_in, d_section, expand_weight)
    sums = spread(jnp.concatenate([early, late], axis=0))
    early, late = sums[:, :32], sums[:, 32:]
    small = late[:, 16].reshape(-1).astype(F32)
    return (
        grad_in,
        from_tiles(late[:, :16], 8),
        small[: 9 * EXP].reshape(3, 3, EXP),
        from_tiles(early[:, 16:], 2),
        from_tiles(early[:96, :16], 6),
        from_tiles(early[96:, :16], 2),
        small[9 * EXP : 9 * EXP + 900].reshape(4, 15, 15),
    )


def solution(mesh):
    placed = (P("lat", "lon", None), P("lat", "lon", None), P(), P(), P(), P(), P(), P())
    return jax.shard_map(
        on_device,
        mesh=mesh,
        in_specs=placed,
        out_specs=(P("lat", "lon", None), P(), P(), P(), P(), P(), P()),
        check_vma=False,
    )
```

time: 362 us -> 279 us (0.77)
  blocking collectives: 72.2 us -> 0 us
  waiting for transfers between devices: 100 us -> 73 us
  Pallas kernels: 78 us -> 104 us
  between operations: 14.5 us -> 1.06 us
  starting transfers between devices: 61.2 us -> 68.6 us
  local copies, waits for them, and re-layouts: 23.1 us -> 19.3 us
    psum x1 -> x0, waiting for transfers between devices: 83.2 us -> none  [on_device(): lax.psum((expand_sum, depth_sum, project_sum, qkv_sum, out_sum, bias_sum)...]
    psum x1 -> x0, blocking collectives: 72.2 us -> none  [on_device(): lax.psum((expand_sum, depth_sum, project_sum, qkv_sum, out_sum, bias_sum)...]
    all_to_all x0 -> x3, waiting for transfers between devices: none -> 47.8 us  [the longest x2 28.2 us: scatter_sum(): lax.all_to_all(tiles, ('lat', 'lon'), split_axis=0, concat_axis=0, tiled=...]
    pallas_call x0 -> x5, Pallas kernels: none -> 23.9 us  [the longest x1 8.19 us: finish(): pl.pallas_call(finish_body, grid=(STEPS,), in_specs=[band((TOK, EXP)), ba...]
    all_to_all x0 -> x3, starting transfers between devices: none -> 21.7 us  [the longest x2 17.2 us: scatter_sum(): lax.all_to_all(tiles, ('lat', 'lon'), split_axis=0, concat_axis=0, tiled=...]
    all_to_all x3, waiting for transfers between devices: 3.05 us -> 21.6 us  [exchange(): lax.all_to_all(pieces, ('lat', 'lon'), split_axis=0, concat_axis=0, axis_...]
    ppermute x3 -> x1, waiting for transfers between devices: 10 us -> 0.01 us  [halo_of(): above = lax.ppermute(bottom, 'lat', south)]
    ppermute x3 -> x1, starting transfers between devices: 9.3 us -> 0.01 us  [halo_of(): lax.ppermute(jnp.concatenate([above[:1], left, below[:1], pad], axis=0),...]
  transfers between devices with their start and end apart: 16 -> 14, of which waited for: 6 -> 6; matrix products, arithmetic and copies ran while one was open for 5% -> 5% of each run, Pallas kernels for 15% -> 21%
where the time goes in v2:
time: 279 us; the launch traced here: 277 us
  Pallas kernels  104 us (37%)
  waiting for transfers between devices  73 us (26%)
  starting transfers between devices  68.6 us (25%)
  local copies, waits for them, and re-layouts  19.3 us (7%)
  other arithmetic  7.29 us (3%)
  matrix products  4.24 us (2%)
    all_to_all x3, starting transfers between devices, exchange(): lax.all_to_all(pieces, ('lat', 'lon'), split_axis=0, concat_axis=0, axis_...  28.9 us
    all_to_all x2, waiting for transfers between devices, scatter_sum(): lax.all_to_all(tiles, ('lat', 'lon'), split_axis=0, concat_axis=0, tiled=...  28.2 us
    pallas_call x1, Pallas kernels, attention(): pl.pallas_call(attention_body, grid=(n_groups // 4,), in_specs=[whole(sha...  21.9 us
    all_to_all x3, waiting for transfers between devices, exchange(): lax.all_to_all(pieces, ('lat', 'lon'), split_axis=0, concat_axis=0, axis_...  21.6 us
    pallas_call x1, Pallas kernels, expand_back(): pl.pallas_call(expand_back_body, grid=(STEPS,), in_specs=[band((BLK, COLS...  21.2 us
    all_to_all x1, waiting for transfers between devices, spread(): lax.all_to_all(copies, ('lat', 'lon'), split_axis=0, concat_axis=0, tiled...  19.6 us
    all_to_all x2, starting transfers between devices, scatter_sum(): lax.all_to_all(tiles, ('lat', 'lon'), split_axis=0, concat_axis=0, tiled=...  17.2 us
    pallas_call x1, Pallas kernels, mix(): pl.pallas_call(mix_body, grid=(STEPS,), in_specs=[band((BLK, COLS, EXP)),...  16 us
  transfers between devices with their start and end apart: 14, of which 6 were waited for; matrix products, arithmetic and copies ran while one was open for 5% of the time, Pallas kernels for 21%

profile of v2, /device:TPU:1, one launch (start us, length us, event | category | flops | bytes accessed | tf_op | source)
XLA Modules:
  0.0 277.3 jit_solution(4530239150291925000)
XLA Ops:
  0.6 0.9 fusion.11
  1.6 4.0 %collective-permute-start = (bf16[2,64,256]{2,0,1:T(2,128)(2,1)S(1)}, bf16[2,64,256]{2,0,1:T(2,128)(2,1)S(1)}, u32[]{:S(2)}, u32[]{:S(2)}) collective-permute-start(bf16[2,64,256]{2,0,1:T(2,128)(2,1)S(1)} %copy.58), channel_id=1, source_target_pairs={{0,16},{16,32},{32,48},{48,64},{64,80},{80,96},{96,112},{1,17},{17... | collective-permute-start | bytes 196616 | tf_op jit(solution)/shard_map/ppermute | solution.py:650
  5.7 1.3 collective-permute-start.1
  7.0 2.3 copy.50
  9.3 11.9 %all-to-all-start.1 = ((bf16[64,32,256]{2,1,0:T(8,128)(2,1)}), bf16[64,32,256]{2,1,0:T(8,128)(2,1)S(1)}, u32[]{:S(2)}, u32[]{:S(2)}) async-start(bf16[64,32,256]{2,1,0:T(8,128)(2,1)} %bitcast.8), calls=%async_computation.1 | async-start | bytes 2097152 | tf_op jit(solution)/shard_map/all_to_all | solution.py:668
  21.3 1.0 fusion.10
  22.6 2.8 collective-permute-start.2
  25.3 9.7 %expand.1 = (bf16[32,64,1024]{2,1,0:T(8,128)(2,1)}, bf16[32,64,1024]{2,1,0:T(8,128)(2,1)}) custom-call(bf16[32,64,256]{2,1,0:T(8,128)(2,1)} %x_ref.7, bf16[256,1024]{1,0:T(8,128)(2,1)} %we_ref.5), custom_call_target="tpu_custom_call" | custom-call | flops 1073741824 | bytes 10485760 | tf_op jit(solution)/shard_map/expand/pallas_call | solution.py:105
  35.7 0.6 copy.48.above_ref
  38.2 5.0 %ring.1 = (bf16[64,1024]{1,0:T(8,128)(2,1)}, bf16[64,1024]{1,0:T(8,128)(2,1)}, f32[8,8,1024]{2,1,0:T(8,128)}, f32[8,8,1024]{2,1,0:T(8,128)}, f32[208,1024]{1,0:T(8,128)}) custom-call(bf16[2,64,256]{2,1,0:T(8,128)(2,1)} %copy.48.above_ref, bf16[2,64,256]{2,1,0:T(8,128)(2,1)} %copy.49.below_ref, bf16[32,64,256]{2,1,0:T(8,128)(2,1)} %x_ref.7, ...), custom_call_target="tpu_custom_call" | custom-call | flops 352321536 | bytes 3145728 | tf_op jit(solution)/shard_map/ring/pallas_call | solution.py:228
  43.2 16.0 %mix.1 = (bf16[64,32,256]{2,1,0:T(8,128)(2,1)}, bf16[32,64,1024]{2,1,0:T(8,128)(2,1)}, bf16[32,64,1024]{2,1,0:T(8,128)(2,1)}) custom-call(bf16[32,64,1024]{2,1,0:T(8,128)(2,1)} %get-tuple-element.34.cur_ref.before_ref.after_ref.hid_ref, bf16[32,64,1024]{2,1,0:T(8,128)(2,1)} %get-tuple-element.34.cur_ref.before_ref.after_ref.hid_ref, ...), custom_call_target="tpu_custom_call" | custom-call | flops 1073741824 | bytes 16777216 | tf_op jit(solution)/shard_map/mix/pallas_call | solution.py:156
  59.2 9.7 %all-to-all-start = ((bf16[64,32,256]{2,1,0:T(8,128)(2,1)}), bf16[64,32,256]{2,1,0:T(8,128)(2,1)S(1)}, u32[]{:S(2)}, u32[]{:S(2)}) async-start(bf16[64,32,256]{2,1,0:T(8,128)(2,1)} %get-tuple-element.39), calls=%async_computation | async-start | bytes 2097152 | tf_op jit(solution)/shard_map/all_to_all | solution.py:668
  69.0 2.8 %fusion.5 = f32[64,4,64]{2,1,0:T(4,128)S(1)} fusion(f32[4,225,1]{1,0,2:T(4,128)S(1)} %reshape.106, s32[64,64]{0,1:T(8,128)S(1)} %copy-done.11), kind=kOutput, calls=%fused_computation.9 | convolution fusion | flops 45158400 | bytes 85520 | tf_op jit(solution)/shard_map/tsr,hr->sht/dot_general | solution.py:702
  71.9 0.8 reshape.89.bias_ref
  72.6 3.2 %prepare.1 = (bf16[32,64,256]{2,1,0:T(8,128)(2,1)}, bf16[32,64,256]{2,1,0:T(8,128)(2,1)}) custom-call(bf16[64,32,256]{2,1,0:T(8,128)(2,1)} %copy-done.1, bf16[256,256]{1,0:T(8,128)(2,1)} %wout_ref.1, bf16[256,256]{1,0:T(8,128)(2,1)} %constant.6.clone.swap_ref), custom_call_target="tpu_custom_call" | custom-call | flops 536870912 | bytes 3145728 | tf_op jit(solution)/shard_map/prepare/pallas_call | solution.py:290
  75.8 7.5 %all-to-all-done.x_ref = bf16[64,32,256]{2,1,0:T(8,128)(2,1)S(1)} async-done(((bf16[64,32,256]{2,1,0:T(8,128)(2,1)}), bf16[64,32,256]{2,1,0:T(8,128)(2,1)S(1)}, u32[]{:S(2)}, u32[]{:S(2)}) %all-to-all-start) | async-done | bytes 1048608 | tf_op jit(solution)/shard_map/all_to_all | solution.py:668
  83.3 1.0 copy-done.2
  84.3 21.9 %attention.1 = (bf16[64,32,256]{2,1,0:T(8,128)(2,1)}, bf16[2048,256]{1,0:T(8,128)(2,1)}, bf16[2048,256]{1,0:T(8,128)(2,1)}, bf16[2048,768]{1,0:T(8,128)(2,1)}, f32[64,256]{1,0:T(8,128)}) custom-call(bf16[64,32,256]{2,1,0:T(8,128)(2,1)} %copy-done.2, bf16[32,64,256]{2,1,0:T(8,128)(2,1)} %get-tuple-element.40.da_ref, bf16[256,768]{1,0:T(8,128)(2,1)} %wqkv_ref.1, ...), custom_call_target="tpu_custom_call" | custom-call | flops 2684354560 | bytes 8388608 | tf_op jit(solution)/shard_map/attention/pallas_call | solution.py:362
  106.2 7.3 %all-to-all-start.2 = ((bf16[64,32,256]{2,1,0:T(8,128)(2,1)}), bf16[64,32,256]{2,1,0:T(8,128)(2,1)S(1)}, u32[]{:S(2)}, u32[]{:S(2)}) async-start(bf16[64,32,256]{2,1,0:T(8,128)(2,1)} %get-tuple-element.41), calls=%async_computation.2 | async-start | bytes 2097152 | tf_op jit(solution)/shard_map/all_to_all | solution.py:668
  113.7 14.1 %all-to-all-done.2.db_ref = bf16[64,32,256]{2,1,0:T(8,128)(2,1)S(1)} async-done(((bf16[64,32,256]{2,1,0:T(8,128)(2,1)}), bf16[64,32,256]{2,1,0:T(8,128)(2,1)S(1)}, u32[]{:S(2)}, u32[]{:S(2)}) %all-to-all-start.2) | async-done | bytes 1048608 | tf_op jit(solution)/shard_map/all_to_all | solution.py:668
  127.8 1.0 copy-done
  128.8 2.2 edges.1
  131.0 3.1 %collective-permute-start.4 = (bf16[64,256]{1,0:T(8,128)(2,1)}, bf16[64,256]{1,0:T(8,128)(2,1)S(1)}, u32[]{:S(2)}, u32[]{:S(2)}) collective-permute-start(bf16[64,256]{1,0:T(8,128)(2,1)} %get-tuple-element.45), channel_id=1, source_target_pairs={{0,16},{16,32},{32,48},{48,64},{64,80},{80,96},{96,112},{1,17},{17... | collective-permute-start | bytes 98312 | tf_op jit(solution)/shard_map/ppermute | solution.py:636
  134.1 1.4 fusion.7
  135.6 1.3 collective-permute-start.5
  136.9 3.5 %collective-permute-done.5 = bf16[64,256]{1,0:T(8,128)(2,1)S(1)} collective-permute-done((bf16[64,256]{1,0:T(8,128)(2,1)}, bf16[64,256]{1,0:T(8,128)(2,1)S(1)}, u32[]{:S(2)}, u32[]{:S(2)}) %collective-permute-start.5) | collective-permute-done | bytes 32800 | tf_op jit(solution)/shard_map/ppermute | solution.py:637
  140.5 0.8 maximum_maximum_fusion.2
  141.3 5.5 %collective-permute-start.6 = (bf16[40,256]{1,0:T(8,128)(2,1)S(1)}, bf16[40,256]{1,0:T(8,128)(2,1)S(1)}, u32[]{:S(2)}, u32[]{:S(2)}) collective-permute-start(bf16[40,256]{1,0:T(8,128)(2,1)S(1)} %get-tuple-element.89), channel_id=1, source_target_pairs={{0,1},{1,2},{2,3},{3,4},{4,5},{5,6},{6,7},{7,8},{8,9},{9,10},{10,1... | collective-permute-start | bytes 61448 | tf_op jit(solution)/shard_map/ppermute | solution.py:639
  146.8 11.0 %project_back.1 = (f32[32,64,256]{2,1,0:T(8,128)}, bf16[32,64,1024]{2,1,0:T(8,128)(2,1)}, bf16[128,16,128]{2,1,0:T(8,128)(2,1)}) custom-call(bf16[32,64,256]{2,1,0:T(8,128)(2,1)} %cot_ref.1, bf16[64,32,256]{2,1,0:T(8,128)(2,1)} %copy-done, bf16[32,64,1024]{2,1,0:T(8,128)(2,1)} %get-tuple-element.42.mixed_ref, ...), custom_call_target="tpu_custom_call" | custom-call | flops 2147483648 | bytes 16777216 | tf_op jit(solution)/shard_map/project_back/pallas_call | solution.py:449
  157.9 0.7 pad_maximum_fusion.1.halo_ref
  158.5 21.2 %expand_back.1 = (bf16[2048,1024]{1,0:T(8,128)(2,1)}, bf16[128,16,128]{2,1,0:T(8,128)(2,1)}, f32[9,1024]{1,0:T(8,128)}) custom-call(bf16[32,64,1024]{2,1,0:T(8,128)(2,1)} %get-tuple-element.44.cur_ref.before_ref.after_ref, bf16[32,64,1024]{2,1,0:T(8,128)(2,1)} %get-tuple-element.44.cur_ref.before_ref.after_ref, ...), custom_call_target="tpu_custom_call" | custom-call | flops 1073741824 | bytes 20971520 | tf_op jit(solution)/shard_map/expand_back/pallas_call | solution.py:533
  179.7 0.8 convert.25
  180.8 2.1 fusion.8
  182.9 12.6 %all-to-all-start.4 = ((bf16[128,24,128]{2,1,0:T(8,128)(2,1)}), bf16[128,24,128]{2,1,0:T(8,128)(2,1)S(1)}, u32[]{:S(2)}, u32[]{:S(2)}) async-start(bf16[128,24,128]{2,1,0:T(8,128)(2,1)} %fusion.8), calls=%async_computation.4 | async-start | bytes 1572864 | tf_op jit(solution)/shard_map/all_to_all | solution.py:679
  195.5 5.3 %attention_sums.1 = bf16[128,16,128]{2,1,0:T(8,128)(2,1)} custom-call(bf16[2048,256]{1,0:T(8,128)(2,1)} %get-tuple-element.53.att_ref, bf16[2048,256]{1,0:T(8,128)(2,1)} %bitcast.80, bf16[2048,256]{1,0:T(8,128)(2,1)} %get-tuple-element.55.norm_ref, bf16[2048,768]{1,0:T(8,128)(2,1)} %get-tuple-element.56.proj_ref), custom_call_target="tpu_custom_call" | custom-call | flops 1073741824 | bytes 6291456 | tf_op jit(solution)/shard_map/attention_sums/pallas_call | solution.py:407
  200.8 2.1 pad_maximum_fusion
  202.9 9.1 %all-to-all-done.4 = bf16[128,24,128]{2,1,0:T(8,128)(2,1)S(1)} async-done(((bf16[128,24,128]{2,1,0:T(8,128)(2,1)}), bf16[128,24,128]{2,1,0:T(8,128)(2,1)S(1)}, u32[]{:S(2)}, u32[]{:S(2)}) %all-to-all-start.4) | async-done | bytes 786464 | tf_op jit(solution)/shard_map/all_to_all | solution.py:679
  212.0 4.5 %all-to-all-start.3 = ((bf16[128,32,128]{2,1,0:T(8,128)(2,1)}), bf16[128,32,128]{2,1,0:T(8,128)(2,1)S(1)}, u32[]{:S(2)}, u32[]{:S(2)}) async-start(bf16[128,32,128]{2,1,0:T(8,128)(2,1)} %pad_maximum_fusion), calls=%async_computation.3 | async-start | bytes 2097152 | tf_op jit(solution)/shard_map/all_to_all | solution.py:679
  216.7 19.1 %all-to-all-done.3 = bf16[128,32,128]{2,1,0:T(8,128)(2,1)S(1)} async-done(((bf16[128,32,128]{2,1,0:T(8,128)(2,1)}), bf16[128,32,128]{2,1,0:T(8,128)(2,1)S(1)}, u32[]{:S(2)}, u32[]{:S(2)}) %all-to-all-start.3) | async-done | bytes 1048608 | tf_op jit(solution)/shard_map/all_to_all | solution.py:679
  236.1 1.5 broadcast_in_dim.20
  237.6 4.6 %all-to-all-start.5 = ((bf16[128,56,128]{2,1,0:T(8,128)(2,1)}), bf16[128,56,128]{2,1,0:T(8,128)(2,1)S(1)}, u32[]{:S(2)}, u32[]{:S(2)}) async-start(bf16[128,56,128]{2,1,0:T(8,128)(2,1)} %broadcast_in_dim.20), calls=%async_computation.5 | async-start | bytes 3670016 | tf_op jit(solution)/shard_map/all_to_all | solution.py:686
  242.2 8.2 %finish.1 = bf16[32,64,256]{2,1,0:T(8,128)(2,1)} custom-call(bf16[2048,1024]{1,0:T(8,128)(2,1)} %get-tuple-element.51.dpre_ref, bf16[32,64,256]{2,1,0:T(8,128)(2,1)} %x_ref.7, f32[32,64,256]{2,1,0:T(8,128)} %get-tuple-element.52.ds_ref, bf16[256,1024]{1,0:T(8,128)(2,1)} %we_ref.5), custom_call_target="tpu_custom_call" | custom-call | flops 1073741824 | bytes 9437184 | tf_op jit(solution)/shard_map/finish/pallas_call | solution.py:566
  250.3 19.6 %all-to-all-done.5 = bf16[128,56,128]{2,1,0:T(8,128)(2,1)S(1)} async-done(((bf16[128,56,128]{2,1,0:T(8,128)(2,1)}), bf16[128,56,128]{2,1,0:T(8,128)(2,1)S(1)}, u32[]{:S(2)}, u32[]{:S(2)}) %all-to-all-start.5) | async-done | bytes 1835040 | tf_op jit(solution)/shard_map/all_to_all | solution.py:686
  270.8 1.0 copy.72
  272.3 1.2 copy.73
  273.8 1.0 copy.74
  275.1 0.7 copy.75
  275.9 0.6 reshape.96
  (75 shorter events, 6.5 us)
Async XLA Ops:
  1.6 20.8 %collective-permute-start = (bf16[2,64,256]{2,0,1:T(2,128)(2,1)S(1)}, bf16[2,64,256]{2,0,1:T(2,128)(2,1)S(1)}, u32[]{:S(2)}, u32[]{:S(2)}) collective-permute-start(bf16[2,64,256]{2,0,1:T(2,128)(2,1)S(1)} %copy.58), channel_id=1, source_target_pairs={{0,16},{16,32},{32,48},{48,64},{64,80},{80,96},{96,112},{1,17},{17... | collective-permute-start | bytes 196616 | tf_op jit(solution)/shard_map/ppermute | solution.py:650
  5.7 16.7 %collective-permute-start.1 = (bf16[2,64,256]{2,0,1:T(2,128)(2,1)S(1)}, bf16[2,64,256]{2,0,1:T(2,128)(2,1)S(1)}, u32[]{:S(2)}, u32[]{:S(2)}) collective-permute-start(bf16[2,64,256]{2,0,1:T(2,128)(2,1)S(1)} %copy.59), channel_id=1, source_target_pairs={{16,0},{32,16},{48,32},{64,48},{80,64},{96,80},{112,96},{17,1},{33... | collective-permute-start | bytes 196616 | tf_op jit(solution)/shard_map/ppermute | solution.py:651
  9.3 49.9 %all-to-all-start.1 = ((bf16[64,32,256]{2,1,0:T(8,128)(2,1)}), bf16[64,32,256]{2,1,0:T(8,128)(2,1)S(1)}, u32[]{:S(2)}, u32[]{:S(2)}) async-start(bf16[64,32,256]{2,1,0:T(8,128)(2,1)} %bitcast.8), calls=%async_computation.1 | async-start | bytes 2097152 | tf_op jit(solution)/shard_map/all_to_all | solution.py:668
  22.3 12.7 %copy-start.7 = (f32[3,3,1024]{2,1,0:T(4,128)S(1)}, f32[3,3,1024]{2,1,0:T(4,128)}, u32[]{:S(2)}) copy-start(f32[3,3,1024]{2,1,0:T(4,128)} %param.16) | copy-start | bytes 110596
  22.5 13.8 %copy-start.4 = (bf16[2,40,256]{2,1,0:T(8,128)(2,1)}, bf16[2,40,256]{2,1,0:T(8,128)(2,1)S(1)}, u32[]{:S(2)}) copy-start(bf16[2,40,256]{2,1,0:T(8,128)(2,1)S(1)} %get-tuple-element.91.own_west_ref) | copy-start | bytes 122884
  22.6 13.8 %copy-start.5 = (bf16[2,40,256]{2,1,0:T(8,128)(2,1)}, bf16[2,40,256]{2,1,0:T(8,128)(2,1)S(1)}, u32[]{:S(2)}) copy-start(bf16[2,40,256]{2,1,0:T(8,128)(2,1)S(1)} %get-tuple-element.92.own_east_ref) | copy-start | bytes 122884
  22.6 14.4 %collective-permute-start.2 = (bf16[2,40,256]{2,1,0:T(8,128)(2,1)S(1)}, bf16[2,40,256]{2,1,0:T(8,128)(2,1)S(1)}, u32[]{:S(2)}, u32[]{:S(2)}) collective-permute-start(bf16[2,40,256]{2,1,0:T(8,128)(2,1)S(1)} %get-tuple-element.92.own_east_ref), channel_id=1, source_target_pairs={{0,1},{1,2},{2,3},{3,4},{4,5},{5,6},{6,7},{7,8},{8,9},{9,10},{10,1... | collective-permute-start | bytes 122888 | tf_op jit(solution)/shard_map/ppermute | solution.py:659
  25.3 11.7 %collective-permute-start.3 = (bf16[2,40,256]{2,1,0:T(8,128)(2,1)S(1)}, bf16[2,40,256]{2,1,0:T(8,128)(2,1)S(1)}, u32[]{:S(2)}, u32[]{:S(2)}) collective-permute-start(bf16[2,40,256]{2,1,0:T(8,128)(2,1)S(1)} %get-tuple-element.91.own_west_ref), channel_id=1, source_target_pairs={{1,0},{2,1},{3,2},{4,3},{5,4},{6,5},{7,6},{8,7},{9,8},{10,9},{11,1... | collective-permute-start | bytes 122888 | tf_op jit(solution)/shard_map/ppermute | solution.py:660
  37.0 0.6 copy-start.8
  37.6 0.6 copy-start.9
  59.2 9.7 %copy-start.10 = (f32[4,15,15]{2,0,1:T(4,128)S(1)}, f32[4,15,15]{2,0,1:T(4,128)}, u32[]{:S(2)}) copy-start(f32[4,15,15]{2,0,1:T(4,128)} %param.20) | copy-start | bytes 10804
  59.2 9.9 %copy-start.11 = (s32[64,64]{0,1:T(8,128)S(1)}, s32[64,64]{0,1:T(8,128)}, u32[]{:S(2)}) copy-start(s32[64,64]{0,1:T(8,128)} %constant.10.clone) | copy-start | bytes 49156
  59.2 13.4 %copy-start.1 = (bf16[64,32,256]{2,1,0:T(8,128)(2,1)}, bf16[64,32,256]{2,1,0:T(8,128)(2,1)S(1)}, u32[]{:S(2)}) copy-start(bf16[64,32,256]{2,1,0:T(8,128)(2,1)S(1)} %all-to-all-done.1.cot_ref) | copy-start | bytes 3145732
  59.2 24.1 %all-to-all-start = ((bf16[64,32,256]{2,1,0:T(8,128)(2,1)}), bf16[64,32,256]{2,1,0:T(8,128)(2,1)S(1)}, u32[]{:S(2)}, u32[]{:S(2)}) async-start(bf16[64,32,256]{2,1,0:T(8,128)(2,1)} %get-tuple-element.39), calls=%async_computation | async-start | bytes 2097152 | tf_op jit(solution)/shard_map/all_to_all | solution.py:668
  83.3 1.0 copy-start.2
  106.2 7.4 %copy-start.6 = (f32[64,256]{1,0:T(8,128)S(1)}, f32[64,256]{1,0:T(8,128)}, u32[]{:S(2)}) copy-start(f32[64,256]{1,0:T(8,128)} %get-tuple-element.60) | copy-start | bytes 196612
  106.2 21.6 %all-to-all-start.2 = ((bf16[64,32,256]{2,1,0:T(8,128)(2,1)}), bf16[64,32,256]{2,1,0:T(8,128)(2,1)S(1)}, u32[]{:S(2)}, u32[]{:S(2)}) async-start(bf16[64,32,256]{2,1,0:T(8,128)(2,1)} %get-tuple-element.41), calls=%async_computation.2 | async-start | bytes 2097152 | tf_op jit(solution)/shard_map/all_to_all | solution.py:668
  127.8 1.0 copy-start
  131.0 5.9 %collective-permute-start.4 = (bf16[64,256]{1,0:T(8,128)(2,1)}, bf16[64,256]{1,0:T(8,128)(2,1)S(1)}, u32[]{:S(2)}, u32[]{:S(2)}) collective-permute-start(bf16[64,256]{1,0:T(8,128)(2,1)} %get-tuple-element.45), channel_id=1, source_target_pairs={{0,16},{16,32},{32,48},{48,64},{64,80},{80,96},{96,112},{1,17},{17... | collective-permute-start | bytes 98312 | tf_op jit(solution)/shard_map/ppermute | solution.py:636
  135.6 4.9 %collective-permute-start.5 = (bf16[64,256]{1,0:T(8,128)(2,1)}, bf16[64,256]{1,0:T(8,128)(2,1)S(1)}, u32[]{:S(2)}, u32[]{:S(2)}) collective-permute-start(bf16[64,256]{1,0:T(8,128)(2,1)} %get-tuple-element.46), channel_id=1, source_target_pairs={{16,0},{32,16},{48,32},{64,48},{80,64},{96,80},{112,96},{17,1},{33... | collective-permute-start | bytes 98312 | tf_op jit(solution)/shard_map/ppermute | solution.py:637
  141.3 16.6 %collective-permute-start.6 = (bf16[40,256]{1,0:T(8,128)(2,1)S(1)}, bf16[40,256]{1,0:T(8,128)(2,1)S(1)}, u32[]{:S(2)}, u32[]{:S(2)}) collective-permute-start(bf16[40,256]{1,0:T(8,128)(2,1)S(1)} %get-tuple-element.89), channel_id=1, source_target_pairs={{0,1},{1,2},{2,3},{3,4},{4,5},{5,6},{6,7},{7,8},{8,9},{9,10},{10,1... | collective-permute-start | bytes 61448 | tf_op jit(solution)/shard_map/ppermute | solution.py:639
  146.8 11.0 %collective-permute-start.7 = (bf16[40,256]{1,0:T(8,128)(2,1)S(1)}, bf16[40,256]{1,0:T(8,128)(2,1)S(1)}, u32[]{:S(2)}, u32[]{:S(2)}) collective-permute-start(bf16[40,256]{1,0:T(8,128)(2,1)S(1)} %get-tuple-element.90), channel_id=1, source_target_pairs={{1,0},{2,1},{3,2},{4,3},{5,4},{6,5},{7,6},{8,7},{9,8},{10,9},{11,1... | collective-permute-start | bytes 61448 | tf_op jit(solution)/shard_map/ppermute | solution.py:642
  182.9 29.2 %all-to-all-start.4 = ((bf16[128,24,128]{2,1,0:T(8,128)(2,1)}), bf16[128,24,128]{2,1,0:T(8,128)(2,1)S(1)}, u32[]{:S(2)}, u32[]{:S(2)}) async-start(bf16[128,24,128]{2,1,0:T(8,128)(2,1)} %fusion.8), calls=%async_computation.4 | async-start | bytes 1572864 | tf_op jit(solution)/shard_map/all_to_all | solution.py:679
  195.5 5.3 %copy-start.3 = (bf16[128,16,128]{2,1,0:T(8,128)(2,1)S(1)}, bf16[128,16,128]{2,1,0:T(8,128)(2,1)}, u32[]{:S(2)}) copy-start(bf16[128,16,128]{2,1,0:T(8,128)(2,1)} %get-tuple-element.57) | copy-start | bytes 1572868
  212.0 23.8 %all-to-all-start.3 = ((bf16[128,32,128]{2,1,0:T(8,128)(2,1)}), bf16[128,32,128]{2,1,0:T(8,128)(2,1)S(1)}, u32[]{:S(2)}, u32[]{:S(2)}) async-start(bf16[128,32,128]{2,1,0:T(8,128)(2,1)} %pad_maximum_fusion), calls=%async_computation.3 | async-start | bytes 2097152 | tf_op jit(solution)/shard_map/all_to_all | solution.py:679
  237.6 32.4 %all-to-all-start.5 = ((bf16[128,56,128]{2,1,0:T(8,128)(2,1)}), bf16[128,56,128]{2,1,0:T(8,128)(2,1)S(1)}, u32[]{:S(2)}, u32[]{:S(2)}) async-start(bf16[128,56,128]{2,1,0:T(8,128)(2,1)} %broadcast_in_dim.20), calls=%async_computation.5 | async-start | bytes 3670016 | tf_op jit(solution)/shard_map/all_to_all | solution.py:686

commit v3 on v2

--- a/solution.py
+++ b/solution.py
@@ -22,6 +22,8 @@
 EDGE = 40
 HALO = 2 * COLS + 2 * EDGE
 LONG = 72
+PACKED = (4, 16, LANES)
+JOINED = (64, 56, 128)
 
 
 def layer_norm(values):
@@ -71,8 +73,12 @@
     return pl.BlockSpec(shape, lambda i: (i,) + (0,) * (len(shape) - 1))
 
 
-ROW_BEFORE = pl.BlockSpec((1, COLS, EXP), lambda i: (jnp.maximum(BLK * i - 1, 0), 0, 0))
-ROW_AFTER = pl.BlockSpec((1, COLS, EXP), lambda i: (jnp.minimum(BLK * i + BLK, ROWS - 1), 0, 0))
+ROW_BEFORE = pl.BlockSpec(
+    (1, COLS, EXP), lambda i: (jnp.maximum(BLK * i - 1, 0), 0, 0)
+)
+ROW_AFTER = pl.BlockSpec(
+    (1, COLS, EXP), lambda i: (jnp.minimum(BLK * i + BLK, ROWS - 1), 0, 0)
+)
 
 
 TILED = (128, 16, 128)
@@ -84,11 +90,6 @@
         for c in range(wide):
             tile = ref[16 * r : 16 * r + 16, 128 * c : 128 * c + 128]
             out_ref[at + wide * r + c, :16] = tile.astype(BF16)
-
-
-def from_tiles(tiles, wide):
-    shaped = tiles.reshape(-1, wide, 16, 128).transpose(0, 2, 1, 3)
-    return shaped.reshape(-1, wide * 128).astype(F32)
 
 
 def expand_body(x_ref, we_ref, hid_ref, slope_ref):
@@ -117,22 +118,36 @@
 
 
 def mix_body(
-    cur_ref, before_ref, after_ref, top_ref, bottom_ref, left_ref, right_ref, dk_ref, wp_ref, x_ref,
-    section_ref, mixed_ref, slope_ref,
+    cur_ref, before_ref, after_ref,
+    above_ref, below_ref, first_ref, last_ref, west_ref, east_ref, own_west_ref, own_east_ref,
+    we_ref, dk_ref, dkb_ref, wp_ref, x_ref,
+    section_ref, mixed_ref, slope_ref, ring_slope_ref,
+    top_ref, bottom_ref, left_ref, right_ref,
 ):
     step = pl.program_id(0)
+
+    @pl.when(step == 0)
+    def _():
+        ring_body(
+            above_ref, below_ref, first_ref, last_ref, west_ref, east_ref, own_west_ref, own_east_ref,
+            we_ref, dk_ref,
+            top_ref, bottom_ref, left_ref, right_ref, ring_slope_ref,
+        )
+
     first, last = step == 0, step == STEPS - 1
     for at in range(0, EXP, LANES):
         span = slice(at, at + LANES)
-        rows = [jnp.where(first, top_ref[:, span], before_ref[0, :, span]).astype(F32)]
-        rows += [cur_ref[r, :, span].astype(F32) for r in range(BLK)]
-        rows += [jnp.where(last, bottom_ref[:, span], after_ref[0, :, span]).astype(F32)]
-        kern = [dk_ref[n, span][None] for n in range(9)]
+        rows = [jnp.where(first, top_ref[:, span], before_ref[0, :, span])]
+        rows += [cur_ref[r, :, span] for r in range(BLK)]
+        rows += [jnp.where(last, bottom_ref[:, span], after_ref[0, :, span])]
+        rows = [row.reshape(PACKED) for row in rows]
+        kern = [dkb_ref[n, :, span][None] for n in range(9)]
         for r in range(BLK):
             parts = [
                 kern[b] * rows[r] + kern[3 + b] * rows[r + 1] + kern[6 + b] * rows[r + 2]
                 for b in range(3)
             ]
+            parts = [part.reshape(COLS, LANES).astype(F32) for part in parts]
             left = left_ref[step, r : r + 1, span]
             right = right_ref[step, r : r + 1, span]
             pre = (
@@ -149,26 +164,6 @@
     for pair in range(2):
         for quad in range(4):
             section_ref[4 * pair + quad] = section[pair, :, quad].reshape(32, CHAN)
-
-
-def mix(hidden, ring_out, dk, wp, x):
-    wide = jax.ShapeDtypeStruct((ROWS, COLS, EXP), BF16)
-    return pl.pallas_call(
-        mix_body,
-        grid=(STEPS,),
-        in_specs=[
-            band((BLK, COLS, EXP)), ROW_BEFORE, ROW_AFTER, whole((COLS, EXP)), whole((COLS, EXP)),
-            whole((STEPS, 8, EXP)), whole((STEPS, 8, EXP)),
-            whole((9, EXP)), whole((EXP, CHAN)), band((BLK, COLS, CHAN)),
-        ],
-        out_specs=[band((8, 32, CHAN)), band((BLK, COLS, EXP)), band((BLK, COLS, EXP))],
-        out_shape=[jax.ShapeDtypeStruct((64, 32, CHAN), BF16), wide, wide],
-        compiler_params=params(58),
-        cost_estimate=pl.CostEstimate(
-            flops=2 * ROWS * COLS * CHAN * EXP, bytes_accessed=16 * MIB, transcendentals=ROWS * COLS * EXP
-        ),
-        name="mix",
-    )(hidden, hidden, hidden, *ring_out, dk, wp, x)
 
 
 def ring_body(
@@ -223,35 +218,37 @@
             slope_ref[out + ROWS + 2 : out + EDGE, span] = jnp.zeros((EDGE - ROWS - 2, 256), F32)
 
 
-def ring(halo, field, we, dk):
+def mix(hidden, halo, we, dk, dkb, wp, x):
     above, below, west, east, own_west, own_east = halo
-    return pl.pallas_call(
-        ring_body,
-        grid=(1,),
+    wide = jax.ShapeDtypeStruct((ROWS, COLS, EXP), BF16)
+    return pl.pallas_call(
+        mix_body,
+        grid=(STEPS,),
         in_specs=[
+            band((BLK, COLS, EXP)), ROW_BEFORE, ROW_AFTER,
             whole((2, COLS, CHAN)), whole((2, COLS, CHAN)),
             pl.BlockSpec((1, COLS, CHAN), lambda i: (0, 0, 0)),
             pl.BlockSpec((1, COLS, CHAN), lambda i: (ROWS - 1, 0, 0)),
             whole((2, EDGE, CHAN)), whole((2, EDGE, CHAN)), whole((2, EDGE, CHAN)), whole((2, EDGE, CHAN)),
-            whole((CHAN, EXP)), whole((9, EXP)),
+            whole((CHAN, EXP)), whole((9, EXP)), whole((9, 16, EXP)), whole((EXP, CHAN)),
+            band((BLK, COLS, CHAN)),
         ],
         out_specs=[
-            whole((COLS, EXP)), whole((COLS, EXP)), whole((STEPS, 8, EXP)), whole((STEPS, 8, EXP)),
-            whole((HALO, EXP)),
+            band((8, 32, CHAN)), band((BLK, COLS, EXP)), band((BLK, COLS, EXP)), whole((HALO, EXP)),
         ],
         out_shape=[
-            jax.ShapeDtypeStruct((COLS, EXP), BF16),
-            jax.ShapeDtypeStruct((COLS, EXP), BF16),
-            jax.ShapeDtypeStruct((STEPS, 8, EXP), F32),
-            jax.ShapeDtypeStruct((STEPS, 8, EXP), F32),
-            jax.ShapeDtypeStruct((HALO, EXP), F32),
-        ],
+            jax.ShapeDtypeStruct((64, 32, CHAN), BF16), wide, wide, jax.ShapeDtypeStruct((HALO, EXP), F32),
+        ],
+        scratch_shapes=[pltpu.VMEM((COLS, EXP), BF16)] * 2 + [pltpu.VMEM((STEPS, 8, EXP), F32)] * 2,
         compiler_params=params(58),
         cost_estimate=pl.CostEstimate(
-            flops=2 * 672 * CHAN * EXP, bytes_accessed=3 * MIB, transcendentals=900 * EXP
+            flops=3 * ROWS * COLS * CHAN * EXP, bytes_accessed=18 * MIB, transcendentals=2 * ROWS * COLS * EXP
         ),
-        name="ring",
-    )(above, below, field, field, west, east, own_west, own_east, we, dk)
+        name="mix",
+    )(
+        hidden, hidden, hidden, above, below, x, x, west, east, own_west, own_east,
+        we, dk, dkb, wp, x,
+    )
 
 
 SWAP = np.zeros((256, 256), np.float32)
@@ -419,58 +416,73 @@
     )(att, cot, normed, proj)
 
 
-def project_body(
-    cot_ref, db_ref, mixed_ref, slope_ref, wp_ref, ds_ref, dm_ref, tiles_ref, sum_ref, turned_ref
-):
-    @pl.when(pl.program_id(0) == 0)
-    def _():
-        sum_ref[...] = jnp.zeros_like(sum_ref)
-
+def section_grad(cot_ref, db_ref):
     pieces = db_ref[...].reshape(2, 4, 2, 16, CHAN)
     branch = jnp.concatenate(
         [pieces[pair, quad, r] for pair in range(2) for r in range(2) for quad in range(4)], axis=0
     )
-    d_section = cot_ref[...].reshape(TOK, CHAN).astype(F32) + branch.astype(F32)
-    ds_ref[...] = d_section.reshape(BLK, COLS, CHAN)
-    d_section_b = d_section.astype(BF16)
-    sum_ref[...] += dot_tn(d_section_b, mixed_ref[...].reshape(TOK, EXP))
+    return cot_ref[...].reshape(TOK, CHAN).astype(F32) + branch.astype(F32)
+
+
+def project_body(cot_ref, db_ref, slope_ref, wp_ref, dm_ref):
+    d_section_b = section_grad(cot_ref, db_ref).astype(BF16)
     for at in range(0, EXP, 256):
         grads = dot_nt(d_section_b, wp_ref[at : at + 256, :])
         slope = slope_ref[:, :, at : at + 256].reshape(TOK, 256).astype(F32)
         dm_ref[:, :, at : at + 256] = (grads * slope).astype(BF16).reshape(BLK, COLS, 256)
 
+
+def project_back(cot, db, slope, wp):
+    return pl.pallas_call(
+        project_body,
+        grid=(STEPS,),
+        in_specs=[
+            band((BLK, COLS, CHAN)), band((8, 32, CHAN)), band((BLK, COLS, EXP)), whole((EXP, CHAN)),
+        ],
+        out_specs=band((BLK, COLS, EXP)),
+        out_shape=jax.ShapeDtypeStruct((ROWS, COLS, EXP), BF16),
+        compiler_params=params(58),
+        cost_estimate=pl.CostEstimate(
+            flops=2 * ROWS * COLS * CHAN * EXP, bytes_accessed=10 * MIB, transcendentals=0
+        ),
+        name="project_back",
+    )(cot, db, slope, wp)
+
+
+def project_sum_body(cot_ref, db_ref, mixed_ref, tiles_ref, sum_ref, turned_ref):
+    @pl.when(pl.program_id(0) == 0)
+    def _():
+        sum_ref[...] = jnp.zeros_like(sum_ref)
+
+    d_section_b = section_grad(cot_ref, db_ref).astype(BF16)
+    sum_ref[...] += dot_tn(d_section_b, mixed_ref[...].reshape(TOK, EXP))
+
     @pl.when(pl.program_id(0) == STEPS - 1)
     def _():
         turned_ref[...] = sum_ref[...].T
         to_tiles(turned_ref, tiles_ref, 0)
 
 
-def project_back(cot, db, mixed, slope, wp):
-    return pl.pallas_call(
-        project_body,
+def project_sum(cot, db, mixed):
+    return pl.pallas_call(
+        project_sum_body,
         grid=(STEPS,),
-        in_specs=[
-            band((BLK, COLS, CHAN)), band((8, 32, CHAN)), band((BLK, COLS, EXP)),
-            band((BLK, COLS, EXP)), whole((EXP, CHAN)),
-        ],
-        out_specs=[band((BLK, COLS, CHAN)), band((BLK, COLS, EXP)), whole(TILED)],
-        out_shape=[
-            jax.ShapeDtypeStruct((ROWS, COLS, CHAN), F32),
-            jax.ShapeDtypeStruct((ROWS, COLS, EXP), BF16),
-            jax.ShapeDtypeStruct(TILED, BF16),
-        ],
+        in_specs=[band((BLK, COLS, CHAN)), band((8, 32, CHAN)), band((BLK, COLS, EXP))],
+        out_specs=whole(TILED),
+        out_shape=jax.ShapeDtypeStruct(TILED, BF16),
         scratch_shapes=[pltpu.VMEM((CHAN, EXP), F32), pltpu.VMEM((EXP, CHAN), F32)],
         compiler_params=params(58),
         cost_estimate=pl.CostEstimate(
-            flops=4 * ROWS * COLS * CHAN * EXP, bytes_accessed=16 * MIB, transcendentals=0
+            flops=2 * ROWS * COLS * CHAN * EXP, bytes_accessed=8 * MIB, transcendentals=0
         ),
-        name="project_back",
-    )(cot, db, mixed, slope, wp)
+        name="project_sum",
+    )(cot, db, mixed)
 
 
 def expand_back_body(
-    cur_ref, before_ref, after_ref, halo_ref, halo_slope_ref, wp_ref, hid_ref, slope_ref, x_ref, dk_ref,
-    dpre_ref, tiles_ref, depth_ref, top_ref, bottom_ref, left_ref, right_ref, acc_ref, sum_ref,
+    cur_ref, before_ref, after_ref, halo_ref, halo_slope_ref, wp_ref, hid_ref, slope_ref, x_ref, dkb_ref,
+    extra_ref,
+    dpre_ref, tiles_ref, top_ref, bottom_ref, left_ref, right_ref, acc_ref, sum_ref, depth_ref,
 ):
     step = pl.program_id(0)
 
@@ -498,28 +510,30 @@
         for r in range(BLK + 2):
             left = left_ref[step, r : r + 1, span]
             right = right_ref[step, r : r + 1, span]
-            shifted.append(
-                (
-                    jnp.concatenate([rows[r][1:], right], axis=0),
-                    rows[r],
-                    jnp.concatenate([left, rows[r][:-1]], axis=0),
-                )
+            moved = (
+                jnp.concatenate([rows[r][1:], right], axis=0),
+                rows[r],
+                jnp.concatenate([left, rows[r][:-1]], axis=0),
             )
-        sums = [acc_ref[n, :, span] for n in range(9)]
+            shifted.append([piece.astype(BF16).reshape(PACKED) for piece in moved])
+        hid = [hid_ref[r, :, span].reshape(PACKED) for r in range(BLK)]
+        totals = [None] * BLK
+        for a in range(3):
+            for b in range(3):
+                n = 3 * a + b
+                kern = dkb_ref[n, :, span][None]
+                terms = []
+                for r in range(BLK):
+                    piece = shifted[r + 2 - a][b]
+                    tap = kern * piece
+                    totals[r] = tap if n == 0 else totals[r] + tap
+                    terms.append(hid[r] * piece)
+                part = (terms[0] + terms[1]) + (terms[2] + terms[3])
+                part = ((part[0] + part[1]) + (part[2] + part[3])).astype(F32)
+                acc_ref[n, :, span] += part[:8] + part[8:]
         for r in range(BLK):
-            hid = hid_ref[r, :, span].astype(F32)
-            total = 0.0
-            for a in range(3):
-                for b in range(3):
-                    piece = shifted[r + 2 - a][b]
-                    n = 3 * a + b
-                    total = total + dk_ref[n, span][None] * piece
-                    sums[n] = sums[n] + jnp.sum((hid * piece).reshape(8, 8, LANES), axis=0)
-            d_pre = total * slope_ref[r, :, span].astype(F32)
-            dpre_ref[r * COLS : (r + 1) * COLS, span] = d_pre.astype(BF16)
-        for n in range(9):
-            acc_ref[n, :, span] = sums[n]
-
+            d_pre = totals[r].reshape(COLS, LANES) * slope_ref[r, :, span]
+            dpre_ref[r * COLS : (r + 1) * COLS, span] = d_pre
     normed, _ = layer_norm(x_ref[...].reshape(TOK, CHAN).astype(F32))
     sum_ref[...] += dot_tn(normed.astype(BF16), dpre_ref[...])
 
@@ -527,47 +541,55 @@
     def _():
         depth_ref[...] = jnp.sum(acc_ref[...], axis=1)
         to_tiles(sum_ref, tiles_ref, 0)
-
-
-def expand_back(d_mixed, halo, halo_slope, wp, hidden, slope, x, dk):
+        first_row = lax.broadcasted_iota(jnp.int32, (8, 128), 0) == 0
+        for n in range(128):
+            extra = extra_ref[n]
+            if n < 72:
+                row = depth_ref[n // 8 : n // 8 + 1, 128 * (n % 8) : 128 * (n % 8) + 128]
+                extra = jnp.where(first_row, row, extra)
+            tiles_ref[n, 16:] = extra.astype(BF16)
+
+
+def expand_back(d_mixed, halo, halo_slope, wp, hidden, slope, x, dkb, extra):
+    tiles = (128, 24, 128)
+    cells = band((BLK, COLS, EXP))
     return pl.pallas_call(
         expand_back_body,
         grid=(STEPS,),
         in_specs=[
-            band((BLK, COLS, EXP)), ROW_BEFORE, ROW_AFTER, whole((HALO, CHAN)), whole((HALO, EXP)),
-            whole((EXP, CHAN)), band((BLK, COLS, EXP)), band((BLK, COLS, EXP)),
-            band((BLK, COLS, CHAN)), whole((9, EXP)),
-        ],
-        out_specs=[band((TOK, EXP)), whole(TILED), whole((9, EXP))],
+            cells, ROW_BEFORE, ROW_AFTER, whole((HALO, CHAN)), whole((HALO, EXP)),
+            whole((EXP, CHAN)), cells, cells, band((BLK, COLS, CHAN)), whole((9, 16, EXP)),
+            whole((128, 8, 128)),
+        ],
+        out_specs=[band((TOK, EXP)), whole(tiles)],
         out_shape=[
             jax.ShapeDtypeStruct((ROWS * COLS, EXP), BF16),
-            jax.ShapeDtypeStruct(TILED, BF16),
-            jax.ShapeDtypeStruct((9, EXP), F32),
+            jax.ShapeDtypeStruct(tiles, BF16),
         ],
         scratch_shapes=[pltpu.VMEM((COLS, EXP), F32)] * 2
         + [pltpu.VMEM((STEPS, 8, EXP), F32)] * 2
-        + [pltpu.VMEM((9, 8, EXP), F32), pltpu.VMEM((CHAN, EXP), F32)],
+        + [pltpu.VMEM((9, 8, EXP), F32), pltpu.VMEM((CHAN, EXP), F32), pltpu.VMEM((9, EXP), F32)],
         compiler_params=params(58),
         cost_estimate=pl.CostEstimate(
             flops=2 * ROWS * COLS * CHAN * EXP, bytes_accessed=20 * MIB, transcendentals=0
         ),
         name="expand_back",
-    )(d_mixed, d_mixed, d_mixed, halo, halo_slope, wp, hidden, slope, x, dk)
-
-
-def finish_body(dpre_ref, x_ref, ds_ref, we_ref, grad_ref):
+    )(d_mixed, d_mixed, d_mixed, halo, halo_slope, wp, hidden, slope, x, dkb, extra)
+
+
+def finish_body(dpre_ref, x_ref, cot_ref, db_ref, we_ref, grad_ref):
     normed, inv_std = layer_norm(x_ref[...].reshape(TOK, CHAN).astype(F32))
-    d_normed = dot_nt(dpre_ref[...], we_ref[...])
-    d_input = layer_norm_back(normed, inv_std, d_normed)
-    grad_ref[...] = (ds_ref[...].reshape(TOK, CHAN) + d_input).astype(BF16).reshape(BLK, COLS, CHAN)
-
-
-def finish(d_pre, x, d_section, we):
+    d_input = layer_norm_back(normed, inv_std, dot_nt(dpre_ref[...], we_ref[...]))
+    grad_ref[...] = (section_grad(cot_ref, db_ref) + d_input).astype(BF16).reshape(BLK, COLS, CHAN)
+
+
+def finish(d_pre, x, cot, db, we):
     return pl.pallas_call(
         finish_body,
         grid=(STEPS,),
         in_specs=[
-            band((TOK, EXP)), band((BLK, COLS, CHAN)), band((BLK, COLS, CHAN)), whole((CHAN, EXP)),
+            band((TOK, EXP)), band((BLK, COLS, CHAN)), band((BLK, COLS, CHAN)), band((8, 32, CHAN)),
+            whole((CHAN, EXP)),
         ],
         out_specs=band((BLK, COLS, CHAN)),
         out_shape=jax.ShapeDtypeStruct((ROWS, COLS, CHAN), BF16),
@@ -576,7 +598,86 @@
             flops=2 * ROWS * COLS * CHAN * EXP, bytes_accessed=9 * MIB, transcendentals=0
         ),
         name="finish",
-    )(d_pre, x, d_section, we)
+    )(d_pre, x, cot, db, we)
+
+
+def join_body(core_ref, *refs):
+    half = pl.ds(core_ref[0] * 64, 64)
+    out_ref = refs[-1]
+    at = 0
+    for own_ref, other_ref in zip(refs[0:-1:2], refs[1:-1:2]):
+        total = own_ref[half].astype(F32) + other_ref[half].astype(F32)
+        out_ref[:, at : at + own_ref.shape[1]] = total.astype(BF16)
+        at += own_ref.shape[1]
+
+
+def join(core, *tiles):
+    vmem = pl.BlockSpec(memory_space=pltpu.VMEM)
+    return pl.pallas_call(
+        join_body,
+        in_specs=[pl.BlockSpec(memory_space=pltpu.SMEM)] + [vmem] * len(tiles),
+        out_shape=jax.ShapeDtypeStruct(JOINED, BF16),
+        compiler_params=params(58),
+        cost_estimate=pl.CostEstimate(flops=MIB, bytes_accessed=4 * MIB, transcendentals=0),
+        name="join",
+    )(core, *tiles)
+
+
+def fold_body(terms_ref, out_ref):
+    factor = float(128 * ROWS * COLS) ** (-0.5)
+    total = jnp.sum(terms_ref[...].astype(F32), axis=0) * factor
+    out_ref[...] = jnp.broadcast_to(total.astype(BF16)[None], out_ref.shape)
+
+
+def fold(terms):
+    return pl.pallas_call(
+        fold_body,
+        out_shape=jax.ShapeDtypeStruct(terms.shape, BF16),
+        compiler_params=params(58),
+        cost_estimate=pl.CostEstimate(flops=terms.size, bytes_accessed=4 * terms.size, transcendentals=0),
+        name="fold",
+    )(terms)
+
+
+def unfold_body(core_ref, own_ref, other_ref, expand_ref, depth_ref, project_ref, qkv_ref, out_ref, bias_ref):
+    first = core_ref[0] == 0
+
+    def tile(n, rows):
+        own, other = own_ref[n % 64, rows].astype(F32), other_ref[n % 64, rows].astype(F32)
+        return jnp.where(first, own, other) if n < 64 else jnp.where(first, other, own)
+
+    parts = ((qkv_ref, 0, 0), (out_ref, 96, 0), (project_ref, 0, 16), (expand_ref, 0, 32))
+    for ref, at, low in parts:
+        wide = ref.shape[1] // 128
+        for r in range(ref.shape[0] // 16):
+            for c in range(wide):
+                piece = tile(at + wide * r + c, slice(low, low + 16))
+                ref[16 * r : 16 * r + 16, 128 * c : 128 * c + 128] = piece
+    for n in range(72):
+        extra = tile(n, slice(48, 56))
+        at = 128 * (n % 8)
+        depth_ref[n // 24, n // 8 % 3 : n // 8 % 3 + 1, at : at + 128] = extra[:1]
+        if n < 60:
+            bias_ref[n % 15, n // 15 : n // 15 + 1, :] = extra[1:2, :15]
+
+
+def unfold(core, own, other):
+    vmem = pl.BlockSpec(memory_space=pltpu.VMEM)
+    return pl.pallas_call(
+        unfold_body,
+        in_specs=[pl.BlockSpec(memory_space=pltpu.SMEM), vmem, vmem],
+        out_shape=[
+            jax.ShapeDtypeStruct((CHAN, EXP), F32),
+            jax.ShapeDtypeStruct((3, 3, EXP), F32),
+            jax.ShapeDtypeStruct((EXP, CHAN), F32),
+            jax.ShapeDtypeStruct((CHAN, 3 * CHAN), F32),
+            jax.ShapeDtypeStruct((CHAN, CHAN), F32),
+            jax.ShapeDtypeStruct((15, 4, 15), F32),
+        ],
+        compiler_params=params(58),
+        cost_estimate=pl.CostEstimate(flops=0, bytes_accessed=5 * MIB, transcendentals=0),
+        name="unfold",
+    )(core, own, other)
 
 
 FIRST_CELL = np.zeros((32, 512), np.float32)
@@ -631,11 +732,14 @@
     return (south, north, east, west)
 
 
-def halo_of(top, bottom, left, right):
-    south, north, east, west = shifts()
-    above = lax.ppermute(bottom, "lat", south)
-    below = lax.ppermute(top, "lat", north)
-    pad = jnp.zeros((EDGE - ROWS - 2, top.shape[1]), top.dtype)
+def rows_of(top, bottom):
+    south, north, _, _ = shifts()
+    return (lax.ppermute(bottom, "lat", south), lax.ppermute(top, "lat", north))
+
+
+def halo_of(above, below, left, right):
+    _, _, east, west = shifts()
+    pad = jnp.zeros((EDGE - ROWS - 2, left.shape[1]), left.dtype)
     from_west = lax.ppermute(
         jnp.concatenate([above[-1:], right, below[-1:], pad], axis=0), "lon", east
     )
@@ -647,8 +751,9 @@
 
 def wide_halo(field):
     south, north, east, west = shifts()
-    above = lax.ppermute(field[-2:], "lat", south)
-    below = lax.ppermute(field[:2], "lat", north)
+    flat = (2 * COLS, CHAN)
+    above = lax.ppermute(field[-2:].reshape(flat), "lat", south).reshape(2, COLS, CHAN)
+    below = lax.ppermute(field[:2].reshape(flat), "lat", north).reshape(2, COLS, CHAN)
     pad = jnp.zeros((2, EDGE - ROWS - 4, field.shape[2]), field.dtype)
 
     def columns(at):
@@ -675,15 +780,13 @@
     return shaped.reshape(64, 32, CHAN)
 
 
-def scatter_sum(tiles):
-    terms = lax.all_to_all(tiles, ("lat", "lon"), split_axis=0, concat_axis=0, tiled=True)
-    factor = float(ROWS * COLS * lax.axis_size("lat") * lax.axis_size("lon")) ** (-0.5)
-    return (jnp.sum(terms.astype(F32), axis=0) * factor).astype(BF16)
-
-
-def spread(tile):
-    copies = jnp.broadcast_to(tile[None], (128,) + tile.shape)
-    return lax.all_to_all(copies, ("lat", "lon"), split_axis=0, concat_axis=0, tiled=True)
+def pairs():
+    return np.arange(lax.axis_size("lon")).reshape(-1, 2).tolist()
+
+
+def other_core(tiles):
+    swaps = [move for a, b in pairs() for move in ((a, b), (b, a))]
+    return lax.ppermute(tiles, "lon", swaps)
 
 
 def rel_table():
@@ -704,48 +807,52 @@
     ).reshape(64, 256)
     dk = depth_kernel.reshape(9, EXP)
 
+    dkb = jnp.broadcast_to(dk[:, None], (9, 16, EXP)).astype(BF16)
+    core = lax.axis_index("lon").astype(jnp.int32).reshape(1) & 1
+    barrier = lax.optimization_barrier
+
     field_halo = wide_halo(field_in)
-    cot_pieces = to_pieces(cotangent)
+    hidden, act_slope = expand(field_in, expand_weight)
+    field_halo, late_cot = barrier((field_halo, cotangent))
+    hidden, cot_pieces = barrier((hidden, to_pieces(late_cot)))
     cot_groups = exchange(cot_pieces)
-    hidden, act_slope = expand(field_in, expand_weight)
-    ring_out = ring(field_halo, field_in, expand_weight, dk)
-    section, mixed, mixed_slope = mix(hidden, ring_out[:4], dk, project_weight, field_in)
+    section, mixed, mixed_slope, ring_slope = mix(
+        hidden, field_halo, expand_weight, dk, dkb, project_weight, field_in
+    )
     groups = exchange(section)
     cot_swapped, d_att = prepare(cot_groups, out_weight, 32)
+    groups, bias, d_att = barrier((groups, bias, d_att))
     d_groups, attended, normed2, d_proj, bias_acc = attention(groups, d_att, qkv_weight, bias)
+
     d_branch = exchange(d_groups)
-    attention_tiles = attention_sums(
-        attended, cot_swapped.reshape(-1, CHAN), normed2, d_proj
-    )
+    attention_tiles = attention_sums(attended, cot_swapped.reshape(-1, CHAN), normed2, d_proj)
     bias_sum = jnp.einsum(
         "sht,tsr->hr", bias_acc.reshape(64, 4, 64), onehot, precision=lax.Precision.HIGHEST
     )
-    d_halo = halo_of(*edges(d_branch, cot_pieces))
-    d_section, d_mixed, project_tiles = project_back(
-        cotangent, d_branch, mixed, mixed_slope, project_weight
-    )
-    early = scatter_sum(jnp.concatenate([attention_tiles, project_tiles], axis=1))
-    d_pre, expand_tiles, depth_sum = expand_back(
-        d_mixed, d_halo, ring_out[4], project_weight, hidden, act_slope, field_in, dk
-    )
-    small = jnp.concatenate(
-        [depth_sum.reshape(-1), bias_sum.reshape(-1), jnp.zeros((128 * 128 - 9 * EXP - 900,), F32)]
-    )
-    small = jnp.pad(small.reshape(128, 1, 128), ((0, 0), (0, 7), (0, 0))).astype(BF16)
-    late = scatter_sum(jnp.concatenate([expand_tiles, small], axis=1))
-    grad_in = finish(d_pre, field_in, d_section, expand_weight)
-    sums = spread(jnp.concatenate([early, late], axis=0))
-    early, late = sums[:, :32], sums[:, 32:]
-    small = late[:, 16].reshape(-1).astype(F32)
-    return (
-        grad_in,
-        from_tiles(late[:, :16], 8),
-        small[: 9 * EXP].reshape(3, 3, EXP),
-        from_tiles(early[:, 16:], 2),
-        from_tiles(early[:96, :16], 6),
-        from_tiles(early[96:, :16], 2),
-        small[9 * EXP : 9 * EXP + 900].reshape(4, 15, 15),
-    )
+    extra = jnp.pad(bias_sum.reshape(60, 1, 15), ((0, 68), (1, 6), (0, 113)))
+    d_branch, attention_tiles, extra = barrier((d_branch, attention_tiles, extra))
+
+    top, bottom, left, right = edges(d_branch, cot_pieces)
+    above, below = rows_of(top, bottom)
+    d_mixed = project_back(cotangent, d_branch, mixed_slope, project_weight)
+    above, below, d_mixed, attention_tiles = barrier((above, below, d_mixed, attention_tiles))
+    d_halo = halo_of(above, below, left, right)
+    project_tiles = project_sum(cotangent, d_branch, mixed)
+    d_halo, project_tiles, d_mixed = barrier((d_halo, project_tiles, d_mixed))
+    attention_pair = (attention_tiles, other_core(attention_tiles))
+    project_pair = (project_tiles, other_core(project_tiles))
+    d_pre, expand_tiles = expand_back(
+        d_mixed, d_halo, ring_slope, project_weight, hidden, act_slope, field_in, dkb, extra
+    )
+
+    joined = join(core, *attention_pair, *project_pair, expand_tiles, other_core(expand_tiles))
+    joined, d_pre = barrier((joined, d_pre))
+    terms = exchange(joined)
+    grad_in = finish(d_pre, field_in, cotangent, d_branch, expand_weight)
+    terms, grad_in = barrier((terms, grad_in))
+    sums = exchange(fold(terms))
+    *grads, bias_grad = unfold(core, sums, other_core(sums))
+    return (grad_in, *grads, bias_grad.transpose(1, 0, 2))
 
 
 def solution(mesh):

time: 279 us -> 249 us (0.89)
  waiting for transfers between devices: 73 us -> 26.3 us
  blocking collectives: 0 us -> 19.2 us
  Pallas kernels: 104 us -> 119 us
  local copies, waits for them, and re-layouts: 19.3 us -> 11.8 us
  other arithmetic: 7.29 us -> 0.82 us
  starting transfers between devices: 68.6 us -> 65.6 us
    all_to_all x3 -> x0, waiting for transfers between devices: 47.8 us -> none  [the longest x2 28.2 us: scatter_sum(): lax.all_to_all(tiles, ('lat', 'lon'), split_axis=0, concat_axis=0, tiled=...]
    all_to_all x3 -> x0, starting transfers between devices: 21.7 us -> none  [the longest x2 17.2 us: scatter_sum(): lax.all_to_all(tiles, ('lat', 'lon'), split_axis=0, concat_axis=0, tiled=...]
    all_to_all x0 -> x1, blocking collectives: none -> 19.2 us  [exchange(): lax.all_to_all(pieces, ('lat', 'lon'), split_axis=0, concat_axis=0, axis_...]
    pallas_call x2 -> x5, Pallas kernels: 26.2 us -> 39.6 us  [the longest x1 23.4 us: expand_back(): pl.pallas_call(expand_back_body, grid=(STEPS,), in_specs=[cells, ROW_BEFO...]
    ppermute x4 -> x8, starting transfers between devices: 9.69 us -> 20.1 us  [the longest x4 9.81 us: other_core(): return lax.ppermute(tiles, 'lon', swaps)]
    all_to_all x3 -> x4, starting transfers between devices: 28.9 us -> 37.5 us  [exchange(): lax.all_to_all(pieces, ('lat', 'lon'), split_axis=0, concat_axis=0, axis_...]
    pallas_call x1, Pallas kernels: 16 us -> 20.3 us  [mix(): pl.pallas_call(mix_body, grid=(STEPS,), in_specs=[band((BLK, COLS, EXP)),...]
    concatenate x3 -> x0, other arithmetic: 4.18 us -> none  [the longest x1 2.09 us: on_device(): jnp.concatenate([attention_tiles, project_tiles], axis=1)]
  transfers between devices with their start and end apart: 14 -> 16, of which waited for: 6 -> 7; matrix products, arithmetic and copies ran while one was open for 5% -> 4% of each run, Pallas kernels for 21% -> 25%
where the time goes in v3:
time: 249 us; the launch traced here: 248 us
  Pallas kernels  119 us (48%)
  starting transfers between devices  65.6 us (26%)
  waiting for transfers between devices  26.3 us (11%)
  blocking collectives  19.2 us (8%)
  local copies, waits for them, and re-layouts  11.8 us (5%)
  matrix products  4.24 us (2%)
    all_to_all x4, starting transfers between devices, exchange(): lax.all_to_all(pieces, ('lat', 'lon'), split_axis=0, concat_axis=0, axis_...  37.5 us
    pallas_call x1, Pallas kernels, expand_back(): pl.pallas_call(expand_back_body, grid=(STEPS,), in_specs=[cells, ROW_BEFO...  23.4 us
    pallas_call x1, Pallas kernels, attention(): pl.pallas_call(attention_body, grid=(n_groups // 4,), in_specs=[whole(sha...  21.9 us
    all_to_all x4, waiting for transfers between devices, exchange(): lax.all_to_all(pieces, ('lat', 'lon'), split_axis=0, concat_axis=0, axis_...  21.2 us
    pallas_call x1, Pallas kernels, mix(): pl.pallas_call(mix_body, grid=(STEPS,), in_specs=[band((BLK, COLS, EXP)),...  20.3 us
    all_to_all x1, blocking collectives, exchange(): lax.all_to_all(pieces, ('lat', 'lon'), split_axis=0, concat_axis=0, axis_...  19.2 us
    ppermute x4, starting transfers between devices, other_core(): return lax.ppermute(tiles, 'lon', swaps)  9.81 us
    pallas_call x1, Pallas kernels, expand(): pl.pallas_call(expand_body, grid=(STEPS,), in_specs=[band((BLK, COLS, CHA...  9.74 us
  transfers between devices with their start and end apart: 16, of which 7 were waited for; matrix products, arithmetic and copies ran while one was open for 4% of the time, Pallas kernels for 25%

profile of v3, /device:TPU:1, one launch (start us, length us, event | category | flops | bytes accessed | tf_op | source)
XLA Modules:
  0.0 247.7 jit_solution(12499540834499396021)
XLA Ops:
  0.6 1.0 fusion.7
  1.6 1.3 collective-permute-start.1
  2.9 4.7 %collective-permute-start = (bf16[128,256]{1,0:T(8,128)(2,1)S(1)}, bf16[128,256]{1,0:T(8,128)(2,1)S(1)}, u32[]{:S(2)}, u32[]{:S(2)}) collective-permute-start(bf16[128,256]{1,0:T(8,128)(2,1)S(1)} %bitcast.42), channel_id=1, source_target_pairs={{0,16},{16,32},{32,48},{48,64},{64,80},{80,96},{96,112},{1,17},{17... | collective-permute-start | bytes 196616 | tf_op jit(solution)/shard_map/ppermute | solution.py:755
  7.6 1.0 fusion.6
  9.0 3.6 %collective-permute-start.2 = (bf16[2,40,256]{2,1,0:T(8,128)(2,1)S(1)}, bf16[2,40,256]{2,1,0:T(8,128)(2,1)S(1)}, u32[]{:S(2)}, u32[]{:S(2)}) collective-permute-start(bf16[2,40,256]{2,1,0:T(8,128)(2,1)S(1)} %get-tuple-element.66.own_east_ref), channel_id=1, source_target_pairs={{0,1},{1,2},{2,3},{3,4},{4,5},{5,6},{6,7},{7,8},{8,9},{9,10},{10,1... | collective-permute-start | bytes 122888 | tf_op jit(solution)/shard_map/ppermute | solution.py:764
  12.6 9.7 %expand.1 = (bf16[32,64,1024]{2,1,0:T(8,128)(2,1)}, bf16[32,64,1024]{2,1,0:T(8,128)(2,1)}) custom-call(bf16[32,64,256]{2,1,0:T(8,128)(2,1)} %x_ref.7, bf16[256,1024]{1,0:T(8,128)(2,1)} %we_ref.5), custom_call_target="tpu_custom_call" | custom-call | flops 1073741824 | bytes 10485760 | tf_op jit(solution)/shard_map/expand/pallas_call | solution.py:106
  22.4 1.1 copy.33
  23.5 13.6 %all-to-all-start.1 = ((bf16[64,32,256]{2,1,0:T(8,128)(2,1)}), bf16[64,32,256]{2,1,0:T(8,128)(2,1)S(1)}, u32[]{:S(2)}, u32[]{:S(2)}) async-start(bf16[64,32,256]{2,1,0:T(8,128)(2,1)} %bitcast.13), calls=%async_computation.1 | async-start | bytes 2097152 | tf_op jit(solution)/shard_map/all_to_all | solution.py:773
  37.2 0.8 broadcast_in_dim.14.dkb_ref
  37.9 20.3 %mix.1 = (bf16[64,32,256]{2,1,0:T(8,128)(2,1)}, bf16[32,64,1024]{2,1,0:T(8,128)(2,1)}, bf16[32,64,1024]{2,1,0:T(8,128)(2,1)}, f32[208,1024]{1,0:T(8,128)}) custom-call(bf16[32,64,1024]{2,1,0:T(8,128)(2,1)} %get-tuple-element.60.cur_ref.before_ref.after_ref.hid_ref, bf16[32,64,1024]{2,1,0:T(8,128)(2,1)} %get-tuple-element.60.cur_ref.before_ref.after_ref.hid_ref, ...), custom_call_target="tpu_custom_call" | custom-call | flops 1610612736 | bytes 18874368 | tf_op jit(solution)/shard_map/mix/pallas_call | solution.py:224
  58.2 9.8 %all-to-all-start = ((bf16[64,32,256]{2,1,0:T(8,128)(2,1)}), bf16[64,32,256]{2,1,0:T(8,128)(2,1)S(1)}, u32[]{:S(2)}, u32[]{:S(2)}) async-start(bf16[64,32,256]{2,1,0:T(8,128)(2,1)} %get-tuple-element.67), calls=%async_computation | async-start | bytes 2097152 | tf_op jit(solution)/shard_map/all_to_all | solution.py:773
  68.2 2.8 %fusion.4 = f32[64,4,64]{2,1,0:T(4,128)S(1)} fusion(f32[4,225,1]{1,0,2:T(4,128)S(1)} %reshape.75, s32[64,64]{0,1:T(8,128)S(1)} %copy-done.23), kind=kOutput, calls=%fused_computation.5 | convolution fusion | flops 45158400 | bytes 85520 | tf_op jit(solution)/shard_map/tsr,hr->sht/dot_general | solution.py:805
  71.0 0.8 reshape.69.bias_ref
  71.8 3.1 %prepare.1 = (bf16[32,64,256]{2,1,0:T(8,128)(2,1)}, bf16[32,64,256]{2,1,0:T(8,128)(2,1)}) custom-call(bf16[64,32,256]{2,1,0:T(8,128)(2,1)} %copy-done.6, bf16[256,256]{1,0:T(8,128)(2,1)} %wout_ref.1, bf16[256,256]{1,0:T(8,128)(2,1)} %constant.22.clone.swap_ref), custom_call_target="tpu_custom_call" | custom-call | flops 536870912 | bytes 3145728 | tf_op jit(solution)/shard_map/prepare/pallas_call | solution.py:287
  74.9 8.4 %all-to-all-done.x_ref = bf16[64,32,256]{2,1,0:T(8,128)(2,1)S(1)} async-done(((bf16[64,32,256]{2,1,0:T(8,128)(2,1)}), bf16[64,32,256]{2,1,0:T(8,128)(2,1)S(1)}, u32[]{:S(2)}, u32[]{:S(2)}) %all-to-all-start) | async-done | bytes 1048608 | tf_op jit(solution)/shard_map/all_to_all | solution.py:773
  83.2 1.0 copy-done.7
  84.2 21.9 %attention.1 = (bf16[64,32,256]{2,1,0:T(8,128)(2,1)}, bf16[2048,256]{1,0:T(8,128)(2,1)}, bf16[2048,256]{1,0:T(8,128)(2,1)}, bf16[2048,768]{1,0:T(8,128)(2,1)}, f32[64,256]{1,0:T(8,128)}) custom-call(bf16[64,32,256]{2,1,0:T(8,128)(2,1)} %copy-done.7, bf16[32,64,256]{2,1,0:T(8,128)(2,1)} %get-tuple-element.71.da_ref, bf16[256,768]{1,0:T(8,128)(2,1)} %wqkv_ref.1, ...), custom_call_target="tpu_custom_call" | custom-call | flops 2684354560 | bytes 8388608 | tf_op jit(solution)/shard_map/attention/pallas_call | solution.py:359
  106.1 6.4 %all-to-all-start.2 = ((bf16[64,32,256]{2,1,0:T(8,128)(2,1)}), bf16[64,32,256]{2,1,0:T(8,128)(2,1)S(1)}, u32[]{:S(2)}, u32[]{:S(2)}) async-start(bf16[64,32,256]{2,1,0:T(8,128)(2,1)} %get-tuple-element.73), calls=%async_computation.2 | async-start | bytes 2097152 | tf_op jit(solution)/shard_map/all_to_all | solution.py:773
  112.6 0.9 reshape.71
  113.6 1.4 fusion.5
  115.1 0.8 pad.4.extra_ref
  116.0 5.3 %attention_sums.1.refs_0_ = bf16[128,16,128]{2,1,0:T(8,128)(2,1)} custom-call(bf16[2048,256]{1,0:T(8,128)(2,1)} %get-tuple-element.74.att_ref, bf16[2048,256]{1,0:T(8,128)(2,1)} %bitcast.37, bf16[2048,256]{1,0:T(8,128)(2,1)} %get-tuple-element.76.norm_ref, bf16[2048,768]{1,0:T(8,128)(2,1)} %get-tuple-element.77.proj_ref), custom_call_target="tpu_custom_call" | custom-call | flops 1073741824 | bytes 6291456 | tf_op jit(solution)/shard_map/attention_sums/pallas_call | solution.py:404
  121.2 5.7 %all-to-all-done.2.db_ref = bf16[64,32,256]{2,1,0:T(8,128)(2,1)S(1)} async-done(((bf16[64,32,256]{2,1,0:T(8,128)(2,1)}), bf16[64,32,256]{2,1,0:T(8,128)(2,1)S(1)}, u32[]{:S(2)}, u32[]{:S(2)}) %all-to-all-start.2) | async-done | bytes 1048608 | tf_op jit(solution)/shard_map/all_to_all | solution.py:773
  126.9 1.0 copy-done
  127.9 2.2 edges.1
  130.1 3.0 %collective-permute-start.4 = (bf16[64,256]{1,0:T(8,128)(2,1)}, bf16[64,256]{1,0:T(8,128)(2,1)S(1)}, u32[]{:S(2)}, u32[]{:S(2)}) collective-permute-start(bf16[64,256]{1,0:T(8,128)(2,1)} %get-tuple-element.80), channel_id=1, source_target_pairs={{0,16},{16,32},{32,48},{48,64},{64,80},{80,96},{96,112},{1,17},{17... | collective-permute-start | bytes 98312 | tf_op jit(solution)/shard_map/ppermute | solution.py:737
  133.1 1.3 collective-permute-start.5
  134.5 8.5 %project_back.1.cur_ref.before_ref.after_ref = bf16[32,64,1024]{2,1,0:T(8,128)(2,1)} custom-call(bf16[32,64,256]{2,1,0:T(8,128)(2,1)} %cot_ref.5, bf16[64,32,256]{2,1,0:T(8,128)(2,1)} %copy-done, bf16[32,64,1024]{2,1,0:T(8,128)(2,1)} %get-tuple-element.82.slope_ref, bf16[1024,256]{1,0:T(8,128)(2,1)} %wp_ref.5), custom_call_target="tpu_custom_call" | custom-call | flops 1073741824 | bytes 10485760 | tf_op jit(solution)/shard_map/project_back/pallas_call | solution.py:436
  143.1 4.4 %collective-permute-start.7 = (bf16[40,256]{1,0:T(8,128)(2,1)S(1)}, bf16[40,256]{1,0:T(8,128)(2,1)S(1)}, u32[]{:S(2)}, u32[]{:S(2)}) collective-permute-start(bf16[40,256]{1,0:T(8,128)(2,1)S(1)} %get-tuple-element.121), channel_id=1, source_target_pairs={{0,1},{1,2},{2,3},{3,4},{4,5},{5,6},{6,7},{7,8},{8,9},{9,10},{10,1... | collective-permute-start | bytes 61448 | tf_op jit(solution)/shard_map/ppermute | solution.py:743
  147.5 7.5 %project_sum.1.refs_2_ = bf16[128,16,128]{2,1,0:T(8,128)(2,1)} custom-call(bf16[32,64,256]{2,1,0:T(8,128)(2,1)} %cot_ref.5, bf16[64,32,256]{2,1,0:T(8,128)(2,1)} %copy-done, bf16[32,64,1024]{2,1,0:T(8,128)(2,1)} %get-tuple-element.89.mixed_ref), custom_call_target="tpu_custom_call" | custom-call | flops 1073741824 | bytes 8388608 | tf_op jit(solution)/shard_map/project_sum/pallas_call | solution.py:467
  155.0 0.7 pad_maximum_fusion.halo_ref
  155.6 23.4 %expand_back.1 = (bf16[2048,1024]{1,0:T(8,128)(2,1)}, bf16[128,24,128]{2,1,0:T(8,128)(2,1)}) custom-call(bf16[32,64,1024]{2,1,0:T(8,128)(2,1)} %project_back.1.cur_ref.before_ref.after_ref, bf16[32,64,1024]{2,1,0:T(8,128)(2,1)} %project_back.1.cur_ref.before_ref.after_ref, bf16[32,64,1024]{2,1,0:T(8,128)(2,1)} %project_back.1.cur_ref.before_ref.after_ref, ...), custom_call_target="tpu_custom_call" | custom-call | flops 1073741824 | bytes 20971520 | tf_op jit(solution)/shard_map/expand_back/pallas_call | solution.py:556
  179.0 5.1 %collective-permute-start.10 = (bf16[128,24,128]{2,1,0:T(8,128)(2,1)}, bf16[128,24,128]{2,1,0:T(8,128)(2,1)S(1)}, u32[]{:S(2)}, u32[]{:S(2)}) collective-permute-start(bf16[128,24,128]{2,1,0:T(8,128)(2,1)} %get-tuple-element.97.refs_4_), channel_id=1, source_target_pairs={{0,1},{1,0},{2,3},{3,2},{4,5},{5,4},{6,7},{7,6},{8,9},{9,8},{10,11... | collective-permute-start | bytes 2359304 | tf_op jit(solution)/shard_map/ppermute | solution.py:789
  184.3 0.4 collective-permute-start.9
  184.7 2.1 collective-permute-done.6.refs_1_
  186.8 0.7 collective-permute-done.9.refs_3_
  187.7 0.8 copy-done.12
  188.6 3.1 %join.1 = bf16[64,56,128]{2,1,0:T(8,128)(2,1)} custom-call(s32[1]{0:T(128)} %bitcast.core_ref, bf16[128,16,128]{2,1,0:T(8,128)(2,1)} %attention_sums.1.refs_0_, bf16[128,16,128]{2,1,0:T(8,128)(2,1)} %copy-done.11, bf16[128,16,128]{2,1,0:T(8,128)(2,1)} %project_sum.1.refs_2_, bf16[128,16,128]{2,1,0:T(8,128)(2,1)} %copy-done.12, ...), custom_call_target="tpu_custom_call" | custom-call | flops 1048576 | bytes 4194304 | tf_op jit(solution)/shard_map/join/pallas_call | solution.py:616
  191.8 7.7 %all-to-all-start.3 = ((bf16[64,56,128]{2,1,0:T(8,128)(2,1)}), bf16[64,56,128]{2,1,0:T(8,128)(2,1)S(1)}, u32[]{:S(2)}, u32[]{:S(2)}) async-start(bf16[64,56,128]{2,1,0:T(8,128)(2,1)} %join.1), calls=%async_computation.3 | async-start | bytes 1835008 | tf_op jit(solution)/shard_map/all_to_all | solution.py:773
  199.5 8.2 %finish.1 = bf16[32,64,256]{2,1,0:T(8,128)(2,1)} custom-call(bf16[2048,1024]{1,0:T(8,128)(2,1)} %get-tuple-element.100.dpre_ref, bf16[32,64,256]{2,1,0:T(8,128)(2,1)} %x_ref.7, bf16[32,64,256]{2,1,0:T(8,128)(2,1)} %cot_ref.5, bf16[64,32,256]{2,1,0:T(8,128)(2,1)} %copy-done, bf16[256,1024]{1,0:T(8,128)(2,1)} %we_ref.5), custom_call_target="tpu_custom_call" | custom-call | flops 1073741824 | bytes 9437184 | tf_op jit(solution)/shard_map/finish/pallas_call | solution.py:587
  207.7 7.1 %all-to-all-done.3.terms_ref = bf16[64,56,128]{2,1,0:T(8,128)(2,1)S(1)} async-done(((bf16[64,56,128]{2,1,0:T(8,128)(2,1)}), bf16[64,56,128]{2,1,0:T(8,128)(2,1)S(1)}, u32[]{:S(2)}, u32[]{:S(2)}) %all-to-all-start.3) | async-done | bytes 917536 | tf_op jit(solution)/shard_map/all_to_all | solution.py:773
  214.8 0.9 copy-done.2
  215.8 2.3 fold.1
  218.0 19.2 %all_to_all.25.own_ref = bf16[64,56,128]{2,1,0:T(8,128)(2,1)S(1)} all-to-all(bf16[64,56,128]{2,1,0:T(8,128)(2,1)} %fold.1), channel_id=1, replica_groups={{0,2,4,6,8,10,12,14,16,18,20,22,24,26,28,30,32,34,36,38,40,42,44,46,48,..., dimensions={0} | all-to-all | bytes 1835008 | tf_op jit(solution)/shard_map/all_to_all | solution.py:773
  237.3 4.2 %collective-permute-start.11 = (bf16[64,56,128]{2,1,0:T(8,128)(2,1)S(1)}, bf16[64,56,128]{2,1,0:T(8,128)(2,1)S(1)}, u32[]{:S(2)}, u32[]{:S(2)}) collective-permute-start(bf16[64,56,128]{2,1,0:T(8,128)(2,1)S(1)} %all_to_all.25.own_ref), channel_id=1, source_target_pairs={{0,1},{1,0},{2,3},{3,2},{4,5},{5,4},{6,7},{7,6},{8,9},{9,8},{10,11... | collective-permute-start | bytes 2752520 | tf_op jit(solution)/shard_map/ppermute | solution.py:789
  241.4 2.1 collective-permute-done.11.other_ref
  243.5 0.9 copy-done.8
  244.5 3.3 %unfold.1 = (f32[256,1024]{1,0:T(8,128)}, f32[3,3,1024]{2,1,0:T(4,128)}, f32[1024,256]{1,0:T(8,128)}, f32[256,768]{1,0:T(8,128)}, f32[256,256]{1,0:T(8,128)}, /*index=5*/f32[15,4,15]{2,1,0:T(4,128)}) custom-call(s32[1]{0:T(128)} %bitcast.core_ref, bf16[64,56,128]{2,1,0:T(8,128)(2,1)} %copy-done.3, bf16[64,56,128]{2,1,0:T(8,128)(2,1)} %copy-done.8), custom_call_target="tpu_custom_call" | custom-call | bytes 5242880 | tf_op jit(solution)/shard_map/unfold/pallas_call | solution.py:666
  (74 shorter events, 1.3 us)
Async XLA Ops:
  0.6 21.7 %copy-start.1 = (bf16[32,64,256]{2,1,0:T(8,128)(2,1)S(1)}, bf16[32,64,256]{2,1,0:T(8,128)(2,1)}, u32[]{:S(2)}) copy-start(bf16[32,64,256]{2,1,0:T(8,128)(2,1)} %cot_ref.5) | copy-start | bytes 3145732
  1.6 7.1 %collective-permute-start.1 = (bf16[128,256]{1,0:T(8,128)(2,1)S(1)}, bf16[128,256]{1,0:T(8,128)(2,1)S(1)}, u32[]{:S(2)}, u32[]{:S(2)}) collective-permute-start(bf16[128,256]{1,0:T(8,128)(2,1)S(1)} %bitcast.43), channel_id=1, source_target_pairs={{16,0},{32,16},{48,32},{64,48},{80,64},{96,80},{112,96},{17,1},{33... | collective-permute-start | bytes 196616 | tf_op jit(solution)/shard_map/ppermute | solution.py:756
  2.9 6.0 %collective-permute-start = (bf16[128,256]{1,0:T(8,128)(2,1)S(1)}, bf16[128,256]{1,0:T(8,128)(2,1)S(1)}, u32[]{:S(2)}, u32[]{:S(2)}) collective-permute-start(bf16[128,256]{1,0:T(8,128)(2,1)S(1)} %bitcast.42), channel_id=1, source_target_pairs={{0,16},{16,32},{32,48},{48,64},{64,80},{80,96},{96,112},{1,17},{17... | collective-permute-start | bytes 196616 | tf_op jit(solution)/shard_map/ppermute | solution.py:755
  8.7 14.8 %copy-start.15 = (bf16[128,256]{1,0:T(8,128)(2,1)}, bf16[128,256]{1,0:T(8,128)(2,1)S(1)}, u32[]{:S(2)}) copy-start(bf16[128,256]{1,0:T(8,128)(2,1)S(1)} %collective-permute-done.1) | copy-start | bytes 196612
  8.7 28.3 %copy-start.17 = (f32[3,3,1024]{2,1,0:T(4,128)S(1)}, f32[3,3,1024]{2,1,0:T(4,128)}, u32[]{:S(2)}) copy-start(f32[3,3,1024]{2,1,0:T(4,128)} %param.16) | copy-start | bytes 110596
  8.9 28.2 %copy-start.16 = (bf16[128,256]{1,0:T(8,128)(2,1)}, bf16[128,256]{1,0:T(8,128)(2,1)S(1)}, u32[]{:S(2)}) copy-start(bf16[128,256]{1,0:T(8,128)(2,1)S(1)} %collective-permute-done) | copy-start | bytes 196612
  9.0 28.1 %copy-start.13 = (bf16[2,40,256]{2,1,0:T(8,128)(2,1)}, bf16[2,40,256]{2,1,0:T(8,128)(2,1)S(1)}, u32[]{:S(2)}) copy-start(bf16[2,40,256]{2,1,0:T(8,128)(2,1)S(1)} %get-tuple-element.65.own_west_ref) | copy-start | bytes 122884
  9.0 28.1 %copy-start.14 = (bf16[2,40,256]{2,1,0:T(8,128)(2,1)}, bf16[2,40,256]{2,1,0:T(8,128)(2,1)S(1)}, u32[]{:S(2)}) copy-start(bf16[2,40,256]{2,1,0:T(8,128)(2,1)S(1)} %get-tuple-element.66.own_east_ref) | copy-start | bytes 122884
  9.0 13.3 %collective-permute-start.2 = (bf16[2,40,256]{2,1,0:T(8,128)(2,1)S(1)}, bf16[2,40,256]{2,1,0:T(8,128)(2,1)S(1)}, u32[]{:S(2)}, u32[]{:S(2)}) collective-permute-start(bf16[2,40,256]{2,1,0:T(8,128)(2,1)S(1)} %get-tuple-element.66.own_east_ref), channel_id=1, source_target_pairs={{0,1},{1,2},{2,3},{3,4},{4,5},{5,6},{6,7},{7,8},{8,9},{9,10},{10,1... | collective-permute-start | bytes 122888 | tf_op jit(solution)/shard_map/ppermute | solution.py:764
  12.6 9.8 %collective-permute-start.3 = (bf16[2,40,256]{2,1,0:T(8,128)(2,1)S(1)}, bf16[2,40,256]{2,1,0:T(8,128)(2,1)S(1)}, u32[]{:S(2)}, u32[]{:S(2)}) collective-permute-start(bf16[2,40,256]{2,1,0:T(8,128)(2,1)S(1)} %get-tuple-element.65.own_west_ref), channel_id=1, source_target_pairs={{1,0},{2,1},{3,2},{4,3},{5,4},{6,5},{7,6},{8,7},{9,8},{10,9},{11,1... | collective-permute-start | bytes 122888 | tf_op jit(solution)/shard_map/ppermute | solution.py:765
  22.3 15.6 %copy-start.18 = (bf16[2,40,256]{2,1,0:T(8,128)(2,1)}, bf16[2,40,256]{2,1,0:T(8,128)(2,1)S(1)}, u32[]{:S(2)}) copy-start(bf16[2,40,256]{2,1,0:T(8,128)(2,1)S(1)} %collective-permute-done.2.west_ref) | copy-start | bytes 122884
  22.4 15.6 %copy-start.19 = (bf16[2,40,256]{2,1,0:T(8,128)(2,1)}, bf16[2,40,256]{2,1,0:T(8,128)(2,1)S(1)}, u32[]{:S(2)}) copy-start(bf16[2,40,256]{2,1,0:T(8,128)(2,1)S(1)} %collective-permute-done.3.east_ref) | copy-start | bytes 122884
  23.5 34.7 %all-to-all-start.1 = ((bf16[64,32,256]{2,1,0:T(8,128)(2,1)}), bf16[64,32,256]{2,1,0:T(8,128)(2,1)S(1)}, u32[]{:S(2)}, u32[]{:S(2)}) async-start(bf16[64,32,256]{2,1,0:T(8,128)(2,1)} %bitcast.13), calls=%async_computation.1 | async-start | bytes 2097152 | tf_op jit(solution)/shard_map/all_to_all | solution.py:773
  37.1 0.8 copy-start.10
  37.9 30.1 %copy-start.20 = (f32[4,15,15]{2,0,1:T(4,128)S(1)}, f32[4,15,15]{2,0,1:T(4,128)}, u32[]{:S(2)}) copy-start(f32[4,15,15]{2,0,1:T(4,128)} %param.20) | copy-start | bytes 10804
  37.9 30.2 %copy-start.23 = (s32[64,64]{0,1:T(8,128)S(1)}, s32[64,64]{0,1:T(8,128)}, u32[]{:S(2)}) copy-start(s32[64,64]{0,1:T(8,128)} %constant.21.clone) | copy-start | bytes 49156
  58.2 13.6 %copy-start.6 = (bf16[64,32,256]{2,1,0:T(8,128)(2,1)}, bf16[64,32,256]{2,1,0:T(8,128)(2,1)S(1)}, u32[]{:S(2)}) copy-start(bf16[64,32,256]{2,1,0:T(8,128)(2,1)S(1)} %all-to-all-done.1.cot_ref) | copy-start | bytes 3145732
  58.2 25.0 %all-to-all-start = ((bf16[64,32,256]{2,1,0:T(8,128)(2,1)}), bf16[64,32,256]{2,1,0:T(8,128)(2,1)S(1)}, u32[]{:S(2)}, u32[]{:S(2)}) async-start(bf16[64,32,256]{2,1,0:T(8,128)(2,1)} %get-tuple-element.67), calls=%async_computation | async-start | bytes 2097152 | tf_op jit(solution)/shard_map/all_to_all | solution.py:773
  83.2 1.0 copy-start.7
  106.1 20.8 %all-to-all-start.2 = ((bf16[64,32,256]{2,1,0:T(8,128)(2,1)}), bf16[64,32,256]{2,1,0:T(8,128)(2,1)S(1)}, u32[]{:S(2)}, u32[]{:S(2)}) async-start(bf16[64,32,256]{2,1,0:T(8,128)(2,1)} %get-tuple-element.73), calls=%async_computation.2 | async-start | bytes 2097152 | tf_op jit(solution)/shard_map/all_to_all | solution.py:773
  126.9 1.0 copy-start
  130.1 12.9 %collective-permute-start.4 = (bf16[64,256]{1,0:T(8,128)(2,1)}, bf16[64,256]{1,0:T(8,128)(2,1)S(1)}, u32[]{:S(2)}, u32[]{:S(2)}) collective-permute-start(bf16[64,256]{1,0:T(8,128)(2,1)} %get-tuple-element.80), channel_id=1, source_target_pairs={{0,16},{16,32},{32,48},{48,64},{64,80},{80,96},{96,112},{1,17},{17... | collective-permute-start | bytes 98312 | tf_op jit(solution)/shard_map/ppermute | solution.py:737
  133.1 9.8 %collective-permute-start.5 = (bf16[64,256]{1,0:T(8,128)(2,1)}, bf16[64,256]{1,0:T(8,128)(2,1)S(1)}, u32[]{:S(2)}, u32[]{:S(2)}) collective-permute-start(bf16[64,256]{1,0:T(8,128)(2,1)} %get-tuple-element.81), channel_id=1, source_target_pairs={{16,0},{32,16},{48,32},{64,48},{80,64},{96,80},{112,96},{17,1},{33... | collective-permute-start | bytes 98312 | tf_op jit(solution)/shard_map/ppermute | solution.py:737
  134.4 8.6 %copy-start.21 = (bf16[32,256]{1,0:T(8,128)(2,1)S(1)}, bf16[32,256]{1,0:T(8,128)(2,1)}, u32[]{:S(2)}) copy-start(bf16[32,256]{1,0:T(8,128)(2,1)} %get-tuple-element.88) | copy-start | bytes 49156
  134.4 8.6 %copy-start.22 = (bf16[32,256]{1,0:T(8,128)(2,1)S(1)}, bf16[32,256]{1,0:T(8,128)(2,1)}, u32[]{:S(2)}) copy-start(bf16[32,256]{1,0:T(8,128)(2,1)} %get-tuple-element.87) | copy-start | bytes 49156
  143.1 11.9 %collective-permute-start.7 = (bf16[40,256]{1,0:T(8,128)(2,1)S(1)}, bf16[40,256]{1,0:T(8,128)(2,1)S(1)}, u32[]{:S(2)}, u32[]{:S(2)}) collective-permute-start(bf16[40,256]{1,0:T(8,128)(2,1)S(1)} %get-tuple-element.121), channel_id=1, source_target_pairs={{0,1},{1,2},{2,3},{3,4},{4,5},{5,6},{6,7},{7,8},{8,9},{9,10},{10,1... | collective-permute-start | bytes 61448 | tf_op jit(solution)/shard_map/ppermute | solution.py:743
  147.5 7.5 %collective-permute-start.8 = (bf16[40,256]{1,0:T(8,128)(2,1)S(1)}, bf16[40,256]{1,0:T(8,128)(2,1)S(1)}, u32[]{:S(2)}, u32[]{:S(2)}) collective-permute-start(bf16[40,256]{1,0:T(8,128)(2,1)S(1)} %get-tuple-element.122), channel_id=1, source_target_pairs={{1,0},{2,1},{3,2},{4,3},{5,4},{6,5},{7,6},{8,7},{9,8},{10,9},{11,1... | collective-permute-start | bytes 61448 | tf_op jit(solution)/shard_map/ppermute | solution.py:746
  155.6 28.5 %copy-start.4 = (bf16[128,16,128]{2,1,0:T(8,128)(2,1)S(1)}, bf16[128,16,128]{2,1,0:T(8,128)(2,1)}, u32[]{:S(2)}) copy-start(bf16[128,16,128]{2,1,0:T(8,128)(2,1)} %attention_sums.1.refs_0_) | copy-start | bytes 1572868
  155.6 28.6 %copy-start.5 = (bf16[128,16,128]{2,1,0:T(8,128)(2,1)S(1)}, bf16[128,16,128]{2,1,0:T(8,128)(2,1)}, u32[]{:S(2)}) copy-start(bf16[128,16,128]{2,1,0:T(8,128)(2,1)} %project_sum.1.refs_2_) | copy-start | bytes 1572868
  179.0 8.6 %collective-permute-start.10 = (bf16[128,24,128]{2,1,0:T(8,128)(2,1)}, bf16[128,24,128]{2,1,0:T(8,128)(2,1)S(1)}, u32[]{:S(2)}, u32[]{:S(2)}) collective-permute-start(bf16[128,24,128]{2,1,0:T(8,128)(2,1)} %get-tuple-element.97.refs_4_), channel_id=1, source_target_pairs={{0,1},{1,0},{2,3},{3,2},{4,5},{5,4},{6,7},{7,6},{8,9},{9,8},{10,11... | collective-permute-start | bytes 2359304 | tf_op jit(solution)/shard_map/ppermute | solution.py:789
  184.2 2.7 %collective-permute-start.6 = (bf16[128,16,128]{2,1,0:T(8,128)(2,1)S(1)}, bf16[128,16,128]{2,1,0:T(8,128)(2,1)S(1)}, u32[]{:S(2)}, u32[]{:S(2)}) collective-permute-start(bf16[128,16,128]{2,1,0:T(8,128)(2,1)S(1)} %copy-done.4), channel_id=1, source_target_pairs={{0,1},{1,0},{2,3},{3,2},{4,5},{5,4},{6,7},{7,6},{8,9},{9,8},{10,11... | collective-permute-start | bytes 1572872 | tf_op jit(solution)/shard_map/ppermute | solution.py:789
  184.3 3.3 %collective-permute-start.9 = (bf16[128,16,128]{2,1,0:T(8,128)(2,1)S(1)}, bf16[128,16,128]{2,1,0:T(8,128)(2,1)S(1)}, u32[]{:S(2)}, u32[]{:S(2)}) collective-permute-start(bf16[128,16,128]{2,1,0:T(8,128)(2,1)S(1)} %copy-done.5), channel_id=1, source_target_pairs={{0,1},{1,0},{2,3},{3,2},{4,5},{5,4},{6,7},{7,6},{8,9},{9,8},{10,11... | collective-permute-start | bytes 1572872 | tf_op jit(solution)/shard_map/ppermute | solution.py:789
  186.8 0.8 copy-start.11
  187.6 0.8 copy-start.12
  187.6 1.0 copy-start.9
  191.8 23.0 %all-to-all-start.3 = ((bf16[64,56,128]{2,1,0:T(8,128)(2,1)}), bf16[64,56,128]{2,1,0:T(8,128)(2,1)S(1)}, u32[]{:S(2)}, u32[]{:S(2)}) async-start(bf16[64,56,128]{2,1,0:T(8,128)(2,1)} %join.1), calls=%async_computation.3 | async-start | bytes 1835008 | tf_op jit(solution)/shard_map/all_to_all | solution.py:773
  214.8 0.9 copy-start.2
  237.3 6.3 %copy-start.3 = (bf16[64,56,128]{2,1,0:T(8,128)(2,1)}, bf16[64,56,128]{2,1,0:T(8,128)(2,1)S(1)}, u32[]{:S(2)}) copy-start(bf16[64,56,128]{2,1,0:T(8,128)(2,1)S(1)} %all_to_all.25.own_ref) | copy-start | bytes 2752516
  237.3 6.3 %collective-permute-start.11 = (bf16[64,56,128]{2,1,0:T(8,128)(2,1)S(1)}, bf16[64,56,128]{2,1,0:T(8,128)(2,1)S(1)}, u32[]{:S(2)}, u32[]{:S(2)}) collective-permute-start(bf16[64,56,128]{2,1,0:T(8,128)(2,1)S(1)} %all_to_all.25.own_ref), channel_id=1, source_target_pairs={{0,1},{1,0},{2,3},{3,2},{4,5},{5,4},{6,7},{7,6},{8,9},{9,8},{10,11... | collective-permute-start | bytes 2752520 | tf_op jit(solution)/shard_map/ppermute | solution.py:789
  243.5 0.9 copy-start.8

commit v4 on v3

--- a/solution.py
+++ b/solution.py
@@ -290,7 +290,7 @@
         in_specs=[whole(shape), whole((CHAN, CHAN)), whole((256, 256))],
         out_specs=[whole(grouped), whole(grouped)],
         out_shape=[jax.ShapeDtypeStruct(grouped, BF16)] * 2,
-        compiler_params=params(58),
+        compiler_params=params(24),
         cost_estimate=pl.CostEstimate(
             flops=n_groups * 64 * 4 * CHAN * CHAN, bytes_accessed=3 * MIB, transcendentals=0
         ),
@@ -482,7 +482,7 @@
 def expand_back_body(
     cur_ref, before_ref, after_ref, halo_ref, halo_slope_ref, wp_ref, hid_ref, slope_ref, x_ref, dkb_ref,
     extra_ref,
-    dpre_ref, tiles_ref, top_ref, bottom_ref, left_ref, right_ref, acc_ref, sum_ref, depth_ref,
+    dpre_ref, tiles_ref, top_ref, bottom_ref, left_ref, right_ref, acc_ref, sum_ref, depth_ref, shift_ref,
 ):
     step = pl.program_id(0)
 
@@ -506,34 +506,42 @@
         rows = [jnp.where(first, top_ref[:, span], before_ref[0, :, span].astype(F32))]
         rows += [cur_ref[r, :, span].astype(F32) for r in range(BLK)]
         rows += [jnp.where(last, bottom_ref[:, span], after_ref[0, :, span].astype(F32))]
-        shifted = []
         for r in range(BLK + 2):
             left = left_ref[step, r : r + 1, span]
             right = right_ref[step, r : r + 1, span]
-            moved = (
-                jnp.concatenate([rows[r][1:], right], axis=0),
-                rows[r],
-                jnp.concatenate([left, rows[r][:-1]], axis=0),
-            )
-            shifted.append([piece.astype(BF16).reshape(PACKED) for piece in moved])
-        hid = [hid_ref[r, :, span].reshape(PACKED) for r in range(BLK)]
-        totals = [None] * BLK
-        for a in range(3):
-            for b in range(3):
-                n = 3 * a + b
-                kern = dkb_ref[n, :, span][None]
-                terms = []
-                for r in range(BLK):
-                    piece = shifted[r + 2 - a][b]
-                    tap = kern * piece
-                    totals[r] = tap if n == 0 else totals[r] + tap
-                    terms.append(hid[r] * piece)
-                part = (terms[0] + terms[1]) + (terms[2] + terms[3])
-                part = ((part[0] + part[1]) + (part[2] + part[3])).astype(F32)
-                acc_ref[n, :, span] += part[:8] + part[8:]
-        for r in range(BLK):
-            d_pre = totals[r].reshape(COLS, LANES) * slope_ref[r, :, span]
-            dpre_ref[r * COLS : (r + 1) * COLS, span] = d_pre
+            shift_ref[0, r, :, span] = jnp.concatenate([rows[r][1:], right], axis=0).astype(BF16)
+            shift_ref[1, r, :, span] = rows[r].astype(BF16)
+            shift_ref[2, r, :, span] = jnp.concatenate([left, rows[r][:-1]], axis=0).astype(BF16)
+        kern = [dkb_ref[n, :, span] for n in range(9)]
+        sums = [acc_ref[n, :, span] for n in range(9)]
+        held = None
+        for j in range(0, COLS, 16):
+            cells = slice(j, j + 16)
+            pieces = [[shift_ref[b, r, cells, span] for b in range(3)] for r in range(BLK + 2)]
+            hid = [hid_ref[r, cells, span] for r in range(BLK)]
+            totals = [None] * BLK
+            parts = []
+            for a in range(3):
+                for b in range(3):
+                    n = 3 * a + b
+                    terms = []
+                    for r in range(BLK):
+                        piece = pieces[r + 2 - a][b]
+                        tap = kern[n] * piece
+                        totals[r] = tap if n == 0 else totals[r] + tap
+                        terms.append(hid[r] * piece)
+                    parts.append((terms[0] + terms[1]) + (terms[2] + terms[3]))
+            if held is None:
+                held = parts
+            else:
+                for n in range(9):
+                    part = (held[n] + parts[n]).astype(F32)
+                    sums[n] = sums[n] + (part[:8] + part[8:])
+                held = None
+            for r in range(BLK):
+                dpre_ref[r * COLS + j : r * COLS + j + 16, span] = totals[r] * slope_ref[r, cells, span]
+        for n in range(9):
+            acc_ref[n, :, span] = sums[n]
     normed, _ = layer_norm(x_ref[...].reshape(TOK, CHAN).astype(F32))
     sum_ref[...] += dot_tn(normed.astype(BF16), dpre_ref[...])
 
@@ -568,7 +576,8 @@
         ],
         scratch_shapes=[pltpu.VMEM((COLS, EXP), F32)] * 2
         + [pltpu.VMEM((STEPS, 8, EXP), F32)] * 2
-        + [pltpu.VMEM((9, 8, EXP), F32), pltpu.VMEM((CHAN, EXP), F32), pltpu.VMEM((9, EXP), F32)],
+        + [pltpu.VMEM((9, 8, EXP), F32), pltpu.VMEM((CHAN, EXP), F32), pltpu.VMEM((9, EXP), F32)]
+        + [pltpu.VMEM((3, BLK + 2, COLS, EXP), BF16)],
         compiler_params=params(58),
         cost_estimate=pl.CostEstimate(
             flops=2 * ROWS * COLS * CHAN * EXP, bytes_accessed=20 * MIB, transcendentals=0
@@ -617,7 +626,7 @@
         join_body,
         in_specs=[pl.BlockSpec(memory_space=pltpu.SMEM)] + [vmem] * len(tiles),
         out_shape=jax.ShapeDtypeStruct(JOINED, BF16),
-        compiler_params=params(58),
+        compiler_params=params(24),
         cost_estimate=pl.CostEstimate(flops=MIB, bytes_accessed=4 * MIB, transcendentals=0),
         name="join",
     )(core, *tiles)
@@ -633,7 +642,7 @@
     return pl.pallas_call(
         fold_body,
         out_shape=jax.ShapeDtypeStruct(terms.shape, BF16),
-        compiler_params=params(58),
+        compiler_params=params(24),
         cost_estimate=pl.CostEstimate(flops=terms.size, bytes_accessed=4 * terms.size, transcendentals=0),
         name="fold",
     )(terms)
@@ -674,7 +683,7 @@
             jax.ShapeDtypeStruct((CHAN, CHAN), F32),
             jax.ShapeDtypeStruct((15, 4, 15), F32),
         ],
-        compiler_params=params(58),
+        compiler_params=params(24),
         cost_estimate=pl.CostEstimate(flops=0, bytes_accessed=5 * MIB, transcendentals=0),
         name="unfold",
     )(core, own, other)
@@ -717,7 +726,7 @@
         out_specs=[whole((COLS, CHAN))] * 2 + [whole((ROWS, CHAN))] * 2,
         out_shape=[jax.ShapeDtypeStruct((COLS, CHAN), BF16)] * 2
         + [jax.ShapeDtypeStruct((ROWS, CHAN), BF16)] * 2,
-        compiler_params=params(58),
+        compiler_params=params(24),
         cost_estimate=pl.CostEstimate(flops=MIB, bytes_accessed=2 * MIB, transcendentals=0),
         name="edges",
     )(*([d_branch, cot] * 4), jnp.asarray(FIRST_CELL, BF16), jnp.asarray(LAST_CELL, BF16))
@@ -749,11 +758,14 @@
     return jnp.concatenate([above, below, from_west, from_east], axis=0)
 
 
-def wide_halo(field):
-    south, north, east, west = shifts()
+def wide_rows(field):
     flat = (2 * COLS, CHAN)
-    above = lax.ppermute(field[-2:].reshape(flat), "lat", south).reshape(2, COLS, CHAN)
-    below = lax.ppermute(field[:2].reshape(flat), "lat", north).reshape(2, COLS, CHAN)
+    above, below = rows_of(field[:2].reshape(flat), field[-2:].reshape(flat))
+    return (above.reshape(2, COLS, CHAN), below.reshape(2, COLS, CHAN))
+
+
+def wide_columns(field, above, below):
+    _, _, east, west = shifts()
     pad = jnp.zeros((2, EDGE - ROWS - 4, field.shape[2]), field.dtype)
 
     def columns(at):
@@ -763,7 +775,7 @@
     own_west, own_east = columns(0), columns(COLS - 2)
     from_west = lax.ppermute(own_east, "lon", east)
     from_east = lax.ppermute(own_west, "lon", west)
-    return (above, below, from_west, from_east, own_west, own_east)
+    return (from_west, from_east, own_west, own_east)
 
 
 def exchange(pieces):
@@ -811,9 +823,10 @@
     core = lax.axis_index("lon").astype(jnp.int32).reshape(1) & 1
     barrier = lax.optimization_barrier
 
-    field_halo = wide_halo(field_in)
+    above, below = wide_rows(field_in)
     hidden, act_slope = expand(field_in, expand_weight)
-    field_halo, late_cot = barrier((field_halo, cotangent))
+    above, below, hidden, late_cot = barrier((above, below, hidden, cotangent))
+    field_halo = (above, below, *wide_columns(field_in, above, below))
     hidden, cot_pieces = barrier((hidden, to_pieces(late_cot)))
     cot_groups = exchange(cot_pieces)
     section, mixed, mixed_slope, ring_slope = mix(

time: 249 us -> 251 us (level)
  waiting for transfers between devices: 26.3 us -> 35.2 us
  Pallas kernels: 119 us -> 115 us
    ppermute x4 -> x2, starting transfers between devices: 9.51 us -> 2.75 us  [the longest x1 2.75 us: wide_columns(): from_west = lax.ppermute(own_east, 'lon', east)]
    ppermute x4 -> x2, waiting for transfers between devices: 0.16 us -> 6.34 us  [the longest x1 3.28 us: wide_columns(): from_east = lax.ppermute(own_west, 'lon', west)]
    ppermute x2 -> x4, starting transfers between devices: 4.33 us -> 9.27 us  [rows_of(): return (lax.ppermute(bottom, 'lat', south), lax.ppermute(top, 'lat', north))]
    pallas_call x1, Pallas kernels: 23.4 us -> 27.3 us  [expand_back(): pl.pallas_call(expand_back_body, grid=(STEPS,), in_specs=[cells, ROW_BEFO...]
    all_to_all x4, waiting for transfers between devices: 21.2 us -> 23.8 us  [exchange(): lax.all_to_all(pieces, ('lat', 'lon'), split_axis=0, concat_axis=0, axis_...]
  transfers between devices with their start and end apart: 16 -> 16, of which waited for: 7 -> 8; matrix products, arithmetic and copies ran while one was open for 4% -> 4% of each run, Pallas kernels for 25% -> 24%
where the time goes in v4:
time: 251 us; the launch traced here: 250 us
  Pallas kernels  115 us (46%)
  starting transfers between devices  64.1 us (26%)
  waiting for transfers between devices  35.2 us (14%)
  blocking collectives  19 us (8%)
  local copies, waits for them, and re-layouts  11.1 us (4%)
  matrix products  4.24 us (2%)
    all_to_all x4, starting transfers between devices, exchange(): lax.all_to_all(pieces, ('lat', 'lon'), split_axis=0, concat_axis=0, axis_...  38.3 us
    pallas_call x1, Pallas kernels, expand_back(): pl.pallas_call(expand_back_body, grid=(STEPS,), in_specs=[cells, ROW_BEFO...  27.3 us
    all_to_all x4, waiting for transfers between devices, exchange(): lax.all_to_all(pieces, ('lat', 'lon'), split_axis=0, concat_axis=0, axis_...  23.8 us
    pallas_call x1, Pallas kernels, attention(): pl.pallas_call(attention_body, grid=(n_groups // 4,), in_specs=[whole(sha...  21.9 us
    pallas_call x1, Pallas kernels, mix(): pl.pallas_call(mix_body, grid=(STEPS,), in_specs=[band((BLK, COLS, EXP)),...  20.3 us
    all_to_all x1, blocking collectives, exchange(): lax.all_to_all(pieces, ('lat', 'lon'), split_axis=0, concat_axis=0, axis_...  19 us
    ppermute x4, starting transfers between devices, other_core(): return lax.ppermute(tiles, 'lon', swaps)  9.81 us
    pallas_call x1, Pallas kernels, expand(): pl.pallas_call(expand_body, grid=(STEPS,), in_specs=[band((BLK, COLS, CHA...  9.72 us
  transfers between devices with their start and end apart: 16, of which 8 were waited for; matrix products, arithmetic and copies ran while one was open for 4% of the time, Pallas kernels for 24%

profile of v4, /device:TPU:1, one launch (start us, length us, event | category | flops | bytes accessed | tf_op | source)
XLA Modules:
  0.0 250.0 jit_solution(13849794280395738076)
XLA Ops:
  0.6 1.0 fusion.7
  1.6 4.0 %collective-permute-start = (bf16[128,256]{1,0:T(8,128)(2,1)S(1)}, bf16[128,256]{1,0:T(8,128)(2,1)S(1)}, u32[]{:S(2)}, u32[]{:S(2)}) collective-permute-start(bf16[128,256]{1,0:T(8,128)(2,1)S(1)} %bitcast.43), channel_id=1, source_target_pairs={{0,16},{16,32},{32,48},{48,64},{64,80},{80,96},{96,112},{1,17},{17... | collective-permute-start | bytes 196616 | tf_op jit(solution)/shard_map/ppermute | solution.py:746
  5.7 1.3 collective-permute-start.1
  7.0 9.7 %expand.1 = (bf16[32,64,1024]{2,1,0:T(8,128)(2,1)}, bf16[32,64,1024]{2,1,0:T(8,128)(2,1)}) custom-call(bf16[32,64,256]{2,1,0:T(8,128)(2,1)} %x_ref.7, bf16[256,1024]{1,0:T(8,128)(2,1)} %we_ref.5), custom_call_target="tpu_custom_call" | custom-call | flops 1073741824 | bytes 10485760 | tf_op jit(solution)/shard_map/expand/pallas_call | solution.py:106
  16.8 1.1 copy.27
  17.9 11.9 %all-to-all-start.1 = ((bf16[64,32,256]{2,1,0:T(8,128)(2,1)}), bf16[64,32,256]{2,1,0:T(8,128)(2,1)S(1)}, u32[]{:S(2)}, u32[]{:S(2)}) async-start(bf16[64,32,256]{2,1,0:T(8,128)(2,1)} %bitcast.7), calls=%async_computation.1 | async-start | bytes 2097152 | tf_op jit(solution)/shard_map/all_to_all | solution.py:785
  29.9 1.0 fusion.6
  31.2 2.7 %collective-permute-start.2 = (bf16[2,40,256]{2,1,0:T(8,128)(2,1)S(1)}, bf16[2,40,256]{2,1,0:T(8,128)(2,1)S(1)}, u32[]{:S(2)}, u32[]{:S(2)}) collective-permute-start(bf16[2,40,256]{2,1,0:T(8,128)(2,1)S(1)} %get-tuple-element.118.own_east_ref), channel_id=1, source_target_pairs={{0,1},{1,2},{2,3},{3,4},{4,5},{5,6},{6,7},{7,8},{8,9},{9,10},{10,1... | collective-permute-start | bytes 122888 | tf_op jit(solution)/shard_map/ppermute | solution.py:776
  34.0 3.1 %collective-permute-done.2.west_ref = bf16[2,40,256]{2,1,0:T(8,128)(2,1)S(1)} collective-permute-done((bf16[2,40,256]{2,1,0:T(8,128)(2,1)S(1)}, bf16[2,40,256]{2,1,0:T(8,128)(2,1)S(1)}, u32[]{:S(2)}, u32[]{:S(2)}) %collective-permute-start.2) | collective-permute-done | bytes 40992 | tf_op jit(solution)/shard_map/ppermute | solution.py:776
  37.0 3.3 %collective-permute-done.3.east_ref = bf16[2,40,256]{2,1,0:T(8,128)(2,1)S(1)} collective-permute-done((bf16[2,40,256]{2,1,0:T(8,128)(2,1)S(1)}, bf16[2,40,256]{2,1,0:T(8,128)(2,1)S(1)}, u32[]{:S(2)}, u32[]{:S(2)}) %collective-permute-start.3) | collective-permute-done | bytes 40992 | tf_op jit(solution)/shard_map/ppermute | solution.py:777
  40.3 0.7 broadcast_in_dim.14.dkb_ref
  41.2 20.3 %mix.1 = (bf16[64,32,256]{2,1,0:T(8,128)(2,1)}, bf16[32,64,1024]{2,1,0:T(8,128)(2,1)}, bf16[32,64,1024]{2,1,0:T(8,128)(2,1)}, f32[208,1024]{1,0:T(8,128)}) custom-call(bf16[32,64,1024]{2,1,0:T(8,128)(2,1)} %get-tuple-element.58.cur_ref.before_ref.after_ref.hid_ref, bf16[32,64,1024]{2,1,0:T(8,128)(2,1)} %get-tuple-element.58.cur_ref.before_ref.after_ref.hid_ref, ...), custom_call_target="tpu_custom_call" | custom-call | flops 1610612736 | bytes 18874368 | tf_op jit(solution)/shard_map/mix/pallas_call | solution.py:224
  61.5 12.9 %all-to-all-start = ((bf16[64,32,256]{2,1,0:T(8,128)(2,1)}), bf16[64,32,256]{2,1,0:T(8,128)(2,1)S(1)}, u32[]{:S(2)}, u32[]{:S(2)}) async-start(bf16[64,32,256]{2,1,0:T(8,128)(2,1)} %get-tuple-element.61), calls=%async_computation | async-start | bytes 2097152 | tf_op jit(solution)/shard_map/all_to_all | solution.py:785
  74.5 2.8 %fusion.4 = f32[64,4,64]{2,1,0:T(4,128)S(1)} fusion(f32[4,225,1]{1,0,2:T(4,128)S(1)} %reshape.75, s32[64,64]{0,1:T(8,128)S(1)} %copy-done.21), kind=kOutput, calls=%fused_computation.5 | convolution fusion | flops 45158400 | bytes 85520 | tf_op jit(solution)/shard_map/tsr,hr->sht/dot_general | solution.py:817
  77.3 0.8 reshape.69.bias_ref
  78.1 0.8 prepare.1
  78.9 1.0 copy-done.3
  79.9 1.0 copy-done.9
  80.8 10.2 %all-to-all-done.x_ref = bf16[64,32,256]{2,1,0:T(8,128)(2,1)S(1)} async-done(((bf16[64,32,256]{2,1,0:T(8,128)(2,1)}), bf16[64,32,256]{2,1,0:T(8,128)(2,1)S(1)}, u32[]{:S(2)}, u32[]{:S(2)}) %all-to-all-start) | async-done | bytes 1048608 | tf_op jit(solution)/shard_map/all_to_all | solution.py:785
  91.0 1.0 copy-done.11
  92.0 21.9 %attention.1 = (bf16[64,32,256]{2,1,0:T(8,128)(2,1)}, bf16[2048,256]{1,0:T(8,128)(2,1)}, bf16[2048,256]{1,0:T(8,128)(2,1)}, bf16[2048,768]{1,0:T(8,128)(2,1)}, f32[64,256]{1,0:T(8,128)}) custom-call(bf16[64,32,256]{2,1,0:T(8,128)(2,1)} %copy-done.11, bf16[32,64,256]{2,1,0:T(8,128)(2,1)} %copy-done.9, bf16[256,768]{1,0:T(8,128)(2,1)} %wqkv_ref.1, ...), custom_call_target="tpu_custom_call" | custom-call | flops 2684354560 | bytes 8388608 | tf_op jit(solution)/shard_map/attention/pallas_call | solution.py:359
  114.0 5.8 %all-to-all-start.2 = ((bf16[64,32,256]{2,1,0:T(8,128)(2,1)}), bf16[64,32,256]{2,1,0:T(8,128)(2,1)S(1)}, u32[]{:S(2)}, u32[]{:S(2)}) async-start(bf16[64,32,256]{2,1,0:T(8,128)(2,1)} %get-tuple-element.67), calls=%async_computation.2 | async-start | bytes 2097152 | tf_op jit(solution)/shard_map/all_to_all | solution.py:785
  119.9 0.9 reshape.71
  120.8 1.4 fusion.5
  122.4 0.8 pad.4.extra_ref
  123.2 5.3 %attention_sums.1.refs_0_ = bf16[128,16,128]{2,1,0:T(8,128)(2,1)} custom-call(bf16[2048,256]{1,0:T(8,128)(2,1)} %get-tuple-element.68.att_ref, bf16[2048,256]{1,0:T(8,128)(2,1)} %bitcast.36, bf16[2048,256]{1,0:T(8,128)(2,1)} %get-tuple-element.70.norm_ref, bf16[2048,768]{1,0:T(8,128)(2,1)} %get-tuple-element.71.proj_ref), custom_call_target="tpu_custom_call" | custom-call | flops 1073741824 | bytes 6291456 | tf_op jit(solution)/shard_map/attention_sums/pallas_call | solution.py:404
  128.5 6.5 %all-to-all-done.2.db_ref = bf16[64,32,256]{2,1,0:T(8,128)(2,1)S(1)} async-done(((bf16[64,32,256]{2,1,0:T(8,128)(2,1)}), bf16[64,32,256]{2,1,0:T(8,128)(2,1)S(1)}, u32[]{:S(2)}, u32[]{:S(2)}) %all-to-all-start.2) | async-done | bytes 1048608 | tf_op jit(solution)/shard_map/all_to_all | solution.py:785
  135.0 1.7 edges.1
  136.8 2.7 %collective-permute-start.4 = (bf16[64,256]{1,0:T(8,128)(2,1)S(1)}, bf16[64,256]{1,0:T(8,128)(2,1)S(1)}, u32[]{:S(2)}, u32[]{:S(2)}) collective-permute-start(bf16[64,256]{1,0:T(8,128)(2,1)S(1)} %get-tuple-element.74), channel_id=1, source_target_pairs={{0,16},{16,32},{32,48},{48,64},{64,80},{80,96},{96,112},{1,17},{17... | collective-permute-start | bytes 98312 | tf_op jit(solution)/shard_map/ppermute | solution.py:746
  139.4 1.3 collective-permute-start.5
  140.7 8.5 %project_back.1.cur_ref.before_ref.after_ref = bf16[32,64,1024]{2,1,0:T(8,128)(2,1)} custom-call(bf16[32,64,256]{2,1,0:T(8,128)(2,1)} %cot_ref.5, bf16[64,32,256]{2,1,0:T(8,128)(2,1)} %copy-done, bf16[32,64,1024]{2,1,0:T(8,128)(2,1)} %get-tuple-element.76.slope_ref, bf16[1024,256]{1,0:T(8,128)(2,1)} %wp_ref.5), custom_call_target="tpu_custom_call" | custom-call | flops 1073741824 | bytes 10485760 | tf_op jit(solution)/shard_map/project_back/pallas_call | solution.py:436
  149.3 3.9 %collective-permute-start.7 = (bf16[40,256]{1,0:T(8,128)(2,1)S(1)}, bf16[40,256]{1,0:T(8,128)(2,1)S(1)}, u32[]{:S(2)}, u32[]{:S(2)}) collective-permute-start(bf16[40,256]{1,0:T(8,128)(2,1)S(1)} %get-tuple-element.115), channel_id=1, source_target_pairs={{0,1},{1,2},{2,3},{3,4},{4,5},{5,6},{6,7},{7,8},{8,9},{9,10},{10,1... | collective-permute-start | bytes 61448 | tf_op jit(solution)/shard_map/ppermute | solution.py:752
  153.3 7.5 %project_sum.1.refs_2_ = bf16[128,16,128]{2,1,0:T(8,128)(2,1)} custom-call(bf16[32,64,256]{2,1,0:T(8,128)(2,1)} %cot_ref.5, bf16[64,32,256]{2,1,0:T(8,128)(2,1)} %copy-done, bf16[32,64,1024]{2,1,0:T(8,128)(2,1)} %get-tuple-element.83.mixed_ref), custom_call_target="tpu_custom_call" | custom-call | flops 1073741824 | bytes 8388608 | tf_op jit(solution)/shard_map/project_sum/pallas_call | solution.py:467
  160.8 0.7 pad_maximum_fusion.halo_ref
  161.4 27.3 %expand_back.1 = (bf16[2048,1024]{1,0:T(8,128)(2,1)}, bf16[128,24,128]{2,1,0:T(8,128)(2,1)}) custom-call(bf16[32,64,1024]{2,1,0:T(8,128)(2,1)} %project_back.1.cur_ref.before_ref.after_ref, bf16[32,64,1024]{2,1,0:T(8,128)(2,1)} %project_back.1.cur_ref.before_ref.after_ref, bf16[32,64,1024]{2,1,0:T(8,128)(2,1)} %project_back.1.cur_ref.before_ref.after_ref, ...), custom_call_target="tpu_custom_call" | custom-call | flops 1073741824 | bytes 20971520 | tf_op jit(solution)/shard_map/expand_back/pallas_call | solution.py:564
  188.8 5.1 %collective-permute-start.10 = (bf16[128,24,128]{2,1,0:T(8,128)(2,1)}, bf16[128,24,128]{2,1,0:T(8,128)(2,1)S(1)}, u32[]{:S(2)}, u32[]{:S(2)}) collective-permute-start(bf16[128,24,128]{2,1,0:T(8,128)(2,1)} %get-tuple-element.91.refs_4_), channel_id=1, source_target_pairs={{0,1},{1,0},{2,3},{3,2},{4,5},{5,4},{6,7},{7,6},{8,9},{9,8},{10,11... | collective-permute-start | bytes 2359304 | tf_op jit(solution)/shard_map/ppermute | solution.py:801
  194.0 0.4 collective-permute-start.9
  194.4 2.1 collective-permute-done.6.refs_1_
  196.6 0.7 collective-permute-done.9.refs_3_
  197.3 1.1 copy-done.4
  198.4 1.1 join.1
  199.6 7.6 %all-to-all-start.3 = ((bf16[64,56,128]{2,1,0:T(8,128)(2,1)}), bf16[64,56,128]{2,1,0:T(8,128)(2,1)S(1)}, u32[]{:S(2)}, u32[]{:S(2)}) async-start(bf16[64,56,128]{2,1,0:T(8,128)(2,1)} %join.1), calls=%async_computation.3 | async-start | bytes 1835008 | tf_op jit(solution)/shard_map/all_to_all | solution.py:785
  207.2 8.2 %finish.1 = bf16[32,64,256]{2,1,0:T(8,128)(2,1)} custom-call(bf16[2048,1024]{1,0:T(8,128)(2,1)} %get-tuple-element.94.dpre_ref, bf16[32,64,256]{2,1,0:T(8,128)(2,1)} %x_ref.7, bf16[32,64,256]{2,1,0:T(8,128)(2,1)} %cot_ref.5, bf16[64,32,256]{2,1,0:T(8,128)(2,1)} %copy-done, bf16[256,1024]{1,0:T(8,128)(2,1)} %we_ref.5), custom_call_target="tpu_custom_call" | custom-call | flops 1073741824 | bytes 9437184 | tf_op jit(solution)/shard_map/finish/pallas_call | solution.py:596
  215.4 7.1 %all-to-all-done.3.terms_ref = bf16[64,56,128]{2,1,0:T(8,128)(2,1)S(1)} async-done(((bf16[64,56,128]{2,1,0:T(8,128)(2,1)}), bf16[64,56,128]{2,1,0:T(8,128)(2,1)S(1)}, u32[]{:S(2)}, u32[]{:S(2)}) %all-to-all-start.3) | async-done | bytes 917536 | tf_op jit(solution)/shard_map/all_to_all | solution.py:785
  222.7 19.0 %all_to_all.25.own_ref = bf16[64,56,128]{2,1,0:T(8,128)(2,1)S(1)} all-to-all(bf16[64,56,128]{2,1,0:T(8,128)(2,1)S(1)} %fold.1), channel_id=1, replica_groups={{0,2,4,6,8,10,12,14,16,18,20,22,24,26,28,30,32,34,36,38,40,42,44,46,48,..., dimensions={0} | all-to-all | bytes 1835008 | tf_op jit(solution)/shard_map/all_to_all | solution.py:785
  241.8 4.2 %collective-permute-start.11 = (bf16[64,56,128]{2,1,0:T(8,128)(2,1)S(1)}, bf16[64,56,128]{2,1,0:T(8,128)(2,1)S(1)}, u32[]{:S(2)}, u32[]{:S(2)}) collective-permute-start(bf16[64,56,128]{2,1,0:T(8,128)(2,1)S(1)} %all_to_all.25.own_ref), channel_id=1, source_target_pairs={{0,1},{1,0},{2,3},{3,2},{4,5},{5,4},{6,7},{7,6},{8,9},{9,8},{10,11... | collective-permute-start | bytes 2752520 | tf_op jit(solution)/shard_map/ppermute | solution.py:801
  245.9 2.1 collective-permute-done.11.other_ref
  248.0 2.0 unfold.1
  (69 shorter events, 1.2 us)
Async XLA Ops:
  0.6 16.2 %copy-start.10 = (bf16[32,64,256]{2,1,0:T(8,128)(2,1)S(1)}, bf16[32,64,256]{2,1,0:T(8,128)(2,1)}, u32[]{:S(2)}) copy-start(bf16[32,64,256]{2,1,0:T(8,128)(2,1)} %cot_ref.5) | copy-start | bytes 3145732
  1.6 15.2 %collective-permute-start = (bf16[128,256]{1,0:T(8,128)(2,1)S(1)}, bf16[128,256]{1,0:T(8,128)(2,1)S(1)}, u32[]{:S(2)}, u32[]{:S(2)}) collective-permute-start(bf16[128,256]{1,0:T(8,128)(2,1)S(1)} %bitcast.43), channel_id=1, source_target_pairs={{0,16},{16,32},{32,48},{48,64},{64,80},{80,96},{96,112},{1,17},{17... | collective-permute-start | bytes 196616 | tf_op jit(solution)/shard_map/ppermute | solution.py:746
  5.7 11.1 %collective-permute-start.1 = (bf16[128,256]{1,0:T(8,128)(2,1)S(1)}, bf16[128,256]{1,0:T(8,128)(2,1)S(1)}, u32[]{:S(2)}, u32[]{:S(2)}) collective-permute-start(bf16[128,256]{1,0:T(8,128)(2,1)S(1)} %bitcast.42), channel_id=1, source_target_pairs={{16,0},{32,16},{48,32},{64,48},{80,64},{96,80},{112,96},{17,1},{33... | collective-permute-start | bytes 196616 | tf_op jit(solution)/shard_map/ppermute | solution.py:746
  7.0 26.9 %copy-start.17 = (f32[3,3,1024]{2,1,0:T(4,128)S(1)}, f32[3,3,1024]{2,1,0:T(4,128)}, u32[]{:S(2)}) copy-start(f32[3,3,1024]{2,1,0:T(4,128)} %param.16) | copy-start | bytes 110596
  16.8 24.3 %copy-start.13 = (bf16[128,256]{1,0:T(8,128)(2,1)}, bf16[128,256]{1,0:T(8,128)(2,1)S(1)}, u32[]{:S(2)}) copy-start(bf16[128,256]{1,0:T(8,128)(2,1)S(1)} %collective-permute-done) | copy-start | bytes 196612
  16.8 24.3 %copy-start.14 = (bf16[128,256]{1,0:T(8,128)(2,1)}, bf16[128,256]{1,0:T(8,128)(2,1)S(1)}, u32[]{:S(2)}) copy-start(bf16[128,256]{1,0:T(8,128)(2,1)S(1)} %collective-permute-done.1) | copy-start | bytes 196612
  17.9 43.6 %all-to-all-start.1 = ((bf16[64,32,256]{2,1,0:T(8,128)(2,1)}), bf16[64,32,256]{2,1,0:T(8,128)(2,1)S(1)}, u32[]{:S(2)}, u32[]{:S(2)}) async-start(bf16[64,32,256]{2,1,0:T(8,128)(2,1)} %bitcast.7), calls=%async_computation.1 | async-start | bytes 2097152 | tf_op jit(solution)/shard_map/all_to_all | solution.py:785
  31.2 9.9 %copy-start.15 = (bf16[2,40,256]{2,1,0:T(8,128)(2,1)}, bf16[2,40,256]{2,1,0:T(8,128)(2,1)S(1)}, u32[]{:S(2)}) copy-start(bf16[2,40,256]{2,1,0:T(8,128)(2,1)S(1)} %get-tuple-element.117.own_west_ref) | copy-start | bytes 122884
  31.2 9.9 %copy-start.16 = (bf16[2,40,256]{2,1,0:T(8,128)(2,1)}, bf16[2,40,256]{2,1,0:T(8,128)(2,1)S(1)}, u32[]{:S(2)}) copy-start(bf16[2,40,256]{2,1,0:T(8,128)(2,1)S(1)} %get-tuple-element.118.own_east_ref) | copy-start | bytes 122884
  31.2 5.9 %collective-permute-start.2 = (bf16[2,40,256]{2,1,0:T(8,128)(2,1)S(1)}, bf16[2,40,256]{2,1,0:T(8,128)(2,1)S(1)}, u32[]{:S(2)}, u32[]{:S(2)}) collective-permute-start(bf16[2,40,256]{2,1,0:T(8,128)(2,1)S(1)} %get-tuple-element.118.own_east_ref), channel_id=1, source_target_pairs={{0,1},{1,2},{2,3},{3,4},{4,5},{5,6},{6,7},{7,8},{8,9},{9,10},{10,1... | collective-permute-start | bytes 122888 | tf_op jit(solution)/shard_map/ppermute | solution.py:776
  33.9 6.4 %collective-permute-start.3 = (bf16[2,40,256]{2,1,0:T(8,128)(2,1)S(1)}, bf16[2,40,256]{2,1,0:T(8,128)(2,1)S(1)}, u32[]{:S(2)}, u32[]{:S(2)}) collective-permute-start(bf16[2,40,256]{2,1,0:T(8,128)(2,1)S(1)} %get-tuple-element.117.own_west_ref), channel_id=1, source_target_pairs={{1,0},{2,1},{3,2},{4,3},{5,4},{6,5},{7,6},{8,7},{9,8},{10,9},{11,1... | collective-permute-start | bytes 122888 | tf_op jit(solution)/shard_map/ppermute | solution.py:777
  34.0 7.1 %copy-start.12 = (f32[9,1024]{1,0:T(8,128)}, f32[9,1024]{1,0:T(8,128)S(1)}, u32[]{:S(2)}) copy-start(f32[9,1024]{1,0:T(8,128)S(1)} %reshape.67.dk_ref) | copy-start | bytes 110596
  37.0 4.1 %copy-start.18 = (bf16[2,40,256]{2,1,0:T(8,128)(2,1)}, bf16[2,40,256]{2,1,0:T(8,128)(2,1)S(1)}, u32[]{:S(2)}) copy-start(bf16[2,40,256]{2,1,0:T(8,128)(2,1)S(1)} %collective-permute-done.2.west_ref) | copy-start | bytes 122884
  40.3 0.8 copy-start.19
  41.1 33.3 %copy-start.20 = (f32[4,15,15]{2,0,1:T(4,128)S(1)}, f32[4,15,15]{2,0,1:T(4,128)}, u32[]{:S(2)}) copy-start(f32[4,15,15]{2,0,1:T(4,128)} %param.20) | copy-start | bytes 10804
  41.1 33.4 %copy-start.21 = (s32[64,64]{0,1:T(8,128)S(1)}, s32[64,64]{0,1:T(8,128)}, u32[]{:S(2)}) copy-start(s32[64,64]{0,1:T(8,128)} %constant.21.clone) | copy-start | bytes 49156
  41.1 37.0 %copy-start.7 = (bf16[256,256]{1,0:T(8,128)(2,1)S(1)}, bf16[256,256]{1,0:T(8,128)(2,1)}, u32[]{:S(2)}) copy-start(bf16[256,256]{1,0:T(8,128)(2,1)} %wout_ref.1) | copy-start | bytes 393220
  41.2 37.0 %copy-start.8 = (bf16[256,256]{1,0:T(8,128)(2,1)S(1)}, bf16[256,256]{1,0:T(8,128)(2,1)}, u32[]{:S(2)}) copy-start(bf16[256,256]{1,0:T(8,128)(2,1)} %constant.22.clone.swap_ref) | copy-start | bytes 393220
  61.5 29.6 %all-to-all-start = ((bf16[64,32,256]{2,1,0:T(8,128)(2,1)}), bf16[64,32,256]{2,1,0:T(8,128)(2,1)S(1)}, u32[]{:S(2)}, u32[]{:S(2)}) async-start(bf16[64,32,256]{2,1,0:T(8,128)(2,1)} %get-tuple-element.61), calls=%async_computation | async-start | bytes 2097152 | tf_op jit(solution)/shard_map/all_to_all | solution.py:785
  78.9 1.0 copy-start.3
  79.9 1.0 copy-start.9
  91.0 1.0 copy-start.11
  114.0 21.0 %all-to-all-start.2 = ((bf16[64,32,256]{2,1,0:T(8,128)(2,1)}), bf16[64,32,256]{2,1,0:T(8,128)(2,1)S(1)}, u32[]{:S(2)}, u32[]{:S(2)}) async-start(bf16[64,32,256]{2,1,0:T(8,128)(2,1)} %get-tuple-element.67), calls=%async_computation.2 | async-start | bytes 2097152 | tf_op jit(solution)/shard_map/all_to_all | solution.py:785
  120.8 14.2 %copy-start.5 = (bf16[32,512]{1,0:T(8,128)(2,1)S(1)}, bf16[32,512]{1,0:T(8,128)(2,1)}, u32[]{:S(2)}) copy-start(bf16[32,512]{1,0:T(8,128)(2,1)} %constant.23.clone.first_ref) | copy-start | bytes 98308
  120.8 14.2 %copy-start.6 = (bf16[32,512]{1,0:T(8,128)(2,1)S(1)}, bf16[32,512]{1,0:T(8,128)(2,1)}, u32[]{:S(2)}) copy-start(bf16[32,512]{1,0:T(8,128)(2,1)} %constant.24.clone.last_ref) | copy-start | bytes 98308
  135.0 1.8 copy-start
  136.8 12.5 %collective-permute-start.4 = (bf16[64,256]{1,0:T(8,128)(2,1)S(1)}, bf16[64,256]{1,0:T(8,128)(2,1)S(1)}, u32[]{:S(2)}, u32[]{:S(2)}) collective-permute-start(bf16[64,256]{1,0:T(8,128)(2,1)S(1)} %get-tuple-element.74), channel_id=1, source_target_pairs={{0,16},{16,32},{32,48},{48,64},{64,80},{80,96},{96,112},{1,17},{17... | collective-permute-start | bytes 98312 | tf_op jit(solution)/shard_map/ppermute | solution.py:746
  139.4 9.8 %collective-permute-start.5 = (bf16[64,256]{1,0:T(8,128)(2,1)S(1)}, bf16[64,256]{1,0:T(8,128)(2,1)S(1)}, u32[]{:S(2)}, u32[]{:S(2)}) collective-permute-start(bf16[64,256]{1,0:T(8,128)(2,1)S(1)} %get-tuple-element.75), channel_id=1, source_target_pairs={{16,0},{32,16},{48,32},{64,48},{80,64},{96,80},{112,96},{17,1},{33... | collective-permute-start | bytes 98312 | tf_op jit(solution)/shard_map/ppermute | solution.py:746
  149.3 11.4 %collective-permute-start.7 = (bf16[40,256]{1,0:T(8,128)(2,1)S(1)}, bf16[40,256]{1,0:T(8,128)(2,1)S(1)}, u32[]{:S(2)}, u32[]{:S(2)}) collective-permute-start(bf16[40,256]{1,0:T(8,128)(2,1)S(1)} %get-tuple-element.115), channel_id=1, source_target_pairs={{0,1},{1,2},{2,3},{3,4},{4,5},{5,6},{6,7},{7,8},{8,9},{9,10},{10,1... | collective-permute-start | bytes 61448 | tf_op jit(solution)/shard_map/ppermute | solution.py:752
  153.3 7.5 %collective-permute-start.8 = (bf16[40,256]{1,0:T(8,128)(2,1)S(1)}, bf16[40,256]{1,0:T(8,128)(2,1)S(1)}, u32[]{:S(2)}, u32[]{:S(2)}) collective-permute-start(bf16[40,256]{1,0:T(8,128)(2,1)S(1)} %get-tuple-element.116), channel_id=1, source_target_pairs={{1,0},{2,1},{3,2},{4,3},{5,4},{6,5},{7,6},{8,7},{9,8},{10,9},{11,1... | collective-permute-start | bytes 61448 | tf_op jit(solution)/shard_map/ppermute | solution.py:755
  161.4 32.5 %copy-start.1 = (bf16[128,16,128]{2,1,0:T(8,128)(2,1)S(1)}, bf16[128,16,128]{2,1,0:T(8,128)(2,1)}, u32[]{:S(2)}) copy-start(bf16[128,16,128]{2,1,0:T(8,128)(2,1)} %attention_sums.1.refs_0_) | copy-start | bytes 1572868
  161.4 32.6 %copy-start.2 = (bf16[128,16,128]{2,1,0:T(8,128)(2,1)S(1)}, bf16[128,16,128]{2,1,0:T(8,128)(2,1)}, u32[]{:S(2)}) copy-start(bf16[128,16,128]{2,1,0:T(8,128)(2,1)} %project_sum.1.refs_2_) | copy-start | bytes 1572868
  188.8 8.6 %collective-permute-start.10 = (bf16[128,24,128]{2,1,0:T(8,128)(2,1)}, bf16[128,24,128]{2,1,0:T(8,128)(2,1)S(1)}, u32[]{:S(2)}, u32[]{:S(2)}) collective-permute-start(bf16[128,24,128]{2,1,0:T(8,128)(2,1)} %get-tuple-element.91.refs_4_), channel_id=1, source_target_pairs={{0,1},{1,0},{2,3},{3,2},{4,5},{5,4},{6,7},{7,6},{8,9},{9,8},{10,11... | collective-permute-start | bytes 2359304 | tf_op jit(solution)/shard_map/ppermute | solution.py:801
  193.9 2.7 %collective-permute-start.6 = (bf16[128,16,128]{2,1,0:T(8,128)(2,1)S(1)}, bf16[128,16,128]{2,1,0:T(8,128)(2,1)S(1)}, u32[]{:S(2)}, u32[]{:S(2)}) collective-permute-start(bf16[128,16,128]{2,1,0:T(8,128)(2,1)S(1)} %copy-done.1), channel_id=1, source_target_pairs={{0,1},{1,0},{2,3},{3,2},{4,5},{5,4},{6,7},{7,6},{8,9},{9,8},{10,11... | collective-permute-start | bytes 1572872 | tf_op jit(solution)/shard_map/ppermute | solution.py:801
  194.0 3.3 %collective-permute-start.9 = (bf16[128,16,128]{2,1,0:T(8,128)(2,1)S(1)}, bf16[128,16,128]{2,1,0:T(8,128)(2,1)S(1)}, u32[]{:S(2)}, u32[]{:S(2)}) collective-permute-start(bf16[128,16,128]{2,1,0:T(8,128)(2,1)S(1)} %copy-done.2), channel_id=1, source_target_pairs={{0,1},{1,0},{2,3},{3,2},{4,5},{5,4},{6,7},{7,6},{8,9},{9,8},{10,11... | collective-permute-start | bytes 1572872 | tf_op jit(solution)/shard_map/ppermute | solution.py:801
  197.3 1.1 copy-start.4
  199.6 22.9 %all-to-all-start.3 = ((bf16[64,56,128]{2,1,0:T(8,128)(2,1)}), bf16[64,56,128]{2,1,0:T(8,128)(2,1)S(1)}, u32[]{:S(2)}, u32[]{:S(2)}) async-start(bf16[64,56,128]{2,1,0:T(8,128)(2,1)} %join.1), calls=%async_computation.3 | async-start | bytes 1835008 | tf_op jit(solution)/shard_map/all_to_all | solution.py:785
  241.8 6.3 %collective-permute-start.11 = (bf16[64,56,128]{2,1,0:T(8,128)(2,1)S(1)}, bf16[64,56,128]{2,1,0:T(8,128)(2,1)S(1)}, u32[]{:S(2)}, u32[]{:S(2)}) collective-permute-start(bf16[64,56,128]{2,1,0:T(8,128)(2,1)S(1)} %all_to_all.25.own_ref), channel_id=1, source_target_pairs={{0,1},{1,0},{2,3},{3,2},{4,5},{5,4},{6,7},{7,6},{8,9},{9,8},{10,11... | collective-permute-start | bytes 2752520 | tf_op jit(solution)/shard_map/ppermute | solution.py:801

commit v5 on v4

--- a/solution.py
+++ b/solution.py
@@ -22,7 +22,6 @@
 EDGE = 40
 HALO = 2 * COLS + 2 * EDGE
 LONG = 72
-PACKED = (4, 16, LANES)
 JOINED = (64, 56, 128)
 
 
@@ -120,7 +119,7 @@
 def mix_body(
     cur_ref, before_ref, after_ref,
     above_ref, below_ref, first_ref, last_ref, west_ref, east_ref, own_west_ref, own_east_ref,
-    we_ref, dk_ref, dkb_ref, wp_ref, x_ref,
+    we_ref, dk_ref, wp_ref, x_ref,
     section_ref, mixed_ref, slope_ref, ring_slope_ref,
     top_ref, bottom_ref, left_ref, right_ref,
 ):
@@ -140,14 +139,13 @@
         rows = [jnp.where(first, top_ref[:, span], before_ref[0, :, span])]
         rows += [cur_ref[r, :, span] for r in range(BLK)]
         rows += [jnp.where(last, bottom_ref[:, span], after_ref[0, :, span])]
-        rows = [row.reshape(PACKED) for row in rows]
-        kern = [dkb_ref[n, :, span][None] for n in range(9)]
+        rows = [row.astype(F32) for row in rows]
+        kern = [dk_ref[n, span][None] for n in range(9)]
         for r in range(BLK):
             parts = [
                 kern[b] * rows[r] + kern[3 + b] * rows[r + 1] + kern[6 + b] * rows[r + 2]
                 for b in range(3)
             ]
-            parts = [part.reshape(COLS, LANES).astype(F32) for part in parts]
             left = left_ref[step, r : r + 1, span]
             right = right_ref[step, r : r + 1, span]
             pre = (
@@ -218,7 +216,7 @@
             slope_ref[out + ROWS + 2 : out + EDGE, span] = jnp.zeros((EDGE - ROWS - 2, 256), F32)
 
 
-def mix(hidden, halo, we, dk, dkb, wp, x):
+def mix(hidden, halo, we, dk, wp, x):
     above, below, west, east, own_west, own_east = halo
     wide = jax.ShapeDtypeStruct((ROWS, COLS, EXP), BF16)
     return pl.pallas_call(
@@ -230,8 +228,7 @@
             pl.BlockSpec((1, COLS, CHAN), lambda i: (0, 0, 0)),
             pl.BlockSpec((1, COLS, CHAN), lambda i: (ROWS - 1, 0, 0)),
             whole((2, EDGE, CHAN)), whole((2, EDGE, CHAN)), whole((2, EDGE, CHAN)), whole((2, EDGE, CHAN)),
-            whole((CHAN, EXP)), whole((9, EXP)), whole((9, 16, EXP)), whole((EXP, CHAN)),
-            band((BLK, COLS, CHAN)),
+            whole((CHAN, EXP)), whole((9, EXP)), whole((EXP, CHAN)), band((BLK, COLS, CHAN)),
         ],
         out_specs=[
             band((8, 32, CHAN)), band((BLK, COLS, EXP)), band((BLK, COLS, EXP)), whole((HALO, EXP)),
@@ -247,7 +244,7 @@
         name="mix",
     )(
         hidden, hidden, hidden, above, below, x, x, west, east, own_west, own_east,
-        we, dk, dkb, wp, x,
+        we, dk, wp, x,
     )
 
 
@@ -317,28 +314,44 @@
     norm_ref[...] = normed_b
     projected = dot(normed_b, wqkv_ref[...]).astype(BF16)
     low = lax.broadcasted_iota(jnp.int32, (64, 128), 1) < 64
-    head_of = lax.broadcasted_iota(jnp.int32, (64, CHAN), 1) // 64
-    masks = [(head_of == h).astype(F32).astype(BF16) for h in range(4)]
-    for g in range(4):
-        part = slice(g * 64, g * 64 + 64)
-        query = projected[part, :CHAN] * 0.125
-        key = projected[part, CHAN : 2 * CHAN]
-        value = projected[part, 2 * CHAN :]
-        da = da_ref[g]
-        query_h = jnp.concatenate([query * m for m in masks], axis=0)
-        da_h = jnp.concatenate([da * m for m in masks], axis=0)
-        scores = dot_nt(key, query_h) + bias_ref[...]
-        scores = jnp.exp(scores - jnp.max(scores, axis=0, keepdims=True))
-        probs = scores * (1.0 / jnp.sum(scores, axis=0, keepdims=True))
-        probs_b = probs.astype(BF16)
-        d_probs = dot_nt(value, da_h)
-        d_scores = probs * (d_probs - jnp.sum(probs * d_probs, axis=0, keepdims=True))
-        bias_sum_ref[...] += d_scores
-        d_scores_b = d_scores.astype(BF16)
-        att_ref[part] = diagonal(dot_tn(probs_b, value), low).astype(BF16)
-        proj_ref[part, :CHAN] = (diagonal(dot_tn(d_scores_b, key), low) * 0.125).astype(BF16)
-        proj_ref[part, CHAN : 2 * CHAN] = dot(d_scores_b, query_h).astype(BF16)
-        proj_ref[part, 2 * CHAN :] = dot(probs_b, da_h).astype(BF16)
+    keep = [low.astype(F32).astype(BF16), (1.0 - low.astype(F32)).astype(BF16)]
+    none = jnp.zeros((128, 128), BF16)
+
+    def by_head(rows):
+        blocks = []
+        for half in range(2):
+            lanes = rows[:, half * 128 : half * 128 + 128]
+            pair = jnp.concatenate([lanes * keep[0], lanes * keep[1]], axis=0)
+            blocks.append(jnp.concatenate([pair, none] if half == 0 else [none, pair], axis=1))
+        return jnp.concatenate(blocks, axis=0)
+
+    four = range(4)
+    part = [slice(g * 64, g * 64 + 64) for g in four]
+    query = (projected[:, :CHAN].astype(F32) * 0.125).astype(BF16)
+    key = [projected[part[g], CHAN : 2 * CHAN] for g in four]
+    value = [projected[part[g], 2 * CHAN :] for g in four]
+    query_h = [by_head(query[part[g]]) for g in four]
+    da_h = [by_head(da_ref[g]) for g in four]
+    scores = [dot_nt(key[g], query_h[g]) + bias_ref[...] for g in four]
+    d_probs = [dot_nt(value[g], da_h[g]) for g in four]
+    tops = [jnp.max(scores[g], axis=0, keepdims=True) for g in four]
+    scores = [jnp.exp(scores[g] - tops[g]) for g in four]
+    scales = [1.0 / jnp.sum(scores[g], axis=0, keepdims=True) for g in four]
+    probs = [scores[g] * scales[g] for g in four]
+    probs_b = [probs[g].astype(BF16) for g in four]
+    crosses = [jnp.sum(probs[g] * d_probs[g], axis=0, keepdims=True) for g in four]
+    d_scores = [probs[g] * (d_probs[g] - crosses[g]) for g in four]
+    bias_sum_ref[...] += (d_scores[0] + d_scores[1]) + (d_scores[2] + d_scores[3])
+    d_scores_b = [d_scores[g].astype(BF16) for g in four]
+    attended = [dot_tn(probs_b[g], value[g]) for g in four]
+    d_query = [dot_tn(d_scores_b[g], key[g]) for g in four]
+    d_key = [dot(d_scores_b[g], query_h[g]) for g in four]
+    d_value = [dot(probs_b[g], da_h[g]) for g in four]
+    for g in four:
+        att_ref[part[g]] = diagonal(attended[g], low).astype(BF16)
+        proj_ref[part[g], :CHAN] = (diagonal(d_query[g], low) * 0.125).astype(BF16)
+        proj_ref[part[g], CHAN : 2 * CHAN] = d_key[g].astype(BF16)
+        proj_ref[part[g], 2 * CHAN :] = d_value[g].astype(BF16)
     d_normed = dot_nt(proj_ref[...], wqkv_ref[...])
     d_tokens = layer_norm_back(normed, inv_std, d_normed).astype(BF16)
     ds_ref[groups] = d_tokens.reshape(4, 64, CHAN)
@@ -509,37 +522,32 @@
         for r in range(BLK + 2):
             left = left_ref[step, r : r + 1, span]
             right = right_ref[step, r : r + 1, span]
-            shift_ref[0, r, :, span] = jnp.concatenate([rows[r][1:], right], axis=0).astype(BF16)
-            shift_ref[1, r, :, span] = rows[r].astype(BF16)
-            shift_ref[2, r, :, span] = jnp.concatenate([left, rows[r][:-1]], axis=0).astype(BF16)
+            shift_ref[0, r, :, span] = jnp.concatenate([rows[r][1:], right], axis=0)
+            shift_ref[1, r, :, span] = rows[r]
+            shift_ref[2, r, :, span] = jnp.concatenate([left, rows[r][:-1]], axis=0)
         kern = [dkb_ref[n, :, span] for n in range(9)]
         sums = [acc_ref[n, :, span] for n in range(9)]
-        held = None
         for j in range(0, COLS, 16):
-            cells = slice(j, j + 16)
-            pieces = [[shift_ref[b, r, cells, span] for b in range(3)] for r in range(BLK + 2)]
-            hid = [hid_ref[r, cells, span] for r in range(BLK)]
-            totals = [None] * BLK
-            parts = []
-            for a in range(3):
-                for b in range(3):
-                    n = 3 * a + b
-                    terms = []
-                    for r in range(BLK):
-                        piece = pieces[r + 2 - a][b]
-                        tap = kern[n] * piece
-                        totals[r] = tap if n == 0 else totals[r] + tap
-                        terms.append(hid[r] * piece)
-                    parts.append((terms[0] + terms[1]) + (terms[2] + terms[3]))
-            if held is None:
-                held = parts
-            else:
-                for n in range(9):
-                    part = (held[n] + parts[n]).astype(F32)
-                    sums[n] = sums[n] + (part[:8] + part[8:])
-                held = None
+            hid = [hid_ref[r, j : j + 16, span].astype(F32) for r in range(BLK)]
+            halves = []
+            for low in (0, 8):
+                cells = slice(j + low, j + low + 8)
+                pieces = [[shift_ref[b, r, cells, span] for b in range(3)] for r in range(BLK + 2)]
+                totals = [None] * BLK
+                for r in range(BLK):
+                    cell = hid[r][low : low + 8]
+                    for a in range(3):
+                        for b in range(3):
+                            n = 3 * a + b
+                            piece = pieces[r + 2 - a][b]
+                            tap = kern[n] * piece
+                            totals[r] = tap if n == 0 else totals[r] + tap
+                            sums[n] = sums[n] + cell * piece
+                halves.append(totals)
             for r in range(BLK):
-                dpre_ref[r * COLS + j : r * COLS + j + 16, span] = totals[r] * slope_ref[r, cells, span]
+                total = jnp.concatenate([halves[0][r], halves[1][r]], axis=0)
+                d_pre = total * slope_ref[r, j : j + 16, span].astype(F32)
+                dpre_ref[r * COLS + j : r * COLS + j + 16, span] = d_pre.astype(BF16)
         for n in range(9):
             acc_ref[n, :, span] = sums[n]
     normed, _ = layer_norm(x_ref[...].reshape(TOK, CHAN).astype(F32))
@@ -566,7 +574,7 @@
         grid=(STEPS,),
         in_specs=[
             cells, ROW_BEFORE, ROW_AFTER, whole((HALO, CHAN)), whole((HALO, EXP)),
-            whole((EXP, CHAN)), cells, cells, band((BLK, COLS, CHAN)), whole((9, 16, EXP)),
+            whole((EXP, CHAN)), cells, cells, band((BLK, COLS, CHAN)), whole((9, 8, EXP)),
             whole((128, 8, 128)),
         ],
         out_specs=[band((TOK, EXP)), whole(tiles)],
@@ -577,7 +585,7 @@
         scratch_shapes=[pltpu.VMEM((COLS, EXP), F32)] * 2
         + [pltpu.VMEM((STEPS, 8, EXP), F32)] * 2
         + [pltpu.VMEM((9, 8, EXP), F32), pltpu.VMEM((CHAN, EXP), F32), pltpu.VMEM((9, EXP), F32)]
-        + [pltpu.VMEM((3, BLK + 2, COLS, EXP), BF16)],
+        + [pltpu.VMEM((3, BLK + 2, COLS, EXP), F32)],
         compiler_params=params(58),
         cost_estimate=pl.CostEstimate(
             flops=2 * ROWS * COLS * CHAN * EXP, bytes_accessed=20 * MIB, transcendentals=0
@@ -819,18 +827,18 @@
     ).reshape(64, 256)
     dk = depth_kernel.reshape(9, EXP)
 
-    dkb = jnp.broadcast_to(dk[:, None], (9, 16, EXP)).astype(BF16)
+    dkb = jnp.broadcast_to(dk[:, None], (9, 8, EXP))
     core = lax.axis_index("lon").astype(jnp.int32).reshape(1) & 1
     barrier = lax.optimization_barrier
 
     above, below = wide_rows(field_in)
     hidden, act_slope = expand(field_in, expand_weight)
-    above, below, hidden, late_cot = barrier((above, below, hidden, cotangent))
     field_halo = (above, below, *wide_columns(field_in, above, below))
+    field_halo, late_cot = barrier((field_halo, cotangent))
     hidden, cot_pieces = barrier((hidden, to_pieces(late_cot)))
     cot_groups = exchange(cot_pieces)
     section, mixed, mixed_slope, ring_slope = mix(
-        hidden, field_halo, expand_weight, dk, dkb, project_weight, field_in
+        hidden, field_halo, expand_weight, dk, project_weight, field_in
     )
     groups = exchange(section)
     cot_swapped, d_att = prepare(cot_groups, out_weight, 32)

time: 251 us -> 233 us (0.928)
  Pallas kernels: 115 us -> 102 us
  waiting for transfers between devices: 35.2 us -> 26.7 us
    pallas_call x1, Pallas kernels: 21.9 us -> 16 us  [attention(): pl.pallas_call(attention_body, grid=(n_groups // 4,), in_specs=[whole(sha...]
    pallas_call x1, Pallas kernels: 27.3 us -> 21.9 us  [expand_back(): pl.pallas_call(expand_back_body, grid=(STEPS,), in_specs=[cells, ROW_BEFO...]
    ppermute x1, waiting for transfers between devices: 3.28 us -> 0.01 us  [wide_columns(): from_east = lax.ppermute(own_west, 'lon', west)]
    ppermute x1, waiting for transfers between devices: 3.06 us -> 0.01 us  [wide_columns(): from_west = lax.ppermute(own_east, 'lon', east)]
  transfers between devices with their start and end apart: 16 -> 16, of which waited for: 8 -> 7; matrix products, arithmetic and copies ran while one was open for 4% -> 4% of each run, Pallas kernels for 24% -> 26%
where the time goes in v5:
time: 233 us; the launch traced here: 231 us
  Pallas kernels  102 us (44%)
  starting transfers between devices  65.6 us (28%)
  waiting for transfers between devices  26.7 us (11%)
  blocking collectives  19 us (8%)
  local copies, waits for them, and re-layouts  11.6 us (5%)
  matrix products  4.24 us (2%)
    all_to_all x4, starting transfers between devices, exchange(): lax.all_to_all(pieces, ('lat', 'lon'), split_axis=0, concat_axis=0, axis_...  37.5 us
    pallas_call x1, Pallas kernels, expand_back(): pl.pallas_call(expand_back_body, grid=(STEPS,), in_specs=[cells, ROW_BEFO...  21.9 us
    all_to_all x4, waiting for transfers between devices, exchange(): lax.all_to_all(pieces, ('lat', 'lon'), split_axis=0, concat_axis=0, axis_...  21.5 us
    pallas_call x1, Pallas kernels, mix(): pl.pallas_call(mix_body, grid=(STEPS,), in_specs=[band((BLK, COLS, EXP)),...  19.4 us
    all_to_all x1, blocking collectives, exchange(): lax.all_to_all(pieces, ('lat', 'lon'), split_axis=0, concat_axis=0, axis_...  19 us
    pallas_call x1, Pallas kernels, attention(): pl.pallas_call(attention_body, grid=(n_groups // 4,), in_specs=[whole(sha...  16 us
    ppermute x4, starting transfers between devices, rows_of(): return (lax.ppermute(bottom, 'lat', south), lax.ppermute(top, 'lat', north))  10.3 us
    ppermute x4, starting transfers between devices, other_core(): return lax.ppermute(tiles, 'lon', swaps)  9.83 us
  transfers between devices with their start and end apart: 16, of which 7 were waited for; matrix products, arithmetic and copies ran while one was open for 4% of the time, Pallas kernels for 26%

profile of v5, /device:TPU:1, one launch (start us, length us, event | category | flops | bytes accessed | tf_op | source)
XLA Modules:
  0.0 231.2 jit_solution(16975458581191084150)
XLA Ops:
  0.6 1.0 fusion.7
  1.6 1.3 collective-permute-start.1
  2.9 4.7 %collective-permute-start = (bf16[128,256]{1,0:T(8,128)(2,1)S(1)}, bf16[128,256]{1,0:T(8,128)(2,1)S(1)}, u32[]{:S(2)}, u32[]{:S(2)}) collective-permute-start(bf16[128,256]{1,0:T(8,128)(2,1)S(1)} %bitcast.42), channel_id=1, source_target_pairs={{0,16},{16,32},{32,48},{48,64},{64,80},{80,96},{96,112},{1,17},{17... | collective-permute-start | bytes 196616 | tf_op jit(solution)/shard_map/ppermute | solution.py:754
  7.6 1.0 fusion.6
  9.0 3.6 %collective-permute-start.2 = (bf16[2,40,256]{2,1,0:T(8,128)(2,1)S(1)}, bf16[2,40,256]{2,1,0:T(8,128)(2,1)S(1)}, u32[]{:S(2)}, u32[]{:S(2)}) collective-permute-start(bf16[2,40,256]{2,1,0:T(8,128)(2,1)S(1)} %get-tuple-element.66.own_east_ref), channel_id=1, source_target_pairs={{0,1},{1,2},{2,3},{3,4},{4,5},{5,6},{6,7},{7,8},{8,9},{9,10},{10,1... | collective-permute-start | bytes 122888 | tf_op jit(solution)/shard_map/ppermute | solution.py:784
  12.6 9.7 %expand.1 = (bf16[32,64,1024]{2,1,0:T(8,128)(2,1)}, bf16[32,64,1024]{2,1,0:T(8,128)(2,1)}) custom-call(bf16[32,64,256]{2,1,0:T(8,128)(2,1)} %x_ref.7, bf16[256,1024]{1,0:T(8,128)(2,1)} %we_ref.5), custom_call_target="tpu_custom_call" | custom-call | flops 1073741824 | bytes 10485760 | tf_op jit(solution)/shard_map/expand/pallas_call | solution.py:105
  22.4 1.1 copy.33
  23.5 13.6 %all-to-all-start.1 = ((bf16[64,32,256]{2,1,0:T(8,128)(2,1)}), bf16[64,32,256]{2,1,0:T(8,128)(2,1)S(1)}, u32[]{:S(2)}, u32[]{:S(2)}) async-start(bf16[64,32,256]{2,1,0:T(8,128)(2,1)} %bitcast.13), calls=%async_computation.1 | async-start | bytes 2097152 | tf_op jit(solution)/shard_map/all_to_all | solution.py:793
  37.1 0.6 reshape.67.dk_ref
  37.8 19.4 %mix.1 = (bf16[64,32,256]{2,1,0:T(8,128)(2,1)}, bf16[32,64,1024]{2,1,0:T(8,128)(2,1)}, bf16[32,64,1024]{2,1,0:T(8,128)(2,1)}, f32[208,1024]{1,0:T(8,128)}) custom-call(bf16[32,64,1024]{2,1,0:T(8,128)(2,1)} %get-tuple-element.60.cur_ref.before_ref.after_ref.hid_ref, bf16[32,64,1024]{2,1,0:T(8,128)(2,1)} %get-tuple-element.60.cur_ref.before_ref.after_ref.hid_ref, ...), custom_call_target="tpu_custom_call" | custom-call | flops 1610612736 | bytes 18874368 | tf_op jit(solution)/shard_map/mix/pallas_call | solution.py:222
  57.2 9.8 %all-to-all-start = ((bf16[64,32,256]{2,1,0:T(8,128)(2,1)}), bf16[64,32,256]{2,1,0:T(8,128)(2,1)S(1)}, u32[]{:S(2)}, u32[]{:S(2)}) async-start(bf16[64,32,256]{2,1,0:T(8,128)(2,1)} %get-tuple-element.67), calls=%async_computation | async-start | bytes 2097152 | tf_op jit(solution)/shard_map/all_to_all | solution.py:793
  67.1 2.8 %fusion.4 = f32[64,4,64]{2,1,0:T(4,128)S(1)} fusion(f32[4,225,1]{1,0,2:T(4,128)S(1)} %reshape.75, s32[64,64]{0,1:T(8,128)S(1)} %copy-done.21), kind=kOutput, calls=%fused_computation.5 | convolution fusion | flops 45158400 | bytes 85520 | tf_op jit(solution)/shard_map/tsr,hr->sht/dot_general | solution.py:825
  69.9 0.8 reshape.69.bias_ref
  70.7 0.8 prepare.1
  71.5 1.0 copy-done.3
  72.5 1.0 copy-done.9
  73.5 8.7 %all-to-all-done.x_ref = bf16[64,32,256]{2,1,0:T(8,128)(2,1)S(1)} async-done(((bf16[64,32,256]{2,1,0:T(8,128)(2,1)}), bf16[64,32,256]{2,1,0:T(8,128)(2,1)S(1)}, u32[]{:S(2)}, u32[]{:S(2)}) %all-to-all-start) | async-done | bytes 1048608 | tf_op jit(solution)/shard_map/all_to_all | solution.py:793
  82.2 1.0 copy-done.11
  83.1 16.0 %attention.1 = (bf16[64,32,256]{2,1,0:T(8,128)(2,1)}, bf16[2048,256]{1,0:T(8,128)(2,1)}, bf16[2048,256]{1,0:T(8,128)(2,1)}, bf16[2048,768]{1,0:T(8,128)(2,1)}, f32[64,256]{1,0:T(8,128)}) custom-call(bf16[64,32,256]{2,1,0:T(8,128)(2,1)} %copy-done.11, bf16[32,64,256]{2,1,0:T(8,128)(2,1)} %copy-done.9, bf16[256,768]{1,0:T(8,128)(2,1)} %wqkv_ref.1, ...), custom_call_target="tpu_custom_call" | custom-call | flops 2684354560 | bytes 8388608 | tf_op jit(solution)/shard_map/attention/pallas_call | solution.py:372
  99.1 6.4 %all-to-all-start.2 = ((bf16[64,32,256]{2,1,0:T(8,128)(2,1)}), bf16[64,32,256]{2,1,0:T(8,128)(2,1)S(1)}, u32[]{:S(2)}, u32[]{:S(2)}) async-start(bf16[64,32,256]{2,1,0:T(8,128)(2,1)} %get-tuple-element.73), calls=%async_computation.2 | async-start | bytes 2097152 | tf_op jit(solution)/shard_map/all_to_all | solution.py:793
  105.6 0.9 reshape.71
  106.6 1.4 fusion.5
  108.1 0.8 pad.4.extra_ref
  109.0 5.3 %attention_sums.1.refs_0_ = bf16[128,16,128]{2,1,0:T(8,128)(2,1)} custom-call(bf16[2048,256]{1,0:T(8,128)(2,1)} %get-tuple-element.74.att_ref, bf16[2048,256]{1,0:T(8,128)(2,1)} %bitcast.36, bf16[2048,256]{1,0:T(8,128)(2,1)} %get-tuple-element.76.norm_ref, bf16[2048,768]{1,0:T(8,128)(2,1)} %get-tuple-element.77.proj_ref), custom_call_target="tpu_custom_call" | custom-call | flops 1073741824 | bytes 6291456 | tf_op jit(solution)/shard_map/attention_sums/pallas_call | solution.py:417
  114.3 5.6 %all-to-all-done.2.db_ref = bf16[64,32,256]{2,1,0:T(8,128)(2,1)S(1)} async-done(((bf16[64,32,256]{2,1,0:T(8,128)(2,1)}), bf16[64,32,256]{2,1,0:T(8,128)(2,1)S(1)}, u32[]{:S(2)}, u32[]{:S(2)}) %all-to-all-start.2) | async-done | bytes 1048608 | tf_op jit(solution)/shard_map/all_to_all | solution.py:793
  119.9 1.7 edges.1
  121.7 3.1 %collective-permute-start.4 = (bf16[64,256]{1,0:T(8,128)(2,1)S(1)}, bf16[64,256]{1,0:T(8,128)(2,1)S(1)}, u32[]{:S(2)}, u32[]{:S(2)}) collective-permute-start(bf16[64,256]{1,0:T(8,128)(2,1)S(1)} %get-tuple-element.80), channel_id=1, source_target_pairs={{0,16},{16,32},{32,48},{48,64},{64,80},{80,96},{96,112},{1,17},{17... | collective-permute-start | bytes 98312 | tf_op jit(solution)/shard_map/ppermute | solution.py:754
  124.7 1.3 collective-permute-start.5
  126.0 8.5 %project_back.1.cur_ref.before_ref.after_ref = bf16[32,64,1024]{2,1,0:T(8,128)(2,1)} custom-call(bf16[32,64,256]{2,1,0:T(8,128)(2,1)} %cot_ref.5, bf16[64,32,256]{2,1,0:T(8,128)(2,1)} %copy-done, bf16[32,64,1024]{2,1,0:T(8,128)(2,1)} %get-tuple-element.82.slope_ref, bf16[1024,256]{1,0:T(8,128)(2,1)} %wp_ref.5), custom_call_target="tpu_custom_call" | custom-call | flops 1073741824 | bytes 10485760 | tf_op jit(solution)/shard_map/project_back/pallas_call | solution.py:449
  134.7 4.4 %collective-permute-start.7 = (bf16[40,256]{1,0:T(8,128)(2,1)S(1)}, bf16[40,256]{1,0:T(8,128)(2,1)S(1)}, u32[]{:S(2)}, u32[]{:S(2)}) collective-permute-start(bf16[40,256]{1,0:T(8,128)(2,1)S(1)} %get-tuple-element.121), channel_id=1, source_target_pairs={{0,1},{1,2},{2,3},{3,4},{4,5},{5,6},{6,7},{7,8},{8,9},{9,10},{10,1... | collective-permute-start | bytes 61448 | tf_op jit(solution)/shard_map/ppermute | solution.py:760
  139.0 7.5 %project_sum.1.refs_2_ = bf16[128,16,128]{2,1,0:T(8,128)(2,1)} custom-call(bf16[32,64,256]{2,1,0:T(8,128)(2,1)} %cot_ref.5, bf16[64,32,256]{2,1,0:T(8,128)(2,1)} %copy-done, bf16[32,64,1024]{2,1,0:T(8,128)(2,1)} %get-tuple-element.89.mixed_ref), custom_call_target="tpu_custom_call" | custom-call | flops 1073741824 | bytes 8388608 | tf_op jit(solution)/shard_map/project_sum/pallas_call | solution.py:480
  146.5 0.7 pad_maximum_fusion.halo_ref
  147.2 0.7 broadcast_in_dim.15.dkb_ref
  147.9 21.9 %expand_back.1 = (bf16[2048,1024]{1,0:T(8,128)(2,1)}, bf16[128,24,128]{2,1,0:T(8,128)(2,1)}) custom-call(bf16[32,64,1024]{2,1,0:T(8,128)(2,1)} %project_back.1.cur_ref.before_ref.after_ref, bf16[32,64,1024]{2,1,0:T(8,128)(2,1)} %project_back.1.cur_ref.before_ref.after_ref, bf16[32,64,1024]{2,1,0:T(8,128)(2,1)} %project_back.1.cur_ref.before_ref.after_ref, ...), custom_call_target="tpu_custom_call" | custom-call | flops 1073741824 | bytes 20971520 | tf_op jit(solution)/shard_map/expand_back/pallas_call | solution.py:572
  169.9 5.2 %collective-permute-start.10 = (bf16[128,24,128]{2,1,0:T(8,128)(2,1)}, bf16[128,24,128]{2,1,0:T(8,128)(2,1)S(1)}, u32[]{:S(2)}, u32[]{:S(2)}) collective-permute-start(bf16[128,24,128]{2,1,0:T(8,128)(2,1)} %get-tuple-element.97.refs_4_), channel_id=1, source_target_pairs={{0,1},{1,0},{2,3},{3,2},{4,5},{5,4},{6,7},{7,6},{8,9},{9,8},{10,11... | collective-permute-start | bytes 2359304 | tf_op jit(solution)/shard_map/ppermute | solution.py:809
  175.0 0.3 collective-permute-start.6
  175.5 2.1 collective-permute-done.6.refs_1_
  177.7 0.7 collective-permute-done.9.refs_3_
  178.4 1.1 copy-done.4
  179.6 1.1 join.1
  180.7 7.7 %all-to-all-start.3 = ((bf16[64,56,128]{2,1,0:T(8,128)(2,1)}), bf16[64,56,128]{2,1,0:T(8,128)(2,1)S(1)}, u32[]{:S(2)}, u32[]{:S(2)}) async-start(bf16[64,56,128]{2,1,0:T(8,128)(2,1)} %join.1), calls=%async_computation.3 | async-start | bytes 1835008 | tf_op jit(solution)/shard_map/all_to_all | solution.py:793
  188.5 8.2 %finish.1 = bf16[32,64,256]{2,1,0:T(8,128)(2,1)} custom-call(bf16[2048,1024]{1,0:T(8,128)(2,1)} %get-tuple-element.100.dpre_ref, bf16[32,64,256]{2,1,0:T(8,128)(2,1)} %x_ref.7, bf16[32,64,256]{2,1,0:T(8,128)(2,1)} %cot_ref.5, bf16[64,32,256]{2,1,0:T(8,128)(2,1)} %copy-done, bf16[256,1024]{1,0:T(8,128)(2,1)} %we_ref.5), custom_call_target="tpu_custom_call" | custom-call | flops 1073741824 | bytes 9437184 | tf_op jit(solution)/shard_map/finish/pallas_call | solution.py:604
  196.6 7.1 %all-to-all-done.3.terms_ref = bf16[64,56,128]{2,1,0:T(8,128)(2,1)S(1)} async-done(((bf16[64,56,128]{2,1,0:T(8,128)(2,1)}), bf16[64,56,128]{2,1,0:T(8,128)(2,1)S(1)}, u32[]{:S(2)}, u32[]{:S(2)}) %all-to-all-start.3) | async-done | bytes 917536 | tf_op jit(solution)/shard_map/all_to_all | solution.py:793
  203.8 0.2 fold.1
  204.0 19.0 %all_to_all.25.own_ref = bf16[64,56,128]{2,1,0:T(8,128)(2,1)S(1)} all-to-all(bf16[64,56,128]{2,1,0:T(8,128)(2,1)S(1)} %fold.1), channel_id=1, replica_groups={{0,2,4,6,8,10,12,14,16,18,20,22,24,26,28,30,32,34,36,38,40,42,44,46,48,..., dimensions={0} | all-to-all | bytes 1835008 | tf_op jit(solution)/shard_map/all_to_all | solution.py:793
  223.0 4.2 %collective-permute-start.11 = (bf16[64,56,128]{2,1,0:T(8,128)(2,1)S(1)}, bf16[64,56,128]{2,1,0:T(8,128)(2,1)S(1)}, u32[]{:S(2)}, u32[]{:S(2)}) collective-permute-start(bf16[64,56,128]{2,1,0:T(8,128)(2,1)S(1)} %all_to_all.25.own_ref), channel_id=1, source_target_pairs={{0,1},{1,0},{2,3},{3,2},{4,5},{5,4},{6,7},{7,6},{8,9},{9,8},{10,11... | collective-permute-start | bytes 2752520 | tf_op jit(solution)/shard_map/ppermute | solution.py:809
  227.1 2.1 collective-permute-done.11.other_ref
  229.2 2.0 unfold.1
  (69 shorter events, 1.0 us)
Async XLA Ops:
  0.6 21.7 %copy-start.10 = (bf16[32,64,256]{2,1,0:T(8,128)(2,1)S(1)}, bf16[32,64,256]{2,1,0:T(8,128)(2,1)}, u32[]{:S(2)}) copy-start(bf16[32,64,256]{2,1,0:T(8,128)(2,1)} %cot_ref.5) | copy-start | bytes 3145732
  1.6 7.1 %collective-permute-start.1 = (bf16[128,256]{1,0:T(8,128)(2,1)S(1)}, bf16[128,256]{1,0:T(8,128)(2,1)S(1)}, u32[]{:S(2)}, u32[]{:S(2)}) collective-permute-start(bf16[128,256]{1,0:T(8,128)(2,1)S(1)} %bitcast.43), channel_id=1, source_target_pairs={{16,0},{32,16},{48,32},{64,48},{80,64},{96,80},{112,96},{17,1},{33... | collective-permute-start | bytes 196616 | tf_op jit(solution)/shard_map/ppermute | solution.py:754
  2.9 6.0 %collective-permute-start = (bf16[128,256]{1,0:T(8,128)(2,1)S(1)}, bf16[128,256]{1,0:T(8,128)(2,1)S(1)}, u32[]{:S(2)}, u32[]{:S(2)}) collective-permute-start(bf16[128,256]{1,0:T(8,128)(2,1)S(1)} %bitcast.42), channel_id=1, source_target_pairs={{0,16},{16,32},{32,48},{48,64},{64,80},{80,96},{96,112},{1,17},{17... | collective-permute-start | bytes 196616 | tf_op jit(solution)/shard_map/ppermute | solution.py:754
  8.7 14.7 %copy-start.15 = (bf16[128,256]{1,0:T(8,128)(2,1)}, bf16[128,256]{1,0:T(8,128)(2,1)S(1)}, u32[]{:S(2)}) copy-start(bf16[128,256]{1,0:T(8,128)(2,1)S(1)} %collective-permute-done.1) | copy-start | bytes 196612
  8.7 28.3 %copy-start.17 = (f32[3,3,1024]{2,1,0:T(4,128)S(1)}, f32[3,3,1024]{2,1,0:T(4,128)}, u32[]{:S(2)}) copy-start(f32[3,3,1024]{2,1,0:T(4,128)} %param.16) | copy-start | bytes 110596
  8.9 28.8 %copy-start.16 = (bf16[128,256]{1,0:T(8,128)(2,1)}, bf16[128,256]{1,0:T(8,128)(2,1)S(1)}, u32[]{:S(2)}) copy-start(bf16[128,256]{1,0:T(8,128)(2,1)S(1)} %collective-permute-done) | copy-start | bytes 196612
  9.0 28.7 %copy-start.13 = (bf16[2,40,256]{2,1,0:T(8,128)(2,1)}, bf16[2,40,256]{2,1,0:T(8,128)(2,1)S(1)}, u32[]{:S(2)}) copy-start(bf16[2,40,256]{2,1,0:T(8,128)(2,1)S(1)} %get-tuple-element.65.own_west_ref) | copy-start | bytes 122884
  9.0 28.7 %copy-start.14 = (bf16[2,40,256]{2,1,0:T(8,128)(2,1)}, bf16[2,40,256]{2,1,0:T(8,128)(2,1)S(1)}, u32[]{:S(2)}) copy-start(bf16[2,40,256]{2,1,0:T(8,128)(2,1)S(1)} %get-tuple-element.66.own_east_ref) | copy-start | bytes 122884
  9.0 13.3 %collective-permute-start.2 = (bf16[2,40,256]{2,1,0:T(8,128)(2,1)S(1)}, bf16[2,40,256]{2,1,0:T(8,128)(2,1)S(1)}, u32[]{:S(2)}, u32[]{:S(2)}) collective-permute-start(bf16[2,40,256]{2,1,0:T(8,128)(2,1)S(1)} %get-tuple-element.66.own_east_ref), channel_id=1, source_target_pairs={{0,1},{1,2},{2,3},{3,4},{4,5},{5,6},{6,7},{7,8},{8,9},{9,10},{10,1... | collective-permute-start | bytes 122888 | tf_op jit(solution)/shard_map/ppermute | solution.py:784
  12.6 9.7 %collective-permute-start.3 = (bf16[2,40,256]{2,1,0:T(8,128)(2,1)S(1)}, bf16[2,40,256]{2,1,0:T(8,128)(2,1)S(1)}, u32[]{:S(2)}, u32[]{:S(2)}) collective-permute-start(bf16[2,40,256]{2,1,0:T(8,128)(2,1)S(1)} %get-tuple-element.65.own_west_ref), channel_id=1, source_target_pairs={{1,0},{2,1},{3,2},{4,3},{5,4},{6,5},{7,6},{8,7},{9,8},{10,9},{11,1... | collective-permute-start | bytes 122888 | tf_op jit(solution)/shard_map/ppermute | solution.py:785
  22.3 15.4 %copy-start.18 = (bf16[2,40,256]{2,1,0:T(8,128)(2,1)}, bf16[2,40,256]{2,1,0:T(8,128)(2,1)S(1)}, u32[]{:S(2)}) copy-start(bf16[2,40,256]{2,1,0:T(8,128)(2,1)S(1)} %collective-permute-done.2.west_ref) | copy-start | bytes 122884
  22.3 15.4 %copy-start.19 = (bf16[2,40,256]{2,1,0:T(8,128)(2,1)}, bf16[2,40,256]{2,1,0:T(8,128)(2,1)S(1)}, u32[]{:S(2)}) copy-start(bf16[2,40,256]{2,1,0:T(8,128)(2,1)S(1)} %collective-permute-done.3.east_ref) | copy-start | bytes 122884
  23.5 33.7 %all-to-all-start.1 = ((bf16[64,32,256]{2,1,0:T(8,128)(2,1)}), bf16[64,32,256]{2,1,0:T(8,128)(2,1)S(1)}, u32[]{:S(2)}, u32[]{:S(2)}) async-start(bf16[64,32,256]{2,1,0:T(8,128)(2,1)} %bitcast.13), calls=%async_computation.1 | async-start | bytes 2097152 | tf_op jit(solution)/shard_map/all_to_all | solution.py:793
  37.7 29.3 %copy-start.20 = (f32[4,15,15]{2,0,1:T(4,128)S(1)}, f32[4,15,15]{2,0,1:T(4,128)}, u32[]{:S(2)}) copy-start(f32[4,15,15]{2,0,1:T(4,128)} %param.20) | copy-start | bytes 10804
  37.7 29.4 %copy-start.21 = (s32[64,64]{0,1:T(8,128)S(1)}, s32[64,64]{0,1:T(8,128)}, u32[]{:S(2)}) copy-start(s32[64,64]{0,1:T(8,128)} %constant.21.clone) | copy-start | bytes 49156
  37.7 33.0 %copy-start.7 = (bf16[256,256]{1,0:T(8,128)(2,1)S(1)}, bf16[256,256]{1,0:T(8,128)(2,1)}, u32[]{:S(2)}) copy-start(bf16[256,256]{1,0:T(8,128)(2,1)} %wout_ref.1) | copy-start | bytes 393220
  37.8 33.0 %copy-start.8 = (bf16[256,256]{1,0:T(8,128)(2,1)S(1)}, bf16[256,256]{1,0:T(8,128)(2,1)}, u32[]{:S(2)}) copy-start(bf16[256,256]{1,0:T(8,128)(2,1)} %constant.22.clone.swap_ref) | copy-start | bytes 393220
  57.2 25.0 %all-to-all-start = ((bf16[64,32,256]{2,1,0:T(8,128)(2,1)}), bf16[64,32,256]{2,1,0:T(8,128)(2,1)S(1)}, u32[]{:S(2)}, u32[]{:S(2)}) async-start(bf16[64,32,256]{2,1,0:T(8,128)(2,1)} %get-tuple-element.67), calls=%async_computation | async-start | bytes 2097152 | tf_op jit(solution)/shard_map/all_to_all | solution.py:793
  71.5 1.0 copy-start.3
  72.5 1.0 copy-start.9
  82.2 1.0 copy-start.11
  99.1 20.8 %all-to-all-start.2 = ((bf16[64,32,256]{2,1,0:T(8,128)(2,1)}), bf16[64,32,256]{2,1,0:T(8,128)(2,1)S(1)}, u32[]{:S(2)}, u32[]{:S(2)}) async-start(bf16[64,32,256]{2,1,0:T(8,128)(2,1)} %get-tuple-element.73), calls=%async_computation.2 | async-start | bytes 2097152 | tf_op jit(solution)/shard_map/all_to_all | solution.py:793
  106.6 13.3 %copy-start.5 = (bf16[32,512]{1,0:T(8,128)(2,1)S(1)}, bf16[32,512]{1,0:T(8,128)(2,1)}, u32[]{:S(2)}) copy-start(bf16[32,512]{1,0:T(8,128)(2,1)} %constant.23.clone.first_ref) | copy-start | bytes 98308
  106.6 13.3 %copy-start.6 = (bf16[32,512]{1,0:T(8,128)(2,1)S(1)}, bf16[32,512]{1,0:T(8,128)(2,1)}, u32[]{:S(2)}) copy-start(bf16[32,512]{1,0:T(8,128)(2,1)} %constant.24.clone.last_ref) | copy-start | bytes 98308
  119.9 1.8 copy-start
  121.7 12.9 %collective-permute-start.4 = (bf16[64,256]{1,0:T(8,128)(2,1)S(1)}, bf16[64,256]{1,0:T(8,128)(2,1)S(1)}, u32[]{:S(2)}, u32[]{:S(2)}) collective-permute-start(bf16[64,256]{1,0:T(8,128)(2,1)S(1)} %get-tuple-element.80), channel_id=1, source_target_pairs={{0,16},{16,32},{32,48},{48,64},{64,80},{80,96},{96,112},{1,17},{17... | collective-permute-start | bytes 98312 | tf_op jit(solution)/shard_map/ppermute | solution.py:754
  124.7 9.8 %collective-permute-start.5 = (bf16[64,256]{1,0:T(8,128)(2,1)S(1)}, bf16[64,256]{1,0:T(8,128)(2,1)S(1)}, u32[]{:S(2)}, u32[]{:S(2)}) collective-permute-start(bf16[64,256]{1,0:T(8,128)(2,1)S(1)} %get-tuple-element.81), channel_id=1, source_target_pairs={{16,0},{32,16},{48,32},{64,48},{80,64},{96,80},{112,96},{17,1},{33... | collective-permute-start | bytes 98312 | tf_op jit(solution)/shard_map/ppermute | solution.py:754
  134.5 12.7 %copy-start.12 = (f32[9,1024]{1,0:T(8,128)S(1)}, f32[9,1024]{1,0:T(8,128)}, u32[]{:S(2)}) copy-start(f32[9,1024]{1,0:T(8,128)} %reshape.67.dk_ref) | copy-start | bytes 110596
  134.7 11.9 %collective-permute-start.7 = (bf16[40,256]{1,0:T(8,128)(2,1)S(1)}, bf16[40,256]{1,0:T(8,128)(2,1)S(1)}, u32[]{:S(2)}, u32[]{:S(2)}) collective-permute-start(bf16[40,256]{1,0:T(8,128)(2,1)S(1)} %get-tuple-element.121), channel_id=1, source_target_pairs={{0,1},{1,2},{2,3},{3,4},{4,5},{5,6},{6,7},{7,8},{8,9},{9,10},{10,1... | collective-permute-start | bytes 61448 | tf_op jit(solution)/shard_map/ppermute | solution.py:760
  139.0 7.5 %collective-permute-start.8 = (bf16[40,256]{1,0:T(8,128)(2,1)S(1)}, bf16[40,256]{1,0:T(8,128)(2,1)S(1)}, u32[]{:S(2)}, u32[]{:S(2)}) collective-permute-start(bf16[40,256]{1,0:T(8,128)(2,1)S(1)} %get-tuple-element.122), channel_id=1, source_target_pairs={{1,0},{2,1},{3,2},{4,3},{5,4},{6,5},{7,6},{8,7},{9,8},{10,9},{11,1... | collective-permute-start | bytes 61448 | tf_op jit(solution)/shard_map/ppermute | solution.py:763
  147.9 27.1 %copy-start.1 = (bf16[128,16,128]{2,1,0:T(8,128)(2,1)S(1)}, bf16[128,16,128]{2,1,0:T(8,128)(2,1)}, u32[]{:S(2)}) copy-start(bf16[128,16,128]{2,1,0:T(8,128)(2,1)} %attention_sums.1.refs_0_) | copy-start | bytes 1572868
  147.9 27.4 %copy-start.2 = (bf16[128,16,128]{2,1,0:T(8,128)(2,1)S(1)}, bf16[128,16,128]{2,1,0:T(8,128)(2,1)}, u32[]{:S(2)}) copy-start(bf16[128,16,128]{2,1,0:T(8,128)(2,1)} %project_sum.1.refs_2_) | copy-start | bytes 1572868
  169.9 8.6 %collective-permute-start.10 = (bf16[128,24,128]{2,1,0:T(8,128)(2,1)}, bf16[128,24,128]{2,1,0:T(8,128)(2,1)S(1)}, u32[]{:S(2)}, u32[]{:S(2)}) collective-permute-start(bf16[128,24,128]{2,1,0:T(8,128)(2,1)} %get-tuple-element.97.refs_4_), channel_id=1, source_target_pairs={{0,1},{1,0},{2,3},{3,2},{4,5},{5,4},{6,7},{7,6},{8,9},{9,8},{10,11... | collective-permute-start | bytes 2359304 | tf_op jit(solution)/shard_map/ppermute | solution.py:809
  175.0 2.7 %collective-permute-start.6 = (bf16[128,16,128]{2,1,0:T(8,128)(2,1)S(1)}, bf16[128,16,128]{2,1,0:T(8,128)(2,1)S(1)}, u32[]{:S(2)}, u32[]{:S(2)}) collective-permute-start(bf16[128,16,128]{2,1,0:T(8,128)(2,1)S(1)} %copy-done.1), channel_id=1, source_target_pairs={{0,1},{1,0},{2,3},{3,2},{4,5},{5,4},{6,7},{7,6},{8,9},{9,8},{10,11... | collective-permute-start | bytes 1572872 | tf_op jit(solution)/shard_map/ppermute | solution.py:809
  175.3 3.1 %collective-permute-start.9 = (bf16[128,16,128]{2,1,0:T(8,128)(2,1)S(1)}, bf16[128,16,128]{2,1,0:T(8,128)(2,1)S(1)}, u32[]{:S(2)}, u32[]{:S(2)}) collective-permute-start(bf16[128,16,128]{2,1,0:T(8,128)(2,1)S(1)} %copy-done.2), channel_id=1, source_target_pairs={{0,1},{1,0},{2,3},{3,2},{4,5},{5,4},{6,7},{7,6},{8,9},{9,8},{10,11... | collective-permute-start | bytes 1572872 | tf_op jit(solution)/shard_map/ppermute | solution.py:809
  178.4 1.1 copy-start.4
  180.7 23.0 %all-to-all-start.3 = ((bf16[64,56,128]{2,1,0:T(8,128)(2,1)}), bf16[64,56,128]{2,1,0:T(8,128)(2,1)S(1)}, u32[]{:S(2)}, u32[]{:S(2)}) async-start(bf16[64,56,128]{2,1,0:T(8,128)(2,1)} %join.1), calls=%async_computation.3 | async-start | bytes 1835008 | tf_op jit(solution)/shard_map/all_to_all | solution.py:793
  223.0 6.3 %collective-permute-start.11 = (bf16[64,56,128]{2,1,0:T(8,128)(2,1)S(1)}, bf16[64,56,128]{2,1,0:T(8,128)(2,1)S(1)}, u32[]{:S(2)}, u32[]{:S(2)}) collective-permute-start(bf16[64,56,128]{2,1,0:T(8,128)(2,1)S(1)} %all_to_all.25.own_ref), channel_id=1, source_target_pairs={{0,1},{1,0},{2,3},{3,2},{4,5},{5,4},{6,7},{7,6},{8,9},{9,8},{10,11... | collective-permute-start | bytes 2752520 | tf_op jit(solution)/shard_map/ppermute | solution.py:809

commit v6 on v5

--- a/solution.py
+++ b/solution.py
@@ -1,3 +1,4 @@
+import functools
 import math
 
 import jax
@@ -15,7 +16,7 @@
 MIB = 1 << 20
 
 ROWS, COLS, CHAN, EXP = 32, 64, 256, 1024
-BLK = 4
+BLK = 8
 STEPS = ROWS // BLK
 TOK = BLK * COLS
 LANES = 128
@@ -39,6 +40,10 @@
     return (grads - mean_grad - normed * mean_cross) * inv_std
 
 
+def gelu(values):
+    return values * (0.5 + 0.5 * jnp.tanh(values * (GELU_C + (GELU_C * 0.044715) * (values * values))))
+
+
 def gelu_slope(values):
     squared = values * values
     tanh_val = jnp.tanh(values * (GELU_C + (GELU_C * 0.044715) * squared))
@@ -91,36 +96,56 @@
             out_ref[at + wide * r + c, :16] = tile.astype(BF16)
 
 
-def expand_body(x_ref, we_ref, hid_ref, slope_ref):
+def expand_body(x_ref, we_ref, out_ref, slopes):
     normed, _ = layer_norm(x_ref[...].reshape(TOK, CHAN).astype(F32))
     normed_b = normed.astype(BF16)
     for at in range(0, EXP, 256):
-        val, slope = gelu_slope(dot(normed_b, we_ref[:, at : at + 256]))
-        hid_ref[:, :, at : at + 256] = val.astype(BF16).reshape(BLK, COLS, 256)
-        slope_ref[:, :, at : at + 256] = slope.astype(BF16).reshape(BLK, COLS, 256)
-
-
-def expand(x, we):
-    wide = jax.ShapeDtypeStruct((ROWS, COLS, EXP), BF16)
-    return pl.pallas_call(
-        expand_body,
+        pre = dot(normed_b, we_ref[:, at : at + 256])
+        result = gelu_slope(pre)[1] if slopes else gelu(pre)
+        out_ref[:, :, at : at + 256] = result.astype(BF16).reshape(BLK, COLS, 256)
+
+
+def expand(x, we, slopes):
+    return pl.pallas_call(
+        functools.partial(expand_body, slopes=slopes),
         grid=(STEPS,),
         in_specs=[band((BLK, COLS, CHAN)), whole((CHAN, EXP))],
-        out_specs=[band((BLK, COLS, EXP))] * 2,
-        out_shape=[wide, wide],
+        out_specs=band((BLK, COLS, EXP)),
+        out_shape=jax.ShapeDtypeStruct((ROWS, COLS, EXP), BF16),
         compiler_params=params(58),
         cost_estimate=pl.CostEstimate(
-            flops=2 * ROWS * COLS * CHAN * EXP, bytes_accessed=10 * MIB, transcendentals=ROWS * COLS * EXP
+            flops=2 * ROWS * COLS * CHAN * EXP, bytes_accessed=6 * MIB, transcendentals=ROWS * COLS * EXP
         ),
-        name="expand",
+        name="expand_slopes" if slopes else "expand",
     )(x, we)
+
+
+def mixed_slopes_body(pre_ref, slope_ref):
+    for at in range(0, EXP, 256):
+        span = slice(at, at + 256)
+        slope_ref[:, :, span] = gelu_slope(pre_ref[:, :, span].astype(F32))[1].astype(BF16)
+
+
+def mixed_slopes(pre):
+    return pl.pallas_call(
+        mixed_slopes_body,
+        grid=(STEPS,),
+        in_specs=[band((BLK, COLS, EXP))],
+        out_specs=band((BLK, COLS, EXP)),
+        out_shape=jax.ShapeDtypeStruct((ROWS, COLS, EXP), BF16),
+        compiler_params=params(58),
+        cost_estimate=pl.CostEstimate(
+            flops=20 * ROWS * COLS * EXP, bytes_accessed=8 * MIB, transcendentals=ROWS * COLS * EXP
+        ),
+        name="mixed_slopes",
+    )(pre)
 
 
 def mix_body(
     cur_ref, before_ref, after_ref,
     above_ref, below_ref, first_ref, last_ref, west_ref, east_ref, own_west_ref, own_east_ref,
     we_ref, dk_ref, wp_ref, x_ref,
-    section_ref, mixed_ref, slope_ref, ring_slope_ref,
+    section_ref, mixed_ref, pre_ref, ring_slope_ref,
     top_ref, bottom_ref, left_ref, right_ref,
 ):
     step = pl.program_id(0)
@@ -134,6 +159,7 @@
         )
 
     first, last = step == 0, step == STEPS - 1
+    branch = None
     for at in range(0, EXP, LANES):
         span = slice(at, at + LANES)
         rows = [jnp.where(first, top_ref[:, span], before_ref[0, :, span])]
@@ -153,13 +179,15 @@
                 + jnp.concatenate([left, parts[0][:-1]], axis=0)
                 + jnp.concatenate([parts[2][1:], right], axis=0)
             )
-            val, slope = gelu_slope(pre)
-            mixed_ref[r, :, span] = val.astype(BF16)
-            slope_ref[r, :, span] = slope.astype(BF16)
-    branch = dot(mixed_ref[...].reshape(TOK, EXP), wp_ref[...])
+            mixed_ref[r, :, span] = gelu(pre).astype(BF16)
+            pre_ref[r, :, span] = pre.astype(BF16)
+        if at % 256:
+            pair = slice(at - LANES, at + LANES)
+            part = dot(mixed_ref[:, :, pair].reshape(TOK, 256), wp_ref[pair, :])
+            branch = part if branch is None else branch + part
     section = (x_ref[...].reshape(TOK, CHAN).astype(F32) + branch).astype(BF16)
-    section = section.reshape(2, 2, 4, 16, CHAN)
-    for pair in range(2):
+    section = section.reshape(BLK // 2, 2, 4, 16, CHAN)
+    for pair in range(BLK // 2):
         for quad in range(4):
             section_ref[4 * pair + quad] = section[pair, :, quad].reshape(32, CHAN)
 
@@ -187,8 +215,7 @@
     south, lefts, rights = 3 * LONG, 6 * LONG, 6 * LONG + 3 * EDGE
     for at in range(0, EXP, 256):
         span = slice(at, at + 256)
-        val, _ = gelu_slope(dot(normed_b, we_ref[:, span]))
-        val = val.astype(BF16).astype(F32)
+        val = gelu(dot(normed_b, we_ref[:, span])).astype(BF16).astype(F32)
         kern = [dk_ref[n, span][None] for n in range(9)]
         top_ref[:, span] = val[LONG + 2 : LONG + 2 + COLS].astype(BF16)
         bottom_ref[:, span] = val[south + LONG + 2 : south + LONG + 2 + COLS].astype(BF16)
@@ -231,12 +258,12 @@
             whole((CHAN, EXP)), whole((9, EXP)), whole((EXP, CHAN)), band((BLK, COLS, CHAN)),
         ],
         out_specs=[
-            band((8, 32, CHAN)), band((BLK, COLS, EXP)), band((BLK, COLS, EXP)), whole((HALO, EXP)),
+            band((2 * BLK, 32, CHAN)), band((BLK, COLS, EXP)), band((BLK, COLS, EXP)), whole((HALO, EXP)),
         ],
         out_shape=[
             jax.ShapeDtypeStruct((64, 32, CHAN), BF16), wide, wide, jax.ShapeDtypeStruct((HALO, EXP), F32),
         ],
-        scratch_shapes=[pltpu.VMEM((COLS, EXP), BF16)] * 2 + [pltpu.VMEM((STEPS, 8, EXP), F32)] * 2,
+        scratch_shapes=[pltpu.VMEM((COLS, EXP), BF16)] * 2 + [pltpu.VMEM((STEPS, 16, EXP), F32)] * 2,
         compiler_params=params(58),
         cost_estimate=pl.CostEstimate(
             flops=3 * ROWS * COLS * CHAN * EXP, bytes_accessed=18 * MIB, transcendentals=2 * ROWS * COLS * EXP
@@ -387,7 +414,7 @@
             jax.ShapeDtypeStruct((64, CHAN), F32),
         ],
         scratch_shapes=[pltpu.VMEM((n_groups, 64, CHAN), BF16)] * 2,
-        compiler_params=params(58),
+        compiler_params=params(26),
         cost_estimate=pl.CostEstimate(
             flops=flat * 4 * CHAN * CHAN * 5, bytes_accessed=8 * MIB, transcendentals=flat * 256
         ),
@@ -421,7 +448,7 @@
         out_specs=whole(TILED),
         out_shape=jax.ShapeDtypeStruct(TILED, BF16),
         scratch_shapes=[pltpu.VMEM((CHAN, 3 * CHAN), F32), pltpu.VMEM((CHAN, CHAN), F32)],
-        compiler_params=params(58),
+        compiler_params=params(26),
         cost_estimate=pl.CostEstimate(
             flops=flat * 8 * CHAN * CHAN, bytes_accessed=6 * MIB, transcendentals=0
         ),
@@ -430,18 +457,19 @@
 
 
 def section_grad(cot_ref, db_ref):
-    pieces = db_ref[...].reshape(2, 4, 2, 16, CHAN)
+    n_pairs = cot_ref.shape[0] // 2
+    pieces = db_ref[...].reshape(n_pairs, 4, 2, 16, CHAN)
     branch = jnp.concatenate(
-        [pieces[pair, quad, r] for pair in range(2) for r in range(2) for quad in range(4)], axis=0
+        [pieces[pair, quad, r] for pair in range(n_pairs) for r in range(2) for quad in range(4)], axis=0
     )
-    return cot_ref[...].reshape(TOK, CHAN).astype(F32) + branch.astype(F32)
+    return cot_ref[...].reshape(-1, CHAN).astype(F32) + branch.astype(F32)
 
 
 def project_body(cot_ref, db_ref, slope_ref, wp_ref, dm_ref):
     d_section_b = section_grad(cot_ref, db_ref).astype(BF16)
     for at in range(0, EXP, 256):
         grads = dot_nt(d_section_b, wp_ref[at : at + 256, :])
-        slope = slope_ref[:, :, at : at + 256].reshape(TOK, 256).astype(F32)
+        slope = slope_ref[:, :, at : at + 256].reshape(-1, 256).astype(F32)
         dm_ref[:, :, at : at + 256] = (grads * slope).astype(BF16).reshape(BLK, COLS, 256)
 
 
@@ -450,7 +478,7 @@
         project_body,
         grid=(STEPS,),
         in_specs=[
-            band((BLK, COLS, CHAN)), band((8, 32, CHAN)), band((BLK, COLS, EXP)), whole((EXP, CHAN)),
+            band((BLK, COLS, CHAN)), band((2 * BLK, 32, CHAN)), band((BLK, COLS, EXP)), whole((EXP, CHAN)),
         ],
         out_specs=band((BLK, COLS, EXP)),
         out_shape=jax.ShapeDtypeStruct((ROWS, COLS, EXP), BF16),
@@ -468,7 +496,7 @@
         sum_ref[...] = jnp.zeros_like(sum_ref)
 
     d_section_b = section_grad(cot_ref, db_ref).astype(BF16)
-    sum_ref[...] += dot_tn(d_section_b, mixed_ref[...].reshape(TOK, EXP))
+    sum_ref[...] += dot_tn(d_section_b, mixed_ref[...].reshape(-1, EXP))
 
     @pl.when(pl.program_id(0) == STEPS - 1)
     def _():
@@ -480,7 +508,7 @@
     return pl.pallas_call(
         project_sum_body,
         grid=(STEPS,),
-        in_specs=[band((BLK, COLS, CHAN)), band((8, 32, CHAN)), band((BLK, COLS, EXP))],
+        in_specs=[band((BLK, COLS, CHAN)), band((2 * BLK, 32, CHAN)), band((BLK, COLS, EXP))],
         out_specs=whole(TILED),
         out_shape=jax.ShapeDtypeStruct(TILED, BF16),
         scratch_shapes=[pltpu.VMEM((CHAN, EXP), F32), pltpu.VMEM((EXP, CHAN), F32)],
@@ -513,6 +541,8 @@
                 for s in range(STEPS):
                     ref[s, : BLK + 2, span] = grads[base + BLK * s : base + BLK * s + BLK + 2]
 
+    normed, _ = layer_norm(x_ref[...].reshape(TOK, CHAN).astype(F32))
+    normed_t = normed.T.astype(BF16)
     first, last = step == 0, step == STEPS - 1
     for at in range(0, EXP, LANES):
         span = slice(at, at + LANES)
@@ -550,8 +580,9 @@
                 dpre_ref[r * COLS + j : r * COLS + j + 16, span] = d_pre.astype(BF16)
         for n in range(9):
             acc_ref[n, :, span] = sums[n]
-    normed, _ = layer_norm(x_ref[...].reshape(TOK, CHAN).astype(F32))
-    sum_ref[...] += dot_tn(normed.astype(BF16), dpre_ref[...])
+        if at % 256:
+            pair = slice(at - LANES, at + LANES)
+            sum_ref[:, pair] += dot(normed_t, dpre_ref[:, pair])
 
     @pl.when(last)
     def _():
@@ -583,7 +614,7 @@
             jax.ShapeDtypeStruct(tiles, BF16),
         ],
         scratch_shapes=[pltpu.VMEM((COLS, EXP), F32)] * 2
-        + [pltpu.VMEM((STEPS, 8, EXP), F32)] * 2
+        + [pltpu.VMEM((STEPS, 16, EXP), F32)] * 2
         + [pltpu.VMEM((9, 8, EXP), F32), pltpu.VMEM((CHAN, EXP), F32), pltpu.VMEM((9, EXP), F32)]
         + [pltpu.VMEM((3, BLK + 2, COLS, EXP), F32)],
         compiler_params=params(58),
@@ -595,7 +626,7 @@
 
 
 def finish_body(dpre_ref, x_ref, cot_ref, db_ref, we_ref, grad_ref):
-    normed, inv_std = layer_norm(x_ref[...].reshape(TOK, CHAN).astype(F32))
+    normed, inv_std = layer_norm(x_ref[...].reshape(-1, CHAN).astype(F32))
     d_input = layer_norm_back(normed, inv_std, dot_nt(dpre_ref[...], we_ref[...]))
     grad_ref[...] = (section_grad(cot_ref, db_ref) + d_input).astype(BF16).reshape(BLK, COLS, CHAN)
 
@@ -605,7 +636,7 @@
         finish_body,
         grid=(STEPS,),
         in_specs=[
-            band((TOK, EXP)), band((BLK, COLS, CHAN)), band((BLK, COLS, CHAN)), band((8, 32, CHAN)),
+            band((BLK * COLS, EXP)), band((BLK, COLS, CHAN)), band((BLK, COLS, CHAN)), band((2 * BLK, 32, CHAN)),
             whole((CHAN, EXP)),
         ],
         out_specs=band((BLK, COLS, CHAN)),
@@ -651,7 +682,7 @@
         fold_body,
         out_shape=jax.ShapeDtypeStruct(terms.shape, BF16),
         compiler_params=params(24),
-        cost_estimate=pl.CostEstimate(flops=terms.size, bytes_accessed=4 * terms.size, transcendentals=0),
+        cost_estimate=pl.CostEstimate(flops=terms.size, bytes_accessed=2 * terms.size, transcendentals=0),
         name="fold",
     )(terms)
 
@@ -786,12 +817,15 @@
     return (from_west, from_east, own_west, own_east)
 
 
-def exchange(pieces):
+def members():
     n_lat, n_lon = lax.axis_size("lat"), lax.axis_size("lon")
     order = np.arange(n_lat * n_lon).reshape(n_lat, n_lon // 2, 2)
-    members = order.transpose(2, 0, 1).reshape(2, -1).tolist()
+    return order.transpose(2, 0, 1).reshape(2, -1).tolist()
+
+
+def exchange(pieces):
     return lax.all_to_all(
-        pieces, ("lat", "lon"), split_axis=0, concat_axis=0, axis_index_groups=members, tiled=True
+        pieces, ("lat", "lon"), split_axis=0, concat_axis=0, axis_index_groups=members(), tiled=True
     )
 
 
@@ -832,17 +866,20 @@
     barrier = lax.optimization_barrier
 
     above, below = wide_rows(field_in)
-    hidden, act_slope = expand(field_in, expand_weight)
+    hidden = expand(field_in, expand_weight, False)
+    above, below, hidden = barrier((above, below, hidden))
     field_halo = (above, below, *wide_columns(field_in, above, below))
     field_halo, late_cot = barrier((field_halo, cotangent))
     hidden, cot_pieces = barrier((hidden, to_pieces(late_cot)))
     cot_groups = exchange(cot_pieces)
-    section, mixed, mixed_slope, ring_slope = mix(
+    section, mixed, mixed_pre, ring_slope = mix(
         hidden, field_halo, expand_weight, dk, project_weight, field_in
     )
     groups = exchange(section)
     cot_swapped, d_att = prepare(cot_groups, out_weight, 32)
-    groups, bias, d_att = barrier((groups, bias, d_att))
+    section_field, _ = barrier((field_in, section))
+    act_slope = expand(section_field, expand_weight, True)
+    groups, bias, d_att, act_slope = barrier((groups, bias, d_att, act_slope))
     d_groups, attended, normed2, d_proj, bias_acc = attention(groups, d_att, qkv_weight, bias)
 
     d_branch = exchange(d_groups)
@@ -851,7 +888,9 @@
         "sht,tsr->hr", bias_acc.reshape(64, 4, 64), onehot, precision=lax.Precision.HIGHEST
     )
     extra = jnp.pad(bias_sum.reshape(60, 1, 15), ((0, 68), (1, 6), (0, 113)))
-    d_branch, attention_tiles, extra = barrier((d_branch, attention_tiles, extra))
+    mixed_pre, _ = barrier((mixed_pre, d_groups))
+    mixed_slope = mixed_slopes(mixed_pre)
+    d_branch, attention_tiles, extra, mixed_slope = barrier((d_branch, attention_tiles, extra, mixed_slope))
 
     top, bottom, left, right = edges(d_branch, cot_pieces)
     above, below = rows_of(top, bottom)

time: 233 us -> 228 us (0.979)
  starting transfers between devices: 65.6 us -> 59 us
  local copies, waits for them, and re-layouts: 11.6 us -> 16.1 us
    pallas_call x2 -> x4, Pallas kernels: 17.9 us -> 27 us  [the longest x2 13.9 us: expand(): pl.pallas_call(functools.partial(expand_body, slopes=slopes), grid=(STEPS...]
    unnamed x45 -> x57, local copies, waits for them, and re-layouts: 4.14 us -> 9.98 us
    all_to_all x4, waiting for transfers between devices: 21.5 us -> 17.9 us  [exchange(): lax.all_to_all(pieces, ('lat', 'lon'), split_axis=0, concat_axis=0, axis_...]
    pallas_call x1, Pallas kernels: 5.29 us -> 2.09 us  [attention_sums(): pl.pallas_call(attention_sums_body, grid=(flat // 512,), in_specs=[band((...]
    ppermute x1, starting transfers between devices: 4.39 us -> 1.27 us  [halo_of(): lax.ppermute(jnp.concatenate([above[-1:], right, below[-1:], pad], axis=0...]
    ppermute x4, starting transfers between devices: 9.83 us -> 7.07 us  [other_core(): return lax.ppermute(tiles, 'lon', swaps)]
    ppermute x1, waiting for transfers between devices: 0.01 us -> 2.62 us  [wide_columns(): from_east = lax.ppermute(own_west, 'lon', west)]
  transfers between devices with their start and end apart: 16 -> 16, of which waited for: 7 -> 8; matrix products, arithmetic and copies ran while one was open for 4% -> 3% of each run, Pallas kernels for 26% -> 26%
where the time goes in v6:
time: 228 us; the launch traced here: 226 us
  Pallas kernels  99.7 us (44%)
  starting transfers between devices  59 us (26%)
  waiting for transfers between devices  26.6 us (12%)
  blocking collectives  19 us (8%)
  local copies, waits for them, and re-layouts  16.1 us (7%)
  matrix products  4.24 us (2%)
    all_to_all x4, starting transfers between devices, exchange(): lax.all_to_all(pieces, ('lat', 'lon'), split_axis=0, concat_axis=0, axis_...  38.7 us
    pallas_call x1, Pallas kernels, expand_back(): pl.pallas_call(expand_back_body, grid=(STEPS,), in_specs=[cells, ROW_BEFO...  21.5 us
    all_to_all x1, blocking collectives, exchange(): lax.all_to_all(pieces, ('lat', 'lon'), split_axis=0, concat_axis=0, axis_...  19 us
    all_to_all x4, waiting for transfers between devices, exchange(): lax.all_to_all(pieces, ('lat', 'lon'), split_axis=0, concat_axis=0, axis_...  17.9 us
    pallas_call x1, Pallas kernels, mix(): pl.pallas_call(mix_body, grid=(STEPS,), in_specs=[band((BLK, COLS, EXP)),...  17.3 us
    pallas_call x1, Pallas kernels, attention(): pl.pallas_call(attention_body, grid=(n_groups // 4,), in_specs=[whole(sha...  14.2 us
    pallas_call x2, Pallas kernels, expand(): pl.pallas_call(functools.partial(expand_body, slopes=slopes), grid=(STEPS...  13.9 us
    unnamed x57, local copies, waits for them, and re-layouts  9.98 us
  transfers between devices with their start and end apart: 16, of which 8 were waited for; matrix products, arithmetic and copies ran while one was open for 3% of the time, Pallas kernels for 26%

profile of v6, /device:TPU:1, one launch (start us, length us, event | category | flops | bytes accessed | tf_op | source)
XLA Modules:
  0.0 226.5 jit_solution(16241829204639969172)
XLA Ops:
  0.6 1.0 fusion.7
  1.6 4.0 %collective-permute-start = (bf16[128,256]{1,0:T(8,128)(2,1)S(1)}, bf16[128,256]{1,0:T(8,128)(2,1)S(1)}, u32[]{:S(2)}, u32[]{:S(2)}) collective-permute-start(bf16[128,256]{1,0:T(8,128)(2,1)S(1)} %bitcast.43), channel_id=1, source_target_pairs={{0,16},{16,32},{32,48},{48,64},{64,80},{80,96},{96,112},{1,17},{17... | collective-permute-start | bytes 196616 | tf_op jit(solution)/shard_map/ppermute | solution.py:785
  5.7 1.3 collective-permute-start.1
  7.0 1.0 fusion.6
  8.1 6.2 %expand.1.cur_ref.before_ref.after_ref.hid_ref = bf16[32,64,1024]{2,1,0:T(8,128)(2,1)} custom-call(bf16[32,64,256]{2,1,0:T(8,128)(2,1)} %x_ref.8, bf16[256,1024]{1,0:T(8,128)(2,1)} %we_ref.7), custom_call_target="tpu_custom_call" | custom-call | flops 1073741824 | bytes 6291456 | tf_op jit(solution)/shard_map/expand/pallas_call | solution.py:109
  14.6 2.5 %collective-permute-start.2 = (bf16[2,40,256]{2,1,0:T(8,128)(2,1)S(1)}, bf16[2,40,256]{2,1,0:T(8,128)(2,1)S(1)}, u32[]{:S(2)}, u32[]{:S(2)}) collective-permute-start(bf16[2,40,256]{2,1,0:T(8,128)(2,1)S(1)} %get-tuple-element.73.own_east_ref), channel_id=1, source_target_pairs={{0,1},{1,2},{2,3},{3,4},{4,5},{5,6},{6,7},{7,8},{8,9},{9,10},{10,1... | collective-permute-start | bytes 122888 | tf_op jit(solution)/shard_map/ppermute | solution.py:815
  17.1 1.1 collective-permute-done.2.west_ref
  18.2 2.6 %collective-permute-done.3.east_ref = bf16[2,40,256]{2,1,0:T(8,128)(2,1)S(1)} collective-permute-done((bf16[2,40,256]{2,1,0:T(8,128)(2,1)S(1)}, bf16[2,40,256]{2,1,0:T(8,128)(2,1)S(1)}, u32[]{:S(2)}, u32[]{:S(2)}) %collective-permute-start.3) | collective-permute-done | bytes 40992 | tf_op jit(solution)/shard_map/ppermute | solution.py:816
  20.9 1.1 copy.33
  22.0 13.4 %all-to-all-start.1 = ((bf16[64,32,256]{2,1,0:T(8,128)(2,1)}), bf16[64,32,256]{2,1,0:T(8,128)(2,1)S(1)}, u32[]{:S(2)}, u32[]{:S(2)}) async-start(bf16[64,32,256]{2,1,0:T(8,128)(2,1)} %bitcast.13), calls=%async_computation.1 | async-start | bytes 2097152 | tf_op jit(solution)/shard_map/all_to_all | solution.py:827
  36.1 17.3 %mix.1 = (bf16[64,32,256]{2,1,0:T(8,128)(2,1)}, bf16[32,64,1024]{2,1,0:T(8,128)(2,1)}, bf16[32,64,1024]{2,1,0:T(8,128)(2,1)}, f32[208,1024]{1,0:T(8,128)}) custom-call(bf16[32,64,1024]{2,1,0:T(8,128)(2,1)} %expand.1.cur_ref.before_ref.after_ref.hid_ref, bf16[32,64,1024]{2,1,0:T(8,128)(2,1)} %expand.1.cur_ref.before_ref.after_ref.hid_ref, ...), custom_call_target="tpu_custom_call" | custom-call | flops 1610612736 | bytes 18874368 | tf_op jit(solution)/shard_map/mix/pallas_call | solution.py:249
  53.4 10.0 %all-to-all-start = ((bf16[64,32,256]{2,1,0:T(8,128)(2,1)}), bf16[64,32,256]{2,1,0:T(8,128)(2,1)S(1)}, u32[]{:S(2)}, u32[]{:S(2)}) async-start(bf16[64,32,256]{2,1,0:T(8,128)(2,1)} %get-tuple-element.74), calls=%async_computation | async-start | bytes 2097152 | tf_op jit(solution)/shard_map/all_to_all | solution.py:827
  63.5 2.8 %fusion.4 = f32[64,4,64]{2,1,0:T(4,128)S(1)} fusion(f32[4,225,1]{1,0,2:T(4,128)S(1)} %reshape.75, s32[64,64]{0,1:T(8,128)S(1)} %copy-done.26), kind=kOutput, calls=%fused_computation.5 | convolution fusion | flops 45158400 | bytes 85520 | tf_op jit(solution)/shard_map/tsr,hr->sht/dot_general | solution.py:859
  66.5 7.7 %expand_slopes.1.slope_ref = bf16[32,64,1024]{2,1,0:T(8,128)(2,1)} custom-call(bf16[32,64,256]{2,1,0:T(8,128)(2,1)} %x_ref.8, bf16[256,1024]{1,0:T(8,128)(2,1)} %we_ref.7), custom_call_target="tpu_custom_call" | custom-call | flops 1073741824 | bytes 6291456 | tf_op jit(solution)/shard_map/expand_slopes/pallas_call | solution.py:109
  74.2 0.8 prepare.1
  75.0 1.0 copy-done.14
  75.9 4.0 %all-to-all-done.x_ref = bf16[64,32,256]{2,1,0:T(8,128)(2,1)S(1)} async-done(((bf16[64,32,256]{2,1,0:T(8,128)(2,1)}), bf16[64,32,256]{2,1,0:T(8,128)(2,1)S(1)}, u32[]{:S(2)}, u32[]{:S(2)}) %all-to-all-start) | async-done | bytes 1048608 | tf_op jit(solution)/shard_map/all_to_all | solution.py:827
  80.0 1.0 copy-done.11
  81.0 1.2 copy-done.15
  82.2 14.2 %attention.1 = (bf16[64,32,256]{2,1,0:T(8,128)(2,1)}, bf16[2048,256]{1,0:T(8,128)(2,1)S(1)}, bf16[2048,256]{1,0:T(8,128)(2,1)S(1)}, bf16[2048,768]{1,0:T(8,128)(2,1)S(1)}, f32[64,256]{1,0:T(8,128)S(1)}) custom-call(bf16[64,32,256]{2,1,0:T(8,128)(2,1)S(1)} %all-to-all-done.x_ref, bf16[32,64,256]{2,1,0:T(8,128)(2,1)S(1)} %copy-done.15, ...), custom_call_target="tpu_custom_call" | custom-call | flops 2684354560 | bytes 8388608 | tf_op jit(solution)/shard_map/attention/pallas_call | solution.py:399
  96.4 1.6 copy-done.1
  98.0 1.0 copy-done.4
  99.0 1.1 copy-done.6
  100.0 5.4 %all-to-all-start.2 = ((bf16[64,32,256]{2,1,0:T(8,128)(2,1)}), bf16[64,32,256]{2,1,0:T(8,128)(2,1)S(1)}, u32[]{:S(2)}, u32[]{:S(2)}) async-start(bf16[64,32,256]{2,1,0:T(8,128)(2,1)} %get-tuple-element.81), calls=%async_computation.2 | async-start | bytes 2097152 | tf_op jit(solution)/shard_map/all_to_all | solution.py:827
  105.7 1.4 fusion.5
  107.2 0.9 pad.4.extra_ref
  108.1 7.2 %mixed_slopes.1.slope_ref = bf16[32,64,1024]{2,1,0:T(8,128)(2,1)} custom-call(bf16[32,64,1024]{2,1,0:T(8,128)(2,1)} %get-tuple-element.88.pre_ref), custom_call_target="tpu_custom_call" | custom-call | flops 41943040 | bytes 8388608 | tf_op jit(solution)/shard_map/mixed_slopes/pallas_call | solution.py:130
  115.3 1.9 copy-done.2
  117.2 2.1 attention_sums.1.refs_0_
  119.3 4.1 %all-to-all-done.2.db_ref = bf16[64,32,256]{2,1,0:T(8,128)(2,1)S(1)} async-done(((bf16[64,32,256]{2,1,0:T(8,128)(2,1)}), bf16[64,32,256]{2,1,0:T(8,128)(2,1)S(1)}, u32[]{:S(2)}, u32[]{:S(2)}) %all-to-all-start.2) | async-done | bytes 1048608 | tf_op jit(solution)/shard_map/all_to_all | solution.py:827
  123.5 1.7 edges.1
  125.2 2.2 collective-permute-start.4
  127.5 1.3 collective-permute-start.5
  128.8 6.3 %project_back.1.cur_ref.before_ref.after_ref = bf16[32,64,1024]{2,1,0:T(8,128)(2,1)} custom-call(bf16[32,64,256]{2,1,0:T(8,128)(2,1)} %cot_ref.5, bf16[64,32,256]{2,1,0:T(8,128)(2,1)} %copy-done, bf16[32,64,1024]{2,1,0:T(8,128)(2,1)} %mixed_slopes.1.slope_ref, bf16[1024,256]{1,0:T(8,128)(2,1)} %wp_ref.5), custom_call_target="tpu_custom_call" | custom-call | flops 1073741824 | bytes 10485760 | tf_op jit(solution)/shard_map/project_back/pallas_call | solution.py:477
  135.7 1.3 collective-permute-start.7
  137.0 5.4 %project_sum.1.refs_2_ = bf16[128,16,128]{2,1,0:T(8,128)(2,1)} custom-call(bf16[32,64,256]{2,1,0:T(8,128)(2,1)} %cot_ref.5, bf16[64,32,256]{2,1,0:T(8,128)(2,1)} %copy-done, bf16[32,64,1024]{2,1,0:T(8,128)(2,1)} %get-tuple-element.99.mixed_ref), custom_call_target="tpu_custom_call" | custom-call | flops 1073741824 | bytes 8388608 | tf_op jit(solution)/shard_map/project_sum/pallas_call | solution.py:508
  143.8 21.5 %expand_back.1 = (bf16[2048,1024]{1,0:T(8,128)(2,1)}, bf16[128,24,128]{2,1,0:T(8,128)(2,1)}) custom-call(bf16[32,64,1024]{2,1,0:T(8,128)(2,1)} %project_back.1.cur_ref.before_ref.after_ref, bf16[32,64,1024]{2,1,0:T(8,128)(2,1)} %project_back.1.cur_ref.before_ref.after_ref, bf16[32,64,1024]{2,1,0:T(8,128)(2,1)} %project_back.1.cur_ref.before_ref.after_ref, ...), custom_call_target="tpu_custom_call" | custom-call | flops 1073741824 | bytes 20971520 | tf_op jit(solution)/shard_map/expand_back/pallas_call | solution.py:603
  165.3 2.5 %collective-permute-start.10 = (bf16[128,24,128]{2,1,0:T(8,128)(2,1)}, bf16[128,24,128]{2,1,0:T(8,128)(2,1)S(1)}, u32[]{:S(2)}, u32[]{:S(2)}) collective-permute-start(bf16[128,24,128]{2,1,0:T(8,128)(2,1)} %get-tuple-element.107.refs_4_), channel_id=1, source_target_pairs={{0,1},{1,0},{2,3},{3,2},{4,5},{5,4},{6,7},{7,6},{8,9},{9,8},{10,11... | collective-permute-start | bytes 2359304 | tf_op jit(solution)/shard_map/ppermute | solution.py:843
  168.3 2.1 collective-permute-done.6.refs_1_
  171.2 1.1 copy-done.8
  172.3 1.1 join.1
  173.5 9.9 %all-to-all-start.3 = ((bf16[64,56,128]{2,1,0:T(8,128)(2,1)}), bf16[64,56,128]{2,1,0:T(8,128)(2,1)S(1)}, u32[]{:S(2)}, u32[]{:S(2)}) async-start(bf16[64,56,128]{2,1,0:T(8,128)(2,1)} %join.1), calls=%async_computation.3 | async-start | bytes 1835008 | tf_op jit(solution)/shard_map/all_to_all | solution.py:827
  183.4 5.9 %finish.1 = bf16[32,64,256]{2,1,0:T(8,128)(2,1)} custom-call(bf16[2048,1024]{1,0:T(8,128)(2,1)} %get-tuple-element.110.dpre_ref, bf16[32,64,256]{2,1,0:T(8,128)(2,1)} %x_ref.8, bf16[32,64,256]{2,1,0:T(8,128)(2,1)} %cot_ref.5, bf16[64,32,256]{2,1,0:T(8,128)(2,1)} %copy-done, bf16[256,1024]{1,0:T(8,128)(2,1)} %we_ref.7), custom_call_target="tpu_custom_call" | custom-call | flops 1073741824 | bytes 9437184 | tf_op jit(solution)/shard_map/finish/pallas_call | solution.py:635
  189.4 9.7 %all-to-all-done.3.terms_ref = bf16[64,56,128]{2,1,0:T(8,128)(2,1)S(1)} async-done(((bf16[64,56,128]{2,1,0:T(8,128)(2,1)}), bf16[64,56,128]{2,1,0:T(8,128)(2,1)S(1)}, u32[]{:S(2)}, u32[]{:S(2)}) %all-to-all-start.3) | async-done | bytes 917536 | tf_op jit(solution)/shard_map/all_to_all | solution.py:827
  199.3 19.0 %all_to_all.25.own_ref = bf16[64,56,128]{2,1,0:T(8,128)(2,1)S(1)} all-to-all(bf16[64,56,128]{2,1,0:T(8,128)(2,1)S(1)} %fold.1), channel_id=1, replica_groups={{0,2,4,6,8,10,12,14,16,18,20,22,24,26,28,30,32,34,36,38,40,42,44,46,48,..., dimensions={0} | all-to-all | bytes 1835008 | tf_op jit(solution)/shard_map/all_to_all | solution.py:827
  218.3 4.1 %collective-permute-start.11 = (bf16[64,56,128]{2,1,0:T(8,128)(2,1)S(1)}, bf16[64,56,128]{2,1,0:T(8,128)(2,1)S(1)}, u32[]{:S(2)}, u32[]{:S(2)}) collective-permute-start(bf16[64,56,128]{2,1,0:T(8,128)(2,1)S(1)} %all_to_all.25.own_ref), channel_id=1, source_target_pairs={{0,1},{1,0},{2,3},{3,2},{4,5},{5,4},{6,7},{7,6},{8,9},{9,8},{10,11... | collective-permute-start | bytes 2752520 | tf_op jit(solution)/shard_map/ppermute | solution.py:843
  222.4 2.1 collective-permute-done.11.other_ref
  224.5 2.0 unfold.1
  (82 shorter events, 5.1 us)
Async XLA Ops:
  0.6 20.2 %copy-start.16 = (bf16[32,64,256]{2,1,0:T(8,128)(2,1)S(1)}, bf16[32,64,256]{2,1,0:T(8,128)(2,1)}, u32[]{:S(2)}) copy-start(bf16[32,64,256]{2,1,0:T(8,128)(2,1)} %cot_ref.5) | copy-start | bytes 3145732
  1.6 12.7 %collective-permute-start = (bf16[128,256]{1,0:T(8,128)(2,1)S(1)}, bf16[128,256]{1,0:T(8,128)(2,1)S(1)}, u32[]{:S(2)}, u32[]{:S(2)}) collective-permute-start(bf16[128,256]{1,0:T(8,128)(2,1)S(1)} %bitcast.43), channel_id=1, source_target_pairs={{0,16},{16,32},{32,48},{48,64},{64,80},{80,96},{96,112},{1,17},{17... | collective-permute-start | bytes 196616 | tf_op jit(solution)/shard_map/ppermute | solution.py:785
  5.7 8.6 %collective-permute-start.1 = (bf16[128,256]{1,0:T(8,128)(2,1)S(1)}, bf16[128,256]{1,0:T(8,128)(2,1)S(1)}, u32[]{:S(2)}, u32[]{:S(2)}) collective-permute-start(bf16[128,256]{1,0:T(8,128)(2,1)S(1)} %bitcast.42), channel_id=1, source_target_pairs={{16,0},{32,16},{48,32},{64,48},{80,64},{96,80},{112,96},{17,1},{33... | collective-permute-start | bytes 196616 | tf_op jit(solution)/shard_map/ppermute | solution.py:785
  8.1 27.3 %copy-start.22 = (f32[3,3,1024]{2,1,0:T(4,128)S(1)}, f32[3,3,1024]{2,1,0:T(4,128)}, u32[]{:S(2)}) copy-start(f32[3,3,1024]{2,1,0:T(4,128)} %param.16) | copy-start | bytes 110596
  14.3 21.7 %copy-start.18 = (bf16[128,256]{1,0:T(8,128)(2,1)}, bf16[128,256]{1,0:T(8,128)(2,1)S(1)}, u32[]{:S(2)}) copy-start(bf16[128,256]{1,0:T(8,128)(2,1)S(1)} %collective-permute-done) | copy-start | bytes 196612
  14.3 21.7 %copy-start.19 = (bf16[128,256]{1,0:T(8,128)(2,1)}, bf16[128,256]{1,0:T(8,128)(2,1)S(1)}, u32[]{:S(2)}) copy-start(bf16[128,256]{1,0:T(8,128)(2,1)S(1)} %collective-permute-done.1) | copy-start | bytes 196612
  14.6 21.4 %copy-start.20 = (bf16[2,40,256]{2,1,0:T(8,128)(2,1)}, bf16[2,40,256]{2,1,0:T(8,128)(2,1)S(1)}, u32[]{:S(2)}) copy-start(bf16[2,40,256]{2,1,0:T(8,128)(2,1)S(1)} %get-tuple-element.72.own_west_ref) | copy-start | bytes 122884
  14.6 21.4 %copy-start.21 = (bf16[2,40,256]{2,1,0:T(8,128)(2,1)}, bf16[2,40,256]{2,1,0:T(8,128)(2,1)S(1)}, u32[]{:S(2)}) copy-start(bf16[2,40,256]{2,1,0:T(8,128)(2,1)S(1)} %get-tuple-element.73.own_east_ref) | copy-start | bytes 122884
  14.6 3.6 %collective-permute-start.2 = (bf16[2,40,256]{2,1,0:T(8,128)(2,1)S(1)}, bf16[2,40,256]{2,1,0:T(8,128)(2,1)S(1)}, u32[]{:S(2)}, u32[]{:S(2)}) collective-permute-start(bf16[2,40,256]{2,1,0:T(8,128)(2,1)S(1)} %get-tuple-element.73.own_east_ref), channel_id=1, source_target_pairs={{0,1},{1,2},{2,3},{3,4},{4,5},{5,6},{6,7},{7,8},{8,9},{9,10},{10,1... | collective-permute-start | bytes 122888 | tf_op jit(solution)/shard_map/ppermute | solution.py:815
  17.1 3.7 %collective-permute-start.3 = (bf16[2,40,256]{2,1,0:T(8,128)(2,1)S(1)}, bf16[2,40,256]{2,1,0:T(8,128)(2,1)S(1)}, u32[]{:S(2)}, u32[]{:S(2)}) collective-permute-start(bf16[2,40,256]{2,1,0:T(8,128)(2,1)S(1)} %get-tuple-element.72.own_west_ref), channel_id=1, source_target_pairs={{1,0},{2,1},{3,2},{4,3},{5,4},{6,5},{7,6},{8,7},{9,8},{10,9},{11,1... | collective-permute-start | bytes 122888 | tf_op jit(solution)/shard_map/ppermute | solution.py:816
  18.2 17.8 %copy-start.23 = (bf16[2,40,256]{2,1,0:T(8,128)(2,1)}, bf16[2,40,256]{2,1,0:T(8,128)(2,1)S(1)}, u32[]{:S(2)}) copy-start(bf16[2,40,256]{2,1,0:T(8,128)(2,1)S(1)} %collective-permute-done.2.west_ref) | copy-start | bytes 122884
  20.9 15.2 %copy-start.24 = (bf16[2,40,256]{2,1,0:T(8,128)(2,1)}, bf16[2,40,256]{2,1,0:T(8,128)(2,1)S(1)}, u32[]{:S(2)}) copy-start(bf16[2,40,256]{2,1,0:T(8,128)(2,1)S(1)} %collective-permute-done.3.east_ref) | copy-start | bytes 122884
  22.0 31.4 %all-to-all-start.1 = ((bf16[64,32,256]{2,1,0:T(8,128)(2,1)}), bf16[64,32,256]{2,1,0:T(8,128)(2,1)S(1)}, u32[]{:S(2)}, u32[]{:S(2)}) async-start(bf16[64,32,256]{2,1,0:T(8,128)(2,1)} %bitcast.13), calls=%async_computation.1 | async-start | bytes 2097152 | tf_op jit(solution)/shard_map/all_to_all | solution.py:827
  36.0 27.3 %copy-start.25 = (f32[4,15,15]{2,0,1:T(4,128)S(1)}, f32[4,15,15]{2,0,1:T(4,128)}, u32[]{:S(2)}) copy-start(f32[4,15,15]{2,0,1:T(4,128)} %param.20) | copy-start | bytes 10804
  36.0 27.4 %copy-start.26 = (s32[64,64]{0,1:T(8,128)S(1)}, s32[64,64]{0,1:T(8,128)}, u32[]{:S(2)}) copy-start(s32[64,64]{0,1:T(8,128)} %constant.21.clone) | copy-start | bytes 49156
  53.4 20.8 %copy-start.12 = (bf16[256,256]{1,0:T(8,128)(2,1)S(1)}, bf16[256,256]{1,0:T(8,128)(2,1)}, u32[]{:S(2)}) copy-start(bf16[256,256]{1,0:T(8,128)(2,1)} %wout_ref.1) | copy-start | bytes 393220
  53.4 20.8 %copy-start.13 = (bf16[256,256]{1,0:T(8,128)(2,1)S(1)}, bf16[256,256]{1,0:T(8,128)(2,1)}, u32[]{:S(2)}) copy-start(bf16[256,256]{1,0:T(8,128)(2,1)} %constant.22.clone.swap_ref) | copy-start | bytes 393220
  53.4 26.6 %all-to-all-start = ((bf16[64,32,256]{2,1,0:T(8,128)(2,1)}), bf16[64,32,256]{2,1,0:T(8,128)(2,1)S(1)}, u32[]{:S(2)}, u32[]{:S(2)}) async-start(bf16[64,32,256]{2,1,0:T(8,128)(2,1)} %get-tuple-element.74), calls=%async_computation | async-start | bytes 2097152 | tf_op jit(solution)/shard_map/all_to_all | solution.py:827
  75.0 1.0 copy-start.14
  80.0 1.0 copy-start.11
  81.0 1.2 copy-start.15
  82.2 23.5 %copy-start.27 = (s32[64,64]{0,1:T(8,128)S(1)}, s32[64,64]{0,1:T(8,128)}, u32[]{:S(2)}) copy-start(s32[64,64]{0,1:T(8,128)} %constant.21.clone) | copy-start | bytes 49156
  96.4 1.6 copy-start.1
  98.0 1.0 copy-start.4
  99.0 1.1 copy-start.6
  100.0 23.4 %all-to-all-start.2 = ((bf16[64,32,256]{2,1,0:T(8,128)(2,1)}), bf16[64,32,256]{2,1,0:T(8,128)(2,1)S(1)}, u32[]{:S(2)}, u32[]{:S(2)}) async-start(bf16[64,32,256]{2,1,0:T(8,128)(2,1)} %get-tuple-element.81), calls=%async_computation.2 | async-start | bytes 2097152 | tf_op jit(solution)/shard_map/all_to_all | solution.py:827
  108.1 7.2 %copy-start.5 = (bf16[2048,256]{1,0:T(8,128)(2,1)S(1)}, bf16[2048,256]{1,0:T(8,128)(2,1)}, u32[]{:S(2)}) copy-start(bf16[2048,256]{1,0:T(8,128)(2,1)} %copy-done.4) | copy-start | bytes 3145732
  108.1 7.2 %copy-start.7 = (bf16[2048,256]{1,0:T(8,128)(2,1)S(1)}, bf16[2048,256]{1,0:T(8,128)(2,1)}, u32[]{:S(2)}) copy-start(bf16[2048,256]{1,0:T(8,128)(2,1)} %copy-done.6) | copy-start | bytes 3145732
  108.1 15.4 %copy-start.9 = (bf16[32,512]{1,0:T(8,128)(2,1)S(1)}, bf16[32,512]{1,0:T(8,128)(2,1)}, u32[]{:S(2)}) copy-start(bf16[32,512]{1,0:T(8,128)(2,1)} %constant.23.clone.first_ref) | copy-start | bytes 98308
  108.1 15.4 %copy-start.10 = (bf16[32,512]{1,0:T(8,128)(2,1)S(1)}, bf16[32,512]{1,0:T(8,128)(2,1)}, u32[]{:S(2)}) copy-start(bf16[32,512]{1,0:T(8,128)(2,1)} %constant.24.clone.last_ref) | copy-start | bytes 98308
  115.3 1.9 copy-start.2
  123.5 1.8 copy-start
  125.2 9.9 %collective-permute-start.4 = (bf16[64,256]{1,0:T(8,128)(2,1)S(1)}, bf16[64,256]{1,0:T(8,128)(2,1)S(1)}, u32[]{:S(2)}, u32[]{:S(2)}) collective-permute-start(bf16[64,256]{1,0:T(8,128)(2,1)S(1)} %get-tuple-element.90), channel_id=1, source_target_pairs={{0,16},{16,32},{32,48},{48,64},{64,80},{80,96},{96,112},{1,17},{17... | collective-permute-start | bytes 98312 | tf_op jit(solution)/shard_map/ppermute | solution.py:785
  127.5 7.6 %collective-permute-start.5 = (bf16[64,256]{1,0:T(8,128)(2,1)S(1)}, bf16[64,256]{1,0:T(8,128)(2,1)S(1)}, u32[]{:S(2)}, u32[]{:S(2)}) collective-permute-start(bf16[64,256]{1,0:T(8,128)(2,1)S(1)} %get-tuple-element.91), channel_id=1, source_target_pairs={{16,0},{32,16},{48,32},{64,48},{80,64},{96,80},{112,96},{17,1},{33... | collective-permute-start | bytes 98312 | tf_op jit(solution)/shard_map/ppermute | solution.py:785
  135.1 7.9 %copy-start.17 = (f32[9,1024]{1,0:T(8,128)S(1)}, f32[9,1024]{1,0:T(8,128)}, u32[]{:S(2)}) copy-start(f32[9,1024]{1,0:T(8,128)} %reshape.67.dk_ref) | copy-start | bytes 110596
  135.2 7.1 %collective-permute-start.8 = (bf16[40,256]{1,0:T(8,128)(2,1)S(1)}, bf16[40,256]{1,0:T(8,128)(2,1)S(1)}, u32[]{:S(2)}, u32[]{:S(2)}) collective-permute-start(bf16[40,256]{1,0:T(8,128)(2,1)S(1)} %get-tuple-element.132), channel_id=1, source_target_pairs={{1,0},{2,1},{3,2},{4,3},{5,4},{6,5},{7,6},{8,7},{9,8},{10,9},{11,1... | collective-permute-start | bytes 61448 | tf_op jit(solution)/shard_map/ppermute | solution.py:794
  135.7 6.7 %collective-permute-start.7 = (bf16[40,256]{1,0:T(8,128)(2,1)S(1)}, bf16[40,256]{1,0:T(8,128)(2,1)S(1)}, u32[]{:S(2)}, u32[]{:S(2)}) collective-permute-start(bf16[40,256]{1,0:T(8,128)(2,1)S(1)} %get-tuple-element.131), channel_id=1, source_target_pairs={{0,1},{1,2},{2,3},{3,4},{4,5},{5,6},{6,7},{7,8},{8,9},{9,10},{10,1... | collective-permute-start | bytes 61448 | tf_op jit(solution)/shard_map/ppermute | solution.py:791
  143.8 24.1 %copy-start.3 = (bf16[128,16,128]{2,1,0:T(8,128)(2,1)S(1)}, bf16[128,16,128]{2,1,0:T(8,128)(2,1)}, u32[]{:S(2)}) copy-start(bf16[128,16,128]{2,1,0:T(8,128)(2,1)} %project_sum.1.refs_2_) | copy-start | bytes 1572868
  165.3 5.9 %collective-permute-start.10 = (bf16[128,24,128]{2,1,0:T(8,128)(2,1)}, bf16[128,24,128]{2,1,0:T(8,128)(2,1)S(1)}, u32[]{:S(2)}, u32[]{:S(2)}) collective-permute-start(bf16[128,24,128]{2,1,0:T(8,128)(2,1)} %get-tuple-element.107.refs_4_), channel_id=1, source_target_pairs={{0,1},{1,0},{2,3},{3,2},{4,5},{5,4},{6,7},{7,6},{8,9},{9,8},{10,11... | collective-permute-start | bytes 2359304 | tf_op jit(solution)/shard_map/ppermute | solution.py:843
  167.8 2.7 %collective-permute-start.6 = (bf16[128,16,128]{2,1,0:T(8,128)(2,1)S(1)}, bf16[128,16,128]{2,1,0:T(8,128)(2,1)S(1)}, u32[]{:S(2)}, u32[]{:S(2)}) collective-permute-start(bf16[128,16,128]{2,1,0:T(8,128)(2,1)S(1)} %attention_sums.1.refs_0_), channel_id=1, source_target_pairs={{0,1},{1,0},{2,3},{3,2},{4,5},{5,4},{6,7},{7,6},{8,9},{9,8},{10,11... | collective-permute-start | bytes 1572872 | tf_op jit(solution)/shard_map/ppermute | solution.py:843
  167.9 3.3 %collective-permute-start.9 = (bf16[128,16,128]{2,1,0:T(8,128)(2,1)S(1)}, bf16[128,16,128]{2,1,0:T(8,128)(2,1)S(1)}, u32[]{:S(2)}, u32[]{:S(2)}) collective-permute-start(bf16[128,16,128]{2,1,0:T(8,128)(2,1)S(1)} %copy-done.3), channel_id=1, source_target_pairs={{0,1},{1,0},{2,3},{3,2},{4,5},{5,4},{6,7},{7,6},{8,9},{9,8},{10,11... | collective-permute-start | bytes 1572872 | tf_op jit(solution)/shard_map/ppermute | solution.py:843
  171.2 1.1 copy-start.8
  173.5 25.6 %all-to-all-start.3 = ((bf16[64,56,128]{2,1,0:T(8,128)(2,1)}), bf16[64,56,128]{2,1,0:T(8,128)(2,1)S(1)}, u32[]{:S(2)}, u32[]{:S(2)}) async-start(bf16[64,56,128]{2,1,0:T(8,128)(2,1)} %join.1), calls=%async_computation.3 | async-start | bytes 1835008 | tf_op jit(solution)/shard_map/all_to_all | solution.py:827
  218.3 6.2 %collective-permute-start.11 = (bf16[64,56,128]{2,1,0:T(8,128)(2,1)S(1)}, bf16[64,56,128]{2,1,0:T(8,128)(2,1)S(1)}, u32[]{:S(2)}, u32[]{:S(2)}) collective-permute-start(bf16[64,56,128]{2,1,0:T(8,128)(2,1)S(1)} %all_to_all.25.own_ref), channel_id=1, source_target_pairs={{0,1},{1,0},{2,3},{3,2},{4,5},{5,4},{6,7},{7,6},{8,9},{9,8},{10,11... | collective-permute-start | bytes 2752520 | tf_op jit(solution)/shard_map/ppermute | solution.py:843

commit v7 on v6

--- a/solution.py
+++ b/solution.py
@@ -414,7 +414,7 @@
             jax.ShapeDtypeStruct((64, CHAN), F32),
         ],
         scratch_shapes=[pltpu.VMEM((n_groups, 64, CHAN), BF16)] * 2,
-        compiler_params=params(26),
+        compiler_params=params(58),
         cost_estimate=pl.CostEstimate(
             flops=flat * 4 * CHAN * CHAN * 5, bytes_accessed=8 * MIB, transcendentals=flat * 256
         ),
@@ -448,7 +448,7 @@
         out_specs=whole(TILED),
         out_shape=jax.ShapeDtypeStruct(TILED, BF16),
         scratch_shapes=[pltpu.VMEM((CHAN, 3 * CHAN), F32), pltpu.VMEM((CHAN, CHAN), F32)],
-        compiler_params=params(26),
+        compiler_params=params(58),
         cost_estimate=pl.CostEstimate(
             flops=flat * 8 * CHAN * CHAN, bytes_accessed=6 * MIB, transcendentals=0
         ),
@@ -524,6 +524,7 @@
     cur_ref, before_ref, after_ref, halo_ref, halo_slope_ref, wp_ref, hid_ref, slope_ref, x_ref, dkb_ref,
     extra_ref,
     dpre_ref, tiles_ref, top_ref, bottom_ref, left_ref, right_ref, acc_ref, sum_ref, depth_ref, shift_ref,
+    narrow_ref,
 ):
     step = pl.program_id(0)
 
@@ -543,6 +544,9 @@
 
     normed, _ = layer_norm(x_ref[...].reshape(TOK, CHAN).astype(F32))
     normed_t = normed.T.astype(BF16)
+    diagonal_cells = lax.broadcasted_iota(jnp.int32, (LANES, LANES), 0) == lax.broadcasted_iota(
+        jnp.int32, (LANES, LANES), 1
+    )
     first, last = step == 0, step == STEPS - 1
     for at in range(0, EXP, LANES):
         span = slice(at, at + LANES)
@@ -552,34 +556,38 @@
         for r in range(BLK + 2):
             left = left_ref[step, r : r + 1, span]
             right = right_ref[step, r : r + 1, span]
-            shift_ref[0, r, :, span] = jnp.concatenate([rows[r][1:], right], axis=0)
-            shift_ref[1, r, :, span] = rows[r]
-            shift_ref[2, r, :, span] = jnp.concatenate([left, rows[r][:-1]], axis=0)
+            moved = (
+                jnp.concatenate([rows[r][1:], right], axis=0),
+                rows[r],
+                jnp.concatenate([left, rows[r][:-1]], axis=0),
+            )
+            for b in range(3):
+                shift_ref[b, r, :, span] = moved[b]
+                narrow_ref[b, r, :, span] = moved[b].astype(BF16)
+        hid_t = hid_ref[:, :, span].reshape(TOK, LANES).T
+        for a in range(3):
+            shifted = [
+                narrow_ref[b, 2 - a : 2 - a + BLK, :, span].reshape(TOK, LANES) for b in range(3)
+            ]
+            product = dot(hid_t, jnp.concatenate(shifted, axis=1))
+            for b in range(3):
+                cross = jnp.where(diagonal_cells, product[:, b * LANES : b * LANES + LANES], 0.0)
+                acc_ref[3 * a + b, :, span] += jnp.sum(cross.reshape(16, 8, LANES), axis=0)
         kern = [dkb_ref[n, :, span] for n in range(9)]
-        sums = [acc_ref[n, :, span] for n in range(9)]
         for j in range(0, COLS, 16):
-            hid = [hid_ref[r, j : j + 16, span].astype(F32) for r in range(BLK)]
             halves = []
             for low in (0, 8):
                 cells = slice(j + low, j + low + 8)
                 pieces = [[shift_ref[b, r, cells, span] for b in range(3)] for r in range(BLK + 2)]
-                totals = [None] * BLK
+                totals = []
                 for r in range(BLK):
-                    cell = hid[r][low : low + 8]
-                    for a in range(3):
-                        for b in range(3):
-                            n = 3 * a + b
-                            piece = pieces[r + 2 - a][b]
-                            tap = kern[n] * piece
-                            totals[r] = tap if n == 0 else totals[r] + tap
-                            sums[n] = sums[n] + cell * piece
+                    taps = [kern[3 * a + b] * pieces[r + 2 - a][b] for a in range(3) for b in range(3)]
+                    totals.append(sum(taps[1:], taps[0]))
                 halves.append(totals)
             for r in range(BLK):
                 total = jnp.concatenate([halves[0][r], halves[1][r]], axis=0)
                 d_pre = total * slope_ref[r, j : j + 16, span].astype(F32)
                 dpre_ref[r * COLS + j : r * COLS + j + 16, span] = d_pre.astype(BF16)
-        for n in range(9):
-            acc_ref[n, :, span] = sums[n]
         if at % 256:
             pair = slice(at - LANES, at + LANES)
             sum_ref[:, pair] += dot(normed_t, dpre_ref[:, pair])
@@ -616,7 +624,7 @@
         scratch_shapes=[pltpu.VMEM((COLS, EXP), F32)] * 2
         + [pltpu.VMEM((STEPS, 16, EXP), F32)] * 2
         + [pltpu.VMEM((9, 8, EXP), F32), pltpu.VMEM((CHAN, EXP), F32), pltpu.VMEM((9, EXP), F32)]
-        + [pltpu.VMEM((3, BLK + 2, COLS, EXP), F32)],
+        + [pltpu.VMEM((3, BLK + 2, COLS, EXP), F32), pltpu.VMEM((3, BLK + 2, COLS, EXP), BF16)],
         compiler_params=params(58),
         cost_estimate=pl.CostEstimate(
             flops=2 * ROWS * COLS * CHAN * EXP, bytes_accessed=20 * MIB, transcendentals=0

time: 228 us -> 234 us (1.026)
  Pallas kernels: 99.7 us -> 112 us
  local copies, waits for them, and re-layouts: 16.1 us -> 11.8 us
  waiting for transfers between devices: 26.6 us -> 22.4 us
  starting transfers between devices: 59 us -> 61.9 us
    pallas_call x1, Pallas kernels: 21.5 us -> 28.9 us  [expand_back(): pl.pallas_call(expand_back_body, grid=(STEPS,), in_specs=[cells, ROW_BEFO...]
    unnamed x57 -> x45, local copies, waits for them, and re-layouts: 9.98 us -> 4.17 us
    all_to_all x4, waiting for transfers between devices: 17.9 us -> 13.6 us  [exchange(): lax.all_to_all(pieces, ('lat', 'lon'), split_axis=0, concat_axis=0, axis_...]
    pallas_call x1, Pallas kernels: 2.09 us -> 5.28 us  [attention_sums(): pl.pallas_call(attention_sums_body, grid=(flat // 512,), in_specs=[band((...]
  transfers between devices with their start and end apart: 16 -> 16, of which waited for: 8 -> 8; matrix products, arithmetic and copies ran while one was open for 3% -> 4% of each run, Pallas kernels for 26% -> 27%
where the time goes in v7:
time: 234 us; the launch traced here: 233 us
  Pallas kernels  112 us (48%)
  starting transfers between devices  61.9 us (26%)
  waiting for transfers between devices  22.4 us (10%)
  blocking collectives  19 us (8%)
  local copies, waits for them, and re-layouts  11.8 us (5%)
  matrix products  4.24 us (2%)
    all_to_all x4, starting transfers between devices, exchange(): lax.all_to_all(pieces, ('lat', 'lon'), split_axis=0, concat_axis=0, axis_...  39.8 us
    pallas_call x1, Pallas kernels, expand_back(): pl.pallas_call(expand_back_body, grid=(STEPS,), in_specs=[cells, ROW_BEFO...  28.9 us
    all_to_all x1, blocking collectives, exchange(): lax.all_to_all(pieces, ('lat', 'lon'), split_axis=0, concat_axis=0, axis_...  19 us
    pallas_call x1, Pallas kernels, mix(): pl.pallas_call(mix_body, grid=(STEPS,), in_specs=[band((BLK, COLS, EXP)),...  17.5 us
    pallas_call x1, Pallas kernels, attention(): pl.pallas_call(attention_body, grid=(n_groups // 4,), in_specs=[whole(sha...  16.1 us
    pallas_call x2, Pallas kernels, expand(): pl.pallas_call(functools.partial(expand_body, slopes=slopes), grid=(STEPS...  13.8 us
    all_to_all x4, waiting for transfers between devices, exchange(): lax.all_to_all(pieces, ('lat', 'lon'), split_axis=0, concat_axis=0, axis_...  13.6 us
    ppermute x4, starting transfers between devices, rows_of(): return (lax.ppermute(bottom, 'lat', south), lax.ppermute(top, 'lat', north))  8.96 us
  transfers between devices with their start and end apart: 16, of which 8 were waited for; matrix products, arithmetic and copies ran while one was open for 4% of the time, Pallas kernels for 27%

profile of v7, /device:TPU:1, one launch (start us, length us, event | category | flops | bytes accessed | tf_op | source)
XLA Modules:
  0.0 233.0 jit_solution(14922485379494588766)
XLA Ops:
  0.6 1.0 fusion.7
  1.6 4.0 %collective-permute-start = (bf16[128,256]{1,0:T(8,128)(2,1)S(1)}, bf16[128,256]{1,0:T(8,128)(2,1)S(1)}, u32[]{:S(2)}, u32[]{:S(2)}) collective-permute-start(bf16[128,256]{1,0:T(8,128)(2,1)S(1)} %bitcast.43), channel_id=1, source_target_pairs={{0,16},{16,32},{32,48},{48,64},{64,80},{80,96},{96,112},{1,17},{17... | collective-permute-start | bytes 196616 | tf_op jit(solution)/shard_map/ppermute | solution.py:793
  5.7 1.3 collective-permute-start.1
  7.0 1.0 fusion.6
  8.1 6.2 %expand.1.cur_ref.before_ref.after_ref.hid_ref = bf16[32,64,1024]{2,1,0:T(8,128)(2,1)} custom-call(bf16[32,64,256]{2,1,0:T(8,128)(2,1)} %x_ref.8, bf16[256,1024]{1,0:T(8,128)(2,1)} %we_ref.7), custom_call_target="tpu_custom_call" | custom-call | flops 1073741824 | bytes 6291456 | tf_op jit(solution)/shard_map/expand/pallas_call | solution.py:109
  14.6 2.5 %collective-permute-start.2 = (bf16[2,40,256]{2,1,0:T(8,128)(2,1)S(1)}, bf16[2,40,256]{2,1,0:T(8,128)(2,1)S(1)}, u32[]{:S(2)}, u32[]{:S(2)}) collective-permute-start(bf16[2,40,256]{2,1,0:T(8,128)(2,1)S(1)} %get-tuple-element.73.own_east_ref), channel_id=1, source_target_pairs={{0,1},{1,2},{2,3},{3,4},{4,5},{5,6},{6,7},{7,8},{8,9},{9,10},{10,1... | collective-permute-start | bytes 122888 | tf_op jit(solution)/shard_map/ppermute | solution.py:823
  17.1 1.1 collective-permute-done.2.west_ref
  18.2 2.6 %collective-permute-done.3.east_ref = bf16[2,40,256]{2,1,0:T(8,128)(2,1)S(1)} collective-permute-done((bf16[2,40,256]{2,1,0:T(8,128)(2,1)S(1)}, bf16[2,40,256]{2,1,0:T(8,128)(2,1)S(1)}, u32[]{:S(2)}, u32[]{:S(2)}) %collective-permute-start.3) | collective-permute-done | bytes 40992 | tf_op jit(solution)/shard_map/ppermute | solution.py:824
  20.9 1.1 copy.33
  22.0 13.4 %all-to-all-start.1 = ((bf16[64,32,256]{2,1,0:T(8,128)(2,1)}), bf16[64,32,256]{2,1,0:T(8,128)(2,1)S(1)}, u32[]{:S(2)}, u32[]{:S(2)}) async-start(bf16[64,32,256]{2,1,0:T(8,128)(2,1)} %bitcast.13), calls=%async_computation.1 | async-start | bytes 2097152 | tf_op jit(solution)/shard_map/all_to_all | solution.py:835
  36.1 17.5 %mix.1 = (bf16[64,32,256]{2,1,0:T(8,128)(2,1)}, bf16[32,64,1024]{2,1,0:T(8,128)(2,1)}, bf16[32,64,1024]{2,1,0:T(8,128)(2,1)}, f32[208,1024]{1,0:T(8,128)}) custom-call(bf16[32,64,1024]{2,1,0:T(8,128)(2,1)} %expand.1.cur_ref.before_ref.after_ref.hid_ref, bf16[32,64,1024]{2,1,0:T(8,128)(2,1)} %expand.1.cur_ref.before_ref.after_ref.hid_ref, ...), custom_call_target="tpu_custom_call" | custom-call | flops 1610612736 | bytes 18874368 | tf_op jit(solution)/shard_map/mix/pallas_call | solution.py:249
  53.6 10.0 %all-to-all-start = ((bf16[64,32,256]{2,1,0:T(8,128)(2,1)}), bf16[64,32,256]{2,1,0:T(8,128)(2,1)S(1)}, u32[]{:S(2)}, u32[]{:S(2)}) async-start(bf16[64,32,256]{2,1,0:T(8,128)(2,1)} %get-tuple-element.74), calls=%async_computation | async-start | bytes 2097152 | tf_op jit(solution)/shard_map/all_to_all | solution.py:835
  63.7 2.8 %fusion.4 = f32[64,4,64]{2,1,0:T(4,128)S(1)} fusion(f32[4,225,1]{1,0,2:T(4,128)S(1)} %reshape.75, s32[64,64]{0,1:T(8,128)S(1)} %copy-done.21), kind=kOutput, calls=%fused_computation.5 | convolution fusion | flops 45158400 | bytes 85520 | tf_op jit(solution)/shard_map/tsr,hr->sht/dot_general | solution.py:867
  66.5 0.8 reshape.69.bias_ref
  67.3 7.6 %expand_slopes.1.slope_ref = bf16[32,64,1024]{2,1,0:T(8,128)(2,1)} custom-call(bf16[32,64,256]{2,1,0:T(8,128)(2,1)} %x_ref.8, bf16[256,1024]{1,0:T(8,128)(2,1)} %we_ref.7), custom_call_target="tpu_custom_call" | custom-call | flops 1073741824 | bytes 6291456 | tf_op jit(solution)/shard_map/expand_slopes/pallas_call | solution.py:109
  74.8 0.8 prepare.1
  75.6 1.0 copy-done.3
  76.6 1.0 copy-done.9
  77.6 2.5 %all-to-all-done.x_ref = bf16[64,32,256]{2,1,0:T(8,128)(2,1)S(1)} async-done(((bf16[64,32,256]{2,1,0:T(8,128)(2,1)}), bf16[64,32,256]{2,1,0:T(8,128)(2,1)S(1)}, u32[]{:S(2)}, u32[]{:S(2)}) %all-to-all-start) | async-done | bytes 1048608 | tf_op jit(solution)/shard_map/all_to_all | solution.py:835
  80.1 1.0 copy-done.11
  81.1 16.1 %attention.1 = (bf16[64,32,256]{2,1,0:T(8,128)(2,1)}, bf16[2048,256]{1,0:T(8,128)(2,1)}, bf16[2048,256]{1,0:T(8,128)(2,1)}, bf16[2048,768]{1,0:T(8,128)(2,1)}, f32[64,256]{1,0:T(8,128)}) custom-call(bf16[64,32,256]{2,1,0:T(8,128)(2,1)} %copy-done.11, bf16[32,64,256]{2,1,0:T(8,128)(2,1)} %copy-done.9, bf16[256,768]{1,0:T(8,128)(2,1)} %wqkv_ref.1, ...), custom_call_target="tpu_custom_call" | custom-call | flops 2684354560 | bytes 8388608 | tf_op jit(solution)/shard_map/attention/pallas_call | solution.py:399
  97.2 7.0 %all-to-all-start.2 = ((bf16[64,32,256]{2,1,0:T(8,128)(2,1)}), bf16[64,32,256]{2,1,0:T(8,128)(2,1)S(1)}, u32[]{:S(2)}, u32[]{:S(2)}) async-start(bf16[64,32,256]{2,1,0:T(8,128)(2,1)} %get-tuple-element.81), calls=%async_computation.2 | async-start | bytes 2097152 | tf_op jit(solution)/shard_map/all_to_all | solution.py:835
  104.2 0.9 reshape.71
  105.2 1.4 fusion.5
  106.7 0.8 pad.4.extra_ref
  107.5 7.1 %mixed_slopes.1.slope_ref = bf16[32,64,1024]{2,1,0:T(8,128)(2,1)} custom-call(bf16[32,64,1024]{2,1,0:T(8,128)(2,1)} %get-tuple-element.88.pre_ref), custom_call_target="tpu_custom_call" | custom-call | flops 41943040 | bytes 8388608 | tf_op jit(solution)/shard_map/mixed_slopes/pallas_call | solution.py:130
  114.6 5.3 %attention_sums.1.refs_0_ = bf16[128,16,128]{2,1,0:T(8,128)(2,1)} custom-call(bf16[2048,256]{1,0:T(8,128)(2,1)} %get-tuple-element.82.att_ref, bf16[2048,256]{1,0:T(8,128)(2,1)} %bitcast.36, bf16[2048,256]{1,0:T(8,128)(2,1)} %get-tuple-element.84.norm_ref, bf16[2048,768]{1,0:T(8,128)(2,1)} %get-tuple-element.85.proj_ref), custom_call_target="tpu_custom_call" | custom-call | flops 1073741824 | bytes 6291456 | tf_op jit(solution)/shard_map/attention_sums/pallas_call | solution.py:444
  119.9 1.4 all-to-all-done.2.db_ref
  121.3 1.7 edges.1
  123.1 2.3 %collective-permute-start.4 = (bf16[64,256]{1,0:T(8,128)(2,1)S(1)}, bf16[64,256]{1,0:T(8,128)(2,1)S(1)}, u32[]{:S(2)}, u32[]{:S(2)}) collective-permute-start(bf16[64,256]{1,0:T(8,128)(2,1)S(1)} %get-tuple-element.90), channel_id=1, source_target_pairs={{0,16},{16,32},{32,48},{48,64},{64,80},{80,96},{96,112},{1,17},{17... | collective-permute-start | bytes 98312 | tf_op jit(solution)/shard_map/ppermute | solution.py:793
  125.5 1.3 collective-permute-start.5
  126.8 6.3 %project_back.1.cur_ref.before_ref.after_ref = bf16[32,64,1024]{2,1,0:T(8,128)(2,1)} custom-call(bf16[32,64,256]{2,1,0:T(8,128)(2,1)} %cot_ref.5, bf16[64,32,256]{2,1,0:T(8,128)(2,1)} %copy-done, bf16[32,64,1024]{2,1,0:T(8,128)(2,1)} %mixed_slopes.1.slope_ref, bf16[1024,256]{1,0:T(8,128)(2,1)} %wp_ref.5), custom_call_target="tpu_custom_call" | custom-call | flops 1073741824 | bytes 10485760 | tf_op jit(solution)/shard_map/project_back/pallas_call | solution.py:477
  133.2 1.7 collective-permute-start.7
  134.9 5.4 %project_sum.1.refs_2_ = bf16[128,16,128]{2,1,0:T(8,128)(2,1)} custom-call(bf16[32,64,256]{2,1,0:T(8,128)(2,1)} %cot_ref.5, bf16[64,32,256]{2,1,0:T(8,128)(2,1)} %copy-done, bf16[32,64,1024]{2,1,0:T(8,128)(2,1)} %get-tuple-element.99.mixed_ref), custom_call_target="tpu_custom_call" | custom-call | flops 1073741824 | bytes 8388608 | tf_op jit(solution)/shard_map/project_sum/pallas_call | solution.py:508
  141.0 0.8 broadcast_in_dim.15.dkb_ref
  141.7 28.9 %expand_back.1 = (bf16[2048,1024]{1,0:T(8,128)(2,1)}, bf16[128,24,128]{2,1,0:T(8,128)(2,1)}) custom-call(bf16[32,64,1024]{2,1,0:T(8,128)(2,1)} %project_back.1.cur_ref.before_ref.after_ref, bf16[32,64,1024]{2,1,0:T(8,128)(2,1)} %project_back.1.cur_ref.before_ref.after_ref, bf16[32,64,1024]{2,1,0:T(8,128)(2,1)} %project_back.1.cur_ref.before_ref.after_ref, ...), custom_call_target="tpu_custom_call" | custom-call | flops 1073741824 | bytes 20971520 | tf_op jit(solution)/shard_map/expand_back/pallas_call | solution.py:611
  170.6 4.1 %collective-permute-start.10 = (bf16[128,24,128]{2,1,0:T(8,128)(2,1)}, bf16[128,24,128]{2,1,0:T(8,128)(2,1)S(1)}, u32[]{:S(2)}, u32[]{:S(2)}) collective-permute-start(bf16[128,24,128]{2,1,0:T(8,128)(2,1)} %get-tuple-element.107.refs_4_), channel_id=1, source_target_pairs={{0,1},{1,0},{2,3},{3,2},{4,5},{5,4},{6,7},{7,6},{8,9},{9,8},{10,11... | collective-permute-start | bytes 2359304 | tf_op jit(solution)/shard_map/ppermute | solution.py:851
  175.3 2.1 collective-permute-done.6.refs_1_
  177.5 0.7 collective-permute-done.9.refs_3_
  178.2 1.1 copy-done.4
  179.3 1.1 join.1
  180.5 9.5 %all-to-all-start.3 = ((bf16[64,56,128]{2,1,0:T(8,128)(2,1)}), bf16[64,56,128]{2,1,0:T(8,128)(2,1)S(1)}, u32[]{:S(2)}, u32[]{:S(2)}) async-start(bf16[64,56,128]{2,1,0:T(8,128)(2,1)} %join.1), calls=%async_computation.3 | async-start | bytes 1835008 | tf_op jit(solution)/shard_map/all_to_all | solution.py:835
  190.0 5.9 %finish.1 = bf16[32,64,256]{2,1,0:T(8,128)(2,1)} custom-call(bf16[2048,1024]{1,0:T(8,128)(2,1)} %get-tuple-element.110.dpre_ref, bf16[32,64,256]{2,1,0:T(8,128)(2,1)} %x_ref.8, bf16[32,64,256]{2,1,0:T(8,128)(2,1)} %cot_ref.5, bf16[64,32,256]{2,1,0:T(8,128)(2,1)} %copy-done, bf16[256,1024]{1,0:T(8,128)(2,1)} %we_ref.7), custom_call_target="tpu_custom_call" | custom-call | flops 1073741824 | bytes 9437184 | tf_op jit(solution)/shard_map/finish/pallas_call | solution.py:643
  196.0 9.7 %all-to-all-done.3.terms_ref = bf16[64,56,128]{2,1,0:T(8,128)(2,1)S(1)} async-done(((bf16[64,56,128]{2,1,0:T(8,128)(2,1)}), bf16[64,56,128]{2,1,0:T(8,128)(2,1)S(1)}, u32[]{:S(2)}, u32[]{:S(2)}) %all-to-all-start.3) | async-done | bytes 917536 | tf_op jit(solution)/shard_map/all_to_all | solution.py:835
  205.9 19.0 %all_to_all.25.own_ref = bf16[64,56,128]{2,1,0:T(8,128)(2,1)S(1)} all-to-all(bf16[64,56,128]{2,1,0:T(8,128)(2,1)S(1)} %fold.1), channel_id=1, replica_groups={{0,2,4,6,8,10,12,14,16,18,20,22,24,26,28,30,32,34,36,38,40,42,44,46,48,..., dimensions={0} | all-to-all | bytes 1835008 | tf_op jit(solution)/shard_map/all_to_all | solution.py:835
  224.9 4.1 %collective-permute-start.11 = (bf16[64,56,128]{2,1,0:T(8,128)(2,1)S(1)}, bf16[64,56,128]{2,1,0:T(8,128)(2,1)S(1)}, u32[]{:S(2)}, u32[]{:S(2)}) collective-permute-start(bf16[64,56,128]{2,1,0:T(8,128)(2,1)S(1)} %all_to_all.25.own_ref), channel_id=1, source_target_pairs={{0,1},{1,0},{2,3},{3,2},{4,5},{5,4},{6,7},{7,6},{8,9},{9,8},{10,11... | collective-permute-start | bytes 2752520 | tf_op jit(solution)/shard_map/ppermute | solution.py:851
  229.0 2.1 collective-permute-done.11.other_ref
  231.1 2.0 unfold.1
  (70 shorter events, 2.9 us)
Async XLA Ops:
  0.6 20.2 %copy-start.10 = (bf16[32,64,256]{2,1,0:T(8,128)(2,1)S(1)}, bf16[32,64,256]{2,1,0:T(8,128)(2,1)}, u32[]{:S(2)}) copy-start(bf16[32,64,256]{2,1,0:T(8,128)(2,1)} %cot_ref.5) | copy-start | bytes 3145732
  1.6 12.7 %collective-permute-start = (bf16[128,256]{1,0:T(8,128)(2,1)S(1)}, bf16[128,256]{1,0:T(8,128)(2,1)S(1)}, u32[]{:S(2)}, u32[]{:S(2)}) collective-permute-start(bf16[128,256]{1,0:T(8,128)(2,1)S(1)} %bitcast.43), channel_id=1, source_target_pairs={{0,16},{16,32},{32,48},{48,64},{64,80},{80,96},{96,112},{1,17},{17... | collective-permute-start | bytes 196616 | tf_op jit(solution)/shard_map/ppermute | solution.py:793
  5.7 8.6 %collective-permute-start.1 = (bf16[128,256]{1,0:T(8,128)(2,1)S(1)}, bf16[128,256]{1,0:T(8,128)(2,1)S(1)}, u32[]{:S(2)}, u32[]{:S(2)}) collective-permute-start(bf16[128,256]{1,0:T(8,128)(2,1)S(1)} %bitcast.42), channel_id=1, source_target_pairs={{16,0},{32,16},{48,32},{64,48},{80,64},{96,80},{112,96},{17,1},{33... | collective-permute-start | bytes 196616 | tf_op jit(solution)/shard_map/ppermute | solution.py:793
  8.1 27.3 %copy-start.17 = (f32[3,3,1024]{2,1,0:T(4,128)S(1)}, f32[3,3,1024]{2,1,0:T(4,128)}, u32[]{:S(2)}) copy-start(f32[3,3,1024]{2,1,0:T(4,128)} %param.16) | copy-start | bytes 110596
  14.3 21.7 %copy-start.13 = (bf16[128,256]{1,0:T(8,128)(2,1)}, bf16[128,256]{1,0:T(8,128)(2,1)S(1)}, u32[]{:S(2)}) copy-start(bf16[128,256]{1,0:T(8,128)(2,1)S(1)} %collective-permute-done) | copy-start | bytes 196612
  14.3 21.7 %copy-start.14 = (bf16[128,256]{1,0:T(8,128)(2,1)}, bf16[128,256]{1,0:T(8,128)(2,1)S(1)}, u32[]{:S(2)}) copy-start(bf16[128,256]{1,0:T(8,128)(2,1)S(1)} %collective-permute-done.1) | copy-start | bytes 196612
  14.6 21.4 %copy-start.15 = (bf16[2,40,256]{2,1,0:T(8,128)(2,1)}, bf16[2,40,256]{2,1,0:T(8,128)(2,1)S(1)}, u32[]{:S(2)}) copy-start(bf16[2,40,256]{2,1,0:T(8,128)(2,1)S(1)} %get-tuple-element.72.own_west_ref) | copy-start | bytes 122884
  14.6 21.4 %copy-start.16 = (bf16[2,40,256]{2,1,0:T(8,128)(2,1)}, bf16[2,40,256]{2,1,0:T(8,128)(2,1)S(1)}, u32[]{:S(2)}) copy-start(bf16[2,40,256]{2,1,0:T(8,128)(2,1)S(1)} %get-tuple-element.73.own_east_ref) | copy-start | bytes 122884
  14.6 3.6 %collective-permute-start.2 = (bf16[2,40,256]{2,1,0:T(8,128)(2,1)S(1)}, bf16[2,40,256]{2,1,0:T(8,128)(2,1)S(1)}, u32[]{:S(2)}, u32[]{:S(2)}) collective-permute-start(bf16[2,40,256]{2,1,0:T(8,128)(2,1)S(1)} %get-tuple-element.73.own_east_ref), channel_id=1, source_target_pairs={{0,1},{1,2},{2,3},{3,4},{4,5},{5,6},{6,7},{7,8},{8,9},{9,10},{10,1... | collective-permute-start | bytes 122888 | tf_op jit(solution)/shard_map/ppermute | solution.py:823
  17.1 3.7 %collective-permute-start.3 = (bf16[2,40,256]{2,1,0:T(8,128)(2,1)S(1)}, bf16[2,40,256]{2,1,0:T(8,128)(2,1)S(1)}, u32[]{:S(2)}, u32[]{:S(2)}) collective-permute-start(bf16[2,40,256]{2,1,0:T(8,128)(2,1)S(1)} %get-tuple-element.72.own_west_ref), channel_id=1, source_target_pairs={{1,0},{2,1},{3,2},{4,3},{5,4},{6,5},{7,6},{8,7},{9,8},{10,9},{11,1... | collective-permute-start | bytes 122888 | tf_op jit(solution)/shard_map/ppermute | solution.py:824
  18.2 17.8 %copy-start.18 = (bf16[2,40,256]{2,1,0:T(8,128)(2,1)}, bf16[2,40,256]{2,1,0:T(8,128)(2,1)S(1)}, u32[]{:S(2)}) copy-start(bf16[2,40,256]{2,1,0:T(8,128)(2,1)S(1)} %collective-permute-done.2.west_ref) | copy-start | bytes 122884
  20.9 15.2 %copy-start.19 = (bf16[2,40,256]{2,1,0:T(8,128)(2,1)}, bf16[2,40,256]{2,1,0:T(8,128)(2,1)S(1)}, u32[]{:S(2)}) copy-start(bf16[2,40,256]{2,1,0:T(8,128)(2,1)S(1)} %collective-permute-done.3.east_ref) | copy-start | bytes 122884
  22.0 31.6 %all-to-all-start.1 = ((bf16[64,32,256]{2,1,0:T(8,128)(2,1)}), bf16[64,32,256]{2,1,0:T(8,128)(2,1)S(1)}, u32[]{:S(2)}, u32[]{:S(2)}) async-start(bf16[64,32,256]{2,1,0:T(8,128)(2,1)} %bitcast.13), calls=%async_computation.1 | async-start | bytes 2097152 | tf_op jit(solution)/shard_map/all_to_all | solution.py:835
  36.0 27.5 %copy-start.20 = (f32[4,15,15]{2,0,1:T(4,128)S(1)}, f32[4,15,15]{2,0,1:T(4,128)}, u32[]{:S(2)}) copy-start(f32[4,15,15]{2,0,1:T(4,128)} %param.20) | copy-start | bytes 10804
  36.0 27.6 %copy-start.21 = (s32[64,64]{0,1:T(8,128)S(1)}, s32[64,64]{0,1:T(8,128)}, u32[]{:S(2)}) copy-start(s32[64,64]{0,1:T(8,128)} %constant.21.clone) | copy-start | bytes 49156
  53.5 21.3 %copy-start.7 = (bf16[256,256]{1,0:T(8,128)(2,1)S(1)}, bf16[256,256]{1,0:T(8,128)(2,1)}, u32[]{:S(2)}) copy-start(bf16[256,256]{1,0:T(8,128)(2,1)} %wout_ref.1) | copy-start | bytes 393220
  53.5 21.3 %copy-start.8 = (bf16[256,256]{1,0:T(8,128)(2,1)S(1)}, bf16[256,256]{1,0:T(8,128)(2,1)}, u32[]{:S(2)}) copy-start(bf16[256,256]{1,0:T(8,128)(2,1)} %constant.22.clone.swap_ref) | copy-start | bytes 393220
  53.6 26.6 %all-to-all-start = ((bf16[64,32,256]{2,1,0:T(8,128)(2,1)}), bf16[64,32,256]{2,1,0:T(8,128)(2,1)S(1)}, u32[]{:S(2)}, u32[]{:S(2)}) async-start(bf16[64,32,256]{2,1,0:T(8,128)(2,1)} %get-tuple-element.74), calls=%async_computation | async-start | bytes 2097152 | tf_op jit(solution)/shard_map/all_to_all | solution.py:835
  75.6 1.0 copy-start.3
  76.6 1.0 copy-start.9
  80.1 1.0 copy-start.11
  97.2 24.2 %all-to-all-start.2 = ((bf16[64,32,256]{2,1,0:T(8,128)(2,1)}), bf16[64,32,256]{2,1,0:T(8,128)(2,1)S(1)}, u32[]{:S(2)}, u32[]{:S(2)}) async-start(bf16[64,32,256]{2,1,0:T(8,128)(2,1)} %get-tuple-element.81), calls=%async_computation.2 | async-start | bytes 2097152 | tf_op jit(solution)/shard_map/all_to_all | solution.py:835
  114.6 6.7 %copy-start.5 = (bf16[32,512]{1,0:T(8,128)(2,1)S(1)}, bf16[32,512]{1,0:T(8,128)(2,1)}, u32[]{:S(2)}) copy-start(bf16[32,512]{1,0:T(8,128)(2,1)} %constant.23.clone.first_ref) | copy-start | bytes 98308
  114.6 6.7 %copy-start.6 = (bf16[32,512]{1,0:T(8,128)(2,1)S(1)}, bf16[32,512]{1,0:T(8,128)(2,1)}, u32[]{:S(2)}) copy-start(bf16[32,512]{1,0:T(8,128)(2,1)} %constant.24.clone.last_ref) | copy-start | bytes 98308
  121.3 1.8 copy-start
  123.1 10.0 %collective-permute-start.4 = (bf16[64,256]{1,0:T(8,128)(2,1)S(1)}, bf16[64,256]{1,0:T(8,128)(2,1)S(1)}, u32[]{:S(2)}, u32[]{:S(2)}) collective-permute-start(bf16[64,256]{1,0:T(8,128)(2,1)S(1)} %get-tuple-element.90), channel_id=1, source_target_pairs={{0,16},{16,32},{32,48},{48,64},{64,80},{80,96},{96,112},{1,17},{17... | collective-permute-start | bytes 98312 | tf_op jit(solution)/shard_map/ppermute | solution.py:793
  125.5 7.6 %collective-permute-start.5 = (bf16[64,256]{1,0:T(8,128)(2,1)S(1)}, bf16[64,256]{1,0:T(8,128)(2,1)S(1)}, u32[]{:S(2)}, u32[]{:S(2)}) collective-permute-start(bf16[64,256]{1,0:T(8,128)(2,1)S(1)} %get-tuple-element.91), channel_id=1, source_target_pairs={{16,0},{32,16},{48,32},{64,48},{80,64},{96,80},{112,96},{17,1},{33... | collective-permute-start | bytes 98312 | tf_op jit(solution)/shard_map/ppermute | solution.py:793
  133.0 7.9 %copy-start.12 = (f32[9,1024]{1,0:T(8,128)S(1)}, f32[9,1024]{1,0:T(8,128)}, u32[]{:S(2)}) copy-start(f32[9,1024]{1,0:T(8,128)} %reshape.67.dk_ref) | copy-start | bytes 110596
  133.2 7.1 %collective-permute-start.8 = (bf16[40,256]{1,0:T(8,128)(2,1)S(1)}, bf16[40,256]{1,0:T(8,128)(2,1)S(1)}, u32[]{:S(2)}, u32[]{:S(2)}) collective-permute-start(bf16[40,256]{1,0:T(8,128)(2,1)S(1)} %get-tuple-element.132), channel_id=1, source_target_pairs={{1,0},{2,1},{3,2},{4,3},{5,4},{6,5},{7,6},{8,7},{9,8},{10,9},{11,1... | collective-permute-start | bytes 61448 | tf_op jit(solution)/shard_map/ppermute | solution.py:802
  133.2 7.1 %collective-permute-start.7 = (bf16[40,256]{1,0:T(8,128)(2,1)S(1)}, bf16[40,256]{1,0:T(8,128)(2,1)S(1)}, u32[]{:S(2)}, u32[]{:S(2)}) collective-permute-start(bf16[40,256]{1,0:T(8,128)(2,1)S(1)} %get-tuple-element.131), channel_id=1, source_target_pairs={{0,1},{1,2},{2,3},{3,4},{4,5},{5,6},{6,7},{7,8},{8,9},{9,10},{10,1... | collective-permute-start | bytes 61448 | tf_op jit(solution)/shard_map/ppermute | solution.py:799
  141.7 33.1 %copy-start.1 = (bf16[128,16,128]{2,1,0:T(8,128)(2,1)S(1)}, bf16[128,16,128]{2,1,0:T(8,128)(2,1)}, u32[]{:S(2)}) copy-start(bf16[128,16,128]{2,1,0:T(8,128)(2,1)} %attention_sums.1.refs_0_) | copy-start | bytes 1572868
  141.7 33.2 %copy-start.2 = (bf16[128,16,128]{2,1,0:T(8,128)(2,1)S(1)}, bf16[128,16,128]{2,1,0:T(8,128)(2,1)}, u32[]{:S(2)}) copy-start(bf16[128,16,128]{2,1,0:T(8,128)(2,1)} %project_sum.1.refs_2_) | copy-start | bytes 1572868
  170.6 7.6 %collective-permute-start.10 = (bf16[128,24,128]{2,1,0:T(8,128)(2,1)}, bf16[128,24,128]{2,1,0:T(8,128)(2,1)S(1)}, u32[]{:S(2)}, u32[]{:S(2)}) collective-permute-start(bf16[128,24,128]{2,1,0:T(8,128)(2,1)} %get-tuple-element.107.refs_4_), channel_id=1, source_target_pairs={{0,1},{1,0},{2,3},{3,2},{4,5},{5,4},{6,7},{7,6},{8,9},{9,8},{10,11... | collective-permute-start | bytes 2359304 | tf_op jit(solution)/shard_map/ppermute | solution.py:851
  174.8 2.7 %collective-permute-start.6 = (bf16[128,16,128]{2,1,0:T(8,128)(2,1)S(1)}, bf16[128,16,128]{2,1,0:T(8,128)(2,1)S(1)}, u32[]{:S(2)}, u32[]{:S(2)}) collective-permute-start(bf16[128,16,128]{2,1,0:T(8,128)(2,1)S(1)} %copy-done.1), channel_id=1, source_target_pairs={{0,1},{1,0},{2,3},{3,2},{4,5},{5,4},{6,7},{7,6},{8,9},{9,8},{10,11... | collective-permute-start | bytes 1572872 | tf_op jit(solution)/shard_map/ppermute | solution.py:851
  174.9 3.3 %collective-permute-start.9 = (bf16[128,16,128]{2,1,0:T(8,128)(2,1)S(1)}, bf16[128,16,128]{2,1,0:T(8,128)(2,1)S(1)}, u32[]{:S(2)}, u32[]{:S(2)}) collective-permute-start(bf16[128,16,128]{2,1,0:T(8,128)(2,1)S(1)} %copy-done.2), channel_id=1, source_target_pairs={{0,1},{1,0},{2,3},{3,2},{4,5},{5,4},{6,7},{7,6},{8,9},{9,8},{10,11... | collective-permute-start | bytes 1572872 | tf_op jit(solution)/shard_map/ppermute | solution.py:851
  178.2 1.1 copy-start.4
  180.5 25.2 %all-to-all-start.3 = ((bf16[64,56,128]{2,1,0:T(8,128)(2,1)}), bf16[64,56,128]{2,1,0:T(8,128)(2,1)S(1)}, u32[]{:S(2)}, u32[]{:S(2)}) async-start(bf16[64,56,128]{2,1,0:T(8,128)(2,1)} %join.1), calls=%async_computation.3 | async-start | bytes 1835008 | tf_op jit(solution)/shard_map/all_to_all | solution.py:835
  224.9 6.2 %collective-permute-start.11 = (bf16[64,56,128]{2,1,0:T(8,128)(2,1)S(1)}, bf16[64,56,128]{2,1,0:T(8,128)(2,1)S(1)}, u32[]{:S(2)}, u32[]{:S(2)}) collective-permute-start(bf16[64,56,128]{2,1,0:T(8,128)(2,1)S(1)} %all_to_all.25.own_ref), channel_id=1, source_target_pairs={{0,1},{1,0},{2,3},{3,2},{4,5},{5,4},{6,7},{7,6},{8,9},{9,8},{10,11... | collective-permute-start | bytes 2752520 | tf_op jit(solution)/shard_map/ppermute | solution.py:851

commit v8 on v6

--- a/solution.py
+++ b/solution.py
@@ -414,7 +414,7 @@
             jax.ShapeDtypeStruct((64, CHAN), F32),
         ],
         scratch_shapes=[pltpu.VMEM((n_groups, 64, CHAN), BF16)] * 2,
-        compiler_params=params(26),
+        compiler_params=params(58),
         cost_estimate=pl.CostEstimate(
             flops=flat * 4 * CHAN * CHAN * 5, bytes_accessed=8 * MIB, transcendentals=flat * 256
         ),
@@ -448,7 +448,7 @@
         out_specs=whole(TILED),
         out_shape=jax.ShapeDtypeStruct(TILED, BF16),
         scratch_shapes=[pltpu.VMEM((CHAN, 3 * CHAN), F32), pltpu.VMEM((CHAN, CHAN), F32)],
-        compiler_params=params(26),
+        compiler_params=params(58),
         cost_estimate=pl.CostEstimate(
             flops=flat * 8 * CHAN * CHAN, bytes_accessed=6 * MIB, transcendentals=0
         ),
@@ -867,10 +867,10 @@
 
     above, below = wide_rows(field_in)
     hidden = expand(field_in, expand_weight, False)
-    above, below, hidden = barrier((above, below, hidden))
+    above, below, hidden, late_cot = barrier((above, below, hidden, cotangent))
     field_halo = (above, below, *wide_columns(field_in, above, below))
-    field_halo, late_cot = barrier((field_halo, cotangent))
-    hidden, cot_pieces = barrier((hidden, to_pieces(late_cot)))
+    field_halo, cot_pieces = barrier((field_halo, to_pieces(late_cot)))
+    hidden, cot_pieces = barrier((hidden, cot_pieces))
     cot_groups = exchange(cot_pieces)
     section, mixed, mixed_pre, ring_slope = mix(
         hidden, field_halo, expand_weight, dk, project_weight, field_in
@@ -894,13 +894,18 @@
 
     top, bottom, left, right = edges(d_branch, cot_pieces)
     above, below = rows_of(top, bottom)
+    project_tiles = project_sum(cotangent, d_branch, mixed)
+    above, below, project_tiles, attention_tiles, mixed_slope = barrier(
+        (above, below, project_tiles, attention_tiles, mixed_slope)
+    )
+    d_halo = halo_of(above, below, left, right)
+    attention_other, project_other = other_core(attention_tiles), other_core(project_tiles)
     d_mixed = project_back(cotangent, d_branch, mixed_slope, project_weight)
-    above, below, d_mixed, attention_tiles = barrier((above, below, d_mixed, attention_tiles))
-    d_halo = halo_of(above, below, left, right)
-    project_tiles = project_sum(cotangent, d_branch, mixed)
-    d_halo, project_tiles, d_mixed = barrier((d_halo, project_tiles, d_mixed))
-    attention_pair = (attention_tiles, other_core(attention_tiles))
-    project_pair = (project_tiles, other_core(project_tiles))
+    d_halo, d_mixed, attention_other, project_other = barrier(
+        (d_halo, d_mixed, attention_other, project_other)
+    )
+    attention_pair = (attention_tiles, attention_other)
+    project_pair = (project_tiles, project_other)
     d_pre, expand_tiles = expand_back(
         d_mixed, d_halo, ring_slope, project_weight, hidden, act_slope, field_in, dkb, extra
     )

time: 228 us -> 225 us (0.987)
  waiting for transfers between devices: 26.6 us -> 20.5 us
  Pallas kernels: 99.7 us -> 105 us
  local copies, waits for them, and re-layouts: 16.1 us -> 11.7 us
  starting transfers between devices: 59 us -> 62 us
    unnamed x57 -> x45, local copies, waits for them, and re-layouts: 9.98 us -> 4.11 us
    all_to_all x4, waiting for transfers between devices: 17.9 us -> 13.6 us  [exchange(): lax.all_to_all(pieces, ('lat', 'lon'), split_axis=0, concat_axis=0, axis_...]
    pallas_call x1, Pallas kernels: 2.09 us -> 5.28 us  [attention_sums(): pl.pallas_call(attention_sums_body, grid=(flat // 512,), in_specs=[band((...]
  transfers between devices with their start and end apart: 16 -> 16, of which waited for: 8 -> 6; matrix products, arithmetic and copies ran while one was open for 3% -> 5% of each run, Pallas kernels for 26% -> 28%
where the time goes in v8:
time: 225 us; the launch traced here: 224 us
  Pallas kernels  105 us (47%)
  starting transfers between devices  62 us (28%)
  waiting for transfers between devices  20.5 us (9%)
  blocking collectives  19 us (8%)
  local copies, waits for them, and re-layouts  11.7 us (5%)
  matrix products  4.24 us (2%)
    all_to_all x4, starting transfers between devices, exchange(): lax.all_to_all(pieces, ('lat', 'lon'), split_axis=0, concat_axis=0, axis_...  40.8 us
    pallas_call x1, Pallas kernels, expand_back(): pl.pallas_call(expand_back_body, grid=(STEPS,), in_specs=[cells, ROW_BEFO...  21.5 us
    all_to_all x1, blocking collectives, exchange(): lax.all_to_all(pieces, ('lat', 'lon'), split_axis=0, concat_axis=0, axis_...  19 us
    pallas_call x1, Pallas kernels, mix(): pl.pallas_call(mix_body, grid=(STEPS,), in_specs=[band((BLK, COLS, EXP)),...  17.6 us
    pallas_call x1, Pallas kernels, attention(): pl.pallas_call(attention_body, grid=(n_groups // 4,), in_specs=[whole(sha...  16.1 us
    pallas_call x2, Pallas kernels, expand(): pl.pallas_call(functools.partial(expand_body, slopes=slopes), grid=(STEPS...  13.8 us
    all_to_all x4, waiting for transfers between devices, exchange(): lax.all_to_all(pieces, ('lat', 'lon'), split_axis=0, concat_axis=0, axis_...  13.6 us
    ppermute x4, starting transfers between devices, rows_of(): return (lax.ppermute(bottom, 'lat', south), lax.ppermute(top, 'lat', north))  9.12 us
  transfers between devices with their start and end apart: 16, of which 6 were waited for; matrix products, arithmetic and copies ran while one was open for 5% of the time, Pallas kernels for 28%

profile of v8, /device:TPU:1, one launch (start us, length us, event | category | flops | bytes accessed | tf_op | source)
XLA Modules:
  0.0 224.1 jit_solution(2591646375701545864)
XLA Ops:
  0.6 1.0 fusion.7
  1.6 4.0 %collective-permute-start = (bf16[128,256]{1,0:T(8,128)(2,1)S(1)}, bf16[128,256]{1,0:T(8,128)(2,1)S(1)}, u32[]{:S(2)}, u32[]{:S(2)}) collective-permute-start(bf16[128,256]{1,0:T(8,128)(2,1)S(1)} %bitcast.43), channel_id=1, source_target_pairs={{0,16},{16,32},{32,48},{48,64},{64,80},{80,96},{96,112},{1,17},{17... | collective-permute-start | bytes 196616 | tf_op jit(solution)/shard_map/ppermute | solution.py:785
  5.7 1.3 collective-permute-start.1
  7.0 1.0 fusion.6
  8.1 6.2 %expand.1.cur_ref.before_ref.after_ref.hid_ref = bf16[32,64,1024]{2,1,0:T(8,128)(2,1)} custom-call(bf16[32,64,256]{2,1,0:T(8,128)(2,1)} %x_ref.8, bf16[256,1024]{1,0:T(8,128)(2,1)} %we_ref.7), custom_call_target="tpu_custom_call" | custom-call | flops 1073741824 | bytes 6291456 | tf_op jit(solution)/shard_map/expand/pallas_call | solution.py:109
  14.6 2.5 %collective-permute-start.2 = (bf16[2,40,256]{2,1,0:T(8,128)(2,1)S(1)}, bf16[2,40,256]{2,1,0:T(8,128)(2,1)S(1)}, u32[]{:S(2)}, u32[]{:S(2)}) collective-permute-start(bf16[2,40,256]{2,1,0:T(8,128)(2,1)S(1)} %get-tuple-element.77.own_east_ref), channel_id=1, source_target_pairs={{0,1},{1,2},{2,3},{3,4},{4,5},{5,6},{6,7},{7,8},{8,9},{9,10},{10,1... | collective-permute-start | bytes 122888 | tf_op jit(solution)/shard_map/ppermute | solution.py:815
  17.1 1.1 copy.33
  18.2 2.6 %collective-permute-done.3.east_ref = bf16[2,40,256]{2,1,0:T(8,128)(2,1)S(1)} collective-permute-done((bf16[2,40,256]{2,1,0:T(8,128)(2,1)S(1)}, bf16[2,40,256]{2,1,0:T(8,128)(2,1)S(1)}, u32[]{:S(2)}, u32[]{:S(2)}) %collective-permute-start.3) | collective-permute-done | bytes 40992 | tf_op jit(solution)/shard_map/ppermute | solution.py:816
  20.9 13.4 %all-to-all-start.1 = ((bf16[64,32,256]{2,1,0:T(8,128)(2,1)}), bf16[64,32,256]{2,1,0:T(8,128)(2,1)S(1)}, u32[]{:S(2)}, u32[]{:S(2)}) async-start(bf16[64,32,256]{2,1,0:T(8,128)(2,1)} %bitcast.13), calls=%async_computation.1 | async-start | bytes 2097152 | tf_op jit(solution)/shard_map/all_to_all | solution.py:827
  34.3 0.6 reshape.67.dk_ref
  34.9 17.6 %mix.1 = (bf16[64,32,256]{2,1,0:T(8,128)(2,1)}, bf16[32,64,1024]{2,1,0:T(8,128)(2,1)}, bf16[32,64,1024]{2,1,0:T(8,128)(2,1)}, f32[208,1024]{1,0:T(8,128)}) custom-call(bf16[32,64,1024]{2,1,0:T(8,128)(2,1)} %expand.1.cur_ref.before_ref.after_ref.hid_ref, bf16[32,64,1024]{2,1,0:T(8,128)(2,1)} %expand.1.cur_ref.before_ref.after_ref.hid_ref, ...), custom_call_target="tpu_custom_call" | custom-call | flops 1610612736 | bytes 18874368 | tf_op jit(solution)/shard_map/mix/pallas_call | solution.py:249
  52.5 10.0 %all-to-all-start = ((bf16[64,32,256]{2,1,0:T(8,128)(2,1)}), bf16[64,32,256]{2,1,0:T(8,128)(2,1)S(1)}, u32[]{:S(2)}, u32[]{:S(2)}) async-start(bf16[64,32,256]{2,1,0:T(8,128)(2,1)} %get-tuple-element.78), calls=%async_computation | async-start | bytes 2097152 | tf_op jit(solution)/shard_map/all_to_all | solution.py:827
  62.6 2.8 %fusion.4 = f32[64,4,64]{2,1,0:T(4,128)S(1)} fusion(f32[4,225,1]{1,0,2:T(4,128)S(1)} %reshape.75, s32[64,64]{0,1:T(8,128)S(1)} %copy-done.21), kind=kOutput, calls=%fused_computation.5 | convolution fusion | flops 45158400 | bytes 85520 | tf_op jit(solution)/shard_map/tsr,hr->sht/dot_general | solution.py:859
  65.5 0.8 reshape.69.bias_ref
  66.2 7.7 %expand_slopes.1.slope_ref = bf16[32,64,1024]{2,1,0:T(8,128)(2,1)} custom-call(bf16[32,64,256]{2,1,0:T(8,128)(2,1)} %x_ref.8, bf16[256,1024]{1,0:T(8,128)(2,1)} %we_ref.7), custom_call_target="tpu_custom_call" | custom-call | flops 1073741824 | bytes 6291456 | tf_op jit(solution)/shard_map/expand_slopes/pallas_call | solution.py:109
  73.9 0.8 prepare.1
  74.7 0.9 copy-done.3
  75.6 1.0 copy-done.9
  76.6 2.5 %all-to-all-done.x_ref = bf16[64,32,256]{2,1,0:T(8,128)(2,1)S(1)} async-done(((bf16[64,32,256]{2,1,0:T(8,128)(2,1)}), bf16[64,32,256]{2,1,0:T(8,128)(2,1)S(1)}, u32[]{:S(2)}, u32[]{:S(2)}) %all-to-all-start) | async-done | bytes 1048608 | tf_op jit(solution)/shard_map/all_to_all | solution.py:827
  79.1 1.0 copy-done.11
  80.1 16.1 %attention.1 = (bf16[64,32,256]{2,1,0:T(8,128)(2,1)}, bf16[2048,256]{1,0:T(8,128)(2,1)}, bf16[2048,256]{1,0:T(8,128)(2,1)}, bf16[2048,768]{1,0:T(8,128)(2,1)}, f32[64,256]{1,0:T(8,128)}) custom-call(bf16[64,32,256]{2,1,0:T(8,128)(2,1)} %copy-done.11, bf16[32,64,256]{2,1,0:T(8,128)(2,1)} %copy-done.9, bf16[256,768]{1,0:T(8,128)(2,1)} %wqkv_ref.1, ...), custom_call_target="tpu_custom_call" | custom-call | flops 2684354560 | bytes 8388608 | tf_op jit(solution)/shard_map/attention/pallas_call | solution.py:399
  96.2 6.9 %all-to-all-start.2 = ((bf16[64,32,256]{2,1,0:T(8,128)(2,1)}), bf16[64,32,256]{2,1,0:T(8,128)(2,1)S(1)}, u32[]{:S(2)}, u32[]{:S(2)}) async-start(bf16[64,32,256]{2,1,0:T(8,128)(2,1)} %get-tuple-element.85), calls=%async_computation.2 | async-start | bytes 2097152 | tf_op jit(solution)/shard_map/all_to_all | solution.py:827
  103.2 0.9 reshape.71
  104.1 1.4 fusion.5
  105.7 0.8 pad.4.extra_ref
  106.5 7.1 %mixed_slopes.1.slope_ref = bf16[32,64,1024]{2,1,0:T(8,128)(2,1)} custom-call(bf16[32,64,1024]{2,1,0:T(8,128)(2,1)} %get-tuple-element.92.pre_ref), custom_call_target="tpu_custom_call" | custom-call | flops 41943040 | bytes 8388608 | tf_op jit(solution)/shard_map/mixed_slopes/pallas_call | solution.py:130
  113.6 5.3 %attention_sums.1.refs_0_ = bf16[128,16,128]{2,1,0:T(8,128)(2,1)} custom-call(bf16[2048,256]{1,0:T(8,128)(2,1)} %get-tuple-element.86.att_ref, bf16[2048,256]{1,0:T(8,128)(2,1)} %bitcast.36, bf16[2048,256]{1,0:T(8,128)(2,1)} %get-tuple-element.88.norm_ref, bf16[2048,768]{1,0:T(8,128)(2,1)} %get-tuple-element.89.proj_ref), custom_call_target="tpu_custom_call" | custom-call | flops 1073741824 | bytes 6291456 | tf_op jit(solution)/shard_map/attention_sums/pallas_call | solution.py:444
  118.9 1.4 all-to-all-done.2.db_ref
  120.3 1.7 edges.1
  122.1 2.5 %collective-permute-start.4 = (bf16[64,256]{1,0:T(8,128)(2,1)S(1)}, bf16[64,256]{1,0:T(8,128)(2,1)S(1)}, u32[]{:S(2)}, u32[]{:S(2)}) collective-permute-start(bf16[64,256]{1,0:T(8,128)(2,1)S(1)} %get-tuple-element.94), channel_id=1, source_target_pairs={{0,16},{16,32},{32,48},{48,64},{64,80},{80,96},{96,112},{1,17},{17... | collective-permute-start | bytes 98312 | tf_op jit(solution)/shard_map/ppermute | solution.py:785
  124.6 1.3 collective-permute-start.5
  125.9 5.4 %project_sum.1.refs_2_ = bf16[128,16,128]{2,1,0:T(8,128)(2,1)} custom-call(bf16[32,64,256]{2,1,0:T(8,128)(2,1)} %cot_ref.5, bf16[64,32,256]{2,1,0:T(8,128)(2,1)} %copy-done, bf16[32,64,1024]{2,1,0:T(8,128)(2,1)} %get-tuple-element.96.mixed_ref), custom_call_target="tpu_custom_call" | custom-call | flops 1073741824 | bytes 8388608 | tf_op jit(solution)/shard_map/project_sum/pallas_call | solution.py:508
  132.1 1.7 collective-permute-start.6
  133.8 6.4 %project_back.1.cur_ref.before_ref.after_ref = bf16[32,64,1024]{2,1,0:T(8,128)(2,1)} custom-call(bf16[32,64,256]{2,1,0:T(8,128)(2,1)} %cot_ref.5, bf16[64,32,256]{2,1,0:T(8,128)(2,1)} %copy-done, bf16[32,64,1024]{2,1,0:T(8,128)(2,1)} %mixed_slopes.1.slope_ref, bf16[1024,256]{1,0:T(8,128)(2,1)} %wp_ref.5), custom_call_target="tpu_custom_call" | custom-call | flops 1073741824 | bytes 10485760 | tf_op jit(solution)/shard_map/project_back/pallas_call | solution.py:477
  140.1 0.7 pad_maximum_fusion.halo_ref
  140.8 0.7 broadcast_in_dim.15.dkb_ref
  141.5 21.5 %expand_back.1 = (bf16[2048,1024]{1,0:T(8,128)(2,1)}, bf16[128,24,128]{2,1,0:T(8,128)(2,1)}) custom-call(bf16[32,64,1024]{2,1,0:T(8,128)(2,1)} %project_back.1.cur_ref.before_ref.after_ref, bf16[32,64,1024]{2,1,0:T(8,128)(2,1)} %project_back.1.cur_ref.before_ref.after_ref, bf16[32,64,1024]{2,1,0:T(8,128)(2,1)} %project_back.1.cur_ref.before_ref.after_ref, ...), custom_call_target="tpu_custom_call" | custom-call | flops 1073741824 | bytes 20971520 | tf_op jit(solution)/shard_map/expand_back/pallas_call | solution.py:603
  163.1 3.1 %collective-permute-start.10 = (bf16[128,24,128]{2,1,0:T(8,128)(2,1)}, bf16[128,24,128]{2,1,0:T(8,128)(2,1)S(1)}, u32[]{:S(2)}, u32[]{:S(2)}) collective-permute-start(bf16[128,24,128]{2,1,0:T(8,128)(2,1)} %get-tuple-element.113.refs_4_), channel_id=1, source_target_pairs={{0,1},{1,0},{2,3},{3,2},{4,5},{5,4},{6,7},{7,6},{8,9},{9,8},{10,11... | collective-permute-start | bytes 2359304 | tf_op jit(solution)/shard_map/ppermute | solution.py:843
  166.2 2.1 collective-permute-done.10.refs_5_
  168.3 1.1 copy-done.4
  169.5 1.1 join.1
  170.6 10.5 %all-to-all-start.3 = ((bf16[64,56,128]{2,1,0:T(8,128)(2,1)}), bf16[64,56,128]{2,1,0:T(8,128)(2,1)S(1)}, u32[]{:S(2)}, u32[]{:S(2)}) async-start(bf16[64,56,128]{2,1,0:T(8,128)(2,1)} %join.1), calls=%async_computation.3 | async-start | bytes 1835008 | tf_op jit(solution)/shard_map/all_to_all | solution.py:827
  181.1 5.9 %finish.1 = bf16[32,64,256]{2,1,0:T(8,128)(2,1)} custom-call(bf16[2048,1024]{1,0:T(8,128)(2,1)} %get-tuple-element.116.dpre_ref, bf16[32,64,256]{2,1,0:T(8,128)(2,1)} %x_ref.8, bf16[32,64,256]{2,1,0:T(8,128)(2,1)} %cot_ref.5, bf16[64,32,256]{2,1,0:T(8,128)(2,1)} %copy-done, bf16[256,1024]{1,0:T(8,128)(2,1)} %we_ref.7), custom_call_target="tpu_custom_call" | custom-call | flops 1073741824 | bytes 9437184 | tf_op jit(solution)/shard_map/finish/pallas_call | solution.py:635
  187.0 9.7 %all-to-all-done.3.terms_ref = bf16[64,56,128]{2,1,0:T(8,128)(2,1)S(1)} async-done(((bf16[64,56,128]{2,1,0:T(8,128)(2,1)}), bf16[64,56,128]{2,1,0:T(8,128)(2,1)S(1)}, u32[]{:S(2)}, u32[]{:S(2)}) %all-to-all-start.3) | async-done | bytes 917536 | tf_op jit(solution)/shard_map/all_to_all | solution.py:827
  197.0 19.0 %all_to_all.25.own_ref = bf16[64,56,128]{2,1,0:T(8,128)(2,1)S(1)} all-to-all(bf16[64,56,128]{2,1,0:T(8,128)(2,1)S(1)} %fold.1), channel_id=1, replica_groups={{0,2,4,6,8,10,12,14,16,18,20,22,24,26,28,30,32,34,36,38,40,42,44,46,48,..., dimensions={0} | all-to-all | bytes 1835008 | tf_op jit(solution)/shard_map/all_to_all | solution.py:827
  216.0 4.1 %collective-permute-start.11 = (bf16[64,56,128]{2,1,0:T(8,128)(2,1)S(1)}, bf16[64,56,128]{2,1,0:T(8,128)(2,1)S(1)}, u32[]{:S(2)}, u32[]{:S(2)}) collective-permute-start(bf16[64,56,128]{2,1,0:T(8,128)(2,1)S(1)} %all_to_all.25.own_ref), channel_id=1, source_target_pairs={{0,1},{1,0},{2,3},{3,2},{4,5},{5,4},{6,7},{7,6},{8,9},{9,8},{10,11... | collective-permute-start | bytes 2752520 | tf_op jit(solution)/shard_map/ppermute | solution.py:843
  220.1 2.1 collective-permute-done.11.other_ref
  222.2 2.0 unfold.1
  (70 shorter events, 1.7 us)
Async XLA Ops:
  0.6 16.5 %copy-start.10 = (bf16[32,64,256]{2,1,0:T(8,128)(2,1)S(1)}, bf16[32,64,256]{2,1,0:T(8,128)(2,1)}, u32[]{:S(2)}) copy-start(bf16[32,64,256]{2,1,0:T(8,128)(2,1)} %cot_ref.5) | copy-start | bytes 3145732
  1.6 12.7 %collective-permute-start = (bf16[128,256]{1,0:T(8,128)(2,1)S(1)}, bf16[128,256]{1,0:T(8,128)(2,1)S(1)}, u32[]{:S(2)}, u32[]{:S(2)}) collective-permute-start(bf16[128,256]{1,0:T(8,128)(2,1)S(1)} %bitcast.43), channel_id=1, source_target_pairs={{0,16},{16,32},{32,48},{48,64},{64,80},{80,96},{96,112},{1,17},{17... | collective-permute-start | bytes 196616 | tf_op jit(solution)/shard_map/ppermute | solution.py:785
  5.7 8.6 %collective-permute-start.1 = (bf16[128,256]{1,0:T(8,128)(2,1)S(1)}, bf16[128,256]{1,0:T(8,128)(2,1)S(1)}, u32[]{:S(2)}, u32[]{:S(2)}) collective-permute-start(bf16[128,256]{1,0:T(8,128)(2,1)S(1)} %bitcast.42), channel_id=1, source_target_pairs={{16,0},{32,16},{48,32},{64,48},{80,64},{96,80},{112,96},{17,1},{33... | collective-permute-start | bytes 196616 | tf_op jit(solution)/shard_map/ppermute | solution.py:785
  8.1 26.1 %copy-start.17 = (f32[3,3,1024]{2,1,0:T(4,128)S(1)}, f32[3,3,1024]{2,1,0:T(4,128)}, u32[]{:S(2)}) copy-start(f32[3,3,1024]{2,1,0:T(4,128)} %param.16) | copy-start | bytes 110596
  14.3 20.6 %copy-start.13 = (bf16[128,256]{1,0:T(8,128)(2,1)}, bf16[128,256]{1,0:T(8,128)(2,1)S(1)}, u32[]{:S(2)}) copy-start(bf16[128,256]{1,0:T(8,128)(2,1)S(1)} %collective-permute-done) | copy-start | bytes 196612
  14.3 20.6 %copy-start.14 = (bf16[128,256]{1,0:T(8,128)(2,1)}, bf16[128,256]{1,0:T(8,128)(2,1)S(1)}, u32[]{:S(2)}) copy-start(bf16[128,256]{1,0:T(8,128)(2,1)S(1)} %collective-permute-done.1) | copy-start | bytes 196612
  14.6 20.3 %copy-start.15 = (bf16[2,40,256]{2,1,0:T(8,128)(2,1)}, bf16[2,40,256]{2,1,0:T(8,128)(2,1)S(1)}, u32[]{:S(2)}) copy-start(bf16[2,40,256]{2,1,0:T(8,128)(2,1)S(1)} %get-tuple-element.76.own_west_ref) | copy-start | bytes 122884
  14.6 20.3 %copy-start.16 = (bf16[2,40,256]{2,1,0:T(8,128)(2,1)}, bf16[2,40,256]{2,1,0:T(8,128)(2,1)S(1)}, u32[]{:S(2)}) copy-start(bf16[2,40,256]{2,1,0:T(8,128)(2,1)S(1)} %get-tuple-element.77.own_east_ref) | copy-start | bytes 122884
  14.6 3.7 %collective-permute-start.2 = (bf16[2,40,256]{2,1,0:T(8,128)(2,1)S(1)}, bf16[2,40,256]{2,1,0:T(8,128)(2,1)S(1)}, u32[]{:S(2)}, u32[]{:S(2)}) collective-permute-start(bf16[2,40,256]{2,1,0:T(8,128)(2,1)S(1)} %get-tuple-element.77.own_east_ref), channel_id=1, source_target_pairs={{0,1},{1,2},{2,3},{3,4},{4,5},{5,6},{6,7},{7,8},{8,9},{9,10},{10,1... | collective-permute-start | bytes 122888 | tf_op jit(solution)/shard_map/ppermute | solution.py:815
  17.1 3.7 %collective-permute-start.3 = (bf16[2,40,256]{2,1,0:T(8,128)(2,1)S(1)}, bf16[2,40,256]{2,1,0:T(8,128)(2,1)S(1)}, u32[]{:S(2)}, u32[]{:S(2)}) collective-permute-start(bf16[2,40,256]{2,1,0:T(8,128)(2,1)S(1)} %get-tuple-element.76.own_west_ref), channel_id=1, source_target_pairs={{1,0},{2,1},{3,2},{4,3},{5,4},{6,5},{7,6},{8,7},{9,8},{10,9},{11,1... | collective-permute-start | bytes 122888 | tf_op jit(solution)/shard_map/ppermute | solution.py:816
  18.2 16.7 %copy-start.18 = (bf16[2,40,256]{2,1,0:T(8,128)(2,1)}, bf16[2,40,256]{2,1,0:T(8,128)(2,1)S(1)}, u32[]{:S(2)}) copy-start(bf16[2,40,256]{2,1,0:T(8,128)(2,1)S(1)} %collective-permute-done.2.west_ref) | copy-start | bytes 122884
  20.9 14.1 %copy-start.19 = (bf16[2,40,256]{2,1,0:T(8,128)(2,1)}, bf16[2,40,256]{2,1,0:T(8,128)(2,1)S(1)}, u32[]{:S(2)}) copy-start(bf16[2,40,256]{2,1,0:T(8,128)(2,1)S(1)} %collective-permute-done.3.east_ref) | copy-start | bytes 122884
  20.9 31.7 %all-to-all-start.1 = ((bf16[64,32,256]{2,1,0:T(8,128)(2,1)}), bf16[64,32,256]{2,1,0:T(8,128)(2,1)S(1)}, u32[]{:S(2)}, u32[]{:S(2)}) async-start(bf16[64,32,256]{2,1,0:T(8,128)(2,1)} %bitcast.13), calls=%async_computation.1 | async-start | bytes 2097152 | tf_op jit(solution)/shard_map/all_to_all | solution.py:827
  34.9 27.6 %copy-start.20 = (f32[4,15,15]{2,0,1:T(4,128)S(1)}, f32[4,15,15]{2,0,1:T(4,128)}, u32[]{:S(2)}) copy-start(f32[4,15,15]{2,0,1:T(4,128)} %param.20) | copy-start | bytes 10804
  34.9 27.7 %copy-start.21 = (s32[64,64]{0,1:T(8,128)S(1)}, s32[64,64]{0,1:T(8,128)}, u32[]{:S(2)}) copy-start(s32[64,64]{0,1:T(8,128)} %constant.21.clone) | copy-start | bytes 49156
  52.5 21.4 %copy-start.7 = (bf16[256,256]{1,0:T(8,128)(2,1)S(1)}, bf16[256,256]{1,0:T(8,128)(2,1)}, u32[]{:S(2)}) copy-start(bf16[256,256]{1,0:T(8,128)(2,1)} %wout_ref.1) | copy-start | bytes 393220
  52.5 21.4 %copy-start.8 = (bf16[256,256]{1,0:T(8,128)(2,1)S(1)}, bf16[256,256]{1,0:T(8,128)(2,1)}, u32[]{:S(2)}) copy-start(bf16[256,256]{1,0:T(8,128)(2,1)} %constant.22.clone.swap_ref) | copy-start | bytes 393220
  52.5 26.6 %all-to-all-start = ((bf16[64,32,256]{2,1,0:T(8,128)(2,1)}), bf16[64,32,256]{2,1,0:T(8,128)(2,1)S(1)}, u32[]{:S(2)}, u32[]{:S(2)}) async-start(bf16[64,32,256]{2,1,0:T(8,128)(2,1)} %get-tuple-element.78), calls=%async_computation | async-start | bytes 2097152 | tf_op jit(solution)/shard_map/all_to_all | solution.py:827
  74.7 1.0 copy-start.3
  75.6 1.0 copy-start.9
  79.1 1.0 copy-start.11
  96.2 24.1 %all-to-all-start.2 = ((bf16[64,32,256]{2,1,0:T(8,128)(2,1)}), bf16[64,32,256]{2,1,0:T(8,128)(2,1)S(1)}, u32[]{:S(2)}, u32[]{:S(2)}) async-start(bf16[64,32,256]{2,1,0:T(8,128)(2,1)} %get-tuple-element.85), calls=%async_computation.2 | async-start | bytes 2097152 | tf_op jit(solution)/shard_map/all_to_all | solution.py:827
  113.6 6.7 %copy-start.5 = (bf16[32,512]{1,0:T(8,128)(2,1)S(1)}, bf16[32,512]{1,0:T(8,128)(2,1)}, u32[]{:S(2)}) copy-start(bf16[32,512]{1,0:T(8,128)(2,1)} %constant.23.clone.first_ref) | copy-start | bytes 98308
  113.6 6.7 %copy-start.6 = (bf16[32,512]{1,0:T(8,128)(2,1)S(1)}, bf16[32,512]{1,0:T(8,128)(2,1)}, u32[]{:S(2)}) copy-start(bf16[32,512]{1,0:T(8,128)(2,1)} %constant.24.clone.last_ref) | copy-start | bytes 98308
  120.3 1.8 copy-start
  122.1 9.2 %copy-start.1 = (bf16[128,16,128]{2,1,0:T(8,128)(2,1)S(1)}, bf16[128,16,128]{2,1,0:T(8,128)(2,1)}, u32[]{:S(2)}) copy-start(bf16[128,16,128]{2,1,0:T(8,128)(2,1)} %attention_sums.1.refs_0_) | copy-start | bytes 1572868
  122.1 9.2 %collective-permute-start.4 = (bf16[64,256]{1,0:T(8,128)(2,1)S(1)}, bf16[64,256]{1,0:T(8,128)(2,1)S(1)}, u32[]{:S(2)}, u32[]{:S(2)}) collective-permute-start(bf16[64,256]{1,0:T(8,128)(2,1)S(1)} %get-tuple-element.94), channel_id=1, source_target_pairs={{0,16},{16,32},{32,48},{48,64},{64,80},{80,96},{96,112},{1,17},{17... | collective-permute-start | bytes 98312 | tf_op jit(solution)/shard_map/ppermute | solution.py:785
  124.6 6.7 %collective-permute-start.5 = (bf16[64,256]{1,0:T(8,128)(2,1)S(1)}, bf16[64,256]{1,0:T(8,128)(2,1)S(1)}, u32[]{:S(2)}, u32[]{:S(2)}) collective-permute-start(bf16[64,256]{1,0:T(8,128)(2,1)S(1)} %get-tuple-element.95), channel_id=1, source_target_pairs={{16,0},{32,16},{48,32},{64,48},{80,64},{96,80},{112,96},{17,1},{33... | collective-permute-start | bytes 98312 | tf_op jit(solution)/shard_map/ppermute | solution.py:785
  131.3 9.5 %collective-permute-start.8 = (bf16[128,16,128]{2,1,0:T(8,128)(2,1)S(1)}, bf16[128,16,128]{2,1,0:T(8,128)(2,1)S(1)}, u32[]{:S(2)}, u32[]{:S(2)}) collective-permute-start(bf16[128,16,128]{2,1,0:T(8,128)(2,1)S(1)} %copy-done.1), channel_id=1, source_target_pairs={{0,1},{1,0},{2,3},{3,2},{4,5},{5,4},{6,7},{7,6},{8,9},{9,8},{10,11... | collective-permute-start | bytes 1572872 | tf_op jit(solution)/shard_map/ppermute | solution.py:843
  131.4 9.4 %collective-permute-start.9 = (bf16[128,16,128]{2,1,0:T(8,128)(2,1)}, bf16[128,16,128]{2,1,0:T(8,128)(2,1)S(1)}, u32[]{:S(2)}, u32[]{:S(2)}) collective-permute-start(bf16[128,16,128]{2,1,0:T(8,128)(2,1)} %project_sum.1.refs_2_), channel_id=1, source_target_pairs={{0,1},{1,0},{2,3},{3,2},{4,5},{5,4},{6,7},{7,6},{8,9},{9,8},{10,11... | collective-permute-start | bytes 1572872 | tf_op jit(solution)/shard_map/ppermute | solution.py:843
  132.0 8.1 %collective-permute-start.7 = (bf16[40,256]{1,0:T(8,128)(2,1)S(1)}, bf16[40,256]{1,0:T(8,128)(2,1)S(1)}, u32[]{:S(2)}, u32[]{:S(2)}) collective-permute-start(bf16[40,256]{1,0:T(8,128)(2,1)S(1)} %get-tuple-element.138), channel_id=1, source_target_pairs={{1,0},{2,1},{3,2},{4,3},{5,4},{6,5},{7,6},{8,7},{9,8},{10,9},{11,1... | collective-permute-start | bytes 61448 | tf_op jit(solution)/shard_map/ppermute | solution.py:794
  132.1 8.7 %copy-start.12 = (f32[9,1024]{1,0:T(8,128)S(1)}, f32[9,1024]{1,0:T(8,128)}, u32[]{:S(2)}) copy-start(f32[9,1024]{1,0:T(8,128)} %reshape.67.dk_ref) | copy-start | bytes 110596
  132.1 8.0 %collective-permute-start.6 = (bf16[40,256]{1,0:T(8,128)(2,1)S(1)}, bf16[40,256]{1,0:T(8,128)(2,1)S(1)}, u32[]{:S(2)}, u32[]{:S(2)}) collective-permute-start(bf16[40,256]{1,0:T(8,128)(2,1)S(1)} %get-tuple-element.137), channel_id=1, source_target_pairs={{0,1},{1,2},{2,3},{3,4},{4,5},{5,6},{6,7},{7,8},{8,9},{9,10},{10,1... | collective-permute-start | bytes 61448 | tf_op jit(solution)/shard_map/ppermute | solution.py:791
  141.5 26.8 %copy-start.2 = (bf16[128,16,128]{2,1,0:T(8,128)(2,1)S(1)}, bf16[128,16,128]{2,1,0:T(8,128)(2,1)}, u32[]{:S(2)}) copy-start(bf16[128,16,128]{2,1,0:T(8,128)(2,1)} %project_sum.1.refs_2_) | copy-start | bytes 1572868
  163.1 5.3 %collective-permute-start.10 = (bf16[128,24,128]{2,1,0:T(8,128)(2,1)}, bf16[128,24,128]{2,1,0:T(8,128)(2,1)S(1)}, u32[]{:S(2)}, u32[]{:S(2)}) collective-permute-start(bf16[128,24,128]{2,1,0:T(8,128)(2,1)} %get-tuple-element.113.refs_4_), channel_id=1, source_target_pairs={{0,1},{1,0},{2,3},{3,2},{4,5},{5,4},{6,7},{7,6},{8,9},{9,8},{10,11... | collective-permute-start | bytes 2359304 | tf_op jit(solution)/shard_map/ppermute | solution.py:843
  168.3 1.1 copy-start.4
  170.6 26.2 %all-to-all-start.3 = ((bf16[64,56,128]{2,1,0:T(8,128)(2,1)}), bf16[64,56,128]{2,1,0:T(8,128)(2,1)S(1)}, u32[]{:S(2)}, u32[]{:S(2)}) async-start(bf16[64,56,128]{2,1,0:T(8,128)(2,1)} %join.1), calls=%async_computation.3 | async-start | bytes 1835008 | tf_op jit(solution)/shard_map/all_to_all | solution.py:827
  216.0 6.2 %collective-permute-start.11 = (bf16[64,56,128]{2,1,0:T(8,128)(2,1)S(1)}, bf16[64,56,128]{2,1,0:T(8,128)(2,1)S(1)}, u32[]{:S(2)}, u32[]{:S(2)}) collective-permute-start(bf16[64,56,128]{2,1,0:T(8,128)(2,1)S(1)} %all_to_all.25.own_ref), channel_id=1, source_target_pairs={{0,1},{1,0},{2,3},{3,2},{4,5},{5,4},{6,7},{7,6},{8,9},{9,8},{10,11... | collective-permute-start | bytes 2752520 | tf_op jit(solution)/shard_map/ppermute | solution.py:843

commit v9 on v8

--- a/solution.py
+++ b/solution.py
@@ -23,6 +23,7 @@
 EDGE = 40
 HALO = 2 * COLS + 2 * EDGE
 LONG = 72
+AT_ONCE = 8
 JOINED = (64, 56, 128)
 
 
@@ -334,8 +335,8 @@
         bias_sum_ref[...] = jnp.zeros_like(bias_sum_ref)
         swap(x_ref, xs_ref, swap_ref, n_groups)
 
-    groups = pl.ds(step * 4, 4)
-    tokens = xs_ref[groups].reshape(256, CHAN)
+    groups = pl.ds(step * AT_ONCE, AT_ONCE)
+    tokens = xs_ref[groups].reshape(AT_ONCE * 64, CHAN)
     normed, inv_std = layer_norm(tokens.astype(F32))
     normed_b = normed.astype(BF16)
     norm_ref[...] = normed_b
@@ -352,38 +353,38 @@
             blocks.append(jnp.concatenate([pair, none] if half == 0 else [none, pair], axis=1))
         return jnp.concatenate(blocks, axis=0)
 
-    four = range(4)
-    part = [slice(g * 64, g * 64 + 64) for g in four]
+    batch = range(AT_ONCE)
+    part = [slice(g * 64, g * 64 + 64) for g in batch]
     query = (projected[:, :CHAN].astype(F32) * 0.125).astype(BF16)
-    key = [projected[part[g], CHAN : 2 * CHAN] for g in four]
-    value = [projected[part[g], 2 * CHAN :] for g in four]
-    query_h = [by_head(query[part[g]]) for g in four]
-    da_h = [by_head(da_ref[g]) for g in four]
-    scores = [dot_nt(key[g], query_h[g]) + bias_ref[...] for g in four]
-    d_probs = [dot_nt(value[g], da_h[g]) for g in four]
-    tops = [jnp.max(scores[g], axis=0, keepdims=True) for g in four]
-    scores = [jnp.exp(scores[g] - tops[g]) for g in four]
-    scales = [1.0 / jnp.sum(scores[g], axis=0, keepdims=True) for g in four]
-    probs = [scores[g] * scales[g] for g in four]
-    probs_b = [probs[g].astype(BF16) for g in four]
-    crosses = [jnp.sum(probs[g] * d_probs[g], axis=0, keepdims=True) for g in four]
-    d_scores = [probs[g] * (d_probs[g] - crosses[g]) for g in four]
-    bias_sum_ref[...] += (d_scores[0] + d_scores[1]) + (d_scores[2] + d_scores[3])
-    d_scores_b = [d_scores[g].astype(BF16) for g in four]
-    attended = [dot_tn(probs_b[g], value[g]) for g in four]
-    d_query = [dot_tn(d_scores_b[g], key[g]) for g in four]
-    d_key = [dot(d_scores_b[g], query_h[g]) for g in four]
-    d_value = [dot(probs_b[g], da_h[g]) for g in four]
-    for g in four:
+    key = [projected[part[g], CHAN : 2 * CHAN] for g in batch]
+    value = [projected[part[g], 2 * CHAN :] for g in batch]
+    query_h = [by_head(query[part[g]]) for g in batch]
+    da_h = [by_head(da_ref[g]) for g in batch]
+    scores = [dot_nt(key[g], query_h[g]) + bias_ref[...] for g in batch]
+    d_probs = [dot_nt(value[g], da_h[g]) for g in batch]
+    tops = [jnp.max(scores[g], axis=0, keepdims=True) for g in batch]
+    scores = [jnp.exp(scores[g] - tops[g]) for g in batch]
+    scales = [1.0 / jnp.sum(scores[g], axis=0, keepdims=True) for g in batch]
+    probs = [scores[g] * scales[g] for g in batch]
+    probs_b = [probs[g].astype(BF16) for g in batch]
+    crosses = [jnp.sum(probs[g] * d_probs[g], axis=0, keepdims=True) for g in batch]
+    d_scores = [probs[g] * (d_probs[g] - crosses[g]) for g in batch]
+    bias_sum_ref[...] += sum(d_scores[1:], d_scores[0])
+    d_scores_b = [d_scores[g].astype(BF16) for g in batch]
+    attended = [dot_tn(probs_b[g], value[g]) for g in batch]
+    d_query = [dot_tn(d_scores_b[g], key[g]) for g in batch]
+    d_key = [dot(d_scores_b[g], query_h[g]) for g in batch]
+    d_value = [dot(probs_b[g], da_h[g]) for g in batch]
+    for g in batch:
         att_ref[part[g]] = diagonal(attended[g], low).astype(BF16)
         proj_ref[part[g], :CHAN] = (diagonal(d_query[g], low) * 0.125).astype(BF16)
         proj_ref[part[g], CHAN : 2 * CHAN] = d_key[g].astype(BF16)
         proj_ref[part[g], 2 * CHAN :] = d_value[g].astype(BF16)
     d_normed = dot_nt(proj_ref[...], wqkv_ref[...])
     d_tokens = layer_norm_back(normed, inv_std, d_normed).astype(BF16)
-    ds_ref[groups] = d_tokens.reshape(4, 64, CHAN)
-
-    @pl.when(step == n_groups // 4 - 1)
+    ds_ref[groups] = d_tokens.reshape(AT_ONCE, 64, CHAN)
+
+    @pl.when(step == n_groups // AT_ONCE - 1)
     def _():
         for s in range(0, 64, 16):
             for g in range(0, n_groups, 16):
@@ -398,13 +399,14 @@
     flat = n_groups * 64
     return pl.pallas_call(
         attention_body,
-        grid=(n_groups // 4,),
+        grid=(n_groups // AT_ONCE,),
         in_specs=[
-            whole(shape), band((4, 64, CHAN)), whole((CHAN, 3 * CHAN)), whole((64, CHAN)),
+            whole(shape), band((AT_ONCE, 64, CHAN)), whole((CHAN, 3 * CHAN)), whole((64, CHAN)),
             whole((256, 256)),
         ],
         out_specs=[
-            whole(shape), band((256, CHAN)), band((256, CHAN)), band((256, 3 * CHAN)), whole((64, CHAN)),
+            whole(shape), band((AT_ONCE * 64, CHAN)), band((AT_ONCE * 64, CHAN)),
+            band((AT_ONCE * 64, 3 * CHAN)), whole((64, CHAN)),
         ],
         out_shape=[
             jax.ShapeDtypeStruct(shape, BF16),

time: 225 us -> 224 us (level)
  no operation moved by 1% of the time
where the time goes in v9:
time: 224 us; the launch traced here: 222 us
  Pallas kernels  103 us (46%)
  starting transfers between devices  62.3 us (28%)
  waiting for transfers between devices  20.5 us (9%)
  blocking collectives  19 us (8%)
  local copies, waits for them, and re-layouts  11.7 us (5%)
  matrix products  4.24 us (2%)
    all_to_all x4, starting transfers between devices, exchange(): lax.all_to_all(pieces, ('lat', 'lon'), split_axis=0, concat_axis=0, axis_...  40.8 us
    pallas_call x1, Pallas kernels, expand_back(): pl.pallas_call(expand_back_body, grid=(STEPS,), in_specs=[cells, ROW_BEFO...  21.5 us
    all_to_all x1, blocking collectives, exchange(): lax.all_to_all(pieces, ('lat', 'lon'), split_axis=0, concat_axis=0, axis_...  19 us
    pallas_call x1, Pallas kernels, mix(): pl.pallas_call(mix_body, grid=(STEPS,), in_specs=[band((BLK, COLS, EXP)),...  17.6 us
    pallas_call x1, Pallas kernels, attention(): pl.pallas_call(attention_body, grid=(n_groups // AT_ONCE,), in_specs=[who...  14.1 us
    pallas_call x2, Pallas kernels, expand(): pl.pallas_call(functools.partial(expand_body, slopes=slopes), grid=(STEPS...  13.8 us
    all_to_all x4, waiting for transfers between devices, exchange(): lax.all_to_all(pieces, ('lat', 'lon'), split_axis=0, concat_axis=0, axis_...  13.6 us
    ppermute x4, starting transfers between devices, rows_of(): return (lax.ppermute(bottom, 'lat', south), lax.ppermute(top, 'lat', north))  9.12 us
  transfers between devices with their start and end apart: 16, of which 6 were waited for; matrix products, arithmetic and copies ran while one was open for 5% of the time, Pallas kernels for 28%

profile of v9, /device:TPU:1, one launch (start us, length us, event | category | flops | bytes accessed | tf_op | source)
XLA Modules:
  0.0 222.4 jit_solution(678706815099523136)
XLA Ops:
  0.6 1.0 fusion.7
  1.6 4.0 %collective-permute-start = (bf16[128,256]{1,0:T(8,128)(2,1)S(1)}, bf16[128,256]{1,0:T(8,128)(2,1)S(1)}, u32[]{:S(2)}, u32[]{:S(2)}) collective-permute-start(bf16[128,256]{1,0:T(8,128)(2,1)S(1)} %bitcast.43), channel_id=1, source_target_pairs={{0,16},{16,32},{32,48},{48,64},{64,80},{80,96},{96,112},{1,17},{17... | collective-permute-start | bytes 196616 | tf_op jit(solution)/shard_map/ppermute | solution.py:787
  5.7 1.3 collective-permute-start.1
  7.0 1.0 fusion.6
  8.1 6.2 %expand.1.cur_ref.before_ref.after_ref.hid_ref = bf16[32,64,1024]{2,1,0:T(8,128)(2,1)} custom-call(bf16[32,64,256]{2,1,0:T(8,128)(2,1)} %x_ref.8, bf16[256,1024]{1,0:T(8,128)(2,1)} %we_ref.7), custom_call_target="tpu_custom_call" | custom-call | flops 1073741824 | bytes 6291456 | tf_op jit(solution)/shard_map/expand/pallas_call | solution.py:110
  14.6 2.5 %collective-permute-start.2 = (bf16[2,40,256]{2,1,0:T(8,128)(2,1)S(1)}, bf16[2,40,256]{2,1,0:T(8,128)(2,1)S(1)}, u32[]{:S(2)}, u32[]{:S(2)}) collective-permute-start(bf16[2,40,256]{2,1,0:T(8,128)(2,1)S(1)} %get-tuple-element.77.own_east_ref), channel_id=1, source_target_pairs={{0,1},{1,2},{2,3},{3,4},{4,5},{5,6},{6,7},{7,8},{8,9},{9,10},{10,1... | collective-permute-start | bytes 122888 | tf_op jit(solution)/shard_map/ppermute | solution.py:817
  17.1 1.1 copy.33
  18.2 2.6 %collective-permute-done.3.east_ref = bf16[2,40,256]{2,1,0:T(8,128)(2,1)S(1)} collective-permute-done((bf16[2,40,256]{2,1,0:T(8,128)(2,1)S(1)}, bf16[2,40,256]{2,1,0:T(8,128)(2,1)S(1)}, u32[]{:S(2)}, u32[]{:S(2)}) %collective-permute-start.3) | collective-permute-done | bytes 40992 | tf_op jit(solution)/shard_map/ppermute | solution.py:818
  20.9 13.4 %all-to-all-start.1 = ((bf16[64,32,256]{2,1,0:T(8,128)(2,1)}), bf16[64,32,256]{2,1,0:T(8,128)(2,1)S(1)}, u32[]{:S(2)}, u32[]{:S(2)}) async-start(bf16[64,32,256]{2,1,0:T(8,128)(2,1)} %bitcast.13), calls=%async_computation.1 | async-start | bytes 2097152 | tf_op jit(solution)/shard_map/all_to_all | solution.py:829
  34.3 0.6 reshape.67.dk_ref
  34.9 17.6 %mix.1 = (bf16[64,32,256]{2,1,0:T(8,128)(2,1)}, bf16[32,64,1024]{2,1,0:T(8,128)(2,1)}, bf16[32,64,1024]{2,1,0:T(8,128)(2,1)}, f32[208,1024]{1,0:T(8,128)}) custom-call(bf16[32,64,1024]{2,1,0:T(8,128)(2,1)} %expand.1.cur_ref.before_ref.after_ref.hid_ref, bf16[32,64,1024]{2,1,0:T(8,128)(2,1)} %expand.1.cur_ref.before_ref.after_ref.hid_ref, ...), custom_call_target="tpu_custom_call" | custom-call | flops 1610612736 | bytes 18874368 | tf_op jit(solution)/shard_map/mix/pallas_call | solution.py:250
  52.5 10.0 %all-to-all-start = ((bf16[64,32,256]{2,1,0:T(8,128)(2,1)}), bf16[64,32,256]{2,1,0:T(8,128)(2,1)S(1)}, u32[]{:S(2)}, u32[]{:S(2)}) async-start(bf16[64,32,256]{2,1,0:T(8,128)(2,1)} %get-tuple-element.78), calls=%async_computation | async-start | bytes 2097152 | tf_op jit(solution)/shard_map/all_to_all | solution.py:829
  62.6 2.8 %fusion.4 = f32[64,4,64]{2,1,0:T(4,128)S(1)} fusion(f32[4,225,1]{1,0,2:T(4,128)S(1)} %reshape.75, s32[64,64]{0,1:T(8,128)S(1)} %copy-done.21), kind=kOutput, calls=%fused_computation.5 | convolution fusion | flops 45158400 | bytes 85520 | tf_op jit(solution)/shard_map/tsr,hr->sht/dot_general | solution.py:861
  65.5 0.8 reshape.69.bias_ref
  66.2 7.7 %expand_slopes.1.slope_ref = bf16[32,64,1024]{2,1,0:T(8,128)(2,1)} custom-call(bf16[32,64,256]{2,1,0:T(8,128)(2,1)} %x_ref.8, bf16[256,1024]{1,0:T(8,128)(2,1)} %we_ref.7), custom_call_target="tpu_custom_call" | custom-call | flops 1073741824 | bytes 6291456 | tf_op jit(solution)/shard_map/expand_slopes/pallas_call | solution.py:110
  73.9 0.8 prepare.1
  74.7 0.9 copy-done.3
  75.6 1.0 copy-done.9
  76.6 2.5 %all-to-all-done.x_ref = bf16[64,32,256]{2,1,0:T(8,128)(2,1)S(1)} async-done(((bf16[64,32,256]{2,1,0:T(8,128)(2,1)}), bf16[64,32,256]{2,1,0:T(8,128)(2,1)S(1)}, u32[]{:S(2)}, u32[]{:S(2)}) %all-to-all-start) | async-done | bytes 1048608 | tf_op jit(solution)/shard_map/all_to_all | solution.py:829
  79.1 1.0 copy-done.11
  80.1 14.1 %attention.1 = (bf16[64,32,256]{2,1,0:T(8,128)(2,1)}, bf16[2048,256]{1,0:T(8,128)(2,1)}, bf16[2048,256]{1,0:T(8,128)(2,1)}, bf16[2048,768]{1,0:T(8,128)(2,1)}, f32[64,256]{1,0:T(8,128)}) custom-call(bf16[64,32,256]{2,1,0:T(8,128)(2,1)} %copy-done.11, bf16[32,64,256]{2,1,0:T(8,128)(2,1)} %copy-done.9, bf16[256,768]{1,0:T(8,128)(2,1)} %wqkv_ref.1, ...), custom_call_target="tpu_custom_call" | custom-call | flops 2684354560 | bytes 8388608 | tf_op jit(solution)/shard_map/attention/pallas_call | solution.py:400
  94.2 6.9 %all-to-all-start.2 = ((bf16[64,32,256]{2,1,0:T(8,128)(2,1)}), bf16[64,32,256]{2,1,0:T(8,128)(2,1)S(1)}, u32[]{:S(2)}, u32[]{:S(2)}) async-start(bf16[64,32,256]{2,1,0:T(8,128)(2,1)} %get-tuple-element.85), calls=%async_computation.2 | async-start | bytes 2097152 | tf_op jit(solution)/shard_map/all_to_all | solution.py:829
  101.2 0.9 reshape.71
  102.2 1.4 fusion.5
  103.7 0.8 pad.4.extra_ref
  104.6 7.1 %mixed_slopes.1.slope_ref = bf16[32,64,1024]{2,1,0:T(8,128)(2,1)} custom-call(bf16[32,64,1024]{2,1,0:T(8,128)(2,1)} %get-tuple-element.92.pre_ref), custom_call_target="tpu_custom_call" | custom-call | flops 41943040 | bytes 8388608 | tf_op jit(solution)/shard_map/mixed_slopes/pallas_call | solution.py:131
  111.7 5.3 %attention_sums.1.refs_0_ = bf16[128,16,128]{2,1,0:T(8,128)(2,1)} custom-call(bf16[2048,256]{1,0:T(8,128)(2,1)} %get-tuple-element.86.att_ref, bf16[2048,256]{1,0:T(8,128)(2,1)} %bitcast.36, bf16[2048,256]{1,0:T(8,128)(2,1)} %get-tuple-element.88.norm_ref, bf16[2048,768]{1,0:T(8,128)(2,1)} %get-tuple-element.89.proj_ref), custom_call_target="tpu_custom_call" | custom-call | flops 1073741824 | bytes 6291456 | tf_op jit(solution)/shard_map/attention_sums/pallas_call | solution.py:446
  116.9 1.4 all-to-all-done.2.db_ref
  118.4 1.7 edges.1
  120.1 2.5 %collective-permute-start.4 = (bf16[64,256]{1,0:T(8,128)(2,1)S(1)}, bf16[64,256]{1,0:T(8,128)(2,1)S(1)}, u32[]{:S(2)}, u32[]{:S(2)}) collective-permute-start(bf16[64,256]{1,0:T(8,128)(2,1)S(1)} %get-tuple-element.94), channel_id=1, source_target_pairs={{0,16},{16,32},{32,48},{48,64},{64,80},{80,96},{96,112},{1,17},{17... | collective-permute-start | bytes 98312 | tf_op jit(solution)/shard_map/ppermute | solution.py:787
  122.6 1.3 collective-permute-start.5
  123.9 5.4 %project_sum.1.refs_2_ = bf16[128,16,128]{2,1,0:T(8,128)(2,1)} custom-call(bf16[32,64,256]{2,1,0:T(8,128)(2,1)} %cot_ref.5, bf16[64,32,256]{2,1,0:T(8,128)(2,1)} %copy-done, bf16[32,64,1024]{2,1,0:T(8,128)(2,1)} %get-tuple-element.96.mixed_ref), custom_call_target="tpu_custom_call" | custom-call | flops 1073741824 | bytes 8388608 | tf_op jit(solution)/shard_map/project_sum/pallas_call | solution.py:510
  130.4 1.7 collective-permute-start.6
  132.0 6.4 %project_back.1.cur_ref.before_ref.after_ref = bf16[32,64,1024]{2,1,0:T(8,128)(2,1)} custom-call(bf16[32,64,256]{2,1,0:T(8,128)(2,1)} %cot_ref.5, bf16[64,32,256]{2,1,0:T(8,128)(2,1)} %copy-done, bf16[32,64,1024]{2,1,0:T(8,128)(2,1)} %mixed_slopes.1.slope_ref, bf16[1024,256]{1,0:T(8,128)(2,1)} %wp_ref.5), custom_call_target="tpu_custom_call" | custom-call | flops 1073741824 | bytes 10485760 | tf_op jit(solution)/shard_map/project_back/pallas_call | solution.py:479
  138.4 0.7 pad_maximum_fusion.halo_ref
  139.1 0.7 broadcast_in_dim.15.dkb_ref
  139.8 21.5 %expand_back.1 = (bf16[2048,1024]{1,0:T(8,128)(2,1)}, bf16[128,24,128]{2,1,0:T(8,128)(2,1)}) custom-call(bf16[32,64,1024]{2,1,0:T(8,128)(2,1)} %project_back.1.cur_ref.before_ref.after_ref, bf16[32,64,1024]{2,1,0:T(8,128)(2,1)} %project_back.1.cur_ref.before_ref.after_ref, bf16[32,64,1024]{2,1,0:T(8,128)(2,1)} %project_back.1.cur_ref.before_ref.after_ref, ...), custom_call_target="tpu_custom_call" | custom-call | flops 1073741824 | bytes 20971520 | tf_op jit(solution)/shard_map/expand_back/pallas_call | solution.py:605
  161.3 3.1 %collective-permute-start.10 = (bf16[128,24,128]{2,1,0:T(8,128)(2,1)}, bf16[128,24,128]{2,1,0:T(8,128)(2,1)S(1)}, u32[]{:S(2)}, u32[]{:S(2)}) collective-permute-start(bf16[128,24,128]{2,1,0:T(8,128)(2,1)} %get-tuple-element.113.refs_4_), channel_id=1, source_target_pairs={{0,1},{1,0},{2,3},{3,2},{4,5},{5,4},{6,7},{7,6},{8,9},{9,8},{10,11... | collective-permute-start | bytes 2359304 | tf_op jit(solution)/shard_map/ppermute | solution.py:845
  164.5 2.1 collective-permute-done.10.refs_5_
  166.6 1.1 copy-done.4
  167.7 1.1 join.1
  168.9 10.5 %all-to-all-start.3 = ((bf16[64,56,128]{2,1,0:T(8,128)(2,1)}), bf16[64,56,128]{2,1,0:T(8,128)(2,1)S(1)}, u32[]{:S(2)}, u32[]{:S(2)}) async-start(bf16[64,56,128]{2,1,0:T(8,128)(2,1)} %join.1), calls=%async_computation.3 | async-start | bytes 1835008 | tf_op jit(solution)/shard_map/all_to_all | solution.py:829
  179.4 5.9 %finish.1 = bf16[32,64,256]{2,1,0:T(8,128)(2,1)} custom-call(bf16[2048,1024]{1,0:T(8,128)(2,1)} %get-tuple-element.116.dpre_ref, bf16[32,64,256]{2,1,0:T(8,128)(2,1)} %x_ref.8, bf16[32,64,256]{2,1,0:T(8,128)(2,1)} %cot_ref.5, bf16[64,32,256]{2,1,0:T(8,128)(2,1)} %copy-done, bf16[256,1024]{1,0:T(8,128)(2,1)} %we_ref.7), custom_call_target="tpu_custom_call" | custom-call | flops 1073741824 | bytes 9437184 | tf_op jit(solution)/shard_map/finish/pallas_call | solution.py:637
  185.3 9.7 %all-to-all-done.3.terms_ref = bf16[64,56,128]{2,1,0:T(8,128)(2,1)S(1)} async-done(((bf16[64,56,128]{2,1,0:T(8,128)(2,1)}), bf16[64,56,128]{2,1,0:T(8,128)(2,1)S(1)}, u32[]{:S(2)}, u32[]{:S(2)}) %all-to-all-start.3) | async-done | bytes 917536 | tf_op jit(solution)/shard_map/all_to_all | solution.py:829
  195.2 19.0 %all_to_all.25.own_ref = bf16[64,56,128]{2,1,0:T(8,128)(2,1)S(1)} all-to-all(bf16[64,56,128]{2,1,0:T(8,128)(2,1)S(1)} %fold.1), channel_id=1, replica_groups={{0,2,4,6,8,10,12,14,16,18,20,22,24,26,28,30,32,34,36,38,40,42,44,46,48,..., dimensions={0} | all-to-all | bytes 1835008 | tf_op jit(solution)/shard_map/all_to_all | solution.py:829
  214.2 4.1 %collective-permute-start.11 = (bf16[64,56,128]{2,1,0:T(8,128)(2,1)S(1)}, bf16[64,56,128]{2,1,0:T(8,128)(2,1)S(1)}, u32[]{:S(2)}, u32[]{:S(2)}) collective-permute-start(bf16[64,56,128]{2,1,0:T(8,128)(2,1)S(1)} %all_to_all.25.own_ref), channel_id=1, source_target_pairs={{0,1},{1,0},{2,3},{3,2},{4,5},{5,4},{6,7},{7,6},{8,9},{9,8},{10,11... | collective-permute-start | bytes 2752520 | tf_op jit(solution)/shard_map/ppermute | solution.py:845
  218.3 2.1 collective-permute-done.11.other_ref
  220.4 2.0 unfold.1
  (70 shorter events, 1.9 us)
Async XLA Ops:
  0.6 16.5 %copy-start.10 = (bf16[32,64,256]{2,1,0:T(8,128)(2,1)S(1)}, bf16[32,64,256]{2,1,0:T(8,128)(2,1)}, u32[]{:S(2)}) copy-start(bf16[32,64,256]{2,1,0:T(8,128)(2,1)} %cot_ref.5) | copy-start | bytes 3145732
  1.6 12.7 %collective-permute-start = (bf16[128,256]{1,0:T(8,128)(2,1)S(1)}, bf16[128,256]{1,0:T(8,128)(2,1)S(1)}, u32[]{:S(2)}, u32[]{:S(2)}) collective-permute-start(bf16[128,256]{1,0:T(8,128)(2,1)S(1)} %bitcast.43), channel_id=1, source_target_pairs={{0,16},{16,32},{32,48},{48,64},{64,80},{80,96},{96,112},{1,17},{17... | collective-permute-start | bytes 196616 | tf_op jit(solution)/shard_map/ppermute | solution.py:787
  5.7 8.6 %collective-permute-start.1 = (bf16[128,256]{1,0:T(8,128)(2,1)S(1)}, bf16[128,256]{1,0:T(8,128)(2,1)S(1)}, u32[]{:S(2)}, u32[]{:S(2)}) collective-permute-start(bf16[128,256]{1,0:T(8,128)(2,1)S(1)} %bitcast.42), channel_id=1, source_target_pairs={{16,0},{32,16},{48,32},{64,48},{80,64},{96,80},{112,96},{17,1},{33... | collective-permute-start | bytes 196616 | tf_op jit(solution)/shard_map/ppermute | solution.py:787
  8.1 26.1 %copy-start.17 = (f32[3,3,1024]{2,1,0:T(4,128)S(1)}, f32[3,3,1024]{2,1,0:T(4,128)}, u32[]{:S(2)}) copy-start(f32[3,3,1024]{2,1,0:T(4,128)} %param.16) | copy-start | bytes 110596
  14.3 20.6 %copy-start.13 = (bf16[128,256]{1,0:T(8,128)(2,1)}, bf16[128,256]{1,0:T(8,128)(2,1)S(1)}, u32[]{:S(2)}) copy-start(bf16[128,256]{1,0:T(8,128)(2,1)S(1)} %collective-permute-done) | copy-start | bytes 196612
  14.3 20.6 %copy-start.14 = (bf16[128,256]{1,0:T(8,128)(2,1)}, bf16[128,256]{1,0:T(8,128)(2,1)S(1)}, u32[]{:S(2)}) copy-start(bf16[128,256]{1,0:T(8,128)(2,1)S(1)} %collective-permute-done.1) | copy-start | bytes 196612
  14.6 20.3 %copy-start.15 = (bf16[2,40,256]{2,1,0:T(8,128)(2,1)}, bf16[2,40,256]{2,1,0:T(8,128)(2,1)S(1)}, u32[]{:S(2)}) copy-start(bf16[2,40,256]{2,1,0:T(8,128)(2,1)S(1)} %get-tuple-element.76.own_west_ref) | copy-start | bytes 122884
  14.6 20.3 %copy-start.16 = (bf16[2,40,256]{2,1,0:T(8,128)(2,1)}, bf16[2,40,256]{2,1,0:T(8,128)(2,1)S(1)}, u32[]{:S(2)}) copy-start(bf16[2,40,256]{2,1,0:T(8,128)(2,1)S(1)} %get-tuple-element.77.own_east_ref) | copy-start | bytes 122884
  14.6 3.7 %collective-permute-start.2 = (bf16[2,40,256]{2,1,0:T(8,128)(2,1)S(1)}, bf16[2,40,256]{2,1,0:T(8,128)(2,1)S(1)}, u32[]{:S(2)}, u32[]{:S(2)}) collective-permute-start(bf16[2,40,256]{2,1,0:T(8,128)(2,1)S(1)} %get-tuple-element.77.own_east_ref), channel_id=1, source_target_pairs={{0,1},{1,2},{2,3},{3,4},{4,5},{5,6},{6,7},{7,8},{8,9},{9,10},{10,1... | collective-permute-start | bytes 122888 | tf_op jit(solution)/shard_map/ppermute | solution.py:817
  17.1 3.7 %collective-permute-start.3 = (bf16[2,40,256]{2,1,0:T(8,128)(2,1)S(1)}, bf16[2,40,256]{2,1,0:T(8,128)(2,1)S(1)}, u32[]{:S(2)}, u32[]{:S(2)}) collective-permute-start(bf16[2,40,256]{2,1,0:T(8,128)(2,1)S(1)} %get-tuple-element.76.own_west_ref), channel_id=1, source_target_pairs={{1,0},{2,1},{3,2},{4,3},{5,4},{6,5},{7,6},{8,7},{9,8},{10,9},{11,1... | collective-permute-start | bytes 122888 | tf_op jit(solution)/shard_map/ppermute | solution.py:818
  18.2 16.7 %copy-start.18 = (bf16[2,40,256]{2,1,0:T(8,128)(2,1)}, bf16[2,40,256]{2,1,0:T(8,128)(2,1)S(1)}, u32[]{:S(2)}) copy-start(bf16[2,40,256]{2,1,0:T(8,128)(2,1)S(1)} %collective-permute-done.2.west_ref) | copy-start | bytes 122884
  20.9 14.1 %copy-start.19 = (bf16[2,40,256]{2,1,0:T(8,128)(2,1)}, bf16[2,40,256]{2,1,0:T(8,128)(2,1)S(1)}, u32[]{:S(2)}) copy-start(bf16[2,40,256]{2,1,0:T(8,128)(2,1)S(1)} %collective-permute-done.3.east_ref) | copy-start | bytes 122884
  20.9 31.7 %all-to-all-start.1 = ((bf16[64,32,256]{2,1,0:T(8,128)(2,1)}), bf16[64,32,256]{2,1,0:T(8,128)(2,1)S(1)}, u32[]{:S(2)}, u32[]{:S(2)}) async-start(bf16[64,32,256]{2,1,0:T(8,128)(2,1)} %bitcast.13), calls=%async_computation.1 | async-start | bytes 2097152 | tf_op jit(solution)/shard_map/all_to_all | solution.py:829
  34.9 27.6 %copy-start.20 = (f32[4,15,15]{2,0,1:T(4,128)S(1)}, f32[4,15,15]{2,0,1:T(4,128)}, u32[]{:S(2)}) copy-start(f32[4,15,15]{2,0,1:T(4,128)} %param.20) | copy-start | bytes 10804
  34.9 27.7 %copy-start.21 = (s32[64,64]{0,1:T(8,128)S(1)}, s32[64,64]{0,1:T(8,128)}, u32[]{:S(2)}) copy-start(s32[64,64]{0,1:T(8,128)} %constant.21.clone) | copy-start | bytes 49156
  52.5 21.4 %copy-start.7 = (bf16[256,256]{1,0:T(8,128)(2,1)S(1)}, bf16[256,256]{1,0:T(8,128)(2,1)}, u32[]{:S(2)}) copy-start(bf16[256,256]{1,0:T(8,128)(2,1)} %wout_ref.1) | copy-start | bytes 393220
  52.5 21.4 %copy-start.8 = (bf16[256,256]{1,0:T(8,128)(2,1)S(1)}, bf16[256,256]{1,0:T(8,128)(2,1)}, u32[]{:S(2)}) copy-start(bf16[256,256]{1,0:T(8,128)(2,1)} %constant.22.clone.swap_ref) | copy-start | bytes 393220
  52.5 26.6 %all-to-all-start = ((bf16[64,32,256]{2,1,0:T(8,128)(2,1)}), bf16[64,32,256]{2,1,0:T(8,128)(2,1)S(1)}, u32[]{:S(2)}, u32[]{:S(2)}) async-start(bf16[64,32,256]{2,1,0:T(8,128)(2,1)} %get-tuple-element.78), calls=%async_computation | async-start | bytes 2097152 | tf_op jit(solution)/shard_map/all_to_all | solution.py:829
  74.7 1.0 copy-start.3
  75.6 1.0 copy-start.9
  79.1 1.0 copy-start.11
  94.2 24.1 %all-to-all-start.2 = ((bf16[64,32,256]{2,1,0:T(8,128)(2,1)}), bf16[64,32,256]{2,1,0:T(8,128)(2,1)S(1)}, u32[]{:S(2)}, u32[]{:S(2)}) async-start(bf16[64,32,256]{2,1,0:T(8,128)(2,1)} %get-tuple-element.85), calls=%async_computation.2 | async-start | bytes 2097152 | tf_op jit(solution)/shard_map/all_to_all | solution.py:829
  111.7 6.7 %copy-start.5 = (bf16[32,512]{1,0:T(8,128)(2,1)S(1)}, bf16[32,512]{1,0:T(8,128)(2,1)}, u32[]{:S(2)}) copy-start(bf16[32,512]{1,0:T(8,128)(2,1)} %constant.23.clone.first_ref) | copy-start | bytes 98308
  111.7 6.7 %copy-start.6 = (bf16[32,512]{1,0:T(8,128)(2,1)S(1)}, bf16[32,512]{1,0:T(8,128)(2,1)}, u32[]{:S(2)}) copy-start(bf16[32,512]{1,0:T(8,128)(2,1)} %constant.24.clone.last_ref) | copy-start | bytes 98308
  118.3 1.8 copy-start
  120.1 9.2 %copy-start.1 = (bf16[128,16,128]{2,1,0:T(8,128)(2,1)S(1)}, bf16[128,16,128]{2,1,0:T(8,128)(2,1)}, u32[]{:S(2)}) copy-start(bf16[128,16,128]{2,1,0:T(8,128)(2,1)} %attention_sums.1.refs_0_) | copy-start | bytes 1572868
  120.1 9.2 %collective-permute-start.4 = (bf16[64,256]{1,0:T(8,128)(2,1)S(1)}, bf16[64,256]{1,0:T(8,128)(2,1)S(1)}, u32[]{:S(2)}, u32[]{:S(2)}) collective-permute-start(bf16[64,256]{1,0:T(8,128)(2,1)S(1)} %get-tuple-element.94), channel_id=1, source_target_pairs={{0,16},{16,32},{32,48},{48,64},{64,80},{80,96},{96,112},{1,17},{17... | collective-permute-start | bytes 98312 | tf_op jit(solution)/shard_map/ppermute | solution.py:787
  122.6 6.7 %collective-permute-start.5 = (bf16[64,256]{1,0:T(8,128)(2,1)S(1)}, bf16[64,256]{1,0:T(8,128)(2,1)S(1)}, u32[]{:S(2)}, u32[]{:S(2)}) collective-permute-start(bf16[64,256]{1,0:T(8,128)(2,1)S(1)} %get-tuple-element.95), channel_id=1, source_target_pairs={{16,0},{32,16},{48,32},{64,48},{80,64},{96,80},{112,96},{17,1},{33... | collective-permute-start | bytes 98312 | tf_op jit(solution)/shard_map/ppermute | solution.py:787
  129.4 9.7 %collective-permute-start.8 = (bf16[128,16,128]{2,1,0:T(8,128)(2,1)S(1)}, bf16[128,16,128]{2,1,0:T(8,128)(2,1)S(1)}, u32[]{:S(2)}, u32[]{:S(2)}) collective-permute-start(bf16[128,16,128]{2,1,0:T(8,128)(2,1)S(1)} %copy-done.1), channel_id=1, source_target_pairs={{0,1},{1,0},{2,3},{3,2},{4,5},{5,4},{6,7},{7,6},{8,9},{9,8},{10,11... | collective-permute-start | bytes 1572872 | tf_op jit(solution)/shard_map/ppermute | solution.py:845
  129.5 9.6 %collective-permute-start.9 = (bf16[128,16,128]{2,1,0:T(8,128)(2,1)}, bf16[128,16,128]{2,1,0:T(8,128)(2,1)S(1)}, u32[]{:S(2)}, u32[]{:S(2)}) collective-permute-start(bf16[128,16,128]{2,1,0:T(8,128)(2,1)} %project_sum.1.refs_2_), channel_id=1, source_target_pairs={{0,1},{1,0},{2,3},{3,2},{4,5},{5,4},{6,7},{7,6},{8,9},{9,8},{10,11... | collective-permute-start | bytes 1572872 | tf_op jit(solution)/shard_map/ppermute | solution.py:845
  130.0 8.3 %collective-permute-start.7 = (bf16[40,256]{1,0:T(8,128)(2,1)S(1)}, bf16[40,256]{1,0:T(8,128)(2,1)S(1)}, u32[]{:S(2)}, u32[]{:S(2)}) collective-permute-start(bf16[40,256]{1,0:T(8,128)(2,1)S(1)} %get-tuple-element.138), channel_id=1, source_target_pairs={{1,0},{2,1},{3,2},{4,3},{5,4},{6,5},{7,6},{8,7},{9,8},{10,9},{11,1... | collective-permute-start | bytes 61448 | tf_op jit(solution)/shard_map/ppermute | solution.py:796
  130.4 8.7 %copy-start.12 = (f32[9,1024]{1,0:T(8,128)S(1)}, f32[9,1024]{1,0:T(8,128)}, u32[]{:S(2)}) copy-start(f32[9,1024]{1,0:T(8,128)} %reshape.67.dk_ref) | copy-start | bytes 110596
  130.4 8.0 %collective-permute-start.6 = (bf16[40,256]{1,0:T(8,128)(2,1)S(1)}, bf16[40,256]{1,0:T(8,128)(2,1)S(1)}, u32[]{:S(2)}, u32[]{:S(2)}) collective-permute-start(bf16[40,256]{1,0:T(8,128)(2,1)S(1)} %get-tuple-element.137), channel_id=1, source_target_pairs={{0,1},{1,2},{2,3},{3,4},{4,5},{5,6},{6,7},{7,8},{8,9},{9,10},{10,1... | collective-permute-start | bytes 61448 | tf_op jit(solution)/shard_map/ppermute | solution.py:793
  139.8 26.8 %copy-start.2 = (bf16[128,16,128]{2,1,0:T(8,128)(2,1)S(1)}, bf16[128,16,128]{2,1,0:T(8,128)(2,1)}, u32[]{:S(2)}) copy-start(bf16[128,16,128]{2,1,0:T(8,128)(2,1)} %project_sum.1.refs_2_) | copy-start | bytes 1572868
  161.3 5.3 %collective-permute-start.10 = (bf16[128,24,128]{2,1,0:T(8,128)(2,1)}, bf16[128,24,128]{2,1,0:T(8,128)(2,1)S(1)}, u32[]{:S(2)}, u32[]{:S(2)}) collective-permute-start(bf16[128,24,128]{2,1,0:T(8,128)(2,1)} %get-tuple-element.113.refs_4_), channel_id=1, source_target_pairs={{0,1},{1,0},{2,3},{3,2},{4,5},{5,4},{6,7},{7,6},{8,9},{9,8},{10,11... | collective-permute-start | bytes 2359304 | tf_op jit(solution)/shard_map/ppermute | solution.py:845
  166.6 1.1 copy-start.4
  168.9 26.2 %all-to-all-start.3 = ((bf16[64,56,128]{2,1,0:T(8,128)(2,1)}), bf16[64,56,128]{2,1,0:T(8,128)(2,1)S(1)}, u32[]{:S(2)}, u32[]{:S(2)}) async-start(bf16[64,56,128]{2,1,0:T(8,128)(2,1)} %join.1), calls=%async_computation.3 | async-start | bytes 1835008 | tf_op jit(solution)/shard_map/all_to_all | solution.py:829
  214.2 6.2 %collective-permute-start.11 = (bf16[64,56,128]{2,1,0:T(8,128)(2,1)S(1)}, bf16[64,56,128]{2,1,0:T(8,128)(2,1)S(1)}, u32[]{:S(2)}, u32[]{:S(2)}) collective-permute-start(bf16[64,56,128]{2,1,0:T(8,128)(2,1)S(1)} %all_to_all.25.own_ref), channel_id=1, source_target_pairs={{0,1},{1,0},{2,3},{3,2},{4,5},{5,4},{6,7},{7,6},{8,9},{9,8},{10,11... | collective-permute-start | bytes 2752520 | tf_op jit(solution)/shard_map/ppermute | solution.py:845

commit v10 on v9

--- a/solution.py
+++ b/solution.py
@@ -23,7 +23,7 @@
 EDGE = 40
 HALO = 2 * COLS + 2 * EDGE
 LONG = 72
-AT_ONCE = 8
+AT_ONCE = 16
 JOINED = (64, 56, 128)
 
 

time: 224 us -> 223 us (level)
  no operation moved by 1% of the time
where the time goes in v10:
time: 223 us; the launch traced here: 222 us
  Pallas kernels  103 us (46%)
  starting transfers between devices  62.3 us (28%)
  waiting for transfers between devices  20.3 us (9%)
  blocking collectives  19 us (9%)
  local copies, waits for them, and re-layouts  11.7 us (5%)
  matrix products  4.24 us (2%)
    all_to_all x4, starting transfers between devices, exchange(): lax.all_to_all(pieces, ('lat', 'lon'), split_axis=0, concat_axis=0, axis_...  41 us
    pallas_call x1, Pallas kernels, expand_back(): pl.pallas_call(expand_back_body, grid=(STEPS,), in_specs=[cells, ROW_BEFO...  21.5 us
    all_to_all x1, blocking collectives, exchange(): lax.all_to_all(pieces, ('lat', 'lon'), split_axis=0, concat_axis=0, axis_...  19 us
    pallas_call x1, Pallas kernels, mix(): pl.pallas_call(mix_body, grid=(STEPS,), in_specs=[band((BLK, COLS, EXP)),...  17.6 us
    pallas_call x2, Pallas kernels, expand(): pl.pallas_call(functools.partial(expand_body, slopes=slopes), grid=(STEPS...  13.8 us
    pallas_call x1, Pallas kernels, attention(): pl.pallas_call(attention_body, grid=(n_groups // AT_ONCE,), in_specs=[who...  13.7 us
    all_to_all x4, waiting for transfers between devices, exchange(): lax.all_to_all(pieces, ('lat', 'lon'), split_axis=0, concat_axis=0, axis_...  13.4 us
    ppermute x4, starting transfers between devices, rows_of(): return (lax.ppermute(bottom, 'lat', south), lax.ppermute(top, 'lat', north))  9.12 us
  transfers between devices with their start and end apart: 16, of which 6 were waited for; matrix products, arithmetic and copies ran while one was open for 5% of the time, Pallas kernels for 28%

profile of v10, /device:TPU:1, one launch (start us, length us, event | category | flops | bytes accessed | tf_op | source)
XLA Modules:
  0.0 221.8 jit_solution(3240013987478207254)
XLA Ops:
  0.6 1.0 fusion.7
  1.6 4.0 %collective-permute-start = (bf16[128,256]{1,0:T(8,128)(2,1)S(1)}, bf16[128,256]{1,0:T(8,128)(2,1)S(1)}, u32[]{:S(2)}, u32[]{:S(2)}) collective-permute-start(bf16[128,256]{1,0:T(8,128)(2,1)S(1)} %bitcast.43), channel_id=1, source_target_pairs={{0,16},{16,32},{32,48},{48,64},{64,80},{80,96},{96,112},{1,17},{17... | collective-permute-start | bytes 196616 | tf_op jit(solution)/shard_map/ppermute | solution.py:787
  5.7 1.3 collective-permute-start.1
  7.0 1.0 fusion.6
  8.1 6.2 %expand.1.cur_ref.before_ref.after_ref.hid_ref = bf16[32,64,1024]{2,1,0:T(8,128)(2,1)} custom-call(bf16[32,64,256]{2,1,0:T(8,128)(2,1)} %x_ref.8, bf16[256,1024]{1,0:T(8,128)(2,1)} %we_ref.7), custom_call_target="tpu_custom_call" | custom-call | flops 1073741824 | bytes 6291456 | tf_op jit(solution)/shard_map/expand/pallas_call | solution.py:110
  14.6 2.5 %collective-permute-start.2 = (bf16[2,40,256]{2,1,0:T(8,128)(2,1)S(1)}, bf16[2,40,256]{2,1,0:T(8,128)(2,1)S(1)}, u32[]{:S(2)}, u32[]{:S(2)}) collective-permute-start(bf16[2,40,256]{2,1,0:T(8,128)(2,1)S(1)} %get-tuple-element.77.own_east_ref), channel_id=1, source_target_pairs={{0,1},{1,2},{2,3},{3,4},{4,5},{5,6},{6,7},{7,8},{8,9},{9,10},{10,1... | collective-permute-start | bytes 122888 | tf_op jit(solution)/shard_map/ppermute | solution.py:817
  17.1 1.1 copy.33
  18.2 2.6 %collective-permute-done.3.east_ref = bf16[2,40,256]{2,1,0:T(8,128)(2,1)S(1)} collective-permute-done((bf16[2,40,256]{2,1,0:T(8,128)(2,1)S(1)}, bf16[2,40,256]{2,1,0:T(8,128)(2,1)S(1)}, u32[]{:S(2)}, u32[]{:S(2)}) %collective-permute-start.3) | collective-permute-done | bytes 40992 | tf_op jit(solution)/shard_map/ppermute | solution.py:818
  20.9 13.4 %all-to-all-start.1 = ((bf16[64,32,256]{2,1,0:T(8,128)(2,1)}), bf16[64,32,256]{2,1,0:T(8,128)(2,1)S(1)}, u32[]{:S(2)}, u32[]{:S(2)}) async-start(bf16[64,32,256]{2,1,0:T(8,128)(2,1)} %bitcast.13), calls=%async_computation.1 | async-start | bytes 2097152 | tf_op jit(solution)/shard_map/all_to_all | solution.py:829
  34.3 0.6 reshape.67.dk_ref
  34.9 17.6 %mix.1 = (bf16[64,32,256]{2,1,0:T(8,128)(2,1)}, bf16[32,64,1024]{2,1,0:T(8,128)(2,1)}, bf16[32,64,1024]{2,1,0:T(8,128)(2,1)}, f32[208,1024]{1,0:T(8,128)}) custom-call(bf16[32,64,1024]{2,1,0:T(8,128)(2,1)} %expand.1.cur_ref.before_ref.after_ref.hid_ref, bf16[32,64,1024]{2,1,0:T(8,128)(2,1)} %expand.1.cur_ref.before_ref.after_ref.hid_ref, ...), custom_call_target="tpu_custom_call" | custom-call | flops 1610612736 | bytes 18874368 | tf_op jit(solution)/shard_map/mix/pallas_call | solution.py:250
  52.5 10.0 %all-to-all-start = ((bf16[64,32,256]{2,1,0:T(8,128)(2,1)}), bf16[64,32,256]{2,1,0:T(8,128)(2,1)S(1)}, u32[]{:S(2)}, u32[]{:S(2)}) async-start(bf16[64,32,256]{2,1,0:T(8,128)(2,1)} %get-tuple-element.78), calls=%async_computation | async-start | bytes 2097152 | tf_op jit(solution)/shard_map/all_to_all | solution.py:829
  62.6 2.8 %fusion.4 = f32[64,4,64]{2,1,0:T(4,128)S(1)} fusion(f32[4,225,1]{1,0,2:T(4,128)S(1)} %reshape.75, s32[64,64]{0,1:T(8,128)S(1)} %copy-done.21), kind=kOutput, calls=%fused_computation.5 | convolution fusion | flops 45158400 | bytes 85520 | tf_op jit(solution)/shard_map/tsr,hr->sht/dot_general | solution.py:861
  65.5 0.8 reshape.69.bias_ref
  66.2 7.7 %expand_slopes.1.slope_ref = bf16[32,64,1024]{2,1,0:T(8,128)(2,1)} custom-call(bf16[32,64,256]{2,1,0:T(8,128)(2,1)} %x_ref.8, bf16[256,1024]{1,0:T(8,128)(2,1)} %we_ref.7), custom_call_target="tpu_custom_call" | custom-call | flops 1073741824 | bytes 6291456 | tf_op jit(solution)/shard_map/expand_slopes/pallas_call | solution.py:110
  73.9 0.8 prepare.1
  74.7 0.9 copy-done.3
  75.6 1.0 copy-done.9
  76.6 2.5 %all-to-all-done.x_ref = bf16[64,32,256]{2,1,0:T(8,128)(2,1)S(1)} async-done(((bf16[64,32,256]{2,1,0:T(8,128)(2,1)}), bf16[64,32,256]{2,1,0:T(8,128)(2,1)S(1)}, u32[]{:S(2)}, u32[]{:S(2)}) %all-to-all-start) | async-done | bytes 1048608 | tf_op jit(solution)/shard_map/all_to_all | solution.py:829
  79.1 1.0 copy-done.11
  80.1 13.7 %attention.1 = (bf16[64,32,256]{2,1,0:T(8,128)(2,1)}, bf16[2048,256]{1,0:T(8,128)(2,1)}, bf16[2048,256]{1,0:T(8,128)(2,1)}, bf16[2048,768]{1,0:T(8,128)(2,1)}, f32[64,256]{1,0:T(8,128)}) custom-call(bf16[64,32,256]{2,1,0:T(8,128)(2,1)} %copy-done.11, bf16[32,64,256]{2,1,0:T(8,128)(2,1)} %copy-done.9, bf16[256,768]{1,0:T(8,128)(2,1)} %wqkv_ref.1, ...), custom_call_target="tpu_custom_call" | custom-call | flops 2684354560 | bytes 8388608 | tf_op jit(solution)/shard_map/attention/pallas_call | solution.py:400
  93.8 7.2 %all-to-all-start.2 = ((bf16[64,32,256]{2,1,0:T(8,128)(2,1)}), bf16[64,32,256]{2,1,0:T(8,128)(2,1)S(1)}, u32[]{:S(2)}, u32[]{:S(2)}) async-start(bf16[64,32,256]{2,1,0:T(8,128)(2,1)} %get-tuple-element.85), calls=%async_computation.2 | async-start | bytes 2097152 | tf_op jit(solution)/shard_map/all_to_all | solution.py:829
  101.1 0.9 reshape.71
  102.0 1.4 fusion.5
  103.6 0.8 pad.4.extra_ref
  104.4 7.1 %mixed_slopes.1.slope_ref = bf16[32,64,1024]{2,1,0:T(8,128)(2,1)} custom-call(bf16[32,64,1024]{2,1,0:T(8,128)(2,1)} %get-tuple-element.92.pre_ref), custom_call_target="tpu_custom_call" | custom-call | flops 41943040 | bytes 8388608 | tf_op jit(solution)/shard_map/mixed_slopes/pallas_call | solution.py:131
  111.5 5.3 %attention_sums.1.refs_0_ = bf16[128,16,128]{2,1,0:T(8,128)(2,1)} custom-call(bf16[2048,256]{1,0:T(8,128)(2,1)} %get-tuple-element.86.att_ref, bf16[2048,256]{1,0:T(8,128)(2,1)} %bitcast.36, bf16[2048,256]{1,0:T(8,128)(2,1)} %get-tuple-element.88.norm_ref, bf16[2048,768]{1,0:T(8,128)(2,1)} %get-tuple-element.89.proj_ref), custom_call_target="tpu_custom_call" | custom-call | flops 1073741824 | bytes 6291456 | tf_op jit(solution)/shard_map/attention_sums/pallas_call | solution.py:446
  116.8 1.2 all-to-all-done.2.db_ref
  118.0 1.7 edges.1
  119.8 2.5 %collective-permute-start.4 = (bf16[64,256]{1,0:T(8,128)(2,1)S(1)}, bf16[64,256]{1,0:T(8,128)(2,1)S(1)}, u32[]{:S(2)}, u32[]{:S(2)}) collective-permute-start(bf16[64,256]{1,0:T(8,128)(2,1)S(1)} %get-tuple-element.94), channel_id=1, source_target_pairs={{0,16},{16,32},{32,48},{48,64},{64,80},{80,96},{96,112},{1,17},{17... | collective-permute-start | bytes 98312 | tf_op jit(solution)/shard_map/ppermute | solution.py:787
  122.3 1.3 collective-permute-start.5
  123.6 5.4 %project_sum.1.refs_2_ = bf16[128,16,128]{2,1,0:T(8,128)(2,1)} custom-call(bf16[32,64,256]{2,1,0:T(8,128)(2,1)} %cot_ref.5, bf16[64,32,256]{2,1,0:T(8,128)(2,1)} %copy-done, bf16[32,64,1024]{2,1,0:T(8,128)(2,1)} %get-tuple-element.96.mixed_ref), custom_call_target="tpu_custom_call" | custom-call | flops 1073741824 | bytes 8388608 | tf_op jit(solution)/shard_map/project_sum/pallas_call | solution.py:510
  129.8 1.7 collective-permute-start.6
  131.4 6.4 %project_back.1.cur_ref.before_ref.after_ref = bf16[32,64,1024]{2,1,0:T(8,128)(2,1)} custom-call(bf16[32,64,256]{2,1,0:T(8,128)(2,1)} %cot_ref.5, bf16[64,32,256]{2,1,0:T(8,128)(2,1)} %copy-done, bf16[32,64,1024]{2,1,0:T(8,128)(2,1)} %mixed_slopes.1.slope_ref, bf16[1024,256]{1,0:T(8,128)(2,1)} %wp_ref.5), custom_call_target="tpu_custom_call" | custom-call | flops 1073741824 | bytes 10485760 | tf_op jit(solution)/shard_map/project_back/pallas_call | solution.py:479
  137.8 0.7 pad_maximum_fusion.halo_ref
  138.5 0.7 broadcast_in_dim.15.dkb_ref
  139.2 21.5 %expand_back.1 = (bf16[2048,1024]{1,0:T(8,128)(2,1)}, bf16[128,24,128]{2,1,0:T(8,128)(2,1)}) custom-call(bf16[32,64,1024]{2,1,0:T(8,128)(2,1)} %project_back.1.cur_ref.before_ref.after_ref, bf16[32,64,1024]{2,1,0:T(8,128)(2,1)} %project_back.1.cur_ref.before_ref.after_ref, bf16[32,64,1024]{2,1,0:T(8,128)(2,1)} %project_back.1.cur_ref.before_ref.after_ref, ...), custom_call_target="tpu_custom_call" | custom-call | flops 1073741824 | bytes 20971520 | tf_op jit(solution)/shard_map/expand_back/pallas_call | solution.py:605
  160.7 3.2 %collective-permute-start.10 = (bf16[128,24,128]{2,1,0:T(8,128)(2,1)}, bf16[128,24,128]{2,1,0:T(8,128)(2,1)S(1)}, u32[]{:S(2)}, u32[]{:S(2)}) collective-permute-start(bf16[128,24,128]{2,1,0:T(8,128)(2,1)} %get-tuple-element.113.refs_4_), channel_id=1, source_target_pairs={{0,1},{1,0},{2,3},{3,2},{4,5},{5,4},{6,7},{7,6},{8,9},{9,8},{10,11... | collective-permute-start | bytes 2359304 | tf_op jit(solution)/shard_map/ppermute | solution.py:845
  163.9 2.1 collective-permute-done.10.refs_5_
  166.0 1.1 copy-done.4
  167.2 1.1 join.1
  168.3 10.5 %all-to-all-start.3 = ((bf16[64,56,128]{2,1,0:T(8,128)(2,1)}), bf16[64,56,128]{2,1,0:T(8,128)(2,1)S(1)}, u32[]{:S(2)}, u32[]{:S(2)}) async-start(bf16[64,56,128]{2,1,0:T(8,128)(2,1)} %join.1), calls=%async_computation.3 | async-start | bytes 1835008 | tf_op jit(solution)/shard_map/all_to_all | solution.py:829
  178.8 5.9 %finish.1 = bf16[32,64,256]{2,1,0:T(8,128)(2,1)} custom-call(bf16[2048,1024]{1,0:T(8,128)(2,1)} %get-tuple-element.116.dpre_ref, bf16[32,64,256]{2,1,0:T(8,128)(2,1)} %x_ref.8, bf16[32,64,256]{2,1,0:T(8,128)(2,1)} %cot_ref.5, bf16[64,32,256]{2,1,0:T(8,128)(2,1)} %copy-done, bf16[256,1024]{1,0:T(8,128)(2,1)} %we_ref.7), custom_call_target="tpu_custom_call" | custom-call | flops 1073741824 | bytes 9437184 | tf_op jit(solution)/shard_map/finish/pallas_call | solution.py:637
  184.7 9.7 %all-to-all-done.3.terms_ref = bf16[64,56,128]{2,1,0:T(8,128)(2,1)S(1)} async-done(((bf16[64,56,128]{2,1,0:T(8,128)(2,1)}), bf16[64,56,128]{2,1,0:T(8,128)(2,1)S(1)}, u32[]{:S(2)}, u32[]{:S(2)}) %all-to-all-start.3) | async-done | bytes 917536 | tf_op jit(solution)/shard_map/all_to_all | solution.py:829
  194.7 19.0 %all_to_all.25.own_ref = bf16[64,56,128]{2,1,0:T(8,128)(2,1)S(1)} all-to-all(bf16[64,56,128]{2,1,0:T(8,128)(2,1)S(1)} %fold.1), channel_id=1, replica_groups={{0,2,4,6,8,10,12,14,16,18,20,22,24,26,28,30,32,34,36,38,40,42,44,46,48,..., dimensions={0} | all-to-all | bytes 1835008 | tf_op jit(solution)/shard_map/all_to_all | solution.py:829
  213.7 4.1 %collective-permute-start.11 = (bf16[64,56,128]{2,1,0:T(8,128)(2,1)S(1)}, bf16[64,56,128]{2,1,0:T(8,128)(2,1)S(1)}, u32[]{:S(2)}, u32[]{:S(2)}) collective-permute-start(bf16[64,56,128]{2,1,0:T(8,128)(2,1)S(1)} %all_to_all.25.own_ref), channel_id=1, source_target_pairs={{0,1},{1,0},{2,3},{3,2},{4,5},{5,4},{6,7},{7,6},{8,9},{9,8},{10,11... | collective-permute-start | bytes 2752520 | tf_op jit(solution)/shard_map/ppermute | solution.py:845
  217.7 2.1 collective-permute-done.11.other_ref
  219.8 2.0 unfold.1
  (70 shorter events, 1.7 us)
Async XLA Ops:
  0.6 16.5 %copy-start.10 = (bf16[32,64,256]{2,1,0:T(8,128)(2,1)S(1)}, bf16[32,64,256]{2,1,0:T(8,128)(2,1)}, u32[]{:S(2)}) copy-start(bf16[32,64,256]{2,1,0:T(8,128)(2,1)} %cot_ref.5) | copy-start | bytes 3145732
  1.6 12.7 %collective-permute-start = (bf16[128,256]{1,0:T(8,128)(2,1)S(1)}, bf16[128,256]{1,0:T(8,128)(2,1)S(1)}, u32[]{:S(2)}, u32[]{:S(2)}) collective-permute-start(bf16[128,256]{1,0:T(8,128)(2,1)S(1)} %bitcast.43), channel_id=1, source_target_pairs={{0,16},{16,32},{32,48},{48,64},{64,80},{80,96},{96,112},{1,17},{17... | collective-permute-start | bytes 196616 | tf_op jit(solution)/shard_map/ppermute | solution.py:787
  5.7 8.6 %collective-permute-start.1 = (bf16[128,256]{1,0:T(8,128)(2,1)S(1)}, bf16[128,256]{1,0:T(8,128)(2,1)S(1)}, u32[]{:S(2)}, u32[]{:S(2)}) collective-permute-start(bf16[128,256]{1,0:T(8,128)(2,1)S(1)} %bitcast.42), channel_id=1, source_target_pairs={{16,0},{32,16},{48,32},{64,48},{80,64},{96,80},{112,96},{17,1},{33... | collective-permute-start | bytes 196616 | tf_op jit(solution)/shard_map/ppermute | solution.py:787
  8.1 26.1 %copy-start.17 = (f32[3,3,1024]{2,1,0:T(4,128)S(1)}, f32[3,3,1024]{2,1,0:T(4,128)}, u32[]{:S(2)}) copy-start(f32[3,3,1024]{2,1,0:T(4,128)} %param.16) | copy-start | bytes 110596
  14.3 20.6 %copy-start.13 = (bf16[128,256]{1,0:T(8,128)(2,1)}, bf16[128,256]{1,0:T(8,128)(2,1)S(1)}, u32[]{:S(2)}) copy-start(bf16[128,256]{1,0:T(8,128)(2,1)S(1)} %collective-permute-done) | copy-start | bytes 196612
  14.3 20.6 %copy-start.14 = (bf16[128,256]{1,0:T(8,128)(2,1)}, bf16[128,256]{1,0:T(8,128)(2,1)S(1)}, u32[]{:S(2)}) copy-start(bf16[128,256]{1,0:T(8,128)(2,1)S(1)} %collective-permute-done.1) | copy-start | bytes 196612
  14.6 20.3 %copy-start.15 = (bf16[2,40,256]{2,1,0:T(8,128)(2,1)}, bf16[2,40,256]{2,1,0:T(8,128)(2,1)S(1)}, u32[]{:S(2)}) copy-start(bf16[2,40,256]{2,1,0:T(8,128)(2,1)S(1)} %get-tuple-element.76.own_west_ref) | copy-start | bytes 122884
  14.6 20.3 %copy-start.16 = (bf16[2,40,256]{2,1,0:T(8,128)(2,1)}, bf16[2,40,256]{2,1,0:T(8,128)(2,1)S(1)}, u32[]{:S(2)}) copy-start(bf16[2,40,256]{2,1,0:T(8,128)(2,1)S(1)} %get-tuple-element.77.own_east_ref) | copy-start | bytes 122884
  14.6 3.7 %collective-permute-start.2 = (bf16[2,40,256]{2,1,0:T(8,128)(2,1)S(1)}, bf16[2,40,256]{2,1,0:T(8,128)(2,1)S(1)}, u32[]{:S(2)}, u32[]{:S(2)}) collective-permute-start(bf16[2,40,256]{2,1,0:T(8,128)(2,1)S(1)} %get-tuple-element.77.own_east_ref), channel_id=1, source_target_pairs={{0,1},{1,2},{2,3},{3,4},{4,5},{5,6},{6,7},{7,8},{8,9},{9,10},{10,1... | collective-permute-start | bytes 122888 | tf_op jit(solution)/shard_map/ppermute | solution.py:817
  17.1 3.7 %collective-permute-start.3 = (bf16[2,40,256]{2,1,0:T(8,128)(2,1)S(1)}, bf16[2,40,256]{2,1,0:T(8,128)(2,1)S(1)}, u32[]{:S(2)}, u32[]{:S(2)}) collective-permute-start(bf16[2,40,256]{2,1,0:T(8,128)(2,1)S(1)} %get-tuple-element.76.own_west_ref), channel_id=1, source_target_pairs={{1,0},{2,1},{3,2},{4,3},{5,4},{6,5},{7,6},{8,7},{9,8},{10,9},{11,1... | collective-permute-start | bytes 122888 | tf_op jit(solution)/shard_map/ppermute | solution.py:818
  18.2 16.7 %copy-start.18 = (bf16[2,40,256]{2,1,0:T(8,128)(2,1)}, bf16[2,40,256]{2,1,0:T(8,128)(2,1)S(1)}, u32[]{:S(2)}) copy-start(bf16[2,40,256]{2,1,0:T(8,128)(2,1)S(1)} %collective-permute-done.2.west_ref) | copy-start | bytes 122884
  20.9 14.1 %copy-start.19 = (bf16[2,40,256]{2,1,0:T(8,128)(2,1)}, bf16[2,40,256]{2,1,0:T(8,128)(2,1)S(1)}, u32[]{:S(2)}) copy-start(bf16[2,40,256]{2,1,0:T(8,128)(2,1)S(1)} %collective-permute-done.3.east_ref) | copy-start | bytes 122884
  20.9 31.7 %all-to-all-start.1 = ((bf16[64,32,256]{2,1,0:T(8,128)(2,1)}), bf16[64,32,256]{2,1,0:T(8,128)(2,1)S(1)}, u32[]{:S(2)}, u32[]{:S(2)}) async-start(bf16[64,32,256]{2,1,0:T(8,128)(2,1)} %bitcast.13), calls=%async_computation.1 | async-start | bytes 2097152 | tf_op jit(solution)/shard_map/all_to_all | solution.py:829
  34.9 27.6 %copy-start.20 = (f32[4,15,15]{2,0,1:T(4,128)S(1)}, f32[4,15,15]{2,0,1:T(4,128)}, u32[]{:S(2)}) copy-start(f32[4,15,15]{2,0,1:T(4,128)} %param.20) | copy-start | bytes 10804
  34.9 27.7 %copy-start.21 = (s32[64,64]{0,1:T(8,128)S(1)}, s32[64,64]{0,1:T(8,128)}, u32[]{:S(2)}) copy-start(s32[64,64]{0,1:T(8,128)} %constant.21.clone) | copy-start | bytes 49156
  52.5 21.4 %copy-start.7 = (bf16[256,256]{1,0:T(8,128)(2,1)S(1)}, bf16[256,256]{1,0:T(8,128)(2,1)}, u32[]{:S(2)}) copy-start(bf16[256,256]{1,0:T(8,128)(2,1)} %wout_ref.1) | copy-start | bytes 393220
  52.5 21.4 %copy-start.8 = (bf16[256,256]{1,0:T(8,128)(2,1)S(1)}, bf16[256,256]{1,0:T(8,128)(2,1)}, u32[]{:S(2)}) copy-start(bf16[256,256]{1,0:T(8,128)(2,1)} %constant.22.clone.swap_ref) | copy-start | bytes 393220
  52.5 26.6 %all-to-all-start = ((bf16[64,32,256]{2,1,0:T(8,128)(2,1)}), bf16[64,32,256]{2,1,0:T(8,128)(2,1)S(1)}, u32[]{:S(2)}, u32[]{:S(2)}) async-start(bf16[64,32,256]{2,1,0:T(8,128)(2,1)} %get-tuple-element.78), calls=%async_computation | async-start | bytes 2097152 | tf_op jit(solution)/shard_map/all_to_all | solution.py:829
  74.7 1.0 copy-start.3
  75.6 1.0 copy-start.9
  79.1 1.0 copy-start.11
  93.8 24.1 %all-to-all-start.2 = ((bf16[64,32,256]{2,1,0:T(8,128)(2,1)}), bf16[64,32,256]{2,1,0:T(8,128)(2,1)S(1)}, u32[]{:S(2)}, u32[]{:S(2)}) async-start(bf16[64,32,256]{2,1,0:T(8,128)(2,1)} %get-tuple-element.85), calls=%async_computation.2 | async-start | bytes 2097152 | tf_op jit(solution)/shard_map/all_to_all | solution.py:829
  111.5 6.5 %copy-start.5 = (bf16[32,512]{1,0:T(8,128)(2,1)S(1)}, bf16[32,512]{1,0:T(8,128)(2,1)}, u32[]{:S(2)}) copy-start(bf16[32,512]{1,0:T(8,128)(2,1)} %constant.23.clone.first_ref) | copy-start | bytes 98308
  111.5 6.5 %copy-start.6 = (bf16[32,512]{1,0:T(8,128)(2,1)S(1)}, bf16[32,512]{1,0:T(8,128)(2,1)}, u32[]{:S(2)}) copy-start(bf16[32,512]{1,0:T(8,128)(2,1)} %constant.24.clone.last_ref) | copy-start | bytes 98308
  118.0 1.8 copy-start
  119.8 9.2 %copy-start.1 = (bf16[128,16,128]{2,1,0:T(8,128)(2,1)S(1)}, bf16[128,16,128]{2,1,0:T(8,128)(2,1)}, u32[]{:S(2)}) copy-start(bf16[128,16,128]{2,1,0:T(8,128)(2,1)} %attention_sums.1.refs_0_) | copy-start | bytes 1572868
  119.8 9.2 %collective-permute-start.4 = (bf16[64,256]{1,0:T(8,128)(2,1)S(1)}, bf16[64,256]{1,0:T(8,128)(2,1)S(1)}, u32[]{:S(2)}, u32[]{:S(2)}) collective-permute-start(bf16[64,256]{1,0:T(8,128)(2,1)S(1)} %get-tuple-element.94), channel_id=1, source_target_pairs={{0,16},{16,32},{32,48},{48,64},{64,80},{80,96},{96,112},{1,17},{17... | collective-permute-start | bytes 98312 | tf_op jit(solution)/shard_map/ppermute | solution.py:787
  122.3 6.7 %collective-permute-start.5 = (bf16[64,256]{1,0:T(8,128)(2,1)S(1)}, bf16[64,256]{1,0:T(8,128)(2,1)S(1)}, u32[]{:S(2)}, u32[]{:S(2)}) collective-permute-start(bf16[64,256]{1,0:T(8,128)(2,1)S(1)} %get-tuple-element.95), channel_id=1, source_target_pairs={{16,0},{32,16},{48,32},{64,48},{80,64},{96,80},{112,96},{17,1},{33... | collective-permute-start | bytes 98312 | tf_op jit(solution)/shard_map/ppermute | solution.py:787
  129.0 9.5 %collective-permute-start.8 = (bf16[128,16,128]{2,1,0:T(8,128)(2,1)S(1)}, bf16[128,16,128]{2,1,0:T(8,128)(2,1)S(1)}, u32[]{:S(2)}, u32[]{:S(2)}) collective-permute-start(bf16[128,16,128]{2,1,0:T(8,128)(2,1)S(1)} %copy-done.1), channel_id=1, source_target_pairs={{0,1},{1,0},{2,3},{3,2},{4,5},{5,4},{6,7},{7,6},{8,9},{9,8},{10,11... | collective-permute-start | bytes 1572872 | tf_op jit(solution)/shard_map/ppermute | solution.py:845
  129.1 9.4 %collective-permute-start.9 = (bf16[128,16,128]{2,1,0:T(8,128)(2,1)}, bf16[128,16,128]{2,1,0:T(8,128)(2,1)S(1)}, u32[]{:S(2)}, u32[]{:S(2)}) collective-permute-start(bf16[128,16,128]{2,1,0:T(8,128)(2,1)} %project_sum.1.refs_2_), channel_id=1, source_target_pairs={{0,1},{1,0},{2,3},{3,2},{4,5},{5,4},{6,7},{7,6},{8,9},{9,8},{10,11... | collective-permute-start | bytes 1572872 | tf_op jit(solution)/shard_map/ppermute | solution.py:845
  129.7 8.1 %collective-permute-start.7 = (bf16[40,256]{1,0:T(8,128)(2,1)S(1)}, bf16[40,256]{1,0:T(8,128)(2,1)S(1)}, u32[]{:S(2)}, u32[]{:S(2)}) collective-permute-start(bf16[40,256]{1,0:T(8,128)(2,1)S(1)} %get-tuple-element.138), channel_id=1, source_target_pairs={{1,0},{2,1},{3,2},{4,3},{5,4},{6,5},{7,6},{8,7},{9,8},{10,9},{11,1... | collective-permute-start | bytes 61448 | tf_op jit(solution)/shard_map/ppermute | solution.py:796
  129.8 8.7 %copy-start.12 = (f32[9,1024]{1,0:T(8,128)S(1)}, f32[9,1024]{1,0:T(8,128)}, u32[]{:S(2)}) copy-start(f32[9,1024]{1,0:T(8,128)} %reshape.67.dk_ref) | copy-start | bytes 110596
  129.8 8.0 %collective-permute-start.6 = (bf16[40,256]{1,0:T(8,128)(2,1)S(1)}, bf16[40,256]{1,0:T(8,128)(2,1)S(1)}, u32[]{:S(2)}, u32[]{:S(2)}) collective-permute-start(bf16[40,256]{1,0:T(8,128)(2,1)S(1)} %get-tuple-element.137), channel_id=1, source_target_pairs={{0,1},{1,2},{2,3},{3,4},{4,5},{5,6},{6,7},{7,8},{8,9},{9,10},{10,1... | collective-permute-start | bytes 61448 | tf_op jit(solution)/shard_map/ppermute | solution.py:793
  139.2 26.8 %copy-start.2 = (bf16[128,16,128]{2,1,0:T(8,128)(2,1)S(1)}, bf16[128,16,128]{2,1,0:T(8,128)(2,1)}, u32[]{:S(2)}) copy-start(bf16[128,16,128]{2,1,0:T(8,128)(2,1)} %project_sum.1.refs_2_) | copy-start | bytes 1572868
  160.7 5.3 %collective-permute-start.10 = (bf16[128,24,128]{2,1,0:T(8,128)(2,1)}, bf16[128,24,128]{2,1,0:T(8,128)(2,1)S(1)}, u32[]{:S(2)}, u32[]{:S(2)}) collective-permute-start(bf16[128,24,128]{2,1,0:T(8,128)(2,1)} %get-tuple-element.113.refs_4_), channel_id=1, source_target_pairs={{0,1},{1,0},{2,3},{3,2},{4,5},{5,4},{6,7},{7,6},{8,9},{9,8},{10,11... | collective-permute-start | bytes 2359304 | tf_op jit(solution)/shard_map/ppermute | solution.py:845
  166.0 1.1 copy-start.4
  168.3 26.2 %all-to-all-start.3 = ((bf16[64,56,128]{2,1,0:T(8,128)(2,1)}), bf16[64,56,128]{2,1,0:T(8,128)(2,1)S(1)}, u32[]{:S(2)}, u32[]{:S(2)}) async-start(bf16[64,56,128]{2,1,0:T(8,128)(2,1)} %join.1), calls=%async_computation.3 | async-start | bytes 1835008 | tf_op jit(solution)/shard_map/all_to_all | solution.py:829
  213.7 6.2 %collective-permute-start.11 = (bf16[64,56,128]{2,1,0:T(8,128)(2,1)S(1)}, bf16[64,56,128]{2,1,0:T(8,128)(2,1)S(1)}, u32[]{:S(2)}, u32[]{:S(2)}) collective-permute-start(bf16[64,56,128]{2,1,0:T(8,128)(2,1)S(1)} %all_to_all.25.own_ref), channel_id=1, source_target_pairs={{0,1},{1,0},{2,3},{3,2},{4,5},{5,4},{6,7},{7,6},{8,9},{9,8},{10,11... | collective-permute-start | bytes 2752520 | tf_op jit(solution)/shard_map/ppermute | solution.py:845
